TPU v7x, 32 devices: a whole 2x2x4 slice. The times are simulated.
32 devices in a mesh: stream: 8 (over y, x, core), strip: 4 (over z).
Axes of the slice: x: 2, y: 2, z: 4, core: 2. Of those that a mesh axis runs over, the one named last changes fastest.
Arguments:
- loader_rows: bfloat16 [8, 512, 48], P('stream', 'strip'), may hold values from -12 to 12
- load_owner: int32 [8, 512], P('stream', 'strip'), may hold values from 0 to 7, as said below
- load_slot: int32 [8, 512], P('stream', 'strip'), may hold values from 0 to 127, as said below
- valid_frames: int32 [8], P('stream'), may hold values from 1 to 8
- next_owner: int32 [8], P('stream'), may hold values from 0 to 7, as said below
- pixel_cache: bfloat16 [8, 2, 64, 48], P('stream', None, 'strip'), may hold values from -6 to 6
- act_cache: bfloat16 [8, 2, 64, 16, 128], P('stream', None, 'strip'), may hold values from -4 to 4
- res_cache: bfloat16 [8, 2, 64, 16, 128], P('stream', None, 'strip'), may hold values from -8 to 8
- stem_weight: bfloat16 [3, 3, 3, 3, 128], replicated, may hold values from -0.625 to 0.625
- norm_gain: float32 [128], replicated, may hold values from 0.1 to 1.9
- norm_bias: float32 [128], replicated, may hold values from -2.5 to 2.5
- conv_weight: bfloat16 [3, 3, 3, 128, 128], replicated, may hold values from -0.109375 to 0.109375
- down_weight: bfloat16 [3, 3, 3, 128, 256], replicated, may hold values from -0.109375 to 0.109375
Outputs:
- latents: bfloat16 [8, 4, 32, 8, 256], P('stream', None, 'strip')
- next_pixel_cache: bfloat16 [8, 2, 64, 48], P('stream', None, 'strip')
- next_act_cache: bfloat16 [8, 2, 64, 16, 128], P('stream', None, 'strip')
- next_res_cache: bfloat16 [8, 2, 64, 16, 128], P('stream', None, 'strip')
Inputs may be any that keep to these rules, and one draw needn't show every extreme that they name: `load_owner`: among the 128 positions of one stream that fall in one strip, every stream is named by exactly 16. `load_slot`: over all loader rows of strip j that name the same owner, the slots are all different, so each owner receives every slot of strip j exactly once. `next_owner`: A permutation made by passes over the index bits 0, 1, 2 and so on in this order, each pass exchanging some pairs of indices that differ only in that bit.
All inputs are finite; a program needn't handle non-finite values.
Results may differ from a plain program's by a relative error of at most 0.0055.
Values may be sent and summed in bfloat16 or wider, within the bound.
No kernel may reach another device: no remote copies, remote signals or barrier semaphores. Data moves between devices by JAX's collectives and lax.ppermute only.
A program may use at most 64 MiB of HBM per device.

v0:
```python
import jax
import jax.numpy as jnp
from jax import lax
from jax.sharding import PartitionSpec as P

FRAMES = 8
GROUPS = 32


EPSILON = 1e-06


def extended_2(value, sides, width):
    for axis, dim in sides:
        size, length = (lax.axis_size(axis), value.shape[dim])
        up = [(i, (i + 1) % size) for i in range(size - 1)]
        down = [(j, i) for i, j in up]
        last = lax.slice_in_dim(value, length - width, length, axis=dim)
        first = lax.slice_in_dim(value, 0, width, axis=dim)
        before = lax.ppermute(last, axis, up)
        after = lax.ppermute(first, axis, down)
        value = jnp.concatenate([before, value, after], axis=dim)
    return value


def passed_along(value, axis, by):
    size = lax.axis_size(axis)
    pairs = [(i, i + by) for i in range(size) if 0 <= i + by < size]
    return lax.ppermute(value, axis, pairs)


def shortened(value):
    return jax.tree.map(lambda a: a.astype(jnp.bfloat16) if a.dtype == jnp.float32 else a, value)


def partner_2(value, axis, stride):
    mask = 2**stride
    pairs = [(source, source ^ mask) for source in range(lax.axis_size(axis))]
    return lax.ppermute(value, axis, pairs)


def conv_same(padded, weight):
    frame_count = padded.shape[0] - 2
    row_count = padded.shape[1] - 2
    col_count = padded.shape[2] - 2
    summed = None
    for tap_t in range(3):
        for tap_h in range(3):
            stacked = jnp.concatenate(
                [
                    padded[
                        tap_t : tap_t + frame_count,
                        tap_h : tap_h + row_count,
                        tap_w : tap_w + col_count,
                        :,
                    ]
                    for tap_w in range(3)
                ],
                axis=-1,
            )
            kernel = weight[tap_t, tap_h].reshape(-1, weight.shape[-1])
            partial_value = jnp.einsum(
                "trwc,co->trwo", stacked, kernel, preferred_element_type=jnp.float32
            )
            summed = partial_value if summed is None else summed + partial_value
    return summed


def conv_down(padded, weight):
    out_t = (padded.shape[0] - 2) // 2
    out_h = (padded.shape[1] - 1) // 2
    out_w = (padded.shape[2] - 1) // 2
    even_t = 2 * out_t + 2
    even_h = 2 * out_h + 2
    even_w = 2 * out_w + 2
    extended = jnp.pad(
        padded,
        (
            (0, even_t - padded.shape[0]),
            (0, even_h - padded.shape[1]),
            (0, even_w - padded.shape[2]),
            (0, 0),
        ),
    )
    channels = extended.shape[3]
    parity = extended.reshape(even_t // 2, 2, even_h // 2, 2, even_w // 2, 2, channels).transpose(
        1, 3, 5, 0, 2, 4, 6
    )
    summed = None
    for tap_t in range(3):
        for tap_h in range(3):
            pieces = []
            for tap_w in range(3):
                plane = parity[tap_t % 2, tap_h % 2, tap_w % 2]
                pieces.append(
                    plane[
                        tap_t // 2 : tap_t // 2 + out_t,
                        tap_h // 2 : tap_h // 2 + out_h,
                        tap_w // 2 : tap_w // 2 + out_w,
                        :,
                    ]
                )
            stacked = jnp.concatenate(pieces, axis=-1)
            kernel = weight[tap_t, tap_h].reshape(-1, weight.shape[-1])
            partial_value = jnp.einsum(
                "trwc,co->trwo", stacked, kernel, preferred_element_type=jnp.float32
            )
            summed = partial_value if summed is None else summed + partial_value
    return summed


def normalize(hidden_in, mean_val, inv_std, gain_row, offset_row):
    dims_in = hidden_in.shape
    grouped = hidden_in.astype(jnp.float32).reshape(
        dims_in[:-1] + (mean_val.shape[1], dims_in[-1] // mean_val.shape[1])
    )
    centered = (grouped - mean_val[:, None, None, :, None]) * inv_std[:, None, None, :, None]
    scaled = centered.reshape(dims_in) * gain_row + offset_row
    return jax.nn.silu(scaled).astype(jnp.bfloat16)


def route(carried, target, stream_pos, section_count, mover):
    for bit_pos in range(section_count):
        partner = mover(carried + (target,), bit_pos)
        keep_mine = target // (1 << bit_pos) % 2 == stream_pos // (1 << bit_pos) % 2
        carried = tuple(
            (
                jnp.where(keep_mine, own_part, other_part)
                for own_part, other_part in zip(carried, partner[:-1])
            )
        )
        target = jnp.where(keep_mine, target, partner[-1])
    return carried


def body(
    loader_rows,
    load_owner,
    load_slot,
    valid_frames,
    next_owner,
    pixel_cache,
    act_cache,
    res_cache,
    stem_weight,
    norm_gain,
    norm_bias,
    conv_weight,
    down_weight,
):
    stream_count = lax.axis_size("stream")
    strip_count = lax.axis_size("strip")
    stream_pos = lax.axis_index("stream")
    section_count = stream_count.bit_length() - 1
    row_block = pixel_cache.shape[2]
    col_count = act_cache.shape[3]
    channels = act_cache.shape[4]
    rows_in = loader_rows[0]
    owner_list = load_owner[0]
    slot_list = load_slot[0]
    row_fill = rows_in.shape[0]
    per_peer = row_fill // stream_count
    onehot = (owner_list[:, None] == jnp.arange(stream_count, dtype=jnp.int32)[None, :]).astype(
        jnp.int32
    )
    rank_in = jnp.sum(jnp.cumsum(onehot, axis=0) * onehot, axis=1) - 1
    send_pos = owner_list * per_peer + rank_in
    order_in = (
        jnp.zeros((row_fill,), jnp.int32).at[send_pos].set(jnp.arange(row_fill, dtype=jnp.int32))
    )
    send_rows = rows_in[order_in].reshape(stream_count, per_peer, rows_in.shape[1])
    send_slots = slot_list[order_in].reshape(stream_count, per_peer)
    got_rows, got_slots = (
        lax.all_to_all(send_rows, "stream", split_axis=0, concat_axis=0, tiled=True),
        lax.all_to_all(send_slots, "stream", split_axis=0, concat_axis=0, tiled=True),
    )
    got_rows = got_rows.reshape(row_fill, rows_in.shape[1])
    got_slots = got_slots.reshape(row_fill)
    placing = (
        jnp.zeros((row_fill,), jnp.int32).at[got_slots].set(jnp.arange(row_fill, dtype=jnp.int32))
    )
    pixels = got_rows[placing].reshape(FRAMES, row_block, rows_in.shape[1])
    valid_count = valid_frames[0]
    target = next_owner[0]
    full_pix = jnp.concatenate([pixel_cache[0], pixels], 0)
    new_pix = lax.dynamic_slice_in_dim(full_pix, valid_count, 2, 0)
    rimmed = extended_2(full_pix, (("strip", 1),), 1)
    planes = rimmed.reshape(FRAMES + 2, row_block + 2, 3, col_count).transpose(0, 1, 3, 2)
    planes = jnp.pad(planes, ((0, 0), (0, 0), (1, 1), (0, 0)))
    stem_out = conv_same(planes, stem_weight).astype(jnp.bfloat16)
    grouped = stem_out.astype(jnp.float32).reshape(
        FRAMES, row_block, col_count, GROUPS, channels // GROUPS
    )
    sum_one = jnp.sum(grouped, axis=(1, 2, 4))
    sum_two = jnp.sum(grouped * grouped, axis=(1, 2, 4))
    sum_one, sum_two = lax.psum((sum_one, sum_two), "strip")
    cell_count = row_block * strip_count * col_count * (channels // GROUPS)
    mean_val = sum_one / cell_count
    inv_std = lax.rsqrt(sum_two / cell_count - mean_val * mean_val + EPSILON)
    act_now = normalize(stem_out, mean_val, inv_std, norm_gain, norm_bias)
    full_act = jnp.concatenate([act_cache[0], act_now], 0)
    new_act = lax.dynamic_slice_in_dim(full_act, valid_count, 2, 0)
    rimmed_act = extended_2(full_act, (("strip", 1),), 1)
    padded_act = jnp.pad(rimmed_act, ((0, 0), (0, 0), (1, 1), (0, 0)))
    res_out = (stem_out.astype(jnp.float32) + conv_same(padded_act, conv_weight)).astype(
        jnp.bfloat16
    )
    full_res = jnp.concatenate([res_cache[0], res_out], 0)
    upper_row = passed_along(full_res[:, -1:], "strip", 1)
    new_res = lax.dynamic_slice_in_dim(full_res, valid_count, 2, 0)
    sent_pix, sent_act, sent_res = route(
        (new_pix, new_act, new_res),
        target,
        stream_pos,
        section_count,
        lambda values, bit_pos: partner_2(
            (values[0], values[1], values[2], shortened(values[3])), "stream", bit_pos
        ),
    )
    padded_res = jnp.concatenate([upper_row, full_res], 1)
    padded_res = jnp.pad(padded_res, ((0, 0), (0, 0), (1, 0), (0, 0)))
    latent = conv_down(padded_res, down_weight)
    live_frame = 2 * jnp.arange(FRAMES // 2, dtype=jnp.int32) < valid_count
    latent = jnp.where(live_frame[:, None, None, None], latent, jnp.zeros((), jnp.float32)).astype(
        jnp.bfloat16
    )
    return (latent[None], sent_pix[None], sent_act[None], sent_res[None])


def solution(mesh):
    in_specs = (
        P("stream", "strip", None),
        P("stream", "strip"),
        P("stream", "strip"),
        P("stream"),
        P("stream"),
        P("stream", None, "strip", None),
        P("stream", None, "strip", None, None),
        P("stream", None, "strip", None, None),
        P(),
        P(),
        P(),
        P(),
        P(),
    )
    out_specs = (
        P("stream", None, "strip", None, None),
        P("stream", None, "strip", None),
        P("stream", None, "strip", None, None),
        P("stream", None, "strip", None, None),
    )
    return jax.shard_map(body, mesh=mesh, in_specs=in_specs, out_specs=out_specs, check_vma=False)
```

profile of v0, /device:TPU:0, one launch (start us, length us, event | category | flops | bytes accessed | tf_op | source)
XLA Modules:
  0.0 122.4 jit_solution(10474082763816171772)
XLA Ops:
  0.7 0.8 fusion.202
  1.7 0.9 select_reduce_fusion
  2.6 0.7 fusion.218
  3.3 1.0 scatter_custom_fusion
  4.3 1.2 %gather_fusion.1 = s32[128]{0:T(128)S(1)} fusion(s32[128]{0:T(128)S(1)} %bitcast.200, s32[1024]{0:T(1024)S(1)} %pad_clamp_fusion.1), kind=kCustom, calls=%fused_computation.1 | custom fusion | bytes 1536 | tf_op jit(solution)/shard_map/gather | solution.py:172
  5.5 0.7 all_to_all.10
  6.2 5.2 %all-to-all-start.1 = ((s32[8,1,16]{2,1,0:T(1,128)}), s32[8,1,16]{2,1,0:T(1,128)S(1)}, u32[]{:S(2)}, u32[]{:S(2)}) async-start(s32[8,1,16]{2,1,0:T(1,128)} %bitcast.11), calls=%async_computation.1 | async-start | bytes 8192 | tf_op jit(solution)/shard_map/all_to_all | solution.py:175
  12.6 0.8 copy.27
  13.4 0.7 gather_fusion
  14.1 0.7 reshape.207
  14.8 0.8 fusion.264
  15.8 0.9 fusion.253
  17.4 0.9 fusion.251
  19.0 3.0 %collective-permute-start.6 = (s32[]{:T(128)}, s32[]{:T(128)}, u32[]{:S(2)}, u32[]{:S(2)}) collective-permute-start(s32[]{:T(128)} %select_n.143), channel_id=1, source_target_pairs={{0,8},{4,12},{8,0},{12,4},{16,24},{20,28},{24,16},{28,20},{1,9},{5... | collective-permute-start | bytes 20 | tf_op jit(solution)/shard_map/ppermute | solution.py:39
  22.0 0.7 collective-permute-done.6
  23.4 3.9 %all-to-all-start = ((bf16[8,2,384]{2,1,0:T(2,128)(2,1)}), bf16[8,2,384]{2,1,0:T(2,128)(2,1)S(1)}, u32[]{:S(2)}, u32[]{:S(2)}) async-start(bf16[8,2,384]{2,1,0:T(2,128)(2,1)} %reshape.207), calls=%async_computation | async-start | bytes 24576 | tf_op jit(solution)/shard_map/all_to_all | solution.py:174
  27.8 0.7 reduce.7
  28.5 1.0 scatter_custom_fusion.1
  29.5 2.5 %all-to-all-done = bf16[8,2,384]{2,1,0:T(2,128)(2,1)S(1)} async-done(((bf16[8,2,384]{2,1,0:T(2,128)(2,1)}), bf16[8,2,384]{2,1,0:T(2,128)(2,1)S(1)}, u32[]{:S(2)}, u32[]{:S(2)}) %all-to-all-start) | async-done | bytes 12320 | tf_op jit(solution)/shard_map/all_to_all | solution.py:174
  32.1 0.7 gather_fusion.2
  33.0 3.5 %collective-permute-start = (bf16[10,1,48]{1,2,0:T(8,128)(2,1)S(1)}, bf16[10,1,48]{1,2,0:T(8,128)(2,1)S(1)}, u32[]{:S(2)}, u32[]{:S(2)}) collective-permute-start(bf16[10,1,48]{1,2,0:T(8,128)(2,1)S(1)} %copy.29), channel_id=1, source_target_pairs={{0,1},{1,2},{2,3},{4,5},{5,6},{6,7},{8,9},{9,10},{10,11},{12,13},{... | collective-permute-start | bytes 2888 | tf_op jit(solution)/shard_map/ppermute | solution.py:20
  36.7 1.5 %collective-permute-start.1 = (bf16[10,1,48]{1,2,0:T(8,128)(2,1)S(1)}, bf16[10,1,48]{1,2,0:T(8,128)(2,1)S(1)}, u32[]{:S(2)}, u32[]{:S(2)}) collective-permute-start(bf16[10,1,48]{1,2,0:T(8,128)(2,1)S(1)} %copy.30), channel_id=1, source_target_pairs={{1,0},{2,1},{3,2},{5,4},{6,5},{7,6},{9,8},{10,9},{11,10},{13,12},{... | collective-permute-start | bytes 2888 | tf_op jit(solution)/shard_map/ppermute | solution.py:21
  38.4 0.6 collective-permute-done
  39.0 4.4 %collective-permute-done.1 = bf16[10,1,48]{1,2,0:T(8,128)(2,1)S(1)} collective-permute-done((bf16[10,1,48]{1,2,0:T(8,128)(2,1)S(1)}, bf16[10,1,48]{1,2,0:T(8,128)(2,1)S(1)}, u32[]{:S(2)}, u32[]{:S(2)}) %collective-permute-start.1) | collective-permute-done | bytes 992 | tf_op jit(solution)/shard_map/ppermute | solution.py:21
  43.6 1.1 copy.32
  44.7 3.8 %pad_slice_fusion.1 = (bf16[8,16,16,3]{3,2,1,0:T(8,128)(2,1)S(1)}, bf16[8,16,16,3]{3,2,1,0:T(8,128)(2,1)S(1)}, bf16[8,16,16,3]{3,2,1,0:T(8,128)(2,1)S(1)}, bf16[...) fusion(bf16[10,18,16,3]{3,2,1,0:T(8,128)(2,1)S(1)} %bitcast.201), kind=kLoop, calls=%fused_computation.13 | loop fusion | bytes 2019328 | tf_op jit(solution)/shard_map/slice | solution.py:51
  48.5 0.7 fusion.254
  49.2 0.6 fusion.108
  49.8 0.6 convolution_add_fusion.7
  50.4 0.6 convolution_add_fusion.6
  51.0 0.6 convolution_add_fusion.5
  51.6 0.6 convolution_add_fusion.4
  52.2 0.6 convolution_add_fusion.3
  52.8 0.6 convolution_add_fusion.2
  53.4 0.6 convolution_add_fusion.1
  54.1 0.7 convert_reduce_fusion
  55.1 17.4 %all-reduce.4 = (f32[8,32]{0,1:T(8,128)S(1)}, f32[8,32]{0,1:T(8,128)S(1)}) all-reduce(f32[8,32]{0,1:T(8,128)S(1)} %reduce_sum.47, f32[8,32]{0,1:T(8,128)S(1)} %reduce_sum.44), channel_id=1, replica_groups=mesh['stream'=8,'strip'=4] {'strip'}, use_global_device_ids=true, to_apply=%region_9.10 | all-reduce | flops 512 | bytes 4096 | tf_op jit(solution)/shard_map/psum | solution.py:196
  73.2 0.7 collective-permute-start.8
  73.9 3.0 %collective-permute-done.8 = bf16[2,16,48]{2,1,0:T(8,128)(2,1)S(1)} collective-permute-done((bf16[2,16,48]{2,1,0:T(8,128)(2,1)S(1)}, bf16[2,16,48]{2,1,0:T(8,128)(2,1)S(1)}, u32[]{:S(2)}, u32[]{:S(2)}) %collective-permute-start.8) | collective-permute-done | bytes 3104 | tf_op jit(solution)/shard_map/ppermute | solution.py:39
  77.5 1.3 %collective-permute-start.2 = (bf16[10,1,16,128]{3,2,1,0:T(8,128)(2,1)S(1)}, bf16[10,1,16,128]{3,2,1,0:T(8,128)(2,1)S(1)}, u32[]{:S(2)}, u32[]{:S(2)}) collective-permute-start(bf16[10,1,16,128]{3,2,1,0:T(8,128)(2,1)S(1)} %get-tuple-element.93), channel_id=1, source_target_pairs={{0,1},{1,2},{2,3},{4,5},{5,6},{6,7},{8,9},{9,10},{10,11},{12,13},{... | collective-permute-start | bytes 122888 | tf_op jit(solution)/shard_map/ppermute | solution.py:20
  78.8 1.5 %collective-permute-start.3 = (bf16[10,1,16,128]{3,2,1,0:T(8,128)(2,1)S(1)}, bf16[10,1,16,128]{3,2,1,0:T(8,128)(2,1)S(1)}, u32[]{:S(2)}, u32[]{:S(2)}) collective-permute-start(bf16[10,1,16,128]{3,2,1,0:T(8,128)(2,1)S(1)} %get-tuple-element.94), channel_id=1, source_target_pairs={{1,0},{2,1},{3,2},{5,4},{6,5},{7,6},{9,8},{10,9},{11,10},{13,12},{... | collective-permute-start | bytes 122888 | tf_op jit(solution)/shard_map/ppermute | solution.py:21
  80.5 0.6 select_bitcast_fusion.2
  81.1 3.5 %collective-permute-done.3 = bf16[10,1,16,128]{3,2,1,0:T(8,128)(2,1)S(1)} collective-permute-done((bf16[10,1,16,128]{3,2,1,0:T(8,128)(2,1)S(1)}, bf16[10,1,16,128]{3,2,1,0:T(8,128)(2,1)S(1)}, u32[]{:S(2)}, u32[]{:S(2)}) %collective-permute-start.3) | collective-permute-done | bytes 40992 | tf_op jit(solution)/shard_map/ppermute | solution.py:21
  84.7 0.6 select_maximum_fusion
  85.3 2.5 %fusion.252 = (bf16[8,16,16,128]{3,2,1,0:T(8,128)(2,1)S(1)}, bf16[8,16,16,128]{3,2,1,0:T(8,128)(2,1)S(1)}, bf16[8,16,16,128]{3,2,1,0:T(8,128)(2,1)S(1)}, bf16[8,...) fusion(bf16[10,18,18,128]{3,2,1,0:T(8,128)(2,1)S(1)} %select_ma, ...), kind=kLoop, calls=%fused_computation.334 | loop fusion | bytes 18874368 | tf_op jit(solution)/shard_map/slice | solution.py:51
  87.9 0.8 fusion.255
  91.5 0.6 fusion.22
  94.2 0.7 fusion.76
  94.8 0.6 fusion.79
  95.7 0.6 fusion.85
  96.6 3.7 %collective-permute-start.4 = (bf16[10,1,16,128]{3,2,1,0:T(8,128)(2,1)S(1)}, bf16[10,1,16,128]{3,2,1,0:T(8,128)(2,1)S(1)}, u32[]{:S(2)}, u32[]{:S(2)}) collective-permute-start(bf16[10,1,16,128]{3,2,1,0:T(8,128)(2,1)S(1)} %fusion.205), channel_id=1, source_target_pairs={{0,1},{1,2},{2,3},{4,5},{5,6},{6,7},{8,9},{9,10},{10,11},{12,13},{... | collective-permute-start | bytes 122888 | tf_op jit(solution)/shard_map/ppermute | solution.py:29
  100.3 0.7 fusion.201
  101.0 0.9 collective-permute-done.4
  106.5 0.9 fusion.90
  107.3 0.9 broadcast_select_fusion.1
  108.4 0.9 broadcast_select_fusion
  109.3 2.1 %collective-permute-start.14 = (bf16[2,16,16,128]{3,2,1,0:T(8,128)(2,1)S(1)}, bf16[2,16,16,128]{3,2,1,0:T(8,128)(2,1)S(1)}, u32[]{:S(2)}, u32[]{:S(2)}) collective-permute-start(bf16[2,16,16,128]{3,2,1,0:T(8,128)(2,1)S(1)} %broadcast_select_fusion), channel_id=1, source_target_pairs={{0,8},{4,12},{8,0},{12,4},{16,24},{20,28},{24,16},{28,20},{1,9},{5... | collective-permute-start | bytes 393224 | tf_op jit(solution)/shard_map/ppermute | solution.py:39
  111.4 3.4 %collective-permute-done.11 = bf16[2,16,16,128]{3,2,1,0:T(8,128)(2,1)S(1)} collective-permute-done((bf16[2,16,16,128]{3,2,1,0:T(8,128)(2,1)S(1)}, bf16[2,16,16,128]{3,2,1,0:T(8,128)(2,1)S(1)}, u32[]{:S(2)}, u32[]{:S(2)}) %collective-permute-start.11) | collective-permute-done | bytes 131104 | tf_op jit(solution)/shard_map/ppermute | solution.py:39
  114.8 1.3 %collective-permute-done.14 = bf16[2,16,16,128]{3,2,1,0:T(8,128)(2,1)S(1)} collective-permute-done((bf16[2,16,16,128]{3,2,1,0:T(8,128)(2,1)S(1)}, bf16[2,16,16,128]{3,2,1,0:T(8,128)(2,1)S(1)}, u32[]{:S(2)}, u32[]{:S(2)}) %collective-permute-start.14) | collective-permute-done | bytes 131104 | tf_op jit(solution)/shard_map/ppermute | solution.py:39
  116.1 0.8 collective-permute-start.15
  116.9 3.4 %collective-permute-done.12 = bf16[2,16,16,128]{3,2,1,0:T(8,128)(2,1)S(1)} collective-permute-done((bf16[2,16,16,128]{3,2,1,0:T(8,128)(2,1)S(1)}, bf16[2,16,16,128]{3,2,1,0:T(8,128)(2,1)S(1)}, u32[]{:S(2)}, u32[]{:S(2)}) %collective-permute-start.12) | collective-permute-done | bytes 131104 | tf_op jit(solution)/shard_map/ppermute | solution.py:39
  120.3 0.7 select_bitcast_fusion.1
  120.9 0.7 collective-permute-done.15
  121.7 0.7 select_bitcast_fusion
  (125 shorter events, 14.1 us)
Async XLA Ops:
  0.6 3.6 %copy-start = (s32[1,128]{1,0:T(1,128)S(1)}, s32[1,128]{1,0:T(1,128)}, u32[]{:S(2)}) copy-start(s32[1,128]{1,0:T(1,128)} %param.15) | copy-start | bytes 1540
  0.6 15.2 %copy-start.5 = (bf16[3,3,3,128,128]{4,3,2,1,0:T(8,128)(2,1)S(1)}, bf16[3,3,3,128,128]{4,3,2,1,0:T(8,128)(2,1)}, u32[]{:S(2)}) copy-start(bf16[3,3,3,128,128]{4,3,2,1,0:T(8,128)(2,1)} %param.24) | copy-start | bytes 2654212
  1.5 15.9 %copy-start.3 = (bf16[3,3,3,128,256]{4,3,2,1,0:T(8,128)(2,1)S(1)}, bf16[3,3,3,128,256]{4,3,2,1,0:T(8,128)(2,1)}, u32[]{:S(2)}) copy-start(bf16[3,3,3,128,256]{4,3,2,1,0:T(8,128)(2,1)} %param.25) | copy-start | bytes 5308420
  6.2 17.2 %all-to-all-start.1 = ((s32[8,1,16]{2,1,0:T(1,128)}), s32[8,1,16]{2,1,0:T(1,128)S(1)}, u32[]{:S(2)}, u32[]{:S(2)}) async-start(s32[8,1,16]{2,1,0:T(1,128)} %bitcast.11), calls=%async_computation.1 | async-start | bytes 8192 | tf_op jit(solution)/shard_map/all_to_all | solution.py:175
  11.4 6.9 %collective-permute-start.5 = (s32[]{:T(128)}, s32[]{:T(128)}, u32[]{:S(2)}, u32[]{:S(2)}) collective-permute-start(s32[]{:T(128)} %bitcast.94), channel_id=1, source_target_pairs={{0,4},{4,0},{8,12},{12,8},{16,20},{20,16},{24,28},{28,24},{1,5},{5... | collective-permute-start | bytes 20 | tf_op jit(solution)/shard_map/ppermute | solution.py:39
  17.3 15.5 %copy-start.16 = (bf16[1,2,16,48]{3,2,1,0:T(8,128)(2,1)S(1)}, bf16[1,2,16,48]{3,2,1,0:T(8,128)(2,1)}, u32[]{:S(2)}) copy-start(bf16[1,2,16,48]{3,2,1,0:T(8,128)(2,1)} %param.18) | copy-start | bytes 9220
  19.0 3.7 %collective-permute-start.6 = (s32[]{:T(128)}, s32[]{:T(128)}, u32[]{:S(2)}, u32[]{:S(2)}) collective-permute-start(s32[]{:T(128)} %select_n.143), channel_id=1, source_target_pairs={{0,8},{4,12},{8,0},{12,4},{16,24},{20,28},{24,16},{28,20},{1,9},{5... | collective-permute-start | bytes 20 | tf_op jit(solution)/shard_map/ppermute | solution.py:39
  23.4 8.6 %all-to-all-start = ((bf16[8,2,384]{2,1,0:T(2,128)(2,1)}), bf16[8,2,384]{2,1,0:T(2,128)(2,1)S(1)}, u32[]{:S(2)}, u32[]{:S(2)}) async-start(bf16[8,2,384]{2,1,0:T(2,128)(2,1)} %reshape.207), calls=%async_computation | async-start | bytes 24576 | tf_op jit(solution)/shard_map/all_to_all | solution.py:174
  33.0 6.0 %collective-permute-start = (bf16[10,1,48]{1,2,0:T(8,128)(2,1)S(1)}, bf16[10,1,48]{1,2,0:T(8,128)(2,1)S(1)}, u32[]{:S(2)}, u32[]{:S(2)}) collective-permute-start(bf16[10,1,48]{1,2,0:T(8,128)(2,1)S(1)} %copy.29), channel_id=1, source_target_pairs={{0,1},{1,2},{2,3},{4,5},{5,6},{6,7},{8,9},{9,10},{10,11},{12,13},{... | collective-permute-start | bytes 2888 | tf_op jit(solution)/shard_map/ppermute | solution.py:20
  36.7 6.8 %collective-permute-start.1 = (bf16[10,1,48]{1,2,0:T(8,128)(2,1)S(1)}, bf16[10,1,48]{1,2,0:T(8,128)(2,1)S(1)}, u32[]{:S(2)}, u32[]{:S(2)}) collective-permute-start(bf16[10,1,48]{1,2,0:T(8,128)(2,1)S(1)} %copy.30), channel_id=1, source_target_pairs={{1,0},{2,1},{3,2},{5,4},{6,5},{7,6},{9,8},{10,9},{11,10},{13,12},{... | collective-permute-start | bytes 2888 | tf_op jit(solution)/shard_map/ppermute | solution.py:21
  38.3 34.8 %collective-permute-start.7 = (bf16[2,16,48]{2,1,0:T(8,128)(2,1)S(1)}, bf16[2,16,48]{2,1,0:T(8,128)(2,1)S(1)}, u32[]{:S(2)}, u32[]{:S(2)}) collective-permute-start(bf16[2,16,48]{2,1,0:T(8,128)(2,1)S(1)} %fusion.206), channel_id=1, source_target_pairs={{0,4},{4,0},{8,12},{12,8},{16,20},{20,16},{24,28},{28,24},{1,5},{5... | collective-permute-start | bytes 9224 | tf_op jit(solution)/shard_map/ppermute | solution.py:39
  54.0 18.6 %copy-start.17 = (f32[128]{0:T(128)S(1)}, f32[128]{0:T(128)}, u32[]{:S(2)}) copy-start(f32[128]{0:T(128)} %param.23) | copy-start | bytes 1540
  54.0 18.6 %copy-start.18 = (f32[128]{0:T(128)S(1)}, f32[128]{0:T(128)}, u32[]{:S(2)}) copy-start(f32[128]{0:T(128)} %param.22) | copy-start | bytes 1540
  54.8 18.3 %copy-start.2 = (bf16[1,2,16,16,128]{4,3,2,1,0:T(8,128)(2,1)S(1)}, bf16[1,2,16,16,128]{4,3,2,1,0:T(8,128)(2,1)}, u32[]{:S(2)}) copy-start(bf16[1,2,16,16,128]{4,3,2,1,0:T(8,128)(2,1)} %param.19) | copy-start | bytes 393220
  73.2 3.7 %collective-permute-start.8 = (bf16[2,16,48]{2,1,0:T(8,128)(2,1)S(1)}, bf16[2,16,48]{2,1,0:T(8,128)(2,1)S(1)}, u32[]{:S(2)}, u32[]{:S(2)}) collective-permute-start(bf16[2,16,48]{2,1,0:T(8,128)(2,1)S(1)} %broadcast_select_fusion.4), channel_id=1, source_target_pairs={{0,8},{4,12},{8,0},{12,4},{16,24},{20,28},{24,16},{28,20},{1,9},{5... | collective-permute-start | bytes 9224 | tf_op jit(solution)/shard_map/ppermute | solution.py:39
  76.9 3.7 %collective-permute-start.9 = (bf16[2,16,48]{2,1,0:T(8,128)(2,1)S(1)}, bf16[2,16,48]{2,1,0:T(8,128)(2,1)S(1)}, u32[]{:S(2)}, u32[]{:S(2)}) collective-permute-start(bf16[2,16,48]{2,1,0:T(8,128)(2,1)S(1)} %broadcast_select_fusion.5), channel_id=1, source_target_pairs={{0,16},{4,20},{8,24},{12,28},{16,0},{20,4},{24,8},{28,12},{1,17},{... | collective-permute-start | bytes 9224 | tf_op jit(solution)/shard_map/ppermute | solution.py:39
  77.5 3.7 %collective-permute-start.2 = (bf16[10,1,16,128]{3,2,1,0:T(8,128)(2,1)S(1)}, bf16[10,1,16,128]{3,2,1,0:T(8,128)(2,1)S(1)}, u32[]{:S(2)}, u32[]{:S(2)}) collective-permute-start(bf16[10,1,16,128]{3,2,1,0:T(8,128)(2,1)S(1)} %get-tuple-element.93), channel_id=1, source_target_pairs={{0,1},{1,2},{2,3},{4,5},{5,6},{6,7},{8,9},{9,10},{10,11},{12,13},{... | collective-permute-start | bytes 122888 | tf_op jit(solution)/shard_map/ppermute | solution.py:20
  78.8 5.9 %collective-permute-start.3 = (bf16[10,1,16,128]{3,2,1,0:T(8,128)(2,1)S(1)}, bf16[10,1,16,128]{3,2,1,0:T(8,128)(2,1)S(1)}, u32[]{:S(2)}, u32[]{:S(2)}) collective-permute-start(bf16[10,1,16,128]{3,2,1,0:T(8,128)(2,1)S(1)} %get-tuple-element.94), channel_id=1, source_target_pairs={{1,0},{2,1},{3,2},{5,4},{6,5},{7,6},{9,8},{10,9},{11,10},{13,12},{... | collective-permute-start | bytes 122888 | tf_op jit(solution)/shard_map/ppermute | solution.py:21
  80.3 27.1 %collective-permute-start.10 = (bf16[2,16,16,128]{3,2,1,0:T(8,128)(2,1)S(1)}, bf16[2,16,16,128]{3,2,1,0:T(8,128)(2,1)}, u32[]{:S(2)}, u32[]{:S(2)}) collective-permute-start(bf16[2,16,16,128]{3,2,1,0:T(8,128)(2,1)S(1)} %fusion.200), channel_id=1, source_target_pairs={{0,4},{4,0},{8,12},{12,8},{16,20},{20,16},{24,28},{28,24},{1,5},{5... | collective-permute-start | bytes 393224 | tf_op jit(solution)/shard_map/ppermute | solution.py:39
  87.9 0.9 copy-start.15
  88.8 0.9 copy-start.14
  89.7 0.9 copy-start.13
  90.6 0.9 copy-start.12
  91.5 0.9 copy-start.11
  92.4 0.9 copy-start.10
  93.3 0.9 copy-start.6
  94.8 0.9 copy-start.9
  95.7 0.9 copy-start.4
  96.6 5.3 %collective-permute-start.4 = (bf16[10,1,16,128]{3,2,1,0:T(8,128)(2,1)S(1)}, bf16[10,1,16,128]{3,2,1,0:T(8,128)(2,1)S(1)}, u32[]{:S(2)}, u32[]{:S(2)}) collective-permute-start(bf16[10,1,16,128]{3,2,1,0:T(8,128)(2,1)S(1)} %fusion.205), channel_id=1, source_target_pairs={{0,1},{1,2},{2,3},{4,5},{5,6},{6,7},{8,9},{9,10},{10,11},{12,13},{... | collective-permute-start | bytes 122888 | tf_op jit(solution)/shard_map/ppermute | solution.py:29
  101.0 7.3 %collective-permute-start.13 = (bf16[2,16,16,128]{3,2,1,0:T(8,128)(2,1)}, bf16[2,16,16,128]{3,2,1,0:T(8,128)(2,1)}, u32[]{:S(2)}, u32[]{:S(2)}) collective-permute-start(bf16[2,16,16,128]{3,2,1,0:T(8,128)(2,1)} %fusion.201), channel_id=1, source_target_pairs={{0,4},{4,0},{8,12},{12,8},{16,20},{20,16},{24,28},{28,24},{1,5},{5... | collective-permute-start | bytes 393224 | tf_op jit(solution)/shard_map/ppermute | solution.py:39
  103.4 0.9 copy-start.8
  105.5 0.9 copy-start.7
  106.2 16.1 %copy-start.1 = (s32[1,128]{1,0:T(1,128)S(1)}, s32[1,128]{1,0:T(1,128)}, u32[]{:S(2)}) copy-start(s32[1,128]{1,0:T(1,128)} %param.15) | copy-start | bytes 1540
  108.3 6.5 %collective-permute-start.11 = (bf16[2,16,16,128]{3,2,1,0:T(8,128)(2,1)S(1)}, bf16[2,16,16,128]{3,2,1,0:T(8,128)(2,1)S(1)}, u32[]{:S(2)}, u32[]{:S(2)}) collective-permute-start(bf16[2,16,16,128]{3,2,1,0:T(8,128)(2,1)S(1)} %broadcast_select_fusion.1), channel_id=1, source_target_pairs={{0,8},{4,12},{8,0},{12,4},{16,24},{20,28},{24,16},{28,20},{1,9},{5... | collective-permute-start | bytes 393224 | tf_op jit(solution)/shard_map/ppermute | solution.py:39
  109.3 6.8 %collective-permute-start.14 = (bf16[2,16,16,128]{3,2,1,0:T(8,128)(2,1)S(1)}, bf16[2,16,16,128]{3,2,1,0:T(8,128)(2,1)S(1)}, u32[]{:S(2)}, u32[]{:S(2)}) collective-permute-start(bf16[2,16,16,128]{3,2,1,0:T(8,128)(2,1)S(1)} %broadcast_select_fusion), channel_id=1, source_target_pairs={{0,8},{4,12},{8,0},{12,4},{16,24},{20,28},{24,16},{28,20},{1,9},{5... | collective-permute-start | bytes 393224 | tf_op jit(solution)/shard_map/ppermute | solution.py:39
  114.7 5.5 %collective-permute-start.12 = (bf16[2,16,16,128]{3,2,1,0:T(8,128)(2,1)S(1)}, bf16[2,16,16,128]{3,2,1,0:T(8,128)(2,1)S(1)}, u32[]{:S(2)}, u32[]{:S(2)}) collective-permute-start(bf16[2,16,16,128]{3,2,1,0:T(8,128)(2,1)S(1)} %broadcast_select_fusion.3), channel_id=1, source_target_pairs={{0,16},{4,20},{8,24},{12,28},{16,0},{20,4},{24,8},{28,12},{1,17},{... | collective-permute-start | bytes 393224 | tf_op jit(solution)/shard_map/ppermute | solution.py:39
  116.1 5.5 %collective-permute-start.15 = (bf16[2,16,16,128]{3,2,1,0:T(8,128)(2,1)S(1)}, bf16[2,16,16,128]{3,2,1,0:T(8,128)(2,1)S(1)}, u32[]{:S(2)}, u32[]{:S(2)}) collective-permute-start(bf16[2,16,16,128]{3,2,1,0:T(8,128)(2,1)S(1)} %broadcast_select_fusion.2), channel_id=1, source_target_pairs={{0,16},{4,20},{8,24},{12,28},{16,0},{20,4},{24,8},{28,12},{1,17},{... | collective-permute-start | bytes 393224 | tf_op jit(solution)/shard_map/ppermute | solution.py:39
where the time goes:
time: 123 us; the launch traced here: 122 us
  starting transfers between devices  28.3 us (23%)
  local copies, waits for them, and re-layouts  24.6 us (20%)
  waiting for transfers between devices  24.6 us (20%)
  blocking collectives  17.4 us (14%)
  matrix products  13.5 us (11%)
  other arithmetic  9.84 us (8%)
  between operations  4.11 us (3%)
    psum x1, blocking collectives, body(): sum_one, sum_two = lax.psum((sum_one, sum_two), 'strip')  17.4 us
    ppermute x11, waiting for transfers between devices, partner_2(): return lax.ppermute(value, axis, pairs)  12.6 us
    dot_general x18, matrix products, conv_same(): jnp.einsum('trwc,co->trwo', stacked, kernel, preferred_element_type=jnp.f...  10.9 us
    ppermute x2, waiting for transfers between devices, extended_2(): after = lax.ppermute(first, axis, down)  7.94 us
    ppermute x11, starting transfers between devices, partner_2(): return lax.ppermute(value, axis, pairs)  7.89 us
    slice x4, local copies, waits for them, and re-layouts, conv_same(): padded[tap_t:tap_t + frame_count, tap_h:tap_h + row_count, tap_w:tap_w +...  7.73 us
    all_to_all x1, starting transfers between devices, body(): lax.all_to_all(send_slots, 'stream', split_axis=0, concat_axis=0, tiled=T...  5.17 us
    unnamed x41, local copies, waits for them, and re-layouts  5 us
  transfers between devices with their start and end apart: 18, of which 12 were waited for; matrix products, arithmetic and copies ran while one was open for 31% of the time, Pallas kernels for 0%

commit v1 on v0

v1 whole, which is shorter than its diff:
```python
import functools

import jax
import jax.numpy as jnp
from jax import lax
from jax.experimental import pallas as pl
from jax.experimental.pallas import tpu as pltpu
from jax.sharding import PartitionSpec as P

FRAMES = 8
GROUPS = 32
EPSILON = 1e-06
F32 = jnp.float32
BF16 = jnp.bfloat16
VM = pl.BlockSpec(memory_space=pltpu.VMEM)
SM = pl.BlockSpec(memory_space=pltpu.SMEM)


def iota(shape, axis):
    return lax.broadcasted_iota(jnp.int32, shape, axis)


def dot(a, b):
    return jnp.dot(a, b, preferred_element_type=F32)


def dot_nt(a, b):
    return lax.dot_general(a, b, (((1,), (1,)), ((), ())), preferred_element_type=F32)


def sort_kernel(streams, rows_ref, owner_ref, slot_ref, out_ref, wide):
    fill = rows_ref.shape[0]
    per = fill // streams
    lines = fill // 2
    wide[...] = jnp.zeros(wide.shape, F32)
    wide[:, 0 : rows_ref.shape[1]] = rows_ref[...].astype(F32)
    owner = owner_ref[...]
    onehot = iota((streams, fill), 0) == owner
    hot = jnp.where(onehot, 1.0, 0.0)
    upper = jnp.where(iota((fill, fill), 0) <= iota((fill, fill), 1), 1.0, 0.0).astype(BF16)
    running = dot(hot.astype(BF16), upper)
    rank = jnp.sum(hot * running, axis=0, keepdims=True).astype(jnp.int32) - 1
    half = rank // (per // 2)
    line = owner * (per // 2) + rank - half * (per // 2)
    line = jnp.broadcast_to(line, (lines, fill))
    half = jnp.broadcast_to(half, (lines, fill))
    here = iota((lines, fill), 0) == line
    slot = jnp.broadcast_to(slot_ref[...].astype(F32), (lines, fill))
    data = wide[...].astype(BF16)
    parts = []
    for side in range(2):
        pick = jnp.where(here & (half == side), 1.0, 0.0)
        picked = dot(pick.astype(BF16), data)
        slots = jnp.sum(pick * slot, axis=1, keepdims=True)
        parts.append(jnp.where(iota((lines, 128), 1) == 48, slots, picked))
    out = jnp.where(iota((lines, 128), 1) < 64, parts[0], pltpu.roll(parts[1], 64, 1))
    out_ref[...] = out.astype(BF16)


def band_kernel(sw_ref, out_ref):
    cols = 16
    for tap in range(27):
        b, a, c = tap // 9, tap // 3 % 3, tap % 3
        for w in range(cols):
            row = iota((cols, 128), 0)
            block = jnp.zeros((cols, 128), F32)
            for e in range(3):
                line = (a * 9 + b * 3 + e) * 3 + c
                block = jnp.where(row == w + e - 1, sw_ref[line : line + 1, :], block)
            out_ref[tap * cols : (tap + 1) * cols, w * 128 : (w + 1) * 128] = block.astype(BF16)


def main_kernel(
    strips,
    valid_ref,
    recv_ref,
    pix0_ref,
    pix1_ref,
    pix2_ref,
    pix3_ref,
    band_ref,
    gain_ref,
    bias_ref,
    conv_ref,
    down_ref,
    act_cache_ref,
    res_cache_ref,
    below_ref,
    above_ref,
    lat_ref,
    new_pix_ref,
    new_act_ref,
    new_res_ref,
    pc,
    zs,
    xs,
    stem,
    act,
    res,
    cache,
    rcache,
    act3,
    res3,
    lat,
):
    j = lax.axis_index("strip")
    valid = valid_ref[0]
    rows_all = strips * 16
    pc[...] = jnp.zeros(pc.shape, F32)
    for k, ref in enumerate((pix0_ref, pix1_ref, pix2_ref, pix3_ref)):
        pc[lax.rem(j + strips - k, strips), :, 0:48] = ref[...].astype(F32)
    zs[...] = jnp.zeros(zs.shape, F32)
    lane = iota((128, 128), 1)
    sub = iota((128, 128), 0)
    slot_lane = jnp.where(iota((8, 128), 1) == 48, 1.0, 0.0).astype(BF16)
    crow, cframe = iota((128, 32), 1) % 16, iota((128, 32), 1) // 16
    csub = iota((128, 32), 0)
    for s in range(strips):
        line = recv_ref[s].astype(F32)
        both = jnp.concatenate([line, pltpu.roll(line, 64, 1)], axis=0)
        slots = dot_nt(slot_lane, both.astype(BF16)).astype(jnp.int32)
        frame, row = slots >> 4, slots & 15
        pixels = jnp.where(lane < 48, both, 0.0)
        source = jnp.concatenate([pixels, pc[s]], axis=0).astype(BF16)
        for a in range(3):
            t = frame + 2 - a
            place = jnp.where(t < FRAMES, row * 8 + (t & 1) * 4 + (t >> 1), -1)
            hit = jnp.where(sub.reshape(16, 8, 128) == place[None], 1.0, 0.0).reshape(128, 128)
            ct = cframe - a
            cplace = jnp.where(ct >= 0, crow * 8 + (ct & 1) * 4 + (ct >> 1), -1)
            chit = jnp.where(csub == cplace, 1.0, 0.0)
            placed = dot(jnp.concatenate([hit, chit], axis=1).astype(BF16), source)
            zs[a, 4 + s * 16 : 4 + (s + 1) * 16] = placed.reshape(16, 8, 128)
    line = recv_ref[j].astype(F32)
    both = jnp.concatenate([line, pltpu.roll(line, 64, 1)], axis=0)
    slots = dot_nt(slot_lane, both.astype(BF16)).astype(jnp.int32)
    goal = (slots >> 4) + 2 - valid
    place = jnp.where((goal >= 0) & (goal < 2), goal * 16 + (slots & 15), -1)
    hit = jnp.where(iota((4, 8, 128), 0) * 8 + iota((4, 8, 128), 1) == place[None], 1.0, 0.0)
    cgoal = iota((32, 32), 1) // 16 - valid
    cplace = jnp.where((cgoal >= 0) & (cgoal < 2), cgoal * 16 + iota((32, 32), 1) % 16, -1)
    chit = jnp.where(iota((32, 32), 0) == cplace, 1.0, 0.0)
    source = jnp.concatenate([jnp.where(lane < 48, both, 0.0), pc[j]], axis=0).astype(BF16)
    fresh = dot(jnp.concatenate([hit.reshape(32, 128), chit], axis=1).astype(BF16), source)
    new_pix_ref[...] = fresh[:, 0:48].astype(BF16)
    high = rows_all + 4
    for b in range(3):
        for a in range(3):
            q = (b * 3 + a) * 48
            xs[2 : high + 2, :, q : q + 48] = zs[a, 1 + b : high + 1 + b, :, 0:48]
    full = xs[4 : 4 + rows_all].reshape(rows_all * 8, 432).astype(BF16)
    base = j * 16 + 2
    first, second = xs[pl.ds(base, 11)], xs[pl.ds(base + 8, 11)]
    low = iota((11, 8, 432), 1) < 4
    own_even = jnp.where(low, first, pltpu.roll(second, 4, 1))
    own_odd = jnp.where(low, pltpu.roll(first, 4, 1), second)
    own = jnp.concatenate([own_even, own_odd], axis=0).reshape(176, 432).astype(BF16)
    s1 = jnp.zeros((8, 256), F32)
    s2 = jnp.zeros((8, 256), F32)
    for chunk in range(8):
        weight = band_ref[:, chunk * 256 : (chunk + 1) * 256]
        out = dot(full, weight).astype(BF16).astype(F32).reshape(rows_all, 8, 256)
        s1 = s1 + jnp.sum(out, axis=0)
        s2 = s2 + jnp.sum(out * out, axis=0)
        mine = dot(own, weight).astype(BF16).astype(F32).reshape(2, 11, 8, 256)
        for i in range(2):
            stem[:, 2 * chunk + i] = mine[:, :, :, i * 128 : (i + 1) * 128]
    s1 = s1[:, 0:128] + s1[:, 128:256]
    s2 = s2[:, 0:128] + s2[:, 128:256]
    same = jnp.where(iota((128, 128), 0) // 4 == iota((128, 128), 1) // 4, 1.0, 0.0)
    count = rows_all * 16 * 4
    exact = functools.partial(
        jnp.dot, preferred_element_type=F32, precision=lax.Precision.HIGHEST
    )
    mean = exact(s1, same) / count
    inv = lax.rsqrt(exact(s2, same) / count - mean * mean + EPSILON)
    low8 = iota((8, 128), 0) < 4
    scale = inv * gain_ref[...]
    shift = bias_ref[...] - mean * scale
    scales = (
        jnp.where(low8, scale, pltpu.roll(scale, 4, 0)),
        jnp.where(low8, pltpu.roll(scale, 4, 0), scale),
    )
    shifts = (
        jnp.where(low8, shift, pltpu.roll(shift, 4, 0)),
        jnp.where(low8, pltpu.roll(shift, 4, 0), shift),
    )
    cache[...] = jnp.zeros(cache.shape, F32)
    rcache[...] = jnp.zeros(rcache.shape, F32)
    has_above = jnp.where(j > 0, 1.0, 0.0)
    has_below = jnp.where(j < strips - 1, 1.0, 0.0)
    for f in range(2):
        cache[f, 0:32] = below_ref[f * 32 : f * 32 + 32].astype(F32) * has_above
        cache[f, 32:288] = act_cache_ref[f].reshape(256, 128).astype(F32)
        cache[f, 288:304] = above_ref[f * 16 : f * 16 + 16].astype(F32) * has_below
        rcache[f, 0:16] = below_ref[64 + f * 16 : 80 + f * 16].astype(F32) * has_above
        rcache[f, 16:272] = res_cache_ref[f].reshape(256, 128).astype(F32)
    half = iota((11, 8, 128), 1) // 4
    line_of = j * 16 + iota((11, 8, 128), 0) - 2 + 8 * half
    inside = jnp.where((line_of >= 0) & (line_of < rows_all), 1.0, 0.0)
    start = iota((11, 8, 128), 1) % 4 == 0
    act3[0] = jnp.zeros(act3.shape[1:], BF16)
    act3[17] = jnp.zeros(act3.shape[1:], BF16)

    def activate(w, carry):
        pair = []
        for p in range(2):
            v = stem[p, w] * scales[p] + shifts[p]
            v = (v / (1.0 + jnp.exp(-v)) * inside).astype(BF16).astype(F32)
            act[p, w] = v
            pair.append(v)
        even, odd = pair
        olds = []
        for f in range(2):
            olds.append(
                jnp.stack([cache[f, pl.ds(y * 16 + w, 8, stride=32)] for y in range(11)], axis=0)
            )
        even_late = jnp.where(start, olds[0], pltpu.roll(even, 1, 1))
        odd_late = jnp.where(start, olds[1], pltpu.roll(odd, 1, 1))
        taps = ((even_late, odd_late), (odd_late, even), (even, odd))
        for a in range(3):
            act3[w + 1, :, :, a * 128 : (a + 1) * 128] = jnp.concatenate(taps[a], axis=1).astype(BF16)
        return carry

    lax.fori_loop(0, 16, activate, 0)
    weights = [
        jnp.concatenate([conv_ref[a, b, e] for a in range(3)], axis=0)
        for b in range(3)
        for e in range(3)
    ]
    weights = jnp.concatenate(weights, axis=0)
    keep = jnp.where((j == 0) & (iota((9, 8, 128), 0) == 0) & (iota((9, 8, 128), 1) < 4), 0.0, 1.0)
    for g in range(4):
        w0 = g * 4
        left = jnp.concatenate(
            [
                act3[w0 + e : w0 + e + 4, b : b + 9].reshape(576, 384)
                for b in range(3)
                for e in range(3)
            ],
            axis=1,
        )
        out = dot(left, weights).reshape(4, 9, 16, 128)
        for p in range(2):
            value = out[:, :, p * 8 : (p + 1) * 8] + stem[p, w0 : w0 + 4, 1:10]
            res[p, w0 : w0 + 4] = (value * keep).astype(BF16).astype(F32)
    begin = iota((9, 8, 128), 1) % 4 == 0
    res3[0] = jnp.zeros(res3.shape[1:], F32)

    def delay(w, carry):
        even, odd = res[0, w], res[1, w]
        olds = []
        for f in range(2):
            olds.append(
                jnp.stack([rcache[f, pl.ds(y * 16 + w, 8, stride=32)] for y in range(9)], axis=0)
            )
        res3[w + 1, :, :, 0:128] = jnp.where(begin, olds[0], pltpu.roll(even, 1, 1))
        res3[w + 1, :, :, 128:256] = jnp.where(begin, olds[1], pltpu.roll(odd, 1, 1))
        res3[w + 1, :, :, 256:384] = even
        return carry

    lax.fori_loop(0, 16, delay, 0)
    total = jnp.zeros((256, 256), F32)
    for b in range(3):
        for e in range(3):
            left = jnp.concatenate(
                [res3[2 * k + e, 2 * i + b] for k in range(8) for i in range(4)], axis=0
            ).astype(BF16)
            right = jnp.concatenate([down_ref[a, b, e] for a in range(3)], axis=0)
            total = total + dot(left, right)
    live = 2 * (iota((256, 256), 0) % 4) < valid
    total = jnp.where(live, total, 0.0)
    for o in range(2):
        lat[o] = total[:, o * 128 : (o + 1) * 128]
    for t in range(4):
        for h in range(2):
            for i in range(4):
                for o in range(2):
                    block = lat[o, pl.ds(i * 8 + h * 4 + t, 8, stride=32)]
                    lat_ref[t, h * 4 + i, :, o * 128 : (o + 1) * 128] = block.astype(BF16)
    act_rows = act.reshape(2 * 16 * 11 * 8, 128)
    res_rows = res.reshape(2 * 16 * 9 * 8, 128)
    for i in range(2):
        g = valid + i
        f = jnp.maximum(g - 2, 0)
        parity, step = f & 1, f >> 1
        old = g < 2
        for y in range(16):
            h, y1 = y // 8, y % 8
            at = parity * (16 * 88) + (y1 + 2) * 8 + h * 4 + step
            block = act_rows[pl.ds(at, 16, stride=88)]
            new_act_ref[i, y] = jnp.where(old, act_cache_ref[1, y].astype(F32), block).astype(BF16)
            at = parity * (16 * 72) + (y1 + 1) * 8 + h * 4 + step
            block = res_rows[pl.ds(at, 16, stride=72)]
            new_res_ref[i, y] = jnp.where(old, res_cache_ref[1, y].astype(F32), block).astype(BF16)


def partner(value, axis, stride):
    pairs = [(source, source ^ stride) for source in range(lax.axis_size(axis))]
    return lax.ppermute(value, axis, pairs)


def shifted(value, axis, by):
    size = lax.axis_size(axis)
    return lax.ppermute(value, axis, [(i, (i + by) % size) for i in range(size)])


def body(
    loader_rows,
    load_owner,
    load_slot,
    valid_frames,
    next_owner,
    pixel_cache,
    act_cache,
    res_cache,
    stem_weight,
    norm_gain,
    norm_bias,
    conv_weight,
    down_weight,
):
    streams = lax.axis_size("stream")
    strips = lax.axis_size("strip")
    stream_pos = lax.axis_index("stream")
    sections = streams.bit_length() - 1
    fill = loader_rows.shape[1]
    per = fill // streams
    pix = pixel_cache[0].reshape(32, 48)
    acts, ress = act_cache[0], res_cache[0]
    below = jnp.concatenate([acts[:, 14:16].reshape(64, 128), ress[:, 15].reshape(32, 128)], 0)
    above = acts[:, 0].reshape(32, 128)
    below = shifted(below, "strip", 1)
    above = shifted(above, "strip", -1)
    others = [shifted(pix, "strip", k) for k in range(1, strips)]
    lines = pl.pallas_call(
        functools.partial(sort_kernel, streams),
        out_shape=jax.ShapeDtypeStruct((fill // 2, 128), BF16),
        in_specs=[VM] * 3,
        out_specs=VM,
        scratch_shapes=[pltpu.VMEM((fill, 128), F32)],
    )(loader_rows[0], load_owner, load_slot)
    lines = lines.reshape(1, streams, per // 2, 128)
    lines = jnp.broadcast_to(lines, (strips, streams, per // 2, 128))
    lines = lines.reshape(strips * streams, per // 2, 128)
    recv = lax.all_to_all(lines, ("strip", "stream"), 0, 0, tiled=True)
    recv = recv.reshape(strips, fill // 2, 128)
    band = pl.pallas_call(
        band_kernel,
        out_shape=jax.ShapeDtypeStruct((432, 2048), BF16),
        in_specs=[VM],
        out_specs=VM,
    )(stem_weight.reshape(81, 128).astype(F32))
    rows_all = strips * 16
    latent, new_pix, new_act, new_res = pl.pallas_call(
        functools.partial(main_kernel, strips),
        out_shape=(
            jax.ShapeDtypeStruct((4, 8, 8, 256), BF16),
            jax.ShapeDtypeStruct((32, 48), BF16),
            jax.ShapeDtypeStruct((2, 16, 16, 128), BF16),
            jax.ShapeDtypeStruct((2, 16, 16, 128), BF16),
        ),
        in_specs=[SM] + [VM] * 14,
        out_specs=(VM,) * 4,
        scratch_shapes=[
            pltpu.VMEM((strips, 32, 128), F32),
            pltpu.VMEM((3, rows_all + 8, 8, 128), F32),
            pltpu.VMEM((rows_all + 8, 8, 432), F32),
            pltpu.VMEM((2, 16, 11, 8, 128), F32),
            pltpu.VMEM((2, 16, 11, 8, 128), F32),
            pltpu.VMEM((2, 16, 9, 8, 128), F32),
            pltpu.VMEM((2, 416, 128), F32),
            pltpu.VMEM((2, 384, 128), F32),
            pltpu.VMEM((18, 11, 16, 384), BF16),
            pltpu.VMEM((17, 9, 8, 384), F32),
            pltpu.VMEM((2, 256, 128), F32),
        ],
        compiler_params=pltpu.CompilerParams(vmem_limit_bytes=48 * 1024 * 1024),
    )(
        valid_frames,
        recv,
        pix,
        *others,
        band,
        norm_gain.reshape(1, 128),
        norm_bias.reshape(1, 128),
        conv_weight,
        down_weight,
        acts,
        ress,
        below,
        above,
    )
    carried = (new_pix, new_act, new_res)
    target = next_owner[0]
    for bit in range(sections):
        other = [partner(v, "stream", 1 << bit) for v in carried + (target,)]
        mine = (target >> bit) & 1 == (stream_pos >> bit) & 1
        carried = tuple(jnp.where(mine, a, b) for a, b in zip(carried, other[:-1]))
        target = jnp.where(mine, target, other[-1])
    new_pix, new_act, new_res = carried
    return (latent[None], new_pix.reshape(1, 2, 16, 48), new_act[None], new_res[None])


def solution(mesh):
    in_specs = (
        P("stream", "strip", None),
        P("stream", "strip"),
        P("stream", "strip"),
        P("stream"),
        P("stream"),
        P("stream", None, "strip", None),
        P("stream", None, "strip", None, None),
        P("stream", None, "strip", None, None),
        P(),
        P(),
        P(),
        P(),
        P(),
    )
    out_specs = (
        P("stream", None, "strip", None, None),
        P("stream", None, "strip", None),
        P("stream", None, "strip", None, None),
        P("stream", None, "strip", None, None),
    )
    return jax.shard_map(body, mesh=mesh, in_specs=in_specs, out_specs=out_specs, check_vma=False)
```

time: 123 us -> 69.9 us (0.57)
  blocking collectives: 17.4 us -> 0 us
  Pallas kernels: 0 us -> 16.5 us
  local copies, waits for them, and re-layouts: 24.6 us -> 9.09 us
  matrix products: 13.5 us -> 0 us
  waiting for transfers between devices: 24.6 us -> 13.4 us
  other arithmetic: 9.84 us -> 2.04 us
  starting transfers between devices: 28.3 us -> 24.8 us
    psum x1 -> x0, blocking collectives: 17.4 us -> none  [body(): sum_one, sum_two = lax.psum((sum_one, sum_two), 'strip')]
    pallas_call x0 -> x3, Pallas kernels: none -> 16.5 us  [the longest x1 12.4 us: body(): pl.pallas_call(functools.partial(main_kernel, strips), out_shape=(jax.Sha...]
    dot_general x27 -> x0, matrix products: 13.5 us -> none  [the longest x18 10.9 us: conv_same(): jnp.einsum('trwc,co->trwo', stacked, kernel, preferred_element_type=jnp.f...]
    slice x17 -> x3, local copies, waits for them, and re-layouts: 10.9 us -> 2.12 us  [the longest x1 0.73 us: body(): acts[:, 14:16].reshape(64, 128)]
    ppermute x16, waiting for transfers between devices: 22.1 us -> 13.4 us  [the longest x11 13.4 us: partner(): return lax.ppermute(value, axis, pairs)]
    gather x3 -> x0, local copies, waits for them, and re-layouts: 2.66 us -> none  [the longest x1 1.23 us: body(): send_slots = slot_list[order_in].reshape(stream_count, per_peer)]
    all_to_all x2 -> x1, waiting for transfers between devices: 2.46 us -> 0.01 us  [body(): recv = lax.all_to_all(lines, ('strip', 'stream'), 0, 0, tiled=True)]
    concatenate x12 -> x1, other arithmetic: 2.22 us -> 0.01 us  [body(): jnp.concatenate([acts[:, 14:16].reshape(64, 128), ress[:, 15].reshape(32,...]
  transfers between devices with their start and end apart: 18 -> 17, of which waited for: 12 -> 8; matrix products, arithmetic and copies ran while one was open for 31% -> 7% of each run, Pallas kernels for 0% -> 3%
where the time goes in v1:
time: 69.9 us; the launch traced here: 69.2 us
  starting transfers between devices  24.8 us (35%)
  Pallas kernels  16.5 us (24%)
  waiting for transfers between devices  13.4 us (19%)
  local copies, waits for them, and re-layouts  9.09 us (13%)
  between operations  3.31 us (5%)
  other arithmetic  2.04 us (3%)
    ppermute x11, waiting for transfers between devices, partner(): return lax.ppermute(value, axis, pairs)  13.4 us
    pallas_call x1, Pallas kernels, body(): pl.pallas_call(functools.partial(main_kernel, strips), out_shape=(jax.Sha...  12.4 us
    ppermute x11, starting transfers between devices, partner(): return lax.ppermute(value, axis, pairs)  9.9 us
    ppermute x5, starting transfers between devices, shifted(): lax.ppermute(value, axis, [(i, (i + by) % size) for i in range(size)])  7.65 us
    all_to_all x1, starting transfers between devices, body(): recv = lax.all_to_all(lines, ('strip', 'stream'), 0, 0, tiled=True)  7.3 us
    unnamed x17, local copies, waits for them, and re-layouts  4.23 us
    pallas_call x1, Pallas kernels, body(): pl.pallas_call(band_kernel, out_shape=jax.ShapeDtypeStruct((432, 2048), B...  2.36 us
    pallas_call x1, Pallas kernels, body(): pl.pallas_call(functools.partial(sort_kernel, streams), out_shape=jax.Sha...  1.75 us
  transfers between devices with their start and end apart: 17, of which 8 were waited for; matrix products, arithmetic and copies ran while one was open for 7% of the time, Pallas kernels for 3%

profile of v1, /device:TPU:0, one launch (start us, length us, event | category | flops | bytes accessed | tf_op | source)
XLA Modules:
  0.0 69.2 jit_solution(18104693008369997625)
XLA Ops:
  0.6 0.0 copy-start.3
  0.6 0.0 copy-start.4
  0.7 0.0 copy-start.5
  0.7 0.0 copy-start.6
  0.7 0.0 copy-start.7
  0.7 0.0 copy-start.1
  0.7 1.6 %copy.17 = bf16[1,128,48]{2,1,0:T(8,128)(2,1)} copy(bf16[1,128,48]{1,2,0:T(8,128)(2,1)} %param.13) | data formatting | bytes 24576 | tf_op args[0]
  2.3 1.7 %shard_map.156 = bf16[64,128]{1,0:T(8,128)(2,1)} custom-call(bf16[128,48]{1,0:T(8,128)(2,1)} %bitcast.33, s32[1,128]{1,0:T(1,128)} %owner_ref.1, s32[1,128]{1,0:T(1,128)} %slot_ref.1), custom_call_target="tpu_custom_call" | custom-call | tf_op jit(solution)/shard_map/pallas_call | solution.py:336
  4.0 1.4 %broadcast_in_dim.17 = bf16[4,8,8,128]{3,2,1,0:T(8,128)(2,1)} broadcast(bf16[8,8,128]{2,1,0:T(8,128)(2,1)} %bitcast.34), dimensions={1,2,3} | broadcast | bytes 81920 | tf_op jit(solution)/shard_map/broadcast_in_dim | solution.py:344
  5.4 7.3 %all-to-all-start = ((bf16[32,8,128]{2,1,0:T(8,128)(2,1)}), bf16[32,8,128]{2,1,0:T(8,128)(2,1)S(1)}, u32[]{:S(2)}, u32[]{:S(2)}) async-start(bf16[32,8,128]{2,1,0:T(8,128)(2,1)} %bitcast.2), calls=%async_computation | async-start | bytes 131072 | tf_op jit(solution)/shard_map/all_to_all | solution.py:346
  12.7 0.7 %slice.12 = bf16[2,2,16,128]{3,2,1,0:T(8,128)(2,1)S(1)} slice(bf16[2,16,16,128]{3,2,1,0:T(8,128)(2,1)} %bitcast.22), slice={[0:2], [14:16], [0:16], [0:128]} | slice | bytes 32768 | tf_op jit(solution)/shard_map/slice | solution.py:331
  13.4 0.7 %slice.13 = bf16[2,1,16,128]{3,2,1,0:T(8,128)(2,1)S(1)} slice(bf16[2,16,16,128]{3,2,1,0:T(8,128)(2,1)} %bitcast.25), slice={[0:2], [15:16], [0:16], [0:128]} | slice | bytes 16384 | tf_op jit(solution)/shard_map/slice | solution.py:331
  14.1 1.8 %collective-permute-start.3 = (bf16[96,128]{1,0:T(8,128)(2,1)S(1)}, bf16[96,128]{1,0:T(8,128)(2,1)S(1)}, u32[]{:S(2)}, u32[]{:S(2)}) collective-permute-start(bf16[96,128]{1,0:T(8,128)(2,1)S(1)} %pad_maximum_fusion), channel_id=1, source_target_pairs={{0,1},{1,2},{2,3},{3,0},{4,5},{5,6},{6,7},{7,4},{8,9},{9,10},{10,1... | collective-permute-start | bytes 73736 | tf_op jit(solution)/shard_map/ppermute | solution.py:305
  15.9 0.7 %slice.14 = bf16[2,1,16,128]{3,2,1,0:T(8,128)(2,1)S(1)} slice(bf16[2,16,16,128]{3,2,1,0:T(8,128)(2,1)} %bitcast.23), slice={[0:2], [0:1], [0:16], [0:128]} | slice | bytes 16384 | tf_op jit(solution)/shard_map/slice | solution.py:332
  16.6 2.1 %collective-permute-start.4 = (bf16[32,128]{1,0:T(8,128)(2,1)S(1)}, bf16[32,128]{1,0:T(8,128)(2,1)S(1)}, u32[]{:S(2)}, u32[]{:S(2)}) collective-permute-start(bf16[32,128]{1,0:T(8,128)(2,1)S(1)} %bitcast.38), channel_id=1, source_target_pairs={{0,3},{1,0},{2,1},{3,2},{4,7},{5,4},{6,5},{7,6},{8,11},{9,8},{10,9... | collective-permute-start | bytes 24584 | tf_op jit(solution)/shard_map/ppermute | solution.py:305
  18.6 0.0 collective-permute-start
  18.6 2.4 %collective-permute-start.1 = (bf16[32,48]{1,0:T(8,128)(2,1)}, bf16[32,48]{1,0:T(8,128)(2,1)S(1)}, u32[]{:S(2)}, u32[]{:S(2)}) collective-permute-start(bf16[32,48]{1,0:T(8,128)(2,1)} %bitcast.28), channel_id=1, source_target_pairs={{0,2},{1,3},{2,0},{3,1},{4,6},{5,7},{6,4},{7,5},{8,10},{9,11},{10,... | collective-permute-start | bytes 9224 | tf_op jit(solution)/shard_map/ppermute | solution.py:305
  21.0 1.4 %collective-permute-start.2 = (bf16[32,48]{1,0:T(8,128)(2,1)}, bf16[32,48]{1,0:T(8,128)(2,1)S(1)}, u32[]{:S(2)}, u32[]{:S(2)}) collective-permute-start(bf16[32,48]{1,0:T(8,128)(2,1)} %bitcast.29), channel_id=1, source_target_pairs={{0,3},{1,0},{2,1},{3,2},{4,7},{5,4},{6,5},{7,6},{8,11},{9,8},{10,9... | collective-permute-start | bytes 9224 | tf_op jit(solution)/shard_map/ppermute | solution.py:305
  22.4 1.4 %reshape.37.sw_ref = f32[81,128]{1,0:T(8,128)} reshape(bf16[3,3,3,3,128]{4,3,2,1,0:T(4,128)(2,1)} %param.21) | data formatting | bytes 62208 | tf_op jit(solution)/shard_map/convert_element_type | solution.py:353
  23.8 2.4 %shard_map.157.band_ref = bf16[432,2048]{1,0:T(8,128)(2,1)} custom-call(f32[81,128]{1,0:T(8,128)} %reshape.37.sw_ref), custom_call_target="tpu_custom_call" | custom-call | tf_op jit(solution)/shard_map/pallas_call | solution.py:348
  26.8 0.0 collective-permute-done.pix1_ref
  26.9 0.0 collective-permute-done.1.pix2_ref
  26.9 0.0 collective-permute-done.2.pix3_ref
  26.9 0.0 collective-permute-done.4.above_ref
  26.9 0.0 collective-permute-done.3.below_ref
  26.9 0.0 all-to-all-done
  26.9 0.0 copy-done.3
  26.9 0.0 copy-done.4
  26.9 0.0 copy-done.5
  26.9 0.0 copy-done.6
  26.9 0.0 copy-done.7
  27.0 0.0 copy-done.1
  27.0 0.0 copy-start
  27.0 1.5 %copy-done = bf16[432,2048]{1,0:T(8,128)(2,1)S(1)} copy-done((bf16[432,2048]{1,0:T(8,128)(2,1)S(1)}, bf16[432,2048]{1,0:T(8,128)(2,1)}, u32[]{:S(2)}) %copy-start) | copy-done | bytes 1769496
  28.4 0.0 copy-start.2
  28.4 1.2 %copy-done.2 = bf16[3,3,3,128,128]{4,3,2,1,0:T(8,128)(2,1)S(1)} copy-done((bf16[3,3,3,128,128]{4,3,2,1,0:T(8,128)(2,1)S(1)}, bf16[3,3,3,128,128]{4,3,2,1,0:T(8,128)(2,1)}, u32[]{:S(2)}) %copy-start.2) | copy-done | bytes 884760
  29.6 12.4 %shard_map.158 = (bf16[4,8,8,256]{3,2,1,0:T(8,128)(2,1)}, bf16[32,48]{1,0:T(8,128)(2,1)S(1)}, bf16[2,16,16,128]{3,2,1,0:T(8,128)(2,1)S(1)}, bf16[2,16,16,128]{3,2,1,0:T(8,128)(2,1)S(1)}) custom-call(s32[1]{0:T(128)S(6)} %copy.18.valid_ref, bf16[4,64,128]{2,1,0:T(8,128)(2,1)S(1)} %bitcast.21, bf16[32,48]{1,0:T(8,128)(2,1)S(1)} %bitcast.30, ...), custom_call_target="tpu_custom_call" | custom-call | tf_op jit(solution)/shard_map/pallas_call | solution.py:355
  42.0 0.0 collective-permute-start.7
  42.7 0.5 collective-permute-done.7
  43.2 1.8 %collective-permute-start.8 = (bf16[32,48]{1,0:T(8,128)(2,1)S(1)}, bf16[32,48]{1,0:T(8,128)(2,1)S(1)}, u32[]{:S(2)}, u32[]{:S(2)}) collective-permute-start(bf16[32,48]{1,0:T(8,128)(2,1)S(1)} %broadcast_select_fusion.4), channel_id=1, source_target_pairs={{0,8},{4,12},{8,0},{12,4},{16,24},{20,28},{24,16},{28,20},{1,9},{5... | collective-permute-start | bytes 9224 | tf_op jit(solution)/shard_map/ppermute | solution.py:300
  45.0 0.0 collective-permute-start.5
  45.0 1.4 %collective-permute-done.5 = s32[]{:T(128)} collective-permute-done((s32[]{:T(128)}, s32[]{:T(128)}, u32[]{:S(2)}, u32[]{:S(2)}) %collective-permute-start.5) | collective-permute-done | bytes 36 | tf_op jit(solution)/shard_map/ppermute | solution.py:300
  46.9 0.0 collective-permute-done.8
  47.0 1.7 %collective-permute-start.9 = (bf16[32,48]{1,0:T(8,128)(2,1)S(1)}, bf16[32,48]{1,0:T(8,128)(2,1)S(1)}, u32[]{:S(2)}, u32[]{:S(2)}) collective-permute-start(bf16[32,48]{1,0:T(8,128)(2,1)S(1)} %broadcast_select_fusion.5), channel_id=1, source_target_pairs={{0,16},{4,20},{8,24},{12,28},{16,0},{20,4},{24,8},{28,12},{1,17},{... | collective-permute-start | bytes 9224 | tf_op jit(solution)/shard_map/ppermute | solution.py:300
  48.6 2.8 %collective-permute-start.6 = (s32[]{:T(128)}, s32[]{:T(128)}, u32[]{:S(2)}, u32[]{:S(2)}) collective-permute-start(s32[]{:T(128)} %select_n.59), channel_id=1, source_target_pairs={{0,8},{4,12},{8,0},{12,4},{16,24},{20,28},{24,16},{28,20},{1,9},{5... | collective-permute-start | bytes 20 | tf_op jit(solution)/shard_map/ppermute | solution.py:300
  51.4 0.9 %collective-permute-done.6 = s32[]{:T(128)} collective-permute-done((s32[]{:T(128)}, s32[]{:T(128)}, u32[]{:S(2)}, u32[]{:S(2)}) %collective-permute-start.6) | collective-permute-done | bytes 36 | tf_op jit(solution)/shard_map/ppermute | solution.py:300
  52.9 0.1 collective-permute-start.13
  52.9 0.5 collective-permute-start.10
  53.4 0.0 collective-permute-done.9
  53.4 0.6 broadcast_select_fusion.6
  54.0 0.2 collective-permute-done.13
  54.3 1.5 %collective-permute-start.14 = (bf16[2,16,16,128]{3,2,1,0:T(8,128)(2,1)S(1)}, bf16[2,16,16,128]{3,2,1,0:T(8,128)(2,1)S(1)}, u32[]{:S(2)}, u32[]{:S(2)}) collective-permute-start(bf16[2,16,16,128]{3,2,1,0:T(8,128)(2,1)S(1)} %broadcast_select_fusion), channel_id=1, source_target_pairs={{0,8},{4,12},{8,0},{12,4},{16,24},{20,28},{24,16},{28,20},{1,9},{5... | collective-permute-start | bytes 393224 | tf_op jit(solution)/shard_map/ppermute | solution.py:300
  55.8 0.0 collective-permute-done.10
  55.8 0.6 collective-permute-start.11
  56.5 4.2 %collective-permute-done.14 = bf16[2,16,16,128]{3,2,1,0:T(8,128)(2,1)S(1)} collective-permute-done((bf16[2,16,16,128]{3,2,1,0:T(8,128)(2,1)S(1)}, bf16[2,16,16,128]{3,2,1,0:T(8,128)(2,1)S(1)}, u32[]{:S(2)}, u32[]{:S(2)}) %collective-permute-start.14) | collective-permute-done | bytes 131104 | tf_op jit(solution)/shard_map/ppermute | solution.py:300
  60.7 0.5 collective-permute-start.15
  61.2 1.5 %collective-permute-done.11 = bf16[2,16,16,128]{3,2,1,0:T(8,128)(2,1)S(1)} collective-permute-done((bf16[2,16,16,128]{3,2,1,0:T(8,128)(2,1)S(1)}, bf16[2,16,16,128]{3,2,1,0:T(8,128)(2,1)S(1)}, u32[]{:S(2)}, u32[]{:S(2)}) %collective-permute-start.11) | collective-permute-done | bytes 131104 | tf_op jit(solution)/shard_map/ppermute | solution.py:300
  62.7 0.5 collective-permute-start.12
  63.2 3.6 %collective-permute-done.15 = bf16[2,16,16,128]{3,2,1,0:T(8,128)(2,1)S(1)} collective-permute-done((bf16[2,16,16,128]{3,2,1,0:T(8,128)(2,1)S(1)}, bf16[2,16,16,128]{3,2,1,0:T(8,128)(2,1)S(1)}, u32[]{:S(2)}, u32[]{:S(2)}) %collective-permute-start.15) | collective-permute-done | bytes 131104 | tf_op jit(solution)/shard_map/ppermute | solution.py:300
  66.9 0.7 select_bitcast_fusion
  67.5 1.0 %collective-permute-done.12 = bf16[2,16,16,128]{3,2,1,0:T(8,128)(2,1)S(1)} collective-permute-done((bf16[2,16,16,128]{3,2,1,0:T(8,128)(2,1)S(1)}, bf16[2,16,16,128]{3,2,1,0:T(8,128)(2,1)S(1)}, u32[]{:S(2)}, u32[]{:S(2)}) %collective-permute-start.12) | collective-permute-done | bytes 131104 | tf_op jit(solution)/shard_map/ppermute | solution.py:300
  68.6 0.7 select_bitcast_fusion.1
  (7 shorter events, 0.1 us)
Async XLA Ops:
  0.6 26.3 %copy-start.3 = (bf16[1,2,16,16,128]{4,3,2,1,0:T(8,128)(2,1)S(1)}, bf16[1,2,16,16,128]{4,3,2,1,0:T(8,128)(2,1)}, u32[]{:S(2)}) copy-start(bf16[1,2,16,16,128]{4,3,2,1,0:T(8,128)(2,1)} %param.19) | copy-start | bytes 393220
  0.6 26.3 %copy-start.4 = (bf16[1,2,16,16,128]{4,3,2,1,0:T(8,128)(2,1)S(1)}, bf16[1,2,16,16,128]{4,3,2,1,0:T(8,128)(2,1)}, u32[]{:S(2)}) copy-start(bf16[1,2,16,16,128]{4,3,2,1,0:T(8,128)(2,1)} %param.20) | copy-start | bytes 393220
  0.7 26.3 %copy-start.5 = (bf16[1,2,16,48]{3,2,1,0:T(8,128)(2,1)S(1)}, bf16[1,2,16,48]{3,2,1,0:T(8,128)(2,1)}, u32[]{:S(2)}) copy-start(bf16[1,2,16,48]{3,2,1,0:T(8,128)(2,1)} %param.18) | copy-start | bytes 9220
  0.7 26.3 %copy-start.6 = (f32[128]{0:T(128)S(1)}, f32[128]{0:T(128)}, u32[]{:S(2)}) copy-start(f32[128]{0:T(128)} %param.22) | copy-start | bytes 1540
  0.7 26.3 %copy-start.7 = (f32[128]{0:T(128)S(1)}, f32[128]{0:T(128)}, u32[]{:S(2)}) copy-start(f32[128]{0:T(128)} %param.23) | copy-start | bytes 1540
  0.7 26.3 %copy-start.1 = (bf16[3,3,3,128,256]{4,3,2,1,0:T(8,128)(2,1)S(1)}, bf16[3,3,3,128,256]{4,3,2,1,0:T(8,128)(2,1)}, u32[]{:S(2)}) copy-start(bf16[3,3,3,128,256]{4,3,2,1,0:T(8,128)(2,1)} %down_ref.1) | copy-start | bytes 5308420
  5.4 21.5 %all-to-all-start = ((bf16[32,8,128]{2,1,0:T(8,128)(2,1)}), bf16[32,8,128]{2,1,0:T(8,128)(2,1)S(1)}, u32[]{:S(2)}, u32[]{:S(2)}) async-start(bf16[32,8,128]{2,1,0:T(8,128)(2,1)} %bitcast.2), calls=%async_computation | async-start | bytes 131072 | tf_op jit(solution)/shard_map/all_to_all | solution.py:346
  14.1 12.8 %collective-permute-start.3 = (bf16[96,128]{1,0:T(8,128)(2,1)S(1)}, bf16[96,128]{1,0:T(8,128)(2,1)S(1)}, u32[]{:S(2)}, u32[]{:S(2)}) collective-permute-start(bf16[96,128]{1,0:T(8,128)(2,1)S(1)} %pad_maximum_fusion), channel_id=1, source_target_pairs={{0,1},{1,2},{2,3},{3,0},{4,5},{5,6},{6,7},{7,4},{8,9},{9,10},{10,1... | collective-permute-start | bytes 73736 | tf_op jit(solution)/shard_map/ppermute | solution.py:305
  16.6 10.3 %collective-permute-start.4 = (bf16[32,128]{1,0:T(8,128)(2,1)S(1)}, bf16[32,128]{1,0:T(8,128)(2,1)S(1)}, u32[]{:S(2)}, u32[]{:S(2)}) collective-permute-start(bf16[32,128]{1,0:T(8,128)(2,1)S(1)} %bitcast.38), channel_id=1, source_target_pairs={{0,3},{1,0},{2,1},{3,2},{4,7},{5,4},{6,5},{7,6},{8,11},{9,8},{10,9... | collective-permute-start | bytes 24584 | tf_op jit(solution)/shard_map/ppermute | solution.py:305
  18.6 8.2 %collective-permute-start = (bf16[32,48]{1,0:T(8,128)(2,1)}, bf16[32,48]{1,0:T(8,128)(2,1)S(1)}, u32[]{:S(2)}, u32[]{:S(2)}) collective-permute-start(bf16[32,48]{1,0:T(8,128)(2,1)} %bitcast.27), channel_id=1, source_target_pairs={{0,1},{1,2},{2,3},{3,0},{4,5},{5,6},{6,7},{7,4},{8,9},{9,10},{10,1... | collective-permute-start | bytes 9224 | tf_op jit(solution)/shard_map/ppermute | solution.py:305
  18.6 8.2 %collective-permute-start.1 = (bf16[32,48]{1,0:T(8,128)(2,1)}, bf16[32,48]{1,0:T(8,128)(2,1)S(1)}, u32[]{:S(2)}, u32[]{:S(2)}) collective-permute-start(bf16[32,48]{1,0:T(8,128)(2,1)} %bitcast.28), channel_id=1, source_target_pairs={{0,2},{1,3},{2,0},{3,1},{4,6},{5,7},{6,4},{7,5},{8,10},{9,11},{10,... | collective-permute-start | bytes 9224 | tf_op jit(solution)/shard_map/ppermute | solution.py:305
  21.0 5.9 %collective-permute-start.2 = (bf16[32,48]{1,0:T(8,128)(2,1)}, bf16[32,48]{1,0:T(8,128)(2,1)S(1)}, u32[]{:S(2)}, u32[]{:S(2)}) collective-permute-start(bf16[32,48]{1,0:T(8,128)(2,1)} %bitcast.29), channel_id=1, source_target_pairs={{0,3},{1,0},{2,1},{3,2},{4,7},{5,4},{6,5},{7,6},{8,11},{9,8},{10,9... | collective-permute-start | bytes 9224 | tf_op jit(solution)/shard_map/ppermute | solution.py:305
  27.0 1.5 %copy-start = (bf16[432,2048]{1,0:T(8,128)(2,1)S(1)}, bf16[432,2048]{1,0:T(8,128)(2,1)}, u32[]{:S(2)}) copy-start(bf16[432,2048]{1,0:T(8,128)(2,1)} %shard_map.157.band_ref) | copy-start | bytes 5308420
  28.4 1.2 %copy-start.2 = (bf16[3,3,3,128,128]{4,3,2,1,0:T(8,128)(2,1)S(1)}, bf16[3,3,3,128,128]{4,3,2,1,0:T(8,128)(2,1)}, u32[]{:S(2)}) copy-start(bf16[3,3,3,128,128]{4,3,2,1,0:T(8,128)(2,1)} %conv_ref.1) | copy-start | bytes 2654212
  42.0 1.2 %collective-permute-start.7 = (bf16[32,48]{1,0:T(8,128)(2,1)S(1)}, bf16[32,48]{1,0:T(8,128)(2,1)S(1)}, u32[]{:S(2)}, u32[]{:S(2)}) collective-permute-start(bf16[32,48]{1,0:T(8,128)(2,1)S(1)} %get-tuple-element.9), channel_id=1, source_target_pairs={{0,4},{4,0},{8,12},{12,8},{16,20},{20,16},{24,28},{28,24},{1,5},{5... | collective-permute-start | bytes 9224 | tf_op jit(solution)/shard_map/ppermute | solution.py:300
  43.2 3.7 %collective-permute-start.8 = (bf16[32,48]{1,0:T(8,128)(2,1)S(1)}, bf16[32,48]{1,0:T(8,128)(2,1)S(1)}, u32[]{:S(2)}, u32[]{:S(2)}) collective-permute-start(bf16[32,48]{1,0:T(8,128)(2,1)S(1)} %broadcast_select_fusion.4), channel_id=1, source_target_pairs={{0,8},{4,12},{8,0},{12,4},{16,24},{20,28},{24,16},{28,20},{1,9},{5... | collective-permute-start | bytes 9224 | tf_op jit(solution)/shard_map/ppermute | solution.py:300
  45.0 1.4 %collective-permute-start.5 = (s32[]{:T(128)}, s32[]{:T(128)}, u32[]{:S(2)}, u32[]{:S(2)}) collective-permute-start(s32[]{:T(128)} %bitcast.13), channel_id=1, source_target_pairs={{0,4},{4,0},{8,12},{12,8},{16,20},{20,16},{24,28},{28,24},{1,5},{5... | collective-permute-start | bytes 20 | tf_op jit(solution)/shard_map/ppermute | solution.py:300
  47.0 6.5 %collective-permute-start.9 = (bf16[32,48]{1,0:T(8,128)(2,1)S(1)}, bf16[32,48]{1,0:T(8,128)(2,1)S(1)}, u32[]{:S(2)}, u32[]{:S(2)}) collective-permute-start(bf16[32,48]{1,0:T(8,128)(2,1)S(1)} %broadcast_select_fusion.5), channel_id=1, source_target_pairs={{0,16},{4,20},{8,24},{12,28},{16,0},{20,4},{24,8},{28,12},{1,17},{... | collective-permute-start | bytes 9224 | tf_op jit(solution)/shard_map/ppermute | solution.py:300
  48.6 3.6 %collective-permute-start.6 = (s32[]{:T(128)}, s32[]{:T(128)}, u32[]{:S(2)}, u32[]{:S(2)}) collective-permute-start(s32[]{:T(128)} %select_n.59), channel_id=1, source_target_pairs={{0,8},{4,12},{8,0},{12,4},{16,24},{20,28},{24,16},{28,20},{1,9},{5... | collective-permute-start | bytes 20 | tf_op jit(solution)/shard_map/ppermute | solution.py:300
  52.9 1.4 %collective-permute-start.13 = (bf16[2,16,16,128]{3,2,1,0:T(8,128)(2,1)S(1)}, bf16[2,16,16,128]{3,2,1,0:T(8,128)(2,1)S(1)}, u32[]{:S(2)}, u32[]{:S(2)}) collective-permute-start(bf16[2,16,16,128]{3,2,1,0:T(8,128)(2,1)S(1)} %get-tuple-element.11), channel_id=1, source_target_pairs={{0,4},{4,0},{8,12},{12,8},{16,20},{20,16},{24,28},{28,24},{1,5},{5... | collective-permute-start | bytes 393224 | tf_op jit(solution)/shard_map/ppermute | solution.py:300
  52.9 2.9 %collective-permute-start.10 = (bf16[2,16,16,128]{3,2,1,0:T(8,128)(2,1)S(1)}, bf16[2,16,16,128]{3,2,1,0:T(8,128)(2,1)S(1)}, u32[]{:S(2)}, u32[]{:S(2)}) collective-permute-start(bf16[2,16,16,128]{3,2,1,0:T(8,128)(2,1)S(1)} %get-tuple-element.10), channel_id=1, source_target_pairs={{0,4},{4,0},{8,12},{12,8},{16,20},{20,16},{24,28},{28,24},{1,5},{5... | collective-permute-start | bytes 393224 | tf_op jit(solution)/shard_map/ppermute | solution.py:300
  54.3 6.4 %collective-permute-start.14 = (bf16[2,16,16,128]{3,2,1,0:T(8,128)(2,1)S(1)}, bf16[2,16,16,128]{3,2,1,0:T(8,128)(2,1)S(1)}, u32[]{:S(2)}, u32[]{:S(2)}) collective-permute-start(bf16[2,16,16,128]{3,2,1,0:T(8,128)(2,1)S(1)} %broadcast_select_fusion), channel_id=1, source_target_pairs={{0,8},{4,12},{8,0},{12,4},{16,24},{20,28},{24,16},{28,20},{1,9},{5... | collective-permute-start | bytes 393224 | tf_op jit(solution)/shard_map/ppermute | solution.py:300
  55.8 6.9 %collective-permute-start.11 = (bf16[2,16,16,128]{3,2,1,0:T(8,128)(2,1)S(1)}, bf16[2,16,16,128]{3,2,1,0:T(8,128)(2,1)S(1)}, u32[]{:S(2)}, u32[]{:S(2)}) collective-permute-start(bf16[2,16,16,128]{3,2,1,0:T(8,128)(2,1)S(1)} %broadcast_select_fusion.1), channel_id=1, source_target_pairs={{0,8},{4,12},{8,0},{12,4},{16,24},{20,28},{24,16},{28,20},{1,9},{5... | collective-permute-start | bytes 393224 | tf_op jit(solution)/shard_map/ppermute | solution.py:300
  60.7 6.2 %collective-permute-start.15 = (bf16[2,16,16,128]{3,2,1,0:T(8,128)(2,1)S(1)}, bf16[2,16,16,128]{3,2,1,0:T(8,128)(2,1)S(1)}, u32[]{:S(2)}, u32[]{:S(2)}) collective-permute-start(bf16[2,16,16,128]{3,2,1,0:T(8,128)(2,1)S(1)} %broadcast_select_fusion.2), channel_id=1, source_target_pairs={{0,16},{4,20},{8,24},{12,28},{16,0},{20,4},{24,8},{28,12},{1,17},{... | collective-permute-start | bytes 393224 | tf_op jit(solution)/shard_map/ppermute | solution.py:300
  62.7 5.8 %collective-permute-start.12 = (bf16[2,16,16,128]{3,2,1,0:T(8,128)(2,1)S(1)}, bf16[2,16,16,128]{3,2,1,0:T(8,128)(2,1)S(1)}, u32[]{:S(2)}, u32[]{:S(2)}) collective-permute-start(bf16[2,16,16,128]{3,2,1,0:T(8,128)(2,1)S(1)} %broadcast_select_fusion.3), channel_id=1, source_target_pairs={{0,16},{4,20},{8,24},{12,28},{16,0},{20,4},{24,8},{28,12},{1,17},{... | collective-permute-start | bytes 393224 | tf_op jit(solution)/shard_map/ppermute | solution.py:300

commit v2 on v1

--- a/solution.py
+++ b/solution.py
@@ -28,87 +28,88 @@
     return lax.dot_general(a, b, (((1,), (1,)), ((), ())), preferred_element_type=F32)
 
 
-def sort_kernel(streams, rows_ref, owner_ref, slot_ref, out_ref, wide):
-    fill = rows_ref.shape[0]
-    per = fill // streams
+def sort_kernel(streams, cols_ref, owner_ref, slot_ref, out_ref, wide):
+    width, fill = cols_ref.shape
+    half_per = fill // streams // 2
     lines = fill // 2
     wide[...] = jnp.zeros(wide.shape, F32)
-    wide[:, 0 : rows_ref.shape[1]] = rows_ref[...].astype(F32)
+    pixels, slots = cols_ref[...].astype(F32), slot_ref[...].astype(F32)
+    for side in range(2):
+        at = side * 64
+        wide[at : at + width, side * fill : (side + 1) * fill] = pixels
+        wide[at + width : at + width + 1, side * fill : (side + 1) * fill] = slots
     owner = owner_ref[...]
-    onehot = iota((streams, fill), 0) == owner
-    hot = jnp.where(onehot, 1.0, 0.0)
+    hot = jnp.where(iota((streams, fill), 0) == owner, 1.0, 0.0)
     upper = jnp.where(iota((fill, fill), 0) <= iota((fill, fill), 1), 1.0, 0.0).astype(BF16)
     running = dot(hot.astype(BF16), upper)
     rank = jnp.sum(hot * running, axis=0, keepdims=True).astype(jnp.int32) - 1
-    half = rank // (per // 2)
-    line = owner * (per // 2) + rank - half * (per // 2)
-    line = jnp.broadcast_to(line, (lines, fill))
-    half = jnp.broadcast_to(half, (lines, fill))
-    here = iota((lines, fill), 0) == line
-    slot = jnp.broadcast_to(slot_ref[...].astype(F32), (lines, fill))
-    data = wide[...].astype(BF16)
-    parts = []
-    for side in range(2):
-        pick = jnp.where(here & (half == side), 1.0, 0.0)
-        picked = dot(pick.astype(BF16), data)
-        slots = jnp.sum(pick * slot, axis=1, keepdims=True)
-        parts.append(jnp.where(iota((lines, 128), 1) == 48, slots, picked))
-    out = jnp.where(iota((lines, 128), 1) < 64, parts[0], pltpu.roll(parts[1], 64, 1))
-    out_ref[...] = out.astype(BF16)
-
-
-def band_kernel(sw_ref, out_ref):
-    cols = 16
+    half = rank // half_per
+    line = owner * half_per + rank - half * half_per
+    line = jnp.concatenate([jnp.where(half == side, line, -1) for side in range(2)], axis=1)
+    pick = jnp.where(iota((lines, 2 * fill), 0) == jnp.broadcast_to(line, (lines, 2 * fill)), 1.0, 0.0)
+    out = dot_nt(pick.astype(BF16), wide[...].astype(BF16)).astype(BF16)
+    if len(out_ref.shape) == 2:
+        out_ref[...] = out
+    else:
+        for strip in range(out_ref.shape[0]):
+            out_ref[strip] = out.reshape(out_ref.shape[1:])
+
+
+def pack_kernel(pix_ref, act_ref, res_ref, down_ref, up_ref, mid_ref):
+    pix = jnp.concatenate(
+        [pix_ref[...].reshape(32, 48).astype(F32), jnp.zeros((32, 80), F32)], axis=1
+    ).astype(BF16)
+    for f in range(2):
+        down_ref[f * 32 : f * 32 + 32] = act_ref[f, 14:16].reshape(32, 128)
+        down_ref[64 + f * 16 : 80 + f * 16] = res_ref[f, 15]
+        up_ref[f * 16 : f * 16 + 16] = act_ref[f, 0]
+    down_ref[96:128] = pix
+    up_ref[32:64] = pix
+    mid_ref[...] = pix
+
+
+def band_kernel(sw_ref, out_ref, wide):
+    wide[...] = jnp.zeros(wide.shape, F32)
     for tap in range(27):
         b, a, c = tap // 9, tap // 3 % 3, tap % 3
-        for w in range(cols):
-            row = iota((cols, 128), 0)
-            block = jnp.zeros((cols, 128), F32)
-            for e in range(3):
-                line = (a * 9 + b * 3 + e) * 3 + c
-                block = jnp.where(row == w + e - 1, sw_ref[line : line + 1, :], block)
-            out_ref[tap * cols : (tap + 1) * cols, w * 128 : (w + 1) * 128] = block.astype(BF16)
-
-
-def main_kernel(
+        for e in range(3):
+            wide[tap, 16 + e : 17 + e] = sw_ref[a, b, e, c : c + 1].astype(F32)
+    for w in range(16):
+        block = wide[:, 17 - w : 33 - w].reshape(432, 128)
+        out_ref[:, w * 128 : (w + 1) * 128] = block.astype(BF16)
+
+
+def stem_kernel(
     strips,
     valid_ref,
+    target_ref,
     recv_ref,
-    pix0_ref,
-    pix1_ref,
-    pix2_ref,
-    pix3_ref,
+    pix_ref,
+    below_ref,
+    above_ref,
+    mid_ref,
     band_ref,
     gain_ref,
     bias_ref,
-    conv_ref,
-    down_ref,
     act_cache_ref,
-    res_cache_ref,
-    below_ref,
-    above_ref,
-    lat_ref,
-    new_pix_ref,
-    new_act_ref,
-    new_res_ref,
+    pay_ref,
+    act3,
+    stem_ref,
     pc,
     zs,
     xs,
     stem,
     act,
-    res,
     cache,
-    rcache,
-    act3,
-    res3,
-    lat,
 ):
     j = lax.axis_index("strip")
     valid = valid_ref[0]
     rows_all = strips * 16
     pc[...] = jnp.zeros(pc.shape, F32)
-    for k, ref in enumerate((pix0_ref, pix1_ref, pix2_ref, pix3_ref)):
-        pc[lax.rem(j + strips - k, strips), :, 0:48] = ref[...].astype(F32)
+    pc[j, :, 0:48] = pix_ref[...].reshape(32, 48).astype(F32)
+    pc[lax.rem(j + strips - 1, strips)] = below_ref[96:128].astype(F32)
+    pc[lax.rem(j + 1, strips)] = above_ref[32:64].astype(F32)
+    pc[lax.rem(j + 2, strips)] = mid_ref[...].astype(F32)
     zs[...] = jnp.zeros(zs.shape, F32)
     lane = iota((128, 128), 1)
     sub = iota((128, 128), 0)
@@ -142,7 +143,9 @@
     chit = jnp.where(iota((32, 32), 0) == cplace, 1.0, 0.0)
     source = jnp.concatenate([jnp.where(lane < 48, both, 0.0), pc[j]], axis=0).astype(BF16)
     fresh = dot(jnp.concatenate([hit.reshape(32, 128), chit], axis=1).astype(BF16), source)
-    new_pix_ref[...] = fresh[:, 0:48].astype(BF16)
+    target = jnp.broadcast_to(target_ref[0].astype(F32), (16, 128))
+    pay_ref[0:16] = target.astype(BF16)
+    pay_ref[16:48] = fresh.astype(BF16)
     high = rows_all + 4
     for b in range(3):
         for a in range(3):
@@ -164,7 +167,9 @@
         s2 = s2 + jnp.sum(out * out, axis=0)
         mine = dot(own, weight).astype(BF16).astype(F32).reshape(2, 11, 8, 256)
         for i in range(2):
-            stem[:, 2 * chunk + i] = mine[:, :, :, i * 128 : (i + 1) * 128]
+            part = mine[:, :, :, i * 128 : (i + 1) * 128]
+            stem[:, 2 * chunk + i] = part
+            stem_ref[2 * chunk + i] = jnp.concatenate([part[0, 1:10], part[1, 1:10]], axis=1).astype(BF16)
     s1 = s1[:, 0:128] + s1[:, 128:256]
     s2 = s2[:, 0:128] + s2[:, 128:256]
     same = jnp.where(iota((128, 128), 0) // 4 == iota((128, 128), 1) // 4, 1.0, 0.0)
@@ -186,15 +191,12 @@
         jnp.where(low8, pltpu.roll(shift, 4, 0), shift),
     )
     cache[...] = jnp.zeros(cache.shape, F32)
-    rcache[...] = jnp.zeros(rcache.shape, F32)
     has_above = jnp.where(j > 0, 1.0, 0.0)
     has_below = jnp.where(j < strips - 1, 1.0, 0.0)
     for f in range(2):
         cache[f, 0:32] = below_ref[f * 32 : f * 32 + 32].astype(F32) * has_above
         cache[f, 32:288] = act_cache_ref[f].reshape(256, 128).astype(F32)
         cache[f, 288:304] = above_ref[f * 16 : f * 16 + 16].astype(F32) * has_below
-        rcache[f, 0:16] = below_ref[64 + f * 16 : 80 + f * 16].astype(F32) * has_above
-        rcache[f, 16:272] = res_cache_ref[f].reshape(256, 128).astype(F32)
     half = iota((11, 8, 128), 1) // 4
     line_of = j * 16 + iota((11, 8, 128), 0) - 2 + 8 * half
     inside = jnp.where((line_of >= 0) & (line_of < rows_all), 1.0, 0.0)
@@ -223,32 +225,87 @@
         return carry
 
     lax.fori_loop(0, 16, activate, 0)
-    weights = [
-        jnp.concatenate([conv_ref[a, b, e] for a in range(3)], axis=0)
-        for b in range(3)
-        for e in range(3)
-    ]
-    weights = jnp.concatenate(weights, axis=0)
-    keep = jnp.where((j == 0) & (iota((9, 8, 128), 0) == 0) & (iota((9, 8, 128), 1) < 4), 0.0, 1.0)
-    for g in range(4):
-        w0 = g * 4
+    act_rows = act.reshape(2 * 16 * 11 * 8, 128)
+    for i in range(2):
+        g = valid + i
+        f = jnp.maximum(g - 2, 0)
+        for y in range(16):
+            at = (f & 1) * (16 * 88) + (y % 8 + 2) * 8 + y // 8 * 4 + (f >> 1)
+            block = act_rows[pl.ds(at, 16, stride=88)]
+            block = jnp.where(g < 2, act_cache_ref[1, y].astype(F32), block)
+            to = 48 + i * 256 + y * 16
+            pay_ref[to : to + 16] = block.astype(BF16)
+
+
+def conv_rows(first, last, act3_ref, stem_ref, conv_ref):
+    j = lax.axis_index("strip")
+    count = last - first
+    weights = jnp.concatenate(
+        [conv_ref[a, b, e] for b in range(3) for e in range(3) for a in range(3)], axis=0
+    )
+    line = first + iota((count, 16, 128), 0)
+    outside = (j == 0) & (line == 0) & (iota((count, 16, 128), 1) % 8 < 4)
+    keep = jnp.where(outside, 0.0, 1.0)
+    groups = []
+    for w0 in range(0, 16, 4):
         left = jnp.concatenate(
             [
-                act3[w0 + e : w0 + e + 4, b : b + 9].reshape(576, 384)
+                act3_ref[w0 + e : w0 + e + 4, first + b : last + b].reshape(4 * count * 16, 384)
                 for b in range(3)
                 for e in range(3)
             ],
             axis=1,
         )
-        out = dot(left, weights).reshape(4, 9, 16, 128)
+        out = dot(left, weights).reshape(4, count, 16, 128)
+        out = out + stem_ref[w0 : w0 + 4, first:last].astype(F32)
+        groups.append((out * keep).astype(BF16))
+    return groups
+
+
+def conv_first_kernel(split, act3_ref, stem_ref, conv_ref, out_ref):
+    for g, value in enumerate(conv_rows(0, split, act3_ref, stem_ref, conv_ref)):
+        out_ref[g * 4 : g * 4 + 4] = value
+
+
+def conv_second_kernel(
+    split, valid_ref, act3_ref, stem_ref, conv_ref, part_ref, res_cache_ref, out_ref, pay_ref, res
+):
+    valid = valid_ref[0]
+    part = part_ref[...].astype(F32)
+    for p in range(2):
+        res[p, :, 0:split] = part[:, :, p * 8 : p * 8 + 8]
+    for g, value in enumerate(conv_rows(split, 9, act3_ref, stem_ref, conv_ref)):
+        out_ref[g * 4 : g * 4 + 4] = value
         for p in range(2):
-            value = out[:, :, p * 8 : (p + 1) * 8] + stem[p, w0 : w0 + 4, 1:10]
-            res[p, w0 : w0 + 4] = (value * keep).astype(BF16).astype(F32)
+            res[p, g * 4 : g * 4 + 4, split:9] = value.astype(F32)[:, :, p * 8 : p * 8 + 8]
+    res_rows = res.reshape(2 * 16 * 9 * 8, 128)
+    for i in range(2):
+        g = valid + i
+        f = jnp.maximum(g - 2, 0)
+        for y in range(16):
+            at = (f & 1) * (16 * 72) + (y % 8 + 1) * 8 + y // 8 * 4 + (f >> 1)
+            block = res_rows[pl.ds(at, 16, stride=72)]
+            block = jnp.where(g < 2, res_cache_ref[1, y].astype(F32), block)
+            to = i * 256 + y * 16
+            pay_ref[to : to + 16] = block.astype(BF16)
+
+
+def down_kernel(
+    split, valid_ref, part_ref, rest_ref, down_ref, res_cache_ref, below_ref, lat_ref, rcache, res3, lat
+):
+    j = lax.axis_index("strip")
+    valid = valid_ref[0]
+    rcache[...] = jnp.zeros(rcache.shape, F32)
+    has_above = jnp.where(j > 0, 1.0, 0.0)
+    for f in range(2):
+        rcache[f, 0:16] = below_ref[64 + f * 16 : 80 + f * 16].astype(F32) * has_above
+        rcache[f, 16:272] = res_cache_ref[f].reshape(256, 128).astype(F32)
     begin = iota((9, 8, 128), 1) % 4 == 0
     res3[0] = jnp.zeros(res3.shape[1:], F32)
 
     def delay(w, carry):
-        even, odd = res[0, w], res[1, w]
+        both = jnp.concatenate([part_ref[w], rest_ref[w]], axis=0).astype(F32)
+        even, odd = both[:, 0:8], both[:, 8:16]
         olds = []
         for f in range(2):
             olds.append(
@@ -278,21 +335,6 @@
                 for o in range(2):
                     block = lat[o, pl.ds(i * 8 + h * 4 + t, 8, stride=32)]
                     lat_ref[t, h * 4 + i, :, o * 128 : (o + 1) * 128] = block.astype(BF16)
-    act_rows = act.reshape(2 * 16 * 11 * 8, 128)
-    res_rows = res.reshape(2 * 16 * 9 * 8, 128)
-    for i in range(2):
-        g = valid + i
-        f = jnp.maximum(g - 2, 0)
-        parity, step = f & 1, f >> 1
-        old = g < 2
-        for y in range(16):
-            h, y1 = y // 8, y % 8
-            at = parity * (16 * 88) + (y1 + 2) * 8 + h * 4 + step
-            block = act_rows[pl.ds(at, 16, stride=88)]
-            new_act_ref[i, y] = jnp.where(old, act_cache_ref[1, y].astype(F32), block).astype(BF16)
-            at = parity * (16 * 72) + (y1 + 1) * 8 + h * 4 + step
-            block = res_rows[pl.ds(at, 16, stride=72)]
-            new_res_ref[i, y] = jnp.where(old, res_cache_ref[1, y].astype(F32), block).astype(BF16)
 
 
 def partner(value, axis, stride):
@@ -326,80 +368,119 @@
     sections = streams.bit_length() - 1
     fill = loader_rows.shape[1]
     per = fill // streams
-    pix = pixel_cache[0].reshape(32, 48)
-    acts, ress = act_cache[0], res_cache[0]
-    below = jnp.concatenate([acts[:, 14:16].reshape(64, 128), ress[:, 15].reshape(32, 128)], 0)
-    above = acts[:, 0].reshape(32, 128)
+    pix, acts, ress = pixel_cache[0], act_cache[0], res_cache[0]
+    mega = 1024 * 1024
+    half_per = fill // streams // 2
+    direct = half_per % 8 == 0
+    line_shape = (strips, streams, half_per, 128) if direct else (fill // 2, 128)
+    lines = pl.pallas_call(
+        functools.partial(sort_kernel, streams),
+        out_shape=jax.ShapeDtypeStruct(line_shape, BF16),
+        in_specs=[VM] * 3,
+        out_specs=VM,
+        scratch_shapes=[pltpu.VMEM((128, 2 * fill), F32)],
+    )(loader_rows[0].T, load_owner, load_slot)
+    if not direct:
+        lines = lines.reshape(1, streams, half_per, 128)
+        lines = jnp.broadcast_to(lines, (strips, streams, half_per, 128))
+    lines = lines.reshape(strips * streams, half_per, 128)
+    recv = lax.all_to_all(lines, ("strip", "stream"), 0, 0, tiled=True)
+    recv = recv.reshape(strips, fill // 2, 128)
+    below, above, mid = pl.pallas_call(
+        pack_kernel,
+        out_shape=(
+            jax.ShapeDtypeStruct((128, 128), BF16),
+            jax.ShapeDtypeStruct((64, 128), BF16),
+            jax.ShapeDtypeStruct((32, 128), BF16),
+        ),
+        in_specs=[VM] * 3,
+        out_specs=(VM,) * 3,
+    )(pix, acts, ress)
     below = shifted(below, "strip", 1)
     above = shifted(above, "strip", -1)
-    others = [shifted(pix, "strip", k) for k in range(1, strips)]
-    lines = pl.pallas_call(
-        functools.partial(sort_kernel, streams),
-        out_shape=jax.ShapeDtypeStruct((fill // 2, 128), BF16),
-        in_specs=[VM] * 3,
-        out_specs=VM,
-        scratch_shapes=[pltpu.VMEM((fill, 128), F32)],
-    )(loader_rows[0], load_owner, load_slot)
-    lines = lines.reshape(1, streams, per // 2, 128)
-    lines = jnp.broadcast_to(lines, (strips, streams, per // 2, 128))
-    lines = lines.reshape(strips * streams, per // 2, 128)
-    recv = lax.all_to_all(lines, ("strip", "stream"), 0, 0, tiled=True)
-    recv = recv.reshape(strips, fill // 2, 128)
+    mid = shifted(mid, "strip", 2)
     band = pl.pallas_call(
         band_kernel,
         out_shape=jax.ShapeDtypeStruct((432, 2048), BF16),
         in_specs=[VM],
         out_specs=VM,
-    )(stem_weight.reshape(81, 128).astype(F32))
+        scratch_shapes=[pltpu.VMEM((27, 40, 128), F32)],
+    )(stem_weight)
     rows_all = strips * 16
-    latent, new_pix, new_act, new_res = pl.pallas_call(
-        functools.partial(main_kernel, strips),
+    first, act3, stem = pl.pallas_call(
+        functools.partial(stem_kernel, strips),
         out_shape=(
-            jax.ShapeDtypeStruct((4, 8, 8, 256), BF16),
-            jax.ShapeDtypeStruct((32, 48), BF16),
-            jax.ShapeDtypeStruct((2, 16, 16, 128), BF16),
-            jax.ShapeDtypeStruct((2, 16, 16, 128), BF16),
+            jax.ShapeDtypeStruct((560, 128), BF16),
+            jax.ShapeDtypeStruct((18, 11, 16, 384), BF16),
+            jax.ShapeDtypeStruct((16, 9, 16, 128), BF16),
         ),
-        in_specs=[SM] + [VM] * 14,
-        out_specs=(VM,) * 4,
+        in_specs=[SM] * 2 + [VM] * 9,
+        out_specs=(VM,) * 3,
         scratch_shapes=[
             pltpu.VMEM((strips, 32, 128), F32),
             pltpu.VMEM((3, rows_all + 8, 8, 128), F32),
             pltpu.VMEM((rows_all + 8, 8, 432), F32),
             pltpu.VMEM((2, 16, 11, 8, 128), F32),
             pltpu.VMEM((2, 16, 11, 8, 128), F32),
-            pltpu.VMEM((2, 16, 9, 8, 128), F32),
             pltpu.VMEM((2, 416, 128), F32),
+        ],
+        compiler_params=pltpu.CompilerParams(vmem_limit_bytes=24 * mega),
+    )(
+        valid_frames,
+        next_owner,
+        recv,
+        pix,
+        below,
+        above,
+        mid,
+        band,
+        norm_gain.reshape(1, 128),
+        norm_bias.reshape(1, 128),
+        acts,
+    )
+    split = 5
+    cost = pl.CostEstimate(flops=2 * 10**9, bytes_accessed=4 * mega, transcendentals=0)
+    part = pl.pallas_call(
+        functools.partial(conv_first_kernel, split),
+        out_shape=jax.ShapeDtypeStruct((16, split, 16, 128), BF16),
+        in_specs=[VM] * 3,
+        out_specs=VM,
+        compiler_params=pltpu.CompilerParams(vmem_limit_bytes=24 * mega),
+        cost_estimate=cost,
+    )(act3, stem, conv_weight)
+    rest, second = pl.pallas_call(
+        functools.partial(conv_second_kernel, split),
+        out_shape=(
+            jax.ShapeDtypeStruct((16, 9 - split, 16, 128), BF16),
+            jax.ShapeDtypeStruct((512, 128), BF16),
+        ),
+        in_specs=[SM] + [VM] * 5,
+        out_specs=(VM,) * 2,
+        scratch_shapes=[pltpu.VMEM((2, 16, 9, 8, 128), F32)],
+        compiler_params=pltpu.CompilerParams(vmem_limit_bytes=24 * mega),
+        cost_estimate=cost,
+    )(valid_frames, act3, stem, conv_weight, part, ress)
+    latent = pl.pallas_call(
+        functools.partial(down_kernel, split),
+        out_shape=jax.ShapeDtypeStruct((4, 8, 8, 256), BF16),
+        in_specs=[SM] + [VM] * 5,
+        out_specs=VM,
+        scratch_shapes=[
             pltpu.VMEM((2, 384, 128), F32),
-            pltpu.VMEM((18, 11, 16, 384), BF16),
             pltpu.VMEM((17, 9, 8, 384), F32),
             pltpu.VMEM((2, 256, 128), F32),
         ],
-        compiler_params=pltpu.CompilerParams(vmem_limit_bytes=48 * 1024 * 1024),
-    )(
-        valid_frames,
-        recv,
-        pix,
-        *others,
-        band,
-        norm_gain.reshape(1, 128),
-        norm_bias.reshape(1, 128),
-        conv_weight,
-        down_weight,
-        acts,
-        ress,
-        below,
-        above,
-    )
-    carried = (new_pix, new_act, new_res)
-    target = next_owner[0]
+        compiler_params=pltpu.CompilerParams(vmem_limit_bytes=24 * mega),
+        cost_estimate=cost,
+    )(valid_frames, part, rest, down_weight, ress, below)
     for bit in range(sections):
-        other = [partner(v, "stream", 1 << bit) for v in carried + (target,)]
-        mine = (target >> bit) & 1 == (stream_pos >> bit) & 1
-        carried = tuple(jnp.where(mine, a, b) for a, b in zip(carried, other[:-1]))
-        target = jnp.where(mine, target, other[-1])
-    new_pix, new_act, new_res = carried
-    return (latent[None], new_pix.reshape(1, 2, 16, 48), new_act[None], new_res[None])
+        mine = (first[0:1].astype(jnp.int32) >> bit) & 1 == (stream_pos >> bit) & 1
+        first, second = (
+            jnp.where(mine, v, partner(v, "stream", 1 << bit)) for v in (first, second)
+        )
+    new_pix = first[16:48, 0:48].reshape(1, 2, 16, 48)
+    new_act = first[48:].reshape(1, 2, 16, 16, 128)
+    return (latent[None], new_pix, new_act, second.reshape(1, 2, 16, 16, 128))
 
 
 def solution(mesh):

time: 69.9 us -> 49.9 us (0.71)
  starting transfers between devices: 24.8 us -> 18.3 us
  local copies, waits for them, and re-layouts: 9.09 us -> 2.77 us
  waiting for transfers between devices: 13.4 us -> 8.08 us
  other arithmetic: 2.04 us -> 0.8 us
  between operations: 3.31 us -> 2.15 us
  Pallas kernels: 16.5 us -> 17.5 us
    ppermute x11 -> x6, waiting for transfers between devices: 13.4 us -> 8.07 us  [partner(): return lax.ppermute(value, axis, pairs)]
    ppermute x11 -> x6, starting transfers between devices: 9.9 us -> 6.28 us  [partner(): return lax.ppermute(value, axis, pairs)]
    ppermute x5 -> x3, starting transfers between devices: 7.65 us -> 4.7 us  [shifted(): lax.ppermute(value, axis, [(i, (i + by) % size) for i in range(size)])]
    unnamed x17 -> x16, local copies, waits for them, and re-layouts: 4.23 us -> 1.51 us
    convert_element_type x1 -> x0, local copies, waits for them, and re-layouts: 1.38 us -> none  [body(): stem_weight.reshape(81, 128).astype(F32)]
    broadcast_in_dim x1 -> x0, local copies, waits for them, and re-layouts: 1.35 us -> none  [body(): lines = jnp.broadcast_to(lines, (strips, streams, per // 2, 128))]
    broadcast_in_dim x2 -> x3, other arithmetic: 1.34 us -> 0.03 us  [body(): jnp.where(mine, v, partner(v, 'stream', 1 << bit))]
    slice x3 -> x2, local copies, waits for them, and re-layouts: 2.12 us -> 1.26 us  [the longest x1 0.66 us: body(): new_act = first[48:].reshape(1, 2, 16, 16, 128)]
  transfers between devices with their start and end apart: 17 -> 10, of which waited for: 8 -> 4; matrix products, arithmetic and copies ran while one was open for 7% -> 2% of each run, Pallas kernels for 3% -> 13%
where the time goes in v2:
time: 49.9 us; the launch traced here: 49.6 us
  starting transfers between devices  18.3 us (37%)
  Pallas kernels  17.5 us (35%)
  waiting for transfers between devices  8.08 us (16%)
  local copies, waits for them, and re-layouts  2.77 us (6%)
  between operations  2.15 us (4%)
  other arithmetic  0.8 us (2%)
    ppermute x6, waiting for transfers between devices, partner(): return lax.ppermute(value, axis, pairs)  8.07 us
    all_to_all x1, starting transfers between devices, body(): recv = lax.all_to_all(lines, ('strip', 'stream'), 0, 0, tiled=True)  7.3 us
    ppermute x6, starting transfers between devices, partner(): return lax.ppermute(value, axis, pairs)  6.28 us
    ppermute x3, starting transfers between devices, shifted(): lax.ppermute(value, axis, [(i, (i + by) % size) for i in range(size)])  4.7 us
    pallas_call x1, Pallas kernels, body(): pl.pallas_call(functools.partial(stem_kernel, strips), out_shape=(jax.Sha...  4.57 us
    pallas_call x1, Pallas kernels, body(): pl.pallas_call(band_kernel, out_shape=jax.ShapeDtypeStruct((432, 2048), B...  2.59 us
    pallas_call x1, Pallas kernels, body(): pl.pallas_call(functools.partial(conv_first_kernel, split), out_shape=jax...  2.46 us
    pallas_call x1, Pallas kernels, body(): pl.pallas_call(functools.partial(down_kernel, split), out_shape=jax.Shape...  2.45 us
  transfers between devices with their start and end apart: 10, of which 4 were waited for; matrix products, arithmetic and copies ran while one was open for 2% of the time, Pallas kernels for 13%

profile of v2, /device:TPU:0, one launch (start us, length us, event | category | flops | bytes accessed | tf_op | source)
XLA Modules:
  0.0 49.6 jit_solution(15010447236626777692)
XLA Ops:
  0.6 0.0 copy-start.3
  0.6 0.0 copy-start.1
  0.7 0.0 copy-start.4
  0.7 0.0 copy-start.5
  0.7 1.7 %shard_map.156 = bf16[4,8,8,128]{3,2,1,0:T(8,128)(2,1)} custom-call(bf16[48,128]{1,0:T(8,128)(2,1)} %bitcast.33, s32[1,128]{1,0:T(1,128)} %owner_ref.1, s32[1,128]{1,0:T(1,128)} %slot_ref.1), custom_call_target="tpu_custom_call" | custom-call | tf_op jit(solution)/shard_map/pallas_call | solution.py:376
  2.4 7.3 %all-to-all-start = ((bf16[32,8,128]{2,1,0:T(8,128)(2,1)}), bf16[32,8,128]{2,1,0:T(8,128)(2,1)S(1)}, u32[]{:S(2)}, u32[]{:S(2)}) async-start(bf16[32,8,128]{2,1,0:T(8,128)(2,1)} %bitcast.30), calls=%async_computation | async-start | bytes 131072 | tf_op jit(solution)/shard_map/all_to_all | solution.py:387
  9.7 1.6 %shard_map.157 = (bf16[128,128]{1,0:T(8,128)(2,1)}, bf16[64,128]{1,0:T(8,128)(2,1)}, bf16[32,128]{1,0:T(8,128)(2,1)}) custom-call(bf16[2,16,48]{2,1,0:T(8,128)(2,1)} %bitcast.26, bf16[2,16,16,128]{3,2,1,0:T(8,128)(2,1)} %bitcast.20, bf16[2,16,16,128]{3,2,1,0:T(8,128)(2,1)} %bitcast.23), custom_call_target="tpu_custom_call" | custom-call | tf_op jit(solution)/shard_map/pallas_call | solution.py:389
  11.3 1.8 %collective-permute-start = (bf16[128,128]{1,0:T(8,128)(2,1)}, bf16[128,128]{1,0:T(8,128)(2,1)S(1)}, u32[]{:S(2)}, u32[]{:S(2)}) collective-permute-start(bf16[128,128]{1,0:T(8,128)(2,1)} %get-tuple-element.12), channel_id=1, source_target_pairs={{0,1},{1,2},{2,3},{3,0},{4,5},{5,6},{6,7},{7,4},{8,9},{9,10},{10,1... | collective-permute-start | bytes 98312 | tf_op jit(solution)/shard_map/ppermute | solution.py:347
  13.1 2.1 %collective-permute-start.1 = (bf16[64,128]{1,0:T(8,128)(2,1)}, bf16[64,128]{1,0:T(8,128)(2,1)S(1)}, u32[]{:S(2)}, u32[]{:S(2)}) collective-permute-start(bf16[64,128]{1,0:T(8,128)(2,1)} %get-tuple-element.13), channel_id=1, source_target_pairs={{0,3},{1,0},{2,1},{3,2},{4,7},{5,4},{6,5},{7,6},{8,11},{9,8},{10,9... | collective-permute-start | bytes 49160 | tf_op jit(solution)/shard_map/ppermute | solution.py:347
  15.1 0.9 %collective-permute-start.2 = (bf16[32,128]{1,0:T(8,128)(2,1)}, bf16[32,128]{1,0:T(8,128)(2,1)S(1)}, u32[]{:S(2)}, u32[]{:S(2)}) collective-permute-start(bf16[32,128]{1,0:T(8,128)(2,1)} %get-tuple-element.14), channel_id=1, source_target_pairs={{0,2},{1,3},{2,0},{3,1},{4,6},{5,7},{6,4},{7,5},{8,10},{9,11},{10,... | collective-permute-start | bytes 24584 | tf_op jit(solution)/shard_map/ppermute | solution.py:347
  16.7 0.0 copy-start.7
  16.7 2.6 %shard_map.158.band_ref = bf16[432,2048]{1,0:T(8,128)(2,1)} custom-call(bf16[3,3,3,3,128]{4,3,2,1,0:T(4,128)(2,1)} %sw_ref.1), custom_call_target="tpu_custom_call" | custom-call | tf_op jit(solution)/shard_map/pallas_call | solution.py:402
  19.9 0.0 collective-permute-done.2.mid_ref
  19.9 0.0 collective-permute-done.1.above_ref
  19.9 0.0 collective-permute-done.below_ref
  19.9 0.0 all-to-all-done
  20.0 0.0 copy-done.3
  20.0 0.0 copy-done.1
  20.0 0.0 copy-done.4
  20.0 0.0 copy-done.5
  20.0 0.0 copy-start
  20.0 1.5 %copy-done = bf16[432,2048]{1,0:T(8,128)(2,1)S(1)} copy-done((bf16[432,2048]{1,0:T(8,128)(2,1)S(1)}, bf16[432,2048]{1,0:T(8,128)(2,1)}, u32[]{:S(2)}) %copy-start) | copy-done | bytes 1769496
  21.5 4.6 %shard_map.159 = (bf16[560,128]{1,0:T(8,128)(2,1)S(1)}, bf16[18,11,16,384]{3,2,1,0:T(8,128)(2,1)S(1)}, bf16[16,9,16,128]{3,2,1,0:T(8,128)(2,1)S(1)}) custom-call(s32[1]{0:T(128)S(6)} %copy.17.valid_ref, s32[1]{0:T(128)S(6)} %copy.18.target_ref, bf16[4,64,128]{2,1,0:T(8,128)(2,1)S(1)} %bitcast.22, bf16[2,16,48]{2,1,0:T(8,128)(2,1)S(1)} %bitcast.27, ...), custom_call_target="tpu_custom_call" | custom-call | tf_op jit(solution)/shard_map/pallas_call | solution.py:410
  26.1 0.0 copy-done.7
  26.1 0.0 copy-start.2
  26.1 2.5 %shard_map.160.part_ref = bf16[16,5,16,128]{3,2,1,0:T(8,128)(2,1)S(1)} custom-call(bf16[18,11,16,384]{3,2,1,0:T(8,128)(2,1)S(1)} %get-tuple-element.15.act3_ref, bf16[16,9,16,128]{3,2,1,0:T(8,128)(2,1)S(1)} %get-tuple-element.16.stem_ref, bf16[3,3,3,128,128]{4,3,2,1,0:T(8,128)(2,1)S(1)} %copy-done.7), custom_call_target="tpu_custom_call" | custom-call | flops 2000000000 | bytes 4194304 | tf_op jit(solution)/shard_map/pallas_call | solution.py:443
  28.5 0.0 copy-done.2
  28.6 0.0 copy-start.6
  28.6 2.1 %shard_map.161 = (bf16[16,4,16,128]{3,2,1,0:T(8,128)(2,1)S(1)}, bf16[512,128]{1,0:T(8,128)(2,1)S(1)}) custom-call(s32[1]{0:T(128)S(6)} %copy.17.valid_ref, bf16[18,11,16,384]{3,2,1,0:T(8,128)(2,1)S(1)} %get-tuple-element.15.act3_ref, bf16[16,9,16,128]{3,2,1,0:T(8,128)(2,1)S(1)} %get-tuple-element.16.stem_ref, bf16[3,3,3,128,128]{4,3,2,1,0:T(8,128)(2,1)S(1)} %copy-done.7, ...), custom_call_target="tpu_custom_call" | custom-call | flops 2000000000 | bytes 4194304 | tf_op jit(solution)/shard_map/pallas_call | solution.py:451
  30.7 0.1 collective-permute-start.6
  30.8 0.5 %collective-permute-start.3 = (bf16[560,128]{1,0:T(8,128)(2,1)S(1)}, bf16[560,128]{1,0:T(8,128)(2,1)S(1)}, u32[]{:S(2)}, u32[]{:S(2)}) collective-permute-start(bf16[560,128]{1,0:T(8,128)(2,1)S(1)} %get-tuple-element.18), channel_id=1, source_target_pairs={{0,4},{4,0},{8,12},{12,8},{16,20},{20,16},{24,28},{28,24},{1,5},{5... | collective-permute-start | bytes 430088 | tf_op jit(solution)/shard_map/ppermute | solution.py:342
  31.3 0.0 copy-done.6
  31.3 2.5 %shard_map.162 = bf16[4,8,8,256]{3,2,1,0:T(8,128)(2,1)} custom-call(s32[1]{0:T(128)S(6)} %copy.17.valid_ref, bf16[16,5,16,128]{3,2,1,0:T(8,128)(2,1)S(1)} %shard_map.160.part_ref, bf16[16,4,16,128]{3,2,1,0:T(8,128)(2,1)S(1)} %get-tuple-element.17.rest_ref, bf16[3,3,3,128,256]{4,3,2,1,0:T(8,128)(2,1)S(1)} %copy-done.6, bf16[2,16,16,128]{3,2,1,0:T(8,128)(2,1)S(1)} %bitcast.25, ...), custom_call_target="tpu_custom_call" | custom-call | flops 2000000000 | bytes 4194304 | tf_op jit(solution)/shard_map/pallas_call | solution.py:463
  33.7 0.0 collective-permute-done.6
  33.8 1.8 %collective-permute-start.7 = (bf16[512,128]{1,0:T(8,128)(2,1)S(1)}, bf16[512,128]{1,0:T(8,128)(2,1)S(1)}, u32[]{:S(2)}, u32[]{:S(2)}) collective-permute-start(bf16[512,128]{1,0:T(8,128)(2,1)S(1)} %broadcast_select_fusion.3), channel_id=1, source_target_pairs={{0,8},{4,12},{8,0},{12,4},{16,24},{20,28},{24,16},{28,20},{1,9},{5... | collective-permute-start | bytes 393224 | tf_op jit(solution)/shard_map/ppermute | solution.py:342
  35.5 0.0 collective-permute-done.3
  35.6 0.4 collective-permute-start.4
  36.0 4.2 %collective-permute-done.7 = bf16[512,128]{1,0:T(8,128)(2,1)S(1)} collective-permute-done((bf16[512,128]{1,0:T(8,128)(2,1)S(1)}, bf16[512,128]{1,0:T(8,128)(2,1)S(1)}, u32[]{:S(2)}, u32[]{:S(2)}) %collective-permute-start.7) | collective-permute-done | bytes 131104 | tf_op jit(solution)/shard_map/ppermute | solution.py:342
  40.2 1.8 %collective-permute-start.8 = (bf16[512,128]{1,0:T(8,128)(2,1)S(1)}, bf16[512,128]{1,0:T(8,128)(2,1)S(1)}, u32[]{:S(2)}, u32[]{:S(2)}) collective-permute-start(bf16[512,128]{1,0:T(8,128)(2,1)S(1)} %broadcast_select_fusion.4), channel_id=1, source_target_pairs={{0,16},{4,20},{8,24},{12,28},{16,0},{20,4},{24,8},{28,12},{1,17},{... | collective-permute-start | bytes 393224 | tf_op jit(solution)/shard_map/ppermute | solution.py:342
  42.0 0.4 collective-permute-done.4
  42.4 1.8 %collective-permute-start.5 = (bf16[560,128]{1,0:T(8,128)(2,1)S(1)}, bf16[560,128]{1,0:T(8,128)(2,1)S(1)}, u32[]{:S(2)}, u32[]{:S(2)}) collective-permute-start(bf16[560,128]{1,0:T(8,128)(2,1)S(1)} %broadcast_select_fusion.1), channel_id=1, source_target_pairs={{0,16},{4,20},{8,24},{12,28},{16,0},{20,4},{24,8},{28,12},{1,17},{... | collective-permute-start | bytes 430088 | tf_op jit(solution)/shard_map/ppermute | solution.py:342
  44.2 2.1 %collective-permute-done.8 = bf16[512,128]{1,0:T(8,128)(2,1)S(1)} collective-permute-done((bf16[512,128]{1,0:T(8,128)(2,1)S(1)}, bf16[512,128]{1,0:T(8,128)(2,1)S(1)}, u32[]{:S(2)}, u32[]{:S(2)}) %collective-permute-start.8) | collective-permute-done | bytes 131104 | tf_op jit(solution)/shard_map/ppermute | solution.py:342
  46.2 0.7 %broadcast_select_fusion.5 = bf16[512,128]{1,0:T(8,128)(2,1)} fusion(bf16[512,128]{1,0:T(8,128)(2,1)S(1)} %broadcast_select_fusion.4, bf16[512,128]{1,0:T(8,128)(2,1)S(1)} %collective-permute-done.8, pred[128]{0:T(512)(128)(4,1)S(1)} %compare_bitcast_fusion), kind=kLoop, calls=%fused_computation.5 | loop fusion | flops 65536 | bytes 393344 | tf_op jit(solution)/shard_map/jit(_where)/select_n | solution.py:479
  46.9 1.4 %collective-permute-done.5 = bf16[560,128]{1,0:T(8,128)(2,1)S(1)} collective-permute-done((bf16[560,128]{1,0:T(8,128)(2,1)S(1)}, bf16[560,128]{1,0:T(8,128)(2,1)S(1)}, u32[]{:S(2)}, u32[]{:S(2)}) %collective-permute-start.5) | collective-permute-done | bytes 143392 | tf_op jit(solution)/shard_map/ppermute | solution.py:342
  48.3 0.7 %slice.23 = bf16[512,128]{1,0:T(8,128)(2,1)} slice(bf16[560,128]{1,0:T(8,128)(2,1)S(1)} %broadcast_select_fusion), slice={[48:560], [0:128]} | slice | bytes 262144 | tf_op jit(solution)/shard_map/slice | solution.py:482
  49.0 0.6 %slice.22 = bf16[32,48]{1,0:T(8,128)(2,1)} slice(bf16[560,128]{1,0:T(8,128)(2,1)S(1)} %broadcast_select_fusion), slice={[16:48], [0:48]} | slice | bytes 6144 | tf_op jit(solution)/shard_map/slice | solution.py:481
  (8 shorter events, 0.1 us)
Async XLA Ops:
  0.6 19.3 %copy-start.3 = (bf16[1,2,16,48]{3,2,1,0:T(8,128)(2,1)S(1)}, bf16[1,2,16,48]{3,2,1,0:T(8,128)(2,1)}, u32[]{:S(2)}) copy-start(bf16[1,2,16,48]{3,2,1,0:T(8,128)(2,1)} %param.18) | copy-start | bytes 9220
  0.6 19.3 %copy-start.1 = (bf16[1,2,16,16,128]{4,3,2,1,0:T(8,128)(2,1)S(1)}, bf16[1,2,16,16,128]{4,3,2,1,0:T(8,128)(2,1)}, u32[]{:S(2)}) copy-start(bf16[1,2,16,16,128]{4,3,2,1,0:T(8,128)(2,1)} %param.19) | copy-start | bytes 393220
  0.7 19.3 %copy-start.4 = (f32[128]{0:T(128)S(1)}, f32[128]{0:T(128)}, u32[]{:S(2)}) copy-start(f32[128]{0:T(128)} %param.22) | copy-start | bytes 1540
  0.7 19.3 %copy-start.5 = (f32[128]{0:T(128)S(1)}, f32[128]{0:T(128)}, u32[]{:S(2)}) copy-start(f32[128]{0:T(128)} %param.23) | copy-start | bytes 1540
  2.4 17.6 %all-to-all-start = ((bf16[32,8,128]{2,1,0:T(8,128)(2,1)}), bf16[32,8,128]{2,1,0:T(8,128)(2,1)S(1)}, u32[]{:S(2)}, u32[]{:S(2)}) async-start(bf16[32,8,128]{2,1,0:T(8,128)(2,1)} %bitcast.30), calls=%async_computation | async-start | bytes 131072 | tf_op jit(solution)/shard_map/all_to_all | solution.py:387
  11.3 8.6 %collective-permute-start = (bf16[128,128]{1,0:T(8,128)(2,1)}, bf16[128,128]{1,0:T(8,128)(2,1)S(1)}, u32[]{:S(2)}, u32[]{:S(2)}) collective-permute-start(bf16[128,128]{1,0:T(8,128)(2,1)} %get-tuple-element.12), channel_id=1, source_target_pairs={{0,1},{1,2},{2,3},{3,0},{4,5},{5,6},{6,7},{7,4},{8,9},{9,10},{10,1... | collective-permute-start | bytes 98312 | tf_op jit(solution)/shard_map/ppermute | solution.py:347
  13.1 6.9 %collective-permute-start.1 = (bf16[64,128]{1,0:T(8,128)(2,1)}, bf16[64,128]{1,0:T(8,128)(2,1)S(1)}, u32[]{:S(2)}, u32[]{:S(2)}) collective-permute-start(bf16[64,128]{1,0:T(8,128)(2,1)} %get-tuple-element.13), channel_id=1, source_target_pairs={{0,3},{1,0},{2,1},{3,2},{4,7},{5,4},{6,5},{7,6},{8,11},{9,8},{10,9... | collective-permute-start | bytes 49160 | tf_op jit(solution)/shard_map/ppermute | solution.py:347
  15.1 4.8 %collective-permute-start.2 = (bf16[32,128]{1,0:T(8,128)(2,1)}, bf16[32,128]{1,0:T(8,128)(2,1)S(1)}, u32[]{:S(2)}, u32[]{:S(2)}) collective-permute-start(bf16[32,128]{1,0:T(8,128)(2,1)} %get-tuple-element.14), channel_id=1, source_target_pairs={{0,2},{1,3},{2,0},{3,1},{4,6},{5,7},{6,4},{7,5},{8,10},{9,11},{10,... | collective-permute-start | bytes 24584 | tf_op jit(solution)/shard_map/ppermute | solution.py:347
  16.7 9.4 %copy-start.7 = (bf16[3,3,3,128,128]{4,3,2,1,0:T(8,128)(2,1)S(1)}, bf16[3,3,3,128,128]{4,3,2,1,0:T(8,128)(2,1)}, u32[]{:S(2)}) copy-start(bf16[3,3,3,128,128]{4,3,2,1,0:T(8,128)(2,1)} %conv_ref.3) | copy-start | bytes 2654212
  20.0 1.5 %copy-start = (bf16[432,2048]{1,0:T(8,128)(2,1)S(1)}, bf16[432,2048]{1,0:T(8,128)(2,1)}, u32[]{:S(2)}) copy-start(bf16[432,2048]{1,0:T(8,128)(2,1)} %shard_map.158.band_ref) | copy-start | bytes 5308420
  26.1 2.5 %copy-start.2 = (bf16[1,2,16,16,128]{4,3,2,1,0:T(8,128)(2,1)S(1)}, bf16[1,2,16,16,128]{4,3,2,1,0:T(8,128)(2,1)}, u32[]{:S(2)}) copy-start(bf16[1,2,16,16,128]{4,3,2,1,0:T(8,128)(2,1)} %param.20) | copy-start | bytes 393220
  28.6 2.7 %copy-start.6 = (bf16[3,3,3,128,256]{4,3,2,1,0:T(8,128)(2,1)S(1)}, bf16[3,3,3,128,256]{4,3,2,1,0:T(8,128)(2,1)}, u32[]{:S(2)}) copy-start(bf16[3,3,3,128,256]{4,3,2,1,0:T(8,128)(2,1)} %down_ref.1) | copy-start | bytes 5308420
  30.7 3.0 %collective-permute-start.6 = (bf16[512,128]{1,0:T(8,128)(2,1)S(1)}, bf16[512,128]{1,0:T(8,128)(2,1)S(1)}, u32[]{:S(2)}, u32[]{:S(2)}) collective-permute-start(bf16[512,128]{1,0:T(8,128)(2,1)S(1)} %get-tuple-element.19), channel_id=1, source_target_pairs={{0,4},{4,0},{8,12},{12,8},{16,20},{20,16},{24,28},{28,24},{1,5},{5... | collective-permute-start | bytes 393224 | tf_op jit(solution)/shard_map/ppermute | solution.py:342
  30.8 4.8 %collective-permute-start.3 = (bf16[560,128]{1,0:T(8,128)(2,1)S(1)}, bf16[560,128]{1,0:T(8,128)(2,1)S(1)}, u32[]{:S(2)}, u32[]{:S(2)}) collective-permute-start(bf16[560,128]{1,0:T(8,128)(2,1)S(1)} %get-tuple-element.18), channel_id=1, source_target_pairs={{0,4},{4,0},{8,12},{12,8},{16,20},{20,16},{24,28},{28,24},{1,5},{5... | collective-permute-start | bytes 430088 | tf_op jit(solution)/shard_map/ppermute | solution.py:342
  33.8 6.4 %collective-permute-start.7 = (bf16[512,128]{1,0:T(8,128)(2,1)S(1)}, bf16[512,128]{1,0:T(8,128)(2,1)S(1)}, u32[]{:S(2)}, u32[]{:S(2)}) collective-permute-start(bf16[512,128]{1,0:T(8,128)(2,1)S(1)} %broadcast_select_fusion.3), channel_id=1, source_target_pairs={{0,8},{4,12},{8,0},{12,4},{16,24},{20,28},{24,16},{28,20},{1,9},{5... | collective-permute-start | bytes 393224 | tf_op jit(solution)/shard_map/ppermute | solution.py:342
  35.6 6.8 %collective-permute-start.4 = (bf16[560,128]{1,0:T(8,128)(2,1)S(1)}, bf16[560,128]{1,0:T(8,128)(2,1)S(1)}, u32[]{:S(2)}, u32[]{:S(2)}) collective-permute-start(bf16[560,128]{1,0:T(8,128)(2,1)S(1)} %broadcast_select_fusion.2), channel_id=1, source_target_pairs={{0,8},{4,12},{8,0},{12,4},{16,24},{20,28},{24,16},{28,20},{1,9},{5... | collective-permute-start | bytes 430088 | tf_op jit(solution)/shard_map/ppermute | solution.py:342
  40.2 6.0 %collective-permute-start.8 = (bf16[512,128]{1,0:T(8,128)(2,1)S(1)}, bf16[512,128]{1,0:T(8,128)(2,1)S(1)}, u32[]{:S(2)}, u32[]{:S(2)}) collective-permute-start(bf16[512,128]{1,0:T(8,128)(2,1)S(1)} %broadcast_select_fusion.4), channel_id=1, source_target_pairs={{0,16},{4,20},{8,24},{12,28},{16,0},{20,4},{24,8},{28,12},{1,17},{... | collective-permute-start | bytes 393224 | tf_op jit(solution)/shard_map/ppermute | solution.py:342
  42.4 5.9 %collective-permute-start.5 = (bf16[560,128]{1,0:T(8,128)(2,1)S(1)}, bf16[560,128]{1,0:T(8,128)(2,1)S(1)}, u32[]{:S(2)}, u32[]{:S(2)}) collective-permute-start(bf16[560,128]{1,0:T(8,128)(2,1)S(1)} %broadcast_select_fusion.1), channel_id=1, source_target_pairs={{0,16},{4,20},{8,24},{12,28},{16,0},{20,4},{24,8},{28,12},{1,17},{... | collective-permute-start | bytes 430088 | tf_op jit(solution)/shard_map/ppermute | solution.py:342

commit v3 on v2

--- a/solution.py
+++ b/solution.py
@@ -13,11 +13,16 @@
 F32 = jnp.float32
 BF16 = jnp.bfloat16
 VM = pl.BlockSpec(memory_space=pltpu.VMEM)
-SM = pl.BlockSpec(memory_space=pltpu.SMEM)
+ANY = pl.BlockSpec(memory_space=pl.ANY)
 
 
 def iota(shape, axis):
     return lax.broadcasted_iota(jnp.int32, shape, axis)
+
+
+def whole(scalars_ref, which):
+    row = scalars_ref[...].astype(F32).reshape(1, 128)
+    return jnp.sum(jnp.where(iota((1, 128), 1) == which, row, 0.0)).astype(jnp.int32)
 
 
 def dot(a, b):
@@ -55,61 +60,66 @@
             out_ref[strip] = out.reshape(out_ref.shape[1:])
 
 
-def pack_kernel(pix_ref, act_ref, res_ref, down_ref, up_ref, mid_ref):
-    pix = jnp.concatenate(
-        [pix_ref[...].reshape(32, 48).astype(F32), jnp.zeros((32, 80), F32)], axis=1
-    ).astype(BF16)
+def pack_kernel(after_ref, pix_ref, sw_ref, act_ref, res_ref, down_ref, up_ref, mid_ref, sw, sems):
+    del after_ref
+    copies = []
     for f in range(2):
-        down_ref[f * 32 : f * 32 + 32] = act_ref[f, 14:16].reshape(32, 128)
-        down_ref[64 + f * 16 : 80 + f * 16] = res_ref[f, 15]
-        up_ref[f * 16 : f * 16 + 16] = act_ref[f, 0]
-    down_ref[96:128] = pix
-    up_ref[32:64] = pix
-    mid_ref[...] = pix
-
-
-def band_kernel(sw_ref, out_ref, wide):
-    wide[...] = jnp.zeros(wide.shape, F32)
-    for tap in range(27):
-        b, a, c = tap // 9, tap // 3 % 3, tap % 3
+        copies.append((act_ref.at[f, 14:16], down_ref.at[2 * f : 2 * f + 2]))
+        copies.append((res_ref.at[f, 15:16], down_ref.at[4 + f : 5 + f]))
+        copies.append((act_ref.at[f, 0:1], up_ref.at[f : f + 1]))
+    copies = [pltpu.make_async_copy(a, b, sems.at[i]) for i, (a, b) in enumerate(copies)]
+    for copy in copies:
+        copy.start()
+    pix = pix_ref[...].reshape(32, 48).astype(F32)
+    pix = jnp.concatenate([pix, jnp.zeros((32, 80), F32)], axis=1)
+    pix = pix.astype(BF16).reshape(2, 16, 128)
+    down_ref[6:8] = pix
+    up_ref[2:4] = pix
+    mid_ref[0:2] = pix
+    sw[...] = jnp.zeros(sw.shape, F32)
+    for k in range(2):
         for e in range(3):
-            wide[tap, 16 + e : 17 + e] = sw_ref[a, b, e, c : c + 1].astype(F32)
-    for w in range(16):
-        block = wide[:, 17 - w : 33 - w].reshape(432, 128)
-        out_ref[:, w * 128 : (w + 1) * 128] = block.astype(BF16)
+            for a in range(3):
+                for b in range(3):
+                    at = 27 * (k + e) + 9 * a + 3 * b
+                    sw[at : at + 3, k * 128 : k * 128 + 128] = sw_ref[a, b, e].astype(F32)
+    for k in range(2):
+        half = sw[:, k * 128 : k * 128 + 128].astype(BF16)
+        mid_ref[2 + 8 * k : 10 + 8 * k] = half.reshape(8, 16, 128)
+    for copy in copies:
+        copy.wait()
 
 
 def stem_kernel(
     strips,
-    valid_ref,
-    target_ref,
+    scalars_ref,
+    gain_ref,
+    bias_ref,
     recv_ref,
     pix_ref,
+    old_ref,
     below_ref,
     above_ref,
     mid_ref,
-    band_ref,
-    gain_ref,
-    bias_ref,
-    act_cache_ref,
     pay_ref,
     act3,
     stem_ref,
     pc,
     zs,
     xs,
+    ys,
     stem,
     act,
     cache,
 ):
     j = lax.axis_index("strip")
-    valid = valid_ref[0]
+    valid = whole(scalars_ref, 0)
     rows_all = strips * 16
-    pc[...] = jnp.zeros(pc.shape, F32)
+    pc[j] = jnp.zeros((32, 128), F32)
     pc[j, :, 0:48] = pix_ref[...].reshape(32, 48).astype(F32)
-    pc[lax.rem(j + strips - 1, strips)] = below_ref[96:128].astype(F32)
-    pc[lax.rem(j + 1, strips)] = above_ref[32:64].astype(F32)
-    pc[lax.rem(j + 2, strips)] = mid_ref[...].astype(F32)
+    pc[lax.rem(j + strips - 1, strips)] = below_ref[6:8].reshape(32, 128).astype(F32)
+    pc[lax.rem(j + 1, strips)] = above_ref[2:4].reshape(32, 128).astype(F32)
+    pc[lax.rem(j + 2, strips)] = mid_ref[0:2].reshape(32, 128).astype(F32)
     zs[...] = jnp.zeros(zs.shape, F32)
     lane = iota((128, 128), 1)
     sub = iota((128, 128), 0)
@@ -143,29 +153,44 @@
     chit = jnp.where(iota((32, 32), 0) == cplace, 1.0, 0.0)
     source = jnp.concatenate([jnp.where(lane < 48, both, 0.0), pc[j]], axis=0).astype(BF16)
     fresh = dot(jnp.concatenate([hit.reshape(32, 128), chit], axis=1).astype(BF16), source)
-    target = jnp.broadcast_to(target_ref[0].astype(F32), (16, 128))
-    pay_ref[0:16] = target.astype(BF16)
+    target = whole(scalars_ref, 1).astype(F32)
+    pay_ref[0:16] = jnp.full((16, 128), target, F32).astype(BF16)
     pay_ref[16:48] = fresh.astype(BF16)
     high = rows_all + 4
     for b in range(3):
         for a in range(3):
             q = (b * 3 + a) * 48
             xs[2 : high + 2, :, q : q + 48] = zs[a, 1 + b : high + 1 + b, :, 0:48]
-    full = xs[4 : 4 + rows_all].reshape(rows_all * 8, 432).astype(BF16)
-    base = j * 16 + 2
-    first, second = xs[pl.ds(base, 11)], xs[pl.ds(base + 8, 11)]
-    low = iota((11, 8, 432), 1) < 4
+    lanes = iota((8, 1024), 1)
+    pair, m = lanes >> 7, lanes & 127
+    col = (m * 2428) >> 16
+    tap = m - 27 * col
+    a = (tap * 7282) >> 16
+    b = ((tap - 9 * a) * 21846) >> 16
+    c = tap - 9 * a - 3 * b
+    w = 2 * pair - 1 + col
+    source = jnp.where((m < 108) & (w >= 0) & (w < 16), (b * 3 + a) * 48 + c * 16 + w, -1)
+    line = iota((54, 8, 1024), 0) * 8 + iota((54, 8, 1024), 1)
+    spread = jnp.where(line == source[None], 1.0, 0.0).reshape(432, 1024).astype(BF16)
+    patches = xs[2 : high + 2].reshape(high * 8, 432).astype(BF16)
+    ys[...] = dot(patches, spread).reshape(high, 8, 1024)
+    full = ys[2 : 2 + rows_all].reshape(rows_all * 8, 1024).astype(BF16)
+    base = j * 16
+    first, second = ys[pl.ds(base, 11)], ys[pl.ds(base + 8, 11)]
+    low = iota((11, 8, 1024), 1) < 4
     own_even = jnp.where(low, first, pltpu.roll(second, 4, 1))
     own_odd = jnp.where(low, pltpu.roll(first, 4, 1), second)
-    own = jnp.concatenate([own_even, own_odd], axis=0).reshape(176, 432).astype(BF16)
+    own = jnp.concatenate([own_even, own_odd], axis=0).reshape(176, 1024).astype(BF16)
+    weight = jnp.concatenate(
+        [mid_ref[2 + 8 * k : 10 + 8 * k].reshape(128, 128) for k in range(2)], axis=1
+    )
     s1 = jnp.zeros((8, 256), F32)
     s2 = jnp.zeros((8, 256), F32)
     for chunk in range(8):
-        weight = band_ref[:, chunk * 256 : (chunk + 1) * 256]
-        out = dot(full, weight).astype(BF16).astype(F32).reshape(rows_all, 8, 256)
+        out = dot(full[:, chunk * 128 : chunk * 128 + 128], weight).astype(BF16).astype(F32).reshape(rows_all, 8, 256)
         s1 = s1 + jnp.sum(out, axis=0)
         s2 = s2 + jnp.sum(out * out, axis=0)
-        mine = dot(own, weight).astype(BF16).astype(F32).reshape(2, 11, 8, 256)
+        mine = dot(own[:, chunk * 128 : chunk * 128 + 128], weight).astype(BF16).astype(F32).reshape(2, 11, 8, 256)
         for i in range(2):
             part = mine[:, :, :, i * 128 : (i + 1) * 128]
             stem[:, 2 * chunk + i] = part
@@ -180,8 +205,8 @@
     mean = exact(s1, same) / count
     inv = lax.rsqrt(exact(s2, same) / count - mean * mean + EPSILON)
     low8 = iota((8, 128), 0) < 4
-    scale = inv * gain_ref[...]
-    shift = bias_ref[...] - mean * scale
+    scale = inv * gain_ref[...].reshape(1, 128)
+    shift = bias_ref[...].reshape(1, 128) - mean * scale
     scales = (
         jnp.where(low8, scale, pltpu.roll(scale, 4, 0)),
         jnp.where(low8, pltpu.roll(scale, 4, 0), scale),
@@ -190,13 +215,13 @@
         jnp.where(low8, shift, pltpu.roll(shift, 4, 0)),
         jnp.where(low8, pltpu.roll(shift, 4, 0), shift),
     )
-    cache[...] = jnp.zeros(cache.shape, F32)
     has_above = jnp.where(j > 0, 1.0, 0.0)
     has_below = jnp.where(j < strips - 1, 1.0, 0.0)
     for f in range(2):
-        cache[f, 0:32] = below_ref[f * 32 : f * 32 + 32].astype(F32) * has_above
-        cache[f, 32:288] = act_cache_ref[f].reshape(256, 128).astype(F32)
-        cache[f, 288:304] = above_ref[f * 16 : f * 16 + 16].astype(F32) * has_below
+        cache[f, 304:416] = jnp.zeros((112, 128), F32)
+        cache[f, 32:288] = old_ref[f].reshape(256, 128).astype(F32)
+        cache[f, 0:32] = below_ref[2 * f : 2 * f + 2].reshape(32, 128).astype(F32) * has_above
+        cache[f, 288:304] = above_ref[f].astype(F32) * has_below
     half = iota((11, 8, 128), 1) // 4
     line_of = j * 16 + iota((11, 8, 128), 0) - 2 + 8 * half
     inside = jnp.where((line_of >= 0) & (line_of < rows_all), 1.0, 0.0)
@@ -232,7 +257,7 @@
         for y in range(16):
             at = (f & 1) * (16 * 88) + (y % 8 + 2) * 8 + y // 8 * 4 + (f >> 1)
             block = act_rows[pl.ds(at, 16, stride=88)]
-            block = jnp.where(g < 2, act_cache_ref[1, y].astype(F32), block)
+            block = jnp.where(g < 2, old_ref[1, y].astype(F32), block)
             to = 48 + i * 256 + y * 16
             pay_ref[to : to + 16] = block.astype(BF16)
 
@@ -240,44 +265,77 @@
 def conv_rows(first, last, act3_ref, stem_ref, conv_ref):
     j = lax.axis_index("strip")
     count = last - first
+    zero = jnp.zeros((384, 128), BF16)
+
+    def weight(col, b, e):
+        if not 0 <= e <= 2:
+            return zero
+        return jnp.concatenate([conv_ref[a, b, e] for a in range(3)], axis=0)
+
     weights = jnp.concatenate(
-        [conv_ref[a, b, e] for b in range(3) for e in range(3) for a in range(3)], axis=0
+        [
+            jnp.concatenate([weight(col, b, col - k) for k in range(2)], axis=1)
+            for col in range(4)
+            for b in range(3)
+        ],
+        axis=0,
     )
     line = first + iota((count, 16, 128), 0)
     outside = (j == 0) & (line == 0) & (iota((count, 16, 128), 1) % 8 < 4)
     keep = jnp.where(outside, 0.0, 1.0)
-    groups = []
-    for w0 in range(0, 16, 4):
+    pairs = []
+    for w0 in range(0, 16, 8):
         left = jnp.concatenate(
             [
-                act3_ref[w0 + e : w0 + e + 4, first + b : last + b].reshape(4 * count * 16, 384)
+                jnp.concatenate(
+                    [
+                        act3_ref[w0 + 2 * k + col, first + b : last + b].reshape(count * 16, 384)
+                        for k in range(4)
+                    ],
+                    axis=0,
+                )
+                for col in range(4)
                 for b in range(3)
-                for e in range(3)
             ],
             axis=1,
         )
-        out = dot(left, weights).reshape(4, count, 16, 128)
-        out = out + stem_ref[w0 : w0 + 4, first:last].astype(F32)
-        groups.append((out * keep).astype(BF16))
-    return groups
+        out = dot(left, weights).reshape(4, count, 16, 256)
+        for k in range(4):
+            for i in range(2):
+                w = w0 + 2 * k + i
+                value = out[k, :, :, i * 128 : i * 128 + 128]
+                value = value + stem_ref[w, first:last].astype(F32)
+                pairs.append((value * keep).astype(BF16))
+    return pairs
 
 
 def conv_first_kernel(split, act3_ref, stem_ref, conv_ref, out_ref):
-    for g, value in enumerate(conv_rows(0, split, act3_ref, stem_ref, conv_ref)):
-        out_ref[g * 4 : g * 4 + 4] = value
+    for w, value in enumerate(conv_rows(0, split, act3_ref, stem_ref, conv_ref)):
+        out_ref[w] = value
 
 
 def conv_second_kernel(
-    split, valid_ref, act3_ref, stem_ref, conv_ref, part_ref, res_cache_ref, out_ref, pay_ref, res
+    split,
+    scalars_ref,
+    act3_ref,
+    stem_ref,
+    conv_ref,
+    part_ref,
+    res_cache_ref,
+    after_ref,
+    out_ref,
+    pay_ref,
+    res,
 ):
-    valid = valid_ref[0]
+    del after_ref
+    valid = whole(scalars_ref, 0)
     part = part_ref[...].astype(F32)
     for p in range(2):
         res[p, :, 0:split] = part[:, :, p * 8 : p * 8 + 8]
-    for g, value in enumerate(conv_rows(split, 9, act3_ref, stem_ref, conv_ref)):
-        out_ref[g * 4 : g * 4 + 4] = value
+    for w, value in enumerate(conv_rows(split, 9, act3_ref, stem_ref, conv_ref)):
+        out_ref[w] = value
         for p in range(2):
-            res[p, g * 4 : g * 4 + 4, split:9] = value.astype(F32)[:, :, p * 8 : p * 8 + 8]
+            res[p, w, split:9] = value.astype(F32)[:, p * 8 : p * 8 + 8]
     res_rows = res.reshape(2 * 16 * 9 * 8, 128)
     for i in range(2):
         g = valid + i
@@ -291,14 +349,26 @@
 
 
 def down_kernel(
-    split, valid_ref, part_ref, rest_ref, down_ref, res_cache_ref, below_ref, lat_ref, rcache, res3, lat
+    split,
+    scalars_ref,
+    part_ref,
+    rest_ref,
+    down_ref,
+    res_cache_ref,
+    below_ref,
+    after_ref,
+    lat_ref,
+    rcache,
+    res3,
+    lat,
 ):
+    del after_ref
     j = lax.axis_index("strip")
-    valid = valid_ref[0]
+    valid = whole(scalars_ref, 0)
     rcache[...] = jnp.zeros(rcache.shape, F32)
     has_above = jnp.where(j > 0, 1.0, 0.0)
     for f in range(2):
-        rcache[f, 0:16] = below_ref[64 + f * 16 : 80 + f * 16].astype(F32) * has_above
+        rcache[f, 0:16] = below_ref[4 + f].astype(F32) * has_above
         rcache[f, 16:272] = res_cache_ref[f].reshape(256, 128).astype(F32)
     begin = iota((9, 8, 128), 1) % 4 == 0
     res3[0] = jnp.zeros(res3.shape[1:], F32)
@@ -370,6 +440,7 @@
     per = fill // streams
     pix, acts, ress = pixel_cache[0], act_cache[0], res_cache[0]
     mega = 1024 * 1024
+    cost = pl.CostEstimate(flops=2 * 10**9, bytes_accessed=4 * mega, transcendentals=0)
     half_per = fill // streams // 2
     direct = half_per % 8 == 0
     line_shape = (strips, streams, half_per, 128) if direct else (fill // 2, 128)
@@ -379,6 +450,7 @@
         in_specs=[VM] * 3,
         out_specs=VM,
         scratch_shapes=[pltpu.VMEM((128, 2 * fill), F32)],
+        cost_estimate=cost,
     )(loader_rows[0].T, load_owner, load_slot)
     if not direct:
         lines = lines.reshape(1, streams, half_per, 128)
@@ -389,23 +461,19 @@
     below, above, mid = pl.pallas_call(
         pack_kernel,
         out_shape=(
-            jax.ShapeDtypeStruct((128, 128), BF16),
-            jax.ShapeDtypeStruct((64, 128), BF16),
-            jax.ShapeDtypeStruct((32, 128), BF16),
+            jax.ShapeDtypeStruct((8, 16, 128), BF16),
+            jax.ShapeDtypeStruct((4, 16, 128), BF16),
+            jax.ShapeDtypeStruct((18, 16, 128), BF16),
         ),
-        in_specs=[VM] * 3,
+        in_specs=[ANY] + [VM] * 2 + [ANY] * 2,
         out_specs=(VM,) * 3,
-    )(pix, acts, ress)
+        scratch_shapes=[pltpu.VMEM((128, 256), F32), pltpu.SemaphoreType.DMA((6,))],
+        compiler_params=pltpu.CompilerParams(vmem_limit_bytes=4 * mega),
+    )(lines, pix, stem_weight, acts, ress)
     below = shifted(below, "strip", 1)
     above = shifted(above, "strip", -1)
     mid = shifted(mid, "strip", 2)
-    band = pl.pallas_call(
-        band_kernel,
-        out_shape=jax.ShapeDtypeStruct((432, 2048), BF16),
-        in_specs=[VM],
-        out_specs=VM,
-        scratch_shapes=[pltpu.VMEM((27, 40, 128), F32)],
-    )(stem_weight)
+    scalars = jnp.concatenate([valid_frames, next_owner, jnp.zeros((126,), jnp.int32)])
     rows_all = strips * 16
     first, act3, stem = pl.pallas_call(
         functools.partial(stem_kernel, strips),
@@ -414,32 +482,31 @@
             jax.ShapeDtypeStruct((18, 11, 16, 384), BF16),
             jax.ShapeDtypeStruct((16, 9, 16, 128), BF16),
         ),
-        in_specs=[SM] * 2 + [VM] * 9,
+        in_specs=[VM] * 9,
         out_specs=(VM,) * 3,
         scratch_shapes=[
             pltpu.VMEM((strips, 32, 128), F32),
             pltpu.VMEM((3, rows_all + 8, 8, 128), F32),
             pltpu.VMEM((rows_all + 8, 8, 432), F32),
+            pltpu.VMEM((rows_all + 4, 8, 1024), F32),
             pltpu.VMEM((2, 16, 11, 8, 128), F32),
             pltpu.VMEM((2, 16, 11, 8, 128), F32),
             pltpu.VMEM((2, 416, 128), F32),
         ],
         compiler_params=pltpu.CompilerParams(vmem_limit_bytes=24 * mega),
+        cost_estimate=cost,
     )(
-        valid_frames,
-        next_owner,
+        scalars,
+        norm_gain,
+        norm_bias,
         recv,
         pix,
+        acts,
         below,
         above,
         mid,
-        band,
-        norm_gain.reshape(1, 128),
-        norm_bias.reshape(1, 128),
-        acts,
     )
     split = 5
-    cost = pl.CostEstimate(flops=2 * 10**9, bytes_accessed=4 * mega, transcendentals=0)
     part = pl.pallas_call(
         functools.partial(conv_first_kernel, split),
         out_shape=jax.ShapeDtypeStruct((16, split, 16, 128), BF16),
@@ -448,22 +515,32 @@
         compiler_params=pltpu.CompilerParams(vmem_limit_bytes=24 * mega),
         cost_estimate=cost,
     )(act3, stem, conv_weight)
+    keeps = []
+
+    def passed(value):
+        bit = len(keeps)
+        keeps.append((value[0:1].astype(jnp.int32) >> bit) & 1 == (stream_pos >> bit) & 1)
+        return jnp.where(keeps[bit], value, partner(value, "stream", 1 << bit))
+
+    first = passed(first)
     rest, second = pl.pallas_call(
         functools.partial(conv_second_kernel, split),
         out_shape=(
             jax.ShapeDtypeStruct((16, 9 - split, 16, 128), BF16),
             jax.ShapeDtypeStruct((512, 128), BF16),
         ),
-        in_specs=[SM] + [VM] * 5,
+        in_specs=[VM] * 6 + [ANY],
         out_specs=(VM,) * 2,
         scratch_shapes=[pltpu.VMEM((2, 16, 9, 8, 128), F32)],
         compiler_params=pltpu.CompilerParams(vmem_limit_bytes=24 * mega),
         cost_estimate=cost,
-    )(valid_frames, act3, stem, conv_weight, part, ress)
+    )(scalars, act3, stem, conv_weight, part, ress, first)
+    for bit in range(1, sections - 1):
+        first = passed(first)
     latent = pl.pallas_call(
         functools.partial(down_kernel, split),
         out_shape=jax.ShapeDtypeStruct((4, 8, 8, 256), BF16),
-        in_specs=[SM] + [VM] * 5,
+        in_specs=[VM] * 6 + [ANY],
         out_specs=VM,
         scratch_shapes=[
             pltpu.VMEM((2, 384, 128), F32),
@@ -472,12 +549,11 @@
         ],
         compiler_params=pltpu.CompilerParams(vmem_limit_bytes=24 * mega),
         cost_estimate=cost,
-    )(valid_frames, part, rest, down_weight, ress, below)
+    )(scalars, part, rest, down_weight, ress, below, first)
+    if sections > 1:
+        first = passed(first)
     for bit in range(sections):
-        mine = (first[0:1].astype(jnp.int32) >> bit) & 1 == (stream_pos >> bit) & 1
-        first, second = (
-            jnp.where(mine, v, partner(v, "stream", 1 << bit)) for v in (first, second)
-        )
+        second = jnp.where(keeps[bit], second, partner(second, "stream", 1 << bit))
     new_pix = first[16:48, 0:48].reshape(1, 2, 16, 48)
     new_act = first[48:].reshape(1, 2, 16, 16, 128)
     return (latent[None], new_pix, new_act, second.reshape(1, 2, 16, 16, 128))

time: 49.9 us -> 42.4 us (0.85)
  Pallas kernels: 17.5 us -> 12 us
  waiting for transfers between devices: 8.08 us -> 6.59 us
  local copies, waits for them, and re-layouts: 2.77 us -> 2.16 us
    pallas_call x2 -> x1, Pallas kernels: 4.2 us -> 0.11 us  [body(): pl.pallas_call(pack_kernel, out_shape=(jax.ShapeDtypeStruct((8, 16, 128),...]
    ppermute x6, waiting for transfers between devices: 8.07 us -> 4.76 us  [partner(): return lax.ppermute(value, axis, pairs)]
    ppermute x3, waiting for transfers between devices: 0.01 us -> 1.83 us  [shifted(): lax.ppermute(value, axis, [(i, (i + by) % size) for i in range(size)])]
    ppermute x3, starting transfers between devices: 4.7 us -> 5.65 us  [shifted(): lax.ppermute(value, axis, [(i, (i + by) % size) for i in range(size)])]
    ppermute x6, starting transfers between devices: 6.28 us -> 5.39 us  [partner(): return lax.ppermute(value, axis, pairs)]
    pallas_call x1, Pallas kernels: 2.46 us -> 1.68 us  [body(): pl.pallas_call(functools.partial(conv_first_kernel, split), out_shape=jax...]
    pallas_call x1, Pallas kernels: 2.12 us -> 1.43 us  [body(): pl.pallas_call(functools.partial(conv_second_kernel, split), out_shape=(j...]
    unnamed x16 -> x18, local copies, waits for them, and re-layouts: 1.51 us -> 0.89 us
  transfers between devices with their start and end apart: 10 -> 10, of which waited for: 4 -> 5; matrix products, arithmetic and copies ran while one was open for 2% -> 3% of each run, Pallas kernels for 13% -> 14%
where the time goes in v3:
time: 42.4 us; the launch traced here: 42.1 us
  starting transfers between devices  18.3 us (43%)
  Pallas kernels  12 us (28%)
  waiting for transfers between devices  6.59 us (16%)
  local copies, waits for them, and re-layouts  2.16 us (5%)
  between operations  2.14 us (5%)
  other arithmetic  0.88 us (2%)
    all_to_all x1, starting transfers between devices, body(): recv = lax.all_to_all(lines, ('strip', 'stream'), 0, 0, tiled=True)  7.3 us
    ppermute x3, starting transfers between devices, shifted(): lax.ppermute(value, axis, [(i, (i + by) % size) for i in range(size)])  5.65 us
    ppermute x6, starting transfers between devices, partner(): return lax.ppermute(value, axis, pairs)  5.39 us
    ppermute x6, waiting for transfers between devices, partner(): return lax.ppermute(value, axis, pairs)  4.76 us
    pallas_call x1, Pallas kernels, body(): pl.pallas_call(functools.partial(stem_kernel, strips), out_shape=(jax.Sha...  4.49 us
    pallas_call x1, Pallas kernels, body(): pl.pallas_call(functools.partial(down_kernel, split), out_shape=jax.Shape...  2.52 us
    ppermute x3, waiting for transfers between devices, shifted(): lax.ppermute(value, axis, [(i, (i + by) % size) for i in range(size)])  1.83 us
    pallas_call x1, Pallas kernels, body(): pl.pallas_call(functools.partial(sort_kernel, streams), out_shape=jax.Sha...  1.77 us
  transfers between devices with their start and end apart: 10, of which 5 were waited for; matrix products, arithmetic and copies ran while one was open for 3% of the time, Pallas kernels for 14%

profile of v3, /device:TPU:0, one launch (start us, length us, event | category | flops | bytes accessed | tf_op | source)
XLA Modules:
  0.0 42.1 jit_solution(8111948786210706973)
XLA Ops:
  0.6 0.0 copy-start.1
  0.6 0.0 copy-start.2
  0.7 0.0 copy-start.3
  0.7 0.0 copy-start.4
  0.7 0.0 copy-start.7
  0.7 0.0 copy-start.8
  0.7 1.8 %shard_map.156 = bf16[4,8,8,128]{3,2,1,0:T(8,128)(2,1)} custom-call(bf16[48,128]{1,0:T(8,128)(2,1)} %bitcast.31, s32[1,128]{1,0:T(1,128)} %owner_ref.1, s32[1,128]{1,0:T(1,128)} %slot_ref.1), custom_call_target="tpu_custom_call" | custom-call | flops 2000000000 | bytes 4194304 | tf_op jit(solution)/shard_map/pallas_call | solution.py:447
  2.5 7.3 %all-to-all-start = ((bf16[32,8,128]{2,1,0:T(8,128)(2,1)}), bf16[32,8,128]{2,1,0:T(8,128)(2,1)S(1)}, u32[]{:S(2)}, u32[]{:S(2)}) async-start(bf16[32,8,128]{2,1,0:T(8,128)(2,1)} %bitcast.18), calls=%async_computation | async-start | bytes 131072 | tf_op jit(solution)/shard_map/all_to_all | solution.py:459
  9.8 0.0 copy-done.1
  9.8 0.0 copy-done.2
  9.8 0.0 copy-done.3
  9.8 0.0 copy-done.4
  9.8 0.0 copy-start
  9.8 0.9 %copy-done = bf16[4,8,8,128]{3,2,1,0:T(8,128)(2,1)S(1)} copy-done((bf16[4,8,8,128]{3,2,1,0:T(8,128)(2,1)S(1)}, bf16[4,8,8,128]{3,2,1,0:T(8,128)(2,1)}, u32[]{:S(2)}) %copy-start) | copy-done | bytes 65560
  10.7 0.1 shard_map.157
  10.8 1.8 %collective-permute-start = (bf16[8,16,128]{2,1,0:T(8,128)(2,1)S(1)}, bf16[8,16,128]{2,1,0:T(8,128)(2,1)S(1)}, u32[]{:S(2)}, u32[]{:S(2)}) collective-permute-start(bf16[8,16,128]{2,1,0:T(8,128)(2,1)S(1)} %get-tuple-element.12), channel_id=1, source_target_pairs={{0,1},{1,2},{2,3},{3,0},{4,5},{5,6},{6,7},{7,4},{8,9},{9,10},{10,1... | collective-permute-start | bytes 98312 | tf_op jit(solution)/shard_map/ppermute | solution.py:417
  12.6 2.4 %collective-permute-start.2 = (bf16[18,16,128]{2,1,0:T(8,128)(2,1)S(1)}, bf16[18,16,128]{2,1,0:T(8,128)(2,1)S(1)}, u32[]{:S(2)}, u32[]{:S(2)}) collective-permute-start(bf16[18,16,128]{2,1,0:T(8,128)(2,1)S(1)} %get-tuple-element.14), channel_id=1, source_target_pairs={{0,2},{1,3},{2,0},{3,1},{4,6},{5,7},{6,4},{7,5},{8,10},{9,11},{10,... | collective-permute-start | bytes 221192 | tf_op jit(solution)/shard_map/ppermute | solution.py:417
  15.0 1.4 %collective-permute-start.1 = (bf16[4,16,128]{2,1,0:T(8,128)(2,1)S(1)}, bf16[4,16,128]{2,1,0:T(8,128)(2,1)S(1)}, u32[]{:S(2)}, u32[]{:S(2)}) collective-permute-start(bf16[4,16,128]{2,1,0:T(8,128)(2,1)S(1)} %get-tuple-element.13), channel_id=1, source_target_pairs={{0,3},{1,0},{2,1},{3,2},{4,7},{5,4},{6,5},{7,6},{8,11},{9,8},{10,9... | collective-permute-start | bytes 49160 | tf_op jit(solution)/shard_map/ppermute | solution.py:417
  17.8 0.1 pad_add_fusion.scalars_ref
  17.8 0.9 %collective-permute-done.1.above_ref = bf16[4,16,128]{2,1,0:T(8,128)(2,1)S(1)} collective-permute-done((bf16[4,16,128]{2,1,0:T(8,128)(2,1)S(1)}, bf16[4,16,128]{2,1,0:T(8,128)(2,1)S(1)}, u32[]{:S(2)}, u32[]{:S(2)}) %collective-permute-start.1) | collective-permute-done | bytes 16416 | tf_op jit(solution)/shard_map/ppermute | solution.py:417
  18.8 0.0 collective-permute-done.below_ref
  18.8 0.9 %collective-permute-done.2.mid_ref = bf16[18,16,128]{2,1,0:T(8,128)(2,1)S(1)} collective-permute-done((bf16[18,16,128]{2,1,0:T(8,128)(2,1)S(1)}, bf16[18,16,128]{2,1,0:T(8,128)(2,1)S(1)}, u32[]{:S(2)}, u32[]{:S(2)}) %collective-permute-start.2) | collective-permute-done | bytes 73760 | tf_op jit(solution)/shard_map/ppermute | solution.py:417
  19.7 0.0 all-to-all-done
  19.7 0.0 copy-done.7
  19.7 0.0 copy-done.8
  19.7 0.0 copy-start.6
  19.7 4.5 %shard_map.158 = (bf16[560,128]{1,0:T(8,128)(2,1)S(1)}, bf16[18,11,16,384]{3,2,1,0:T(8,128)(2,1)S(1)}, bf16[16,9,16,128]{3,2,1,0:T(8,128)(2,1)S(1)}) custom-call(s32[128]{0:T(128)S(1)} %pad_add_fusion.scalars_ref, f32[128]{0:T(128)S(1)} %copy-done.7, f32[128]{0:T(128)S(1)} %copy-done.8, bf16[4,64,128]{2,1,0:T(8,128)(2,1)S(1)} %bitcast.25, ...), custom_call_target="tpu_custom_call" | custom-call | flops 2000000000 | bytes 4194304 | tf_op jit(solution)/shard_map/pallas_call | solution.py:478
  24.2 0.1 collective-permute-start.3
  24.3 0.0 copy-done.6
  24.3 1.7 %shard_map.159.part_ref = bf16[16,5,16,128]{3,2,1,0:T(8,128)(2,1)S(1)} custom-call(bf16[18,11,16,384]{3,2,1,0:T(8,128)(2,1)S(1)} %get-tuple-element.15.act3_ref, bf16[16,9,16,128]{3,2,1,0:T(8,128)(2,1)S(1)} %get-tuple-element.16.stem_ref, bf16[3,3,3,128,128]{4,3,2,1,0:T(8,128)(2,1)S(1)} %copy-done.6), custom_call_target="tpu_custom_call" | custom-call | flops 2000000000 | bytes 4194304 | tf_op jit(solution)/shard_map/pallas_call | solution.py:510
  26.0 0.0 collective-permute-done.3
  26.0 0.0 copy-start.5
  26.0 1.6 %collective-permute-start.4 = (bf16[560,128]{1,0:T(8,128)(2,1)S(1)}, bf16[560,128]{1,0:T(8,128)(2,1)S(1)}, u32[]{:S(2)}, u32[]{:S(2)}) collective-permute-start(bf16[560,128]{1,0:T(8,128)(2,1)S(1)} %broadcast_select_fusion.2.after_ref), channel_id=1, source_target_pairs={{0,8},{4,12},{8,0},{12,4},{16,24},{20,28},{24,16},{28,20},{1,9},{5... | collective-permute-start | bytes 430088 | tf_op jit(solution)/shard_map/ppermute | solution.py:412
  27.6 1.4 %shard_map.160 = (bf16[16,4,16,128]{3,2,1,0:T(8,128)(2,1)S(1)}, bf16[512,128]{1,0:T(8,128)(2,1)S(1)}) custom-call(s32[128]{0:T(128)S(1)} %pad_add_fusion.scalars_ref, bf16[18,11,16,384]{3,2,1,0:T(8,128)(2,1)S(1)} %get-tuple-element.15.act3_ref, bf16[16,9,16,128]{3,2,1,0:T(8,128)(2,1)S(1)} %get-tuple-element.16.stem_ref, ...), custom_call_target="tpu_custom_call" | custom-call | flops 2000000000 | bytes 4194304 | tf_op jit(solution)/shard_map/pallas_call | solution.py:526
  29.1 0.3 collective-permute-start.6
  29.3 1.1 %collective-permute-done.6 = bf16[512,128]{1,0:T(8,128)(2,1)S(1)} collective-permute-done((bf16[512,128]{1,0:T(8,128)(2,1)S(1)}, bf16[512,128]{1,0:T(8,128)(2,1)S(1)}, u32[]{:S(2)}, u32[]{:S(2)}) %collective-permute-start.6) | collective-permute-done | bytes 131104 | tf_op jit(solution)/shard_map/ppermute | solution.py:412
  30.5 0.6 %collective-permute-start.7 = (bf16[512,128]{1,0:T(8,128)(2,1)S(1)}, bf16[512,128]{1,0:T(8,128)(2,1)S(1)}, u32[]{:S(2)}, u32[]{:S(2)}) collective-permute-start(bf16[512,128]{1,0:T(8,128)(2,1)S(1)} %broadcast_select_fusion.3), channel_id=1, source_target_pairs={{0,8},{4,12},{8,0},{12,4},{16,24},{20,28},{24,16},{28,20},{1,9},{5... | collective-permute-start | bytes 393224 | tf_op jit(solution)/shard_map/ppermute | solution.py:412
  31.1 1.2 %collective-permute-done.4 = bf16[560,128]{1,0:T(8,128)(2,1)S(1)} collective-permute-done((bf16[560,128]{1,0:T(8,128)(2,1)S(1)}, bf16[560,128]{1,0:T(8,128)(2,1)S(1)}, u32[]{:S(2)}, u32[]{:S(2)}) %collective-permute-start.4) | collective-permute-done | bytes 143392 | tf_op jit(solution)/shard_map/ppermute | solution.py:412
  32.3 1.6 %collective-permute-start.5 = (bf16[560,128]{1,0:T(8,128)(2,1)S(1)}, bf16[560,128]{1,0:T(8,128)(2,1)S(1)}, u32[]{:S(2)}, u32[]{:S(2)}) collective-permute-start(bf16[560,128]{1,0:T(8,128)(2,1)S(1)} %broadcast_select_fusion.1.after_ref), channel_id=1, source_target_pairs={{0,16},{4,20},{8,24},{12,28},{16,0},{20,4},{24,8},{28,12},{1,17},{... | collective-permute-start | bytes 430088 | tf_op jit(solution)/shard_map/ppermute | solution.py:412
  33.9 0.0 copy-done.5
  33.9 2.5 %shard_map.161 = bf16[4,8,8,256]{3,2,1,0:T(8,128)(2,1)} custom-call(s32[128]{0:T(128)S(1)} %pad_add_fusion.scalars_ref, bf16[16,5,16,128]{3,2,1,0:T(8,128)(2,1)S(1)} %shard_map.159.part_ref, bf16[16,4,16,128]{3,2,1,0:T(8,128)(2,1)S(1)} %get-tuple-element.18.rest_ref, bf16[3,3,3,128,256]{4,3,2,1,0:T(8,128)(2,1)S(1)} %copy-done.5, ...), custom_call_target="tpu_custom_call" | custom-call | flops 2000000000 | bytes 4194304 | tf_op jit(solution)/shard_map/pallas_call | solution.py:540
  36.4 0.0 collective-permute-done.7
  36.4 1.3 %collective-permute-start.8 = (bf16[512,128]{1,0:T(8,128)(2,1)S(1)}, bf16[512,128]{1,0:T(8,128)(2,1)S(1)}, u32[]{:S(2)}, u32[]{:S(2)}) collective-permute-start(bf16[512,128]{1,0:T(8,128)(2,1)S(1)} %broadcast_select_fusion.4), channel_id=1, source_target_pairs={{0,16},{4,20},{8,24},{12,28},{16,0},{20,4},{24,8},{28,12},{1,17},{... | collective-permute-start | bytes 393224 | tf_op jit(solution)/shard_map/ppermute | solution.py:412
  37.7 0.0 collective-permute-done.5
  37.7 0.7 %slice.23 = bf16[512,128]{1,0:T(8,128)(2,1)} slice(bf16[560,128]{1,0:T(8,128)(2,1)S(1)} %broadcast_select_fusion), slice={[48:560], [0:128]} | slice | bytes 262144 | tf_op jit(solution)/shard_map/slice | solution.py:558
  38.4 0.6 %slice.22 = bf16[32,48]{1,0:T(8,128)(2,1)} slice(bf16[560,128]{1,0:T(8,128)(2,1)S(1)} %broadcast_select_fusion), slice={[16:48], [0:48]} | slice | bytes 6144 | tf_op jit(solution)/shard_map/slice | solution.py:557
  39.0 2.4 %collective-permute-done.8 = bf16[512,128]{1,0:T(8,128)(2,1)S(1)} collective-permute-done((bf16[512,128]{1,0:T(8,128)(2,1)S(1)}, bf16[512,128]{1,0:T(8,128)(2,1)S(1)}, u32[]{:S(2)}, u32[]{:S(2)}) %collective-permute-start.8) | collective-permute-done | bytes 131104 | tf_op jit(solution)/shard_map/ppermute | solution.py:412
  41.5 0.7 %broadcast_select_fusion.5 = bf16[512,128]{1,0:T(8,128)(2,1)} fusion(bf16[512,128]{1,0:T(8,128)(2,1)S(1)} %broadcast_select_fusion.4, bf16[512,128]{1,0:T(8,128)(2,1)S(1)} %collective-permute-done.8, pred[128]{0:T(512)(128)(4,1)S(1)} %compare_bitcast_fusion), kind=kLoop, calls=%fused_computation.5 | loop fusion | flops 65536 | bytes 393344 | tf_op jit(solution)/shard_map/jit(_where)/select_n | solution.py:556
  (9 shorter events, 0.1 us)
Async XLA Ops:
  0.6 9.1 %copy-start.1 = (bf16[1,2,16,16,128]{4,3,2,1,0:T(8,128)(2,1)S(1)}, bf16[1,2,16,16,128]{4,3,2,1,0:T(8,128)(2,1)}, u32[]{:S(2)}) copy-start(bf16[1,2,16,16,128]{4,3,2,1,0:T(8,128)(2,1)} %param.19) | copy-start | bytes 393220
  0.6 9.1 %copy-start.2 = (bf16[1,2,16,16,128]{4,3,2,1,0:T(8,128)(2,1)S(1)}, bf16[1,2,16,16,128]{4,3,2,1,0:T(8,128)(2,1)}, u32[]{:S(2)}) copy-start(bf16[1,2,16,16,128]{4,3,2,1,0:T(8,128)(2,1)} %param.20) | copy-start | bytes 393220
  0.7 9.1 %copy-start.3 = (bf16[3,3,3,3,128]{4,3,2,1,0:T(4,128)(2,1)S(1)}, bf16[3,3,3,3,128]{4,3,2,1,0:T(4,128)(2,1)}, u32[]{:S(2)}) copy-start(bf16[3,3,3,3,128]{4,3,2,1,0:T(4,128)(2,1)} %sw_ref.1) | copy-start | bytes 62212
  0.7 9.1 %copy-start.4 = (bf16[1,2,16,48]{3,2,1,0:T(8,128)(2,1)S(1)}, bf16[1,2,16,48]{3,2,1,0:T(8,128)(2,1)}, u32[]{:S(2)}) copy-start(bf16[1,2,16,48]{3,2,1,0:T(8,128)(2,1)} %param.18) | copy-start | bytes 9220
  0.7 19.0 %copy-start.7 = (f32[128]{0:T(128)S(1)}, f32[128]{0:T(128)}, u32[]{:S(2)}) copy-start(f32[128]{0:T(128)} %gain_ref.1) | copy-start | bytes 1540
  0.7 19.0 %copy-start.8 = (f32[128]{0:T(128)S(1)}, f32[128]{0:T(128)}, u32[]{:S(2)}) copy-start(f32[128]{0:T(128)} %bias_ref.1) | copy-start | bytes 1540
  2.5 17.2 %all-to-all-start = ((bf16[32,8,128]{2,1,0:T(8,128)(2,1)}), bf16[32,8,128]{2,1,0:T(8,128)(2,1)S(1)}, u32[]{:S(2)}, u32[]{:S(2)}) async-start(bf16[32,8,128]{2,1,0:T(8,128)(2,1)} %bitcast.18), calls=%async_computation | async-start | bytes 131072 | tf_op jit(solution)/shard_map/all_to_all | solution.py:459
  9.8 0.9 %copy-start = (bf16[4,8,8,128]{3,2,1,0:T(8,128)(2,1)S(1)}, bf16[4,8,8,128]{3,2,1,0:T(8,128)(2,1)}, u32[]{:S(2)}) copy-start(bf16[4,8,8,128]{3,2,1,0:T(8,128)(2,1)} %shard_map.156) | copy-start | bytes 196612
  10.8 8.0 %collective-permute-start = (bf16[8,16,128]{2,1,0:T(8,128)(2,1)S(1)}, bf16[8,16,128]{2,1,0:T(8,128)(2,1)S(1)}, u32[]{:S(2)}, u32[]{:S(2)}) collective-permute-start(bf16[8,16,128]{2,1,0:T(8,128)(2,1)S(1)} %get-tuple-element.12), channel_id=1, source_target_pairs={{0,1},{1,2},{2,3},{3,0},{4,5},{5,6},{6,7},{7,4},{8,9},{9,10},{10,1... | collective-permute-start | bytes 98312 | tf_op jit(solution)/shard_map/ppermute | solution.py:417
  12.6 7.0 %collective-permute-start.2 = (bf16[18,16,128]{2,1,0:T(8,128)(2,1)S(1)}, bf16[18,16,128]{2,1,0:T(8,128)(2,1)S(1)}, u32[]{:S(2)}, u32[]{:S(2)}) collective-permute-start(bf16[18,16,128]{2,1,0:T(8,128)(2,1)S(1)} %get-tuple-element.14), channel_id=1, source_target_pairs={{0,2},{1,3},{2,0},{3,1},{4,6},{5,7},{6,4},{7,5},{8,10},{9,11},{10,... | collective-permute-start | bytes 221192 | tf_op jit(solution)/shard_map/ppermute | solution.py:417
  15.0 3.7 %collective-permute-start.1 = (bf16[4,16,128]{2,1,0:T(8,128)(2,1)S(1)}, bf16[4,16,128]{2,1,0:T(8,128)(2,1)S(1)}, u32[]{:S(2)}, u32[]{:S(2)}) collective-permute-start(bf16[4,16,128]{2,1,0:T(8,128)(2,1)S(1)} %get-tuple-element.13), channel_id=1, source_target_pairs={{0,3},{1,0},{2,1},{3,2},{4,7},{5,4},{6,5},{7,6},{8,11},{9,8},{10,9... | collective-permute-start | bytes 49160 | tf_op jit(solution)/shard_map/ppermute | solution.py:417
  19.7 4.6 %copy-start.6 = (bf16[3,3,3,128,128]{4,3,2,1,0:T(8,128)(2,1)S(1)}, bf16[3,3,3,128,128]{4,3,2,1,0:T(8,128)(2,1)}, u32[]{:S(2)}) copy-start(bf16[3,3,3,128,128]{4,3,2,1,0:T(8,128)(2,1)} %conv_ref.3) | copy-start | bytes 2654212
  24.2 1.8 %collective-permute-start.3 = (bf16[560,128]{1,0:T(8,128)(2,1)S(1)}, bf16[560,128]{1,0:T(8,128)(2,1)S(1)}, u32[]{:S(2)}, u32[]{:S(2)}) collective-permute-start(bf16[560,128]{1,0:T(8,128)(2,1)S(1)} %get-tuple-element.17), channel_id=1, source_target_pairs={{0,4},{4,0},{8,12},{12,8},{16,20},{20,16},{24,28},{28,24},{1,5},{5... | collective-permute-start | bytes 430088 | tf_op jit(solution)/shard_map/ppermute | solution.py:412
  26.0 7.9 %copy-start.5 = (bf16[3,3,3,128,256]{4,3,2,1,0:T(8,128)(2,1)S(1)}, bf16[3,3,3,128,256]{4,3,2,1,0:T(8,128)(2,1)}, u32[]{:S(2)}) copy-start(bf16[3,3,3,128,256]{4,3,2,1,0:T(8,128)(2,1)} %down_ref.1) | copy-start | bytes 5308420
  26.0 6.2 %collective-permute-start.4 = (bf16[560,128]{1,0:T(8,128)(2,1)S(1)}, bf16[560,128]{1,0:T(8,128)(2,1)S(1)}, u32[]{:S(2)}, u32[]{:S(2)}) collective-permute-start(bf16[560,128]{1,0:T(8,128)(2,1)S(1)} %broadcast_select_fusion.2.after_ref), channel_id=1, source_target_pairs={{0,8},{4,12},{8,0},{12,4},{16,24},{20,28},{24,16},{28,20},{1,9},{5... | collective-permute-start | bytes 430088 | tf_op jit(solution)/shard_map/ppermute | solution.py:412
  29.1 1.4 %collective-permute-start.6 = (bf16[512,128]{1,0:T(8,128)(2,1)S(1)}, bf16[512,128]{1,0:T(8,128)(2,1)S(1)}, u32[]{:S(2)}, u32[]{:S(2)}) collective-permute-start(bf16[512,128]{1,0:T(8,128)(2,1)S(1)} %get-tuple-element.19), channel_id=1, source_target_pairs={{0,4},{4,0},{8,12},{12,8},{16,20},{20,16},{24,28},{28,24},{1,5},{5... | collective-permute-start | bytes 393224 | tf_op jit(solution)/shard_map/ppermute | solution.py:412
  30.5 5.9 %collective-permute-start.7 = (bf16[512,128]{1,0:T(8,128)(2,1)S(1)}, bf16[512,128]{1,0:T(8,128)(2,1)S(1)}, u32[]{:S(2)}, u32[]{:S(2)}) collective-permute-start(bf16[512,128]{1,0:T(8,128)(2,1)S(1)} %broadcast_select_fusion.3), channel_id=1, source_target_pairs={{0,8},{4,12},{8,0},{12,4},{16,24},{20,28},{24,16},{28,20},{1,9},{5... | collective-permute-start | bytes 393224 | tf_op jit(solution)/shard_map/ppermute | solution.py:412
  32.3 5.5 %collective-permute-start.5 = (bf16[560,128]{1,0:T(8,128)(2,1)S(1)}, bf16[560,128]{1,0:T(8,128)(2,1)S(1)}, u32[]{:S(2)}, u32[]{:S(2)}) collective-permute-start(bf16[560,128]{1,0:T(8,128)(2,1)S(1)} %broadcast_select_fusion.1.after_ref), channel_id=1, source_target_pairs={{0,16},{4,20},{8,24},{12,28},{16,0},{20,4},{24,8},{28,12},{1,17},{... | collective-permute-start | bytes 430088 | tf_op jit(solution)/shard_map/ppermute | solution.py:412
  36.4 5.0 %collective-permute-start.8 = (bf16[512,128]{1,0:T(8,128)(2,1)S(1)}, bf16[512,128]{1,0:T(8,128)(2,1)S(1)}, u32[]{:S(2)}, u32[]{:S(2)}) collective-permute-start(bf16[512,128]{1,0:T(8,128)(2,1)S(1)} %broadcast_select_fusion.4), channel_id=1, source_target_pairs={{0,16},{4,20},{8,24},{12,28},{16,0},{20,4},{24,8},{28,12},{1,17},{... | collective-permute-start | bytes 393224 | tf_op jit(solution)/shard_map/ppermute | solution.py:412

commit v4 on v3

v4 whole, which is shorter than its diff:
```python
import functools

import jax
import jax.numpy as jnp
from jax import lax
from jax.experimental import pallas as pl
from jax.experimental.pallas import tpu as pltpu
from jax.sharding import PartitionSpec as P

FRAMES = 8
GROUPS = 32
EPSILON = 1e-06
F32 = jnp.float32
BF16 = jnp.bfloat16
VM = pl.BlockSpec(memory_space=pltpu.VMEM)
ANY = pl.BlockSpec(memory_space=pl.ANY)


def iota(shape, axis):
    return lax.broadcasted_iota(jnp.int32, shape, axis)


def whole(scalars_ref, which):
    row = scalars_ref[...].astype(F32).reshape(1, 128)
    return jnp.sum(jnp.where(iota((1, 128), 1) == which, row, 0.0)).astype(jnp.int32)


def dot(a, b):
    return jnp.dot(a, b, preferred_element_type=F32)


def dot_nt(a, b):
    return lax.dot_general(a, b, (((1,), (1,)), ((), ())), preferred_element_type=F32)


def sort_kernel(streams, cols_ref, owner_ref, slot_ref, out_ref, wide):
    width, fill = cols_ref.shape
    half_per = fill // streams // 2
    lines = fill // 2
    wide[...] = jnp.zeros(wide.shape, F32)
    pixels, slots = cols_ref[...].astype(F32), slot_ref[...].astype(F32)
    for side in range(2):
        at = side * 64
        wide[at : at + width, side * fill : (side + 1) * fill] = pixels
        wide[at + width : at + width + 1, side * fill : (side + 1) * fill] = slots
    owner = owner_ref[...]
    hot = jnp.where(iota((streams, fill), 0) == owner, 1.0, 0.0)
    upper = jnp.where(iota((fill, fill), 0) <= iota((fill, fill), 1), 1.0, 0.0).astype(BF16)
    running = dot(hot.astype(BF16), upper)
    rank = jnp.sum(hot * running, axis=0, keepdims=True).astype(jnp.int32) - 1
    half = rank // half_per
    line = owner * half_per + rank - half * half_per
    line = jnp.concatenate([jnp.where(half == side, line, -1) for side in range(2)], axis=1)
    pick = jnp.where(iota((lines, 2 * fill), 0) == jnp.broadcast_to(line, (lines, 2 * fill)), 1.0, 0.0)
    out = dot_nt(pick.astype(BF16), wide[...].astype(BF16)).astype(BF16)
    if len(out_ref.shape) == 2:
        out_ref[...] = out
    else:
        for strip in range(out_ref.shape[0]):
            out_ref[strip] = out.reshape(out_ref.shape[1:])


def pack_kernel(pix_ref, sw_ref, act_ref, res_ref, down_ref, up_ref, mid_ref, sw, sems):
    copies = []
    for f in range(2):
        copies.append((act_ref.at[f, 14:16], down_ref.at[2 * f : 2 * f + 2]))
        copies.append((res_ref.at[f, 15:16], down_ref.at[4 + f : 5 + f]))
        copies.append((act_ref.at[f, 0:1], up_ref.at[f : f + 1]))
    copies = [pltpu.make_async_copy(a, b, sems.at[i]) for i, (a, b) in enumerate(copies)]
    for copy in copies:
        copy.start()
    pix = pix_ref[...].reshape(32, 48).astype(F32)
    pix = jnp.concatenate([pix, jnp.zeros((32, 80), F32)], axis=1)
    pix = pix.astype(BF16).reshape(2, 16, 128)
    down_ref[6:8] = pix
    up_ref[2:4] = pix
    mid_ref[0:2] = pix
    sw[...] = jnp.zeros(sw.shape, F32)
    for k in range(2):
        for e in range(3):
            for a in range(3):
                for b in range(3):
                    at = 27 * (k + e) + 9 * a + 3 * b
                    sw[at : at + 3, k * 128 : k * 128 + 128] = sw_ref[a, b, e].astype(F32)
    for k in range(2):
        half = sw[:, k * 128 : k * 128 + 128].astype(BF16)
        mid_ref[2 + 8 * k : 10 + 8 * k] = half.reshape(8, 16, 128)
    for copy in copies:
        copy.wait()


def received(line):
    line = line.astype(F32)
    both = jnp.concatenate([line, pltpu.roll(line, 64, 1)], axis=0)
    slot_lane = jnp.where(iota((8, 128), 1) == 48, 1.0, 0.0).astype(BF16)
    slots = dot_nt(slot_lane, both.astype(BF16)).astype(jnp.int32)
    return jnp.where(iota((128, 128), 1) < 48, both, 0.0), slots


def gather_pixels(strips, j, pc, pix_ref, below_ref, above_ref, mid_ref):
    pc[j] = jnp.zeros((32, 128), F32)
    pc[j, :, 0:48] = pix_ref[...].reshape(32, 48).astype(F32)
    pc[lax.rem(j + strips - 1, strips)] = below_ref[6:8].reshape(32, 128).astype(F32)
    pc[lax.rem(j + 1, strips)] = above_ref[2:4].reshape(32, 128).astype(F32)
    pc[lax.rem(j + 2, strips)] = mid_ref[0:2].reshape(32, 128).astype(F32)


def widen_cache(strips, j, cache, old_ref, below_ref, above_ref):
    has_above = jnp.where(j > 0, 1.0, 0.0)
    has_below = jnp.where(j < strips - 1, 1.0, 0.0)
    for f in range(2):
        cache[f, 304:416] = jnp.zeros((112, 128), F32)
        cache[f, 32:288] = old_ref[f].reshape(256, 128).astype(F32)
        cache[f, 0:32] = below_ref[2 * f : 2 * f + 2].reshape(32, 128).astype(F32) * has_above
        cache[f, 288:304] = above_ref[f].astype(F32) * has_below


def stem_weight_of(mid_ref):
    return jnp.concatenate(
        [mid_ref[2 + 8 * k : 10 + 8 * k].reshape(128, 128) for k in range(2)], axis=1
    )


def spread_matrix():
    lanes = iota((8, 1024), 1)
    pair, m = lanes >> 7, lanes & 127
    col = (m * 2428) >> 16
    tap = m - 27 * col
    a = (tap * 7282) >> 16
    b = ((tap - 9 * a) * 21846) >> 16
    c = tap - 9 * a - 3 * b
    w = 2 * pair - 1 + col
    source = jnp.where((m < 108) & (w >= 0) & (w < 16), (b * 3 + a) * 48 + c * 16 + w, -1)
    line = iota((54, 8, 1024), 0) * 8 + iota((54, 8, 1024), 1)
    return jnp.where(line == source[None], 1.0, 0.0).reshape(432, 1024).astype(BF16)


def norm_rows(strips, s1, s2, gain_ref, bias_ref):
    same = jnp.where(iota((128, 128), 0) // 4 == iota((128, 128), 1) // 4, 1.0, 0.0)
    count = strips * 16 * 16 * 4
    exact = functools.partial(
        jnp.dot, preferred_element_type=F32, precision=lax.Precision.HIGHEST
    )
    mean = exact(s1, same) / count
    inv = lax.rsqrt(exact(s2, same) / count - mean * mean + EPSILON)
    scale = inv * gain_ref[...].reshape(1, 128)
    return scale, bias_ref[...].reshape(1, 128) - mean * scale


def silu(v):
    h = 0.5 * v
    return h + h * jnp.tanh(h)


def pair_weight(conv_ref):
    zero = jnp.zeros((384, 128), BF16)

    def weight(b, e):
        if not 0 <= e <= 2:
            return zero
        return jnp.concatenate([conv_ref[a, b, e] for a in range(3)], axis=0)

    return jnp.concatenate(
        [
            jnp.concatenate([weight(b, col - k) for k in range(2)], axis=1)
            for col in range(4)
            for b in range(3)
        ],
        axis=0,
    )


def row_at(t, y):
    t = jnp.maximum(t, 0)
    h = 1 if y >= 8 else 0
    return (t & 1) * (16 * 88) + (y + 2 - 8 * h) * 8 + h * 4 + (t >> 1)


def stem_kernel(
    strips,
    scalars_ref,
    gain_ref,
    bias_ref,
    recv_ref,
    pix_ref,
    old_ref,
    below_ref,
    above_ref,
    mid_ref,
    pay_ref,
    act,
    stem,
    pc,
    zs,
    xs,
    ys,
):
    j = lax.axis_index("strip")
    valid = whole(scalars_ref, 0)
    rows_all = strips * 16
    gather_pixels(strips, j, pc, pix_ref, below_ref, above_ref, mid_ref)
    zs[:, 0:4] = jnp.zeros((3, 4, 8, 128), F32)
    zs[:, 4 + rows_all :] = jnp.zeros((3, 4, 8, 128), F32)
    sub = iota((128, 128), 0)
    crow, cframe = iota((128, 32), 1) % 16, iota((128, 32), 1) // 16
    csub = iota((128, 32), 0)
    for s in range(strips):
        pixels, slots = received(recv_ref[s])
        frame, row = slots >> 4, slots & 15
        source = jnp.concatenate([pixels, pc[s]], axis=0).astype(BF16)
        hits = []
        for a in range(3):
            t = frame + 2 - a
            place = jnp.where(t < FRAMES, row * 8 + (t & 1) * 4 + (t >> 1), -1)
            hit = jnp.where(sub.reshape(16, 8, 128) == place[None], 1.0, 0.0).reshape(128, 128)
            ct = cframe - a
            cplace = jnp.where(ct >= 0, crow * 8 + (ct & 1) * 4 + (ct >> 1), -1)
            chit = jnp.where(csub == cplace, 1.0, 0.0)
            hits.append(jnp.concatenate([hit, chit], axis=1).astype(BF16))
        placed = dot(jnp.concatenate(hits, axis=0), source).reshape(3, 16, 8, 128)
        for a in range(3):
            zs[a, 4 + s * 16 : 4 + (s + 1) * 16] = placed[a]
    pixels, slots = received(recv_ref[j])
    goal = (slots >> 4) + 2 - valid
    place = jnp.where((goal >= 0) & (goal < 2), goal * 16 + (slots & 15), -1)
    hit = jnp.where(iota((4, 8, 128), 0) * 8 + iota((4, 8, 128), 1) == place[None], 1.0, 0.0)
    cgoal = iota((32, 32), 1) // 16 - valid
    cplace = jnp.where((cgoal >= 0) & (cgoal < 2), cgoal * 16 + iota((32, 32), 1) % 16, -1)
    chit = jnp.where(iota((32, 32), 0) == cplace, 1.0, 0.0)
    source = jnp.concatenate([pixels, pc[j]], axis=0).astype(BF16)
    fresh = dot(jnp.concatenate([hit.reshape(32, 128), chit], axis=1).astype(BF16), source)
    target = whole(scalars_ref, 1).astype(F32)
    pay_ref[0:16] = jnp.full((16, 128), target, F32).astype(BF16)
    pay_ref[16:48] = fresh.astype(BF16)
    high = rows_all + 4
    for b in range(3):
        for a in range(3):
            q = (b * 3 + a) * 48
            xs[2 : high + 2, :, q : q + 48] = zs[a, 1 + b : high + 1 + b, :, 0:48]
    patches = xs[2 : high + 2].reshape(high * 8, 432).astype(BF16)
    ys[...] = dot(patches, spread_matrix()).reshape(high, 8, 1024)
    full = ys[2 : 2 + rows_all].reshape(rows_all * 8, 1024).astype(BF16)
    base = j * 16
    first, second = ys[pl.ds(base, 11)], ys[pl.ds(base + 8, 11)]
    low = iota((11, 8, 1024), 1) < 4
    own_even = jnp.where(low, first, pltpu.roll(second, 4, 1))
    own_odd = jnp.where(low, pltpu.roll(first, 4, 1), second)
    own = jnp.concatenate([own_even, own_odd], axis=0).reshape(176, 1024).astype(BF16)
    weight = stem_weight_of(mid_ref)
    s1 = jnp.zeros((8, 256), F32)
    s2 = jnp.zeros((8, 256), F32)
    for chunk in range(8):
        out = dot(full[:, chunk * 128 : chunk * 128 + 128], weight).astype(BF16).astype(F32).reshape(rows_all, 8, 256)
        s1 = s1 + jnp.sum(out, axis=0)
        s2 = s2 + jnp.sum(out * out, axis=0)
        mine = dot(own[:, chunk * 128 : chunk * 128 + 128], weight).astype(BF16).astype(F32).reshape(2, 11, 8, 256)
        for i in range(2):
            stem[:, 2 * chunk + i] = mine[:, :, :, i * 128 : (i + 1) * 128]
    s1 = s1[:, 0:128] + s1[:, 128:256]
    s2 = s2[:, 0:128] + s2[:, 128:256]
    scale, shift = norm_rows(strips, s1, s2, gain_ref, bias_ref)
    low8 = iota((8, 128), 0) < 4
    scales = (
        jnp.where(low8, scale, pltpu.roll(scale, 4, 0)),
        jnp.where(low8, pltpu.roll(scale, 4, 0), scale),
    )
    shifts = (
        jnp.where(low8, shift, pltpu.roll(shift, 4, 0)),
        jnp.where(low8, pltpu.roll(shift, 4, 0), shift),
    )
    half = iota((11, 8, 128), 1) // 4
    line_of = j * 16 + iota((11, 8, 128), 0) - 2 + 8 * half
    inside = jnp.where((line_of >= 0) & (line_of < rows_all), 1.0, 0.0)

    def activate(w, carry):
        for p in range(2):
            act[p, w] = silu(stem[p, w] * scales[p] + shifts[p]) * inside
        return carry

    lax.fori_loop(0, 16, activate, 0, unroll=4)
    act_rows = act.reshape(2 * 16 * 11 * 8, 128)
    for i in range(2):
        for y in range(16):
            block = act_rows[pl.ds(row_at(valid - 2 + i, y), 16, stride=88)]
            block = jnp.where(valid + i < 2, old_ref[1, y].astype(F32), block)
            to = 48 + i * 256 + y * 16
            pay_ref[to : to + 16] = block.astype(BF16)


def last_kernel(
    after_ref,
    scalars_ref,
    act,
    stem,
    old_ref,
    res_old_ref,
    below_ref,
    above_ref,
    conv_ref,
    pay_ref,
    lines,
):
    del after_ref
    j = lax.axis_index("strip")
    valid = whole(scalars_ref, 0)
    act_rows = act.reshape(2 * 16 * 11 * 8, 128)
    stem_rows = stem.reshape(2 * 16 * 11 * 8, 128)
    column = iota((16, 128), 0)

    def side_by_side(m, y, block):
        before = jnp.where(column == 0, 0.0, pltpu.roll(block, 1, 0))
        after = jnp.where(column == 15, 0.0, pltpu.roll(block, 15, 0))
        lines[m, y + 1] = jnp.concatenate([before, block, after], axis=1).astype(BF16)

    for m in range(4):
        from_cache = valid - 2 + m

        @pl.when(from_cache >= 2)
        def _(m=m, from_cache=from_cache):
            for y in range(-1, 17):
                block = act_rows[pl.ds(row_at(from_cache - 2, y), 16, stride=88)]
                side_by_side(m, y, block)

        @pl.when(from_cache < 2)
        def _(m=m, from_cache=from_cache):
            f = jnp.clip(from_cache, 0, 1)
            has_above = jnp.where(j > 0, 1.0, 0.0)
            has_below = jnp.where(j < lax.axis_size("strip") - 1, 1.0, 0.0)
            side_by_side(m, -1, below_ref[2 * f + 1].astype(F32) * has_above)
            for y in range(16):
                side_by_side(m, y, old_ref[f, y].astype(F32))
            side_by_side(m, 16, above_ref[f].astype(F32) * has_below)

    zero = jnp.zeros((384, 128), BF16)

    def weight(a, b):
        if not 0 <= b <= 2:
            return zero
        return jnp.concatenate([conv_ref[a, b, e] for e in range(3)], axis=0)

    weights = jnp.concatenate(
        [
            jnp.concatenate([weight(a, y - k) for k in range(2)], axis=1)
            for y in range(4)
            for a in range(3)
        ],
        axis=0,
    )
    left = jnp.concatenate(
        [
            jnp.concatenate(
                [lines[i + a, 2 * k + y] for i in range(2) for k in range(8)], axis=0
            )
            for y in range(4)
            for a in range(3)
        ],
        axis=1,
    )
    out = dot(left, weights).reshape(2, 8, 16, 256)
    for i in range(2):
        for y in range(16):
            block = stem_rows[pl.ds(row_at(valid - 2 + i, y), 16, stride=88)]
            block = block + out[i, y // 2, :, y % 2 * 128 : y % 2 * 128 + 128]
            if i == 0:
                block = jnp.where(valid < 2, res_old_ref[1, y].astype(F32), block)
            to = i * 256 + y * 16
            pay_ref[to : to + 16] = block.astype(BF16)


def conv_kernel(
    strips,
    w0,
    after_ref,
    after_too_ref,
    act,
    stem,
    old_ref,
    below_ref,
    above_ref,
    conv_ref,
    out_ref,
    cache,
    act3,
):
    del after_ref, after_too_ref
    j = lax.axis_index("strip")
    widen_cache(strips, j, cache, old_ref, below_ref, above_ref)
    at0 = iota((11, 8, 128), 1) == 0
    at4 = iota((11, 8, 128), 1) == 4
    edge = 0 if w0 == 0 else 9
    act3[edge] = jnp.zeros(act3.shape[1:], BF16)
    shift = 1 if w0 == 0 else 1 - w0

    def arrange(w, carry):
        late = []
        for f in range(2):
            rows = [
                jnp.broadcast_to(cache[f, pl.ds(y * 16 + w, 1)], (8, 128)) for y in range(19)
            ]
            upper, lower = jnp.stack(rows[0:11], axis=0), jnp.stack(rows[8:19], axis=0)
            rolled = pltpu.roll(act[f, w], 1, 1)
            late.append(jnp.where(at0, upper, jnp.where(at4, lower, rolled)))
        even, odd = act[0, w], act[1, w]
        taps = ((late[0], late[1]), (late[1], even), (even, odd))
        for a in range(3):
            act3[w + shift, :, :, a * 128 : (a + 1) * 128] = jnp.concatenate(taps[a], axis=1).astype(BF16)
        return carry

    lax.fori_loop(max(w0 - 1, 0), min(w0 + 9, 16), arrange, 0, unroll=3)
    weights = pair_weight(conv_ref)
    outside = (j == 0) & (iota((9, 16, 128), 0) == 0) & (iota((9, 16, 128), 1) % 8 < 4)
    keep = jnp.where(outside, 0.0, 1.0)
    left = jnp.concatenate(
        [
            jnp.concatenate(
                [act3[2 * k + col, b : b + 9].reshape(144, 384) for k in range(4)],
                axis=0,
            )
            for col in range(4)
            for b in range(3)
        ],
        axis=1,
    )
    out = dot(left, weights).reshape(4, 9, 16, 256)
    for k in range(4):
        for n in range(2):
            w = w0 + 2 * k + n
            value = out[k, :, :, n * 128 : n * 128 + 128]
            value = value + jnp.concatenate([stem[0, w, 1:10], stem[1, w, 1:10]], axis=1)
            out_ref[w - w0] = (value * keep).astype(BF16)


def down_kernel(
    scalars_ref,
    part_ref,
    rest_ref,
    down_ref,
    res_cache_ref,
    below_ref,
    after_ref,
    lat_ref,
    rcache,
    res3,
    lat,
):
    del after_ref
    j = lax.axis_index("strip")
    valid = whole(scalars_ref, 0)
    rcache[...] = jnp.zeros(rcache.shape, F32)
    has_above = jnp.where(j > 0, 1.0, 0.0)
    for f in range(2):
        rcache[f, 0:16] = below_ref[4 + f].astype(F32) * has_above
        rcache[f, 16:272] = res_cache_ref[f].reshape(256, 128).astype(F32)
    at0 = iota((9, 8, 128), 1) == 0
    at4 = iota((9, 8, 128), 1) == 4
    res3[0] = jnp.zeros(res3.shape[1:], F32)

    for w0, ref in ((0, part_ref), (8, rest_ref)):

        def delay(w, carry, w0=w0, ref=ref):
            both = ref[w].astype(F32)
            even, odd = both[:, 0:8], both[:, 8:16]
            olds = []
            for f in range(2):
                rows = [
                    jnp.broadcast_to(rcache[f, pl.ds(y * 16 + w0 + w, 1)], (8, 128))
                    for y in range(17)
                ]
                olds.append((jnp.stack(rows[0:9], axis=0), jnp.stack(rows[8:17], axis=0)))
            at = w0 + w + 1
            for f, v in enumerate((even, odd)):
                rolled = pltpu.roll(v, 1, 1)
                late = jnp.where(at0, olds[f][0], jnp.where(at4, olds[f][1], rolled))
                res3[at, :, :, f * 128 : f * 128 + 128] = late
            res3[at, :, :, 256:384] = even
            return carry

        lax.fori_loop(0, 8, delay, 0, unroll=2)
    total = jnp.zeros((256, 256), F32)
    for b in range(3):
        for e in range(3):
            left = jnp.concatenate(
                [res3[2 * k + e, 2 * i + b] for k in range(8) for i in range(4)], axis=0
            ).astype(BF16)
            right = jnp.concatenate([down_ref[a, b, e] for a in range(3)], axis=0)
            total = total + dot(left, right)
    live = 2 * (iota((256, 256), 0) % 4) < valid
    total = jnp.where(live, total, 0.0)
    for o in range(2):
        lat[o] = total[:, o * 128 : (o + 1) * 128]
    for t in range(4):
        for h in range(2):
            for i in range(4):
                for o in range(2):
                    block = lat[o, pl.ds(i * 8 + h * 4 + t, 8, stride=32)]
                    lat_ref[t, h * 4 + i, :, o * 128 : (o + 1) * 128] = block.astype(BF16)


def partner(value, axis, stride):
    pairs = [(source, source ^ stride) for source in range(lax.axis_size(axis))]
    return lax.ppermute(value, axis, pairs)


def shifted(value, axis, by):
    size = lax.axis_size(axis)
    return lax.ppermute(value, axis, [(i, (i + by) % size) for i in range(size)])


def body(
    loader_rows,
    load_owner,
    load_slot,
    valid_frames,
    next_owner,
    pixel_cache,
    act_cache,
    res_cache,
    stem_weight,
    norm_gain,
    norm_bias,
    conv_weight,
    down_weight,
):
    streams = lax.axis_size("stream")
    strips = lax.axis_size("strip")
    stream_pos = lax.axis_index("stream")
    sections = streams.bit_length() - 1
    fill = loader_rows.shape[1]
    per = fill // streams
    pix, acts, ress = pixel_cache[0], act_cache[0], res_cache[0]
    mega = 1024 * 1024
    cost = pl.CostEstimate(flops=2 * 10**9, bytes_accessed=4 * mega, transcendentals=0)
    half_per = fill // streams // 2
    direct = half_per % 8 == 0
    line_shape = (strips, streams, half_per, 128) if direct else (fill // 2, 128)
    lines = pl.pallas_call(
        functools.partial(sort_kernel, streams),
        out_shape=jax.ShapeDtypeStruct(line_shape, BF16),
        in_specs=[VM] * 3,
        out_specs=VM,
        scratch_shapes=[pltpu.VMEM((128, 2 * fill), F32)],
        cost_estimate=cost,
    )(loader_rows[0].T, load_owner, load_slot)
    if not direct:
        lines = lines.reshape(1, streams, half_per, 128)
        lines = jnp.broadcast_to(lines, (strips, streams, half_per, 128))
    lines = lines.reshape(strips * streams, half_per, 128)
    recv = lax.all_to_all(lines, ("strip", "stream"), 0, 0, tiled=True)
    recv = recv.reshape(strips, fill // 2, 128)
    below, above, mid = pl.pallas_call(
        pack_kernel,
        out_shape=(
            jax.ShapeDtypeStruct((8, 16, 128), BF16),
            jax.ShapeDtypeStruct((4, 16, 128), BF16),
            jax.ShapeDtypeStruct((18, 16, 128), BF16),
        ),
        in_specs=[VM] * 2 + [ANY] * 2,
        out_specs=(VM,) * 3,
        scratch_shapes=[pltpu.VMEM((128, 256), F32), pltpu.SemaphoreType.DMA((6,))],
        compiler_params=pltpu.CompilerParams(vmem_limit_bytes=4 * mega),
    )(pix, stem_weight, acts, ress)
    below = shifted(below, "strip", 1)
    above = shifted(above, "strip", -1)
    mid = shifted(mid, "strip", 2)
    scalars = jnp.concatenate([valid_frames, next_owner, jnp.zeros((126,), jnp.int32)])
    rows_all = strips * 16
    window = jax.ShapeDtypeStruct((2, 16, 11, 8, 128), F32)
    first, act, stem = pl.pallas_call(
        functools.partial(stem_kernel, strips),
        out_shape=(jax.ShapeDtypeStruct((560, 128), BF16), window, window),
        in_specs=[VM] * 9,
        out_specs=(VM,) * 3,
        scratch_shapes=[
            pltpu.VMEM((strips, 32, 128), F32),
            pltpu.VMEM((3, rows_all + 8, 8, 128), F32),
            pltpu.VMEM((rows_all + 8, 8, 432), F32),
            pltpu.VMEM((rows_all + 4, 8, 1024), F32),
        ],
        compiler_params=pltpu.CompilerParams(vmem_limit_bytes=24 * mega),
        cost_estimate=cost,
    )(scalars, norm_gain, norm_bias, recv, pix, acts, below, above, mid)
    keeps = []

    def passed(value, bit):
        if bit == len(keeps):
            keeps.append((value[0:1].astype(jnp.int32) >> bit) & 1 == (stream_pos >> bit) & 1)
        return jnp.where(keeps[bit], value, partner(value, "stream", 1 << bit))

    first = passed(first, 0)
    second = pl.pallas_call(
        last_kernel,
        out_shape=jax.ShapeDtypeStruct((512, 128), BF16),
        in_specs=[ANY] + [VM] * 8,
        out_specs=VM,
        scratch_shapes=[pltpu.VMEM((4, 18, 16, 384), BF16)],
        compiler_params=pltpu.CompilerParams(vmem_limit_bytes=24 * mega),
        cost_estimate=cost,
    )(first, scalars, act, stem, acts, ress, below, above, conv_weight)
    second = passed(second, 0)

    def convolved(w0, after, after_too):
        return pl.pallas_call(
            functools.partial(conv_kernel, strips, w0),
            out_shape=jax.ShapeDtypeStruct((8, 9, 16, 128), BF16),
            in_specs=[ANY] * 2 + [VM] * 6,
            out_specs=VM,
            scratch_shapes=[
                pltpu.VMEM((2, 416, 128), F32),
                pltpu.VMEM((10, 11, 16, 384), BF16),
            ],
            compiler_params=pltpu.CompilerParams(vmem_limit_bytes=24 * mega),
            cost_estimate=cost,
        )(after, after_too, act, stem, acts, below, above, conv_weight)

    part = convolved(0, first, second)
    for bit in range(1, sections - 1):
        first = passed(first, bit)
    rest = convolved(8, first, part)
    for bit in range(1, sections - 1):
        second = passed(second, bit)
    latent = pl.pallas_call(
        down_kernel,
        out_shape=jax.ShapeDtypeStruct((4, 8, 8, 256), BF16),
        in_specs=[VM] * 6 + [ANY],
        out_specs=VM,
        scratch_shapes=[
            pltpu.VMEM((2, 384, 128), F32),
            pltpu.VMEM((17, 9, 8, 384), F32),
            pltpu.VMEM((2, 256, 128), F32),
        ],
        compiler_params=pltpu.CompilerParams(vmem_limit_bytes=24 * mega),
        cost_estimate=cost,
    )(scalars, part, rest, down_weight, ress, below, second)
    if sections > 1:
        first = passed(first, sections - 1)
        second = passed(second, sections - 1)
    new_pix = first[16:48, 0:48].reshape(1, 2, 16, 48)
    new_act = first[48:].reshape(1, 2, 16, 16, 128)
    return (latent[None], new_pix, new_act, second.reshape(1, 2, 16, 16, 128))


def solution(mesh):
    in_specs = (
        P("stream", "strip", None),
        P("stream", "strip"),
        P("stream", "strip"),
        P("stream"),
        P("stream"),
        P("stream", None, "strip", None),
        P("stream", None, "strip", None, None),
        P("stream", None, "strip", None, None),
        P(),
        P(),
        P(),
        P(),
        P(),
    )
    out_specs = (
        P("stream", None, "strip", None, None),
        P("stream", None, "strip", None),
        P("stream", None, "strip", None, None),
        P("stream", None, "strip", None, None),
    )
    return jax.shard_map(body, mesh=mesh, in_specs=in_specs, out_specs=out_specs, check_vma=False)
```

time: 42.4 us -> 40.2 us (0.948)
  starting transfers between devices: 18.3 us -> 17.2 us
  local copies, waits for them, and re-layouts: 2.16 us -> 1.3 us
    ppermute x3, waiting for transfers between devices: 1.83 us -> 3.55 us  [shifted(): lax.ppermute(value, axis, [(i, (i + by) % size) for i in range(size)])]
    ppermute x6, waiting for transfers between devices: 4.76 us -> 3.18 us  [partner(): return lax.ppermute(value, axis, pairs)]
    pallas_call x1, Pallas kernels: 4.49 us -> 3.13 us  [body(): pl.pallas_call(functools.partial(stem_kernel, strips), out_shape=(jax.Sha...]
    pallas_call x3 -> x4, Pallas kernels: 5.63 us -> 6.67 us  [the longest x2 3.61 us: convolved(): pl.pallas_call(functools.partial(conv_kernel, strips, w0), out_shape=jax....]
    ppermute x3, starting transfers between devices: 5.65 us -> 4.75 us  [shifted(): lax.ppermute(value, axis, [(i, (i + by) % size) for i in range(size)])]
    unnamed x18 -> x16, local copies, waits for them, and re-layouts: 0.89 us -> 0.04 us
    select_n x3 -> x0, other arithmetic: 0.71 us -> none  [body(): second = jnp.where(keeps[bit], second, partner(second, 'stream', 1 << bit))]
    select_n x3 -> x6, other arithmetic: 0.06 us -> 0.77 us  [passed(): return jnp.where(keeps[bit], value, partner(value, 'stream', 1 << bit))]
  transfers between devices with their start and end apart: 10 -> 10, of which waited for: 5 -> 5; matrix products, arithmetic and copies ran while one was open for 3% -> 4% of each run, Pallas kernels for 14% -> 17%
where the time goes in v4:
time: 40.2 us; the launch traced here: 40 us
  starting transfers between devices  17.2 us (43%)
  Pallas kernels  11.7 us (29%)
  waiting for transfers between devices  6.74 us (17%)
  between operations  2.15 us (5%)
  local copies, waits for them, and re-layouts  1.3 us (3%)
  other arithmetic  0.88 us (2%)
    all_to_all x1, starting transfers between devices, body(): recv = lax.all_to_all(lines, ('strip', 'stream'), 0, 0, tiled=True)  7.3 us
    ppermute x6, starting transfers between devices, partner(): return lax.ppermute(value, axis, pairs)  5.16 us
    ppermute x3, starting transfers between devices, shifted(): lax.ppermute(value, axis, [(i, (i + by) % size) for i in range(size)])  4.75 us
    pallas_call x2, Pallas kernels, convolved(): pl.pallas_call(functools.partial(conv_kernel, strips, w0), out_shape=jax....  3.61 us
    ppermute x3, waiting for transfers between devices, shifted(): lax.ppermute(value, axis, [(i, (i + by) % size) for i in range(size)])  3.55 us
    ppermute x6, waiting for transfers between devices, partner(): return lax.ppermute(value, axis, pairs)  3.18 us
    pallas_call x1, Pallas kernels, body(): pl.pallas_call(functools.partial(stem_kernel, strips), out_shape=(jax.Sha...  3.13 us
    pallas_call x1, Pallas kernels, body(): pl.pallas_call(down_kernel, out_shape=jax.ShapeDtypeStruct((4, 8, 8, 256)...  1.93 us
  transfers between devices with their start and end apart: 10, of which 5 were waited for; matrix products, arithmetic and copies ran while one was open for 4% of the time, Pallas kernels for 17%

profile of v4, /device:TPU:0, one launch (start us, length us, event | category | flops | bytes accessed | tf_op | source)
XLA Modules:
  0.0 40.0 jit_solution(15409015794289331791)
XLA Ops:
  0.6 0.0 copy-start
  0.6 0.0 copy-start.1
  0.7 0.0 copy-start.2
  0.7 0.0 copy-start.3
  0.7 0.0 copy-start.6
  0.7 0.0 copy-start.7
  0.7 1.8 %shard_map.156 = bf16[4,8,8,128]{3,2,1,0:T(8,128)(2,1)} custom-call(bf16[48,128]{1,0:T(8,128)(2,1)} %bitcast.33, s32[1,128]{1,0:T(1,128)} %owner_ref.1, s32[1,128]{1,0:T(1,128)} %slot_ref.1), custom_call_target="tpu_custom_call" | custom-call | flops 2000000000 | bytes 4194304 | tf_op jit(solution)/shard_map/pallas_call | solution.py:536
  2.5 7.3 %all-to-all-start = ((bf16[32,8,128]{2,1,0:T(8,128)(2,1)}), bf16[32,8,128]{2,1,0:T(8,128)(2,1)S(1)}, u32[]{:S(2)}, u32[]{:S(2)}) async-start(bf16[32,8,128]{2,1,0:T(8,128)(2,1)} %bitcast.31), calls=%async_computation | async-start | bytes 131072 | tf_op jit(solution)/shard_map/all_to_all | solution.py:548
  9.8 0.0 copy-done
  9.8 0.0 copy-done.1
  9.8 0.0 copy-done.2
  9.8 0.0 copy-done.3
  9.8 0.1 shard_map.157
  10.0 1.8 %collective-permute-start = (bf16[8,16,128]{2,1,0:T(8,128)(2,1)S(1)}, bf16[8,16,128]{2,1,0:T(8,128)(2,1)S(1)}, u32[]{:S(2)}, u32[]{:S(2)}) collective-permute-start(bf16[8,16,128]{2,1,0:T(8,128)(2,1)S(1)} %get-tuple-element.10), channel_id=1, source_target_pairs={{0,1},{1,2},{2,3},{3,0},{4,5},{5,6},{6,7},{7,4},{8,9},{9,10},{10,1... | collective-permute-start | bytes 98312 | tf_op jit(solution)/shard_map/ppermute | solution.py:506
  11.8 2.1 %collective-permute-start.1 = (bf16[4,16,128]{2,1,0:T(8,128)(2,1)S(1)}, bf16[4,16,128]{2,1,0:T(8,128)(2,1)S(1)}, u32[]{:S(2)}, u32[]{:S(2)}) collective-permute-start(bf16[4,16,128]{2,1,0:T(8,128)(2,1)S(1)} %get-tuple-element.11), channel_id=1, source_target_pairs={{0,3},{1,0},{2,1},{3,2},{4,7},{5,4},{6,5},{7,6},{8,11},{9,8},{10,9... | collective-permute-start | bytes 49160 | tf_op jit(solution)/shard_map/ppermute | solution.py:506
  13.8 0.9 %collective-permute-start.2 = (bf16[18,16,128]{2,1,0:T(8,128)(2,1)S(1)}, bf16[18,16,128]{2,1,0:T(8,128)(2,1)S(1)}, u32[]{:S(2)}, u32[]{:S(2)}) collective-permute-start(bf16[18,16,128]{2,1,0:T(8,128)(2,1)S(1)} %get-tuple-element.12), channel_id=1, source_target_pairs={{0,2},{1,3},{2,0},{3,1},{4,6},{5,7},{6,4},{7,5},{8,10},{9,11},{10,... | collective-permute-start | bytes 221192 | tf_op jit(solution)/shard_map/ppermute | solution.py:506
  16.0 0.1 pad_add_fusion.scalars_ref
  16.1 0.0 collective-permute-done.1.above_ref
  16.1 0.3 collective-permute-done.below_ref
  16.4 3.3 %collective-permute-done.2.mid_ref = bf16[18,16,128]{2,1,0:T(8,128)(2,1)S(1)} collective-permute-done((bf16[18,16,128]{2,1,0:T(8,128)(2,1)S(1)}, bf16[18,16,128]{2,1,0:T(8,128)(2,1)S(1)}, u32[]{:S(2)}, u32[]{:S(2)}) %collective-permute-start.2) | collective-permute-done | bytes 73760 | tf_op jit(solution)/shard_map/ppermute | solution.py:506
  19.6 0.0 all-to-all-done
  19.6 0.0 copy-done.6
  19.7 0.0 copy-done.7
  19.7 0.0 copy-start.5
  19.7 3.1 %shard_map.158 = (bf16[560,128]{1,0:T(8,128)(2,1)S(1)}, f32[2,16,11,8,128]{4,3,2,1,0:T(8,128)S(1)}, f32[2,16,11,8,128]{4,3,2,1,0:T(8,128)S(1)}) custom-call(s32[128]{0:T(128)S(1)} %pad_add_fusion.scalars_ref, f32[128]{0:T(128)S(1)} %copy-done.6, f32[128]{0:T(128)S(1)} %copy-done.7, bf16[4,64,128]{2,1,0:T(8,128)(2,1)S(1)} %bitcast.26, ...), custom_call_target="tpu_custom_call" | custom-call | flops 2000000000 | bytes 4194304 | tf_op jit(solution)/shard_map/pallas_call | solution.py:568
  22.8 0.1 collective-permute-start.3
  22.9 1.3 %collective-permute-done.3 = bf16[560,128]{1,0:T(8,128)(2,1)S(1)} collective-permute-done((bf16[560,128]{1,0:T(8,128)(2,1)S(1)}, bf16[560,128]{1,0:T(8,128)(2,1)S(1)}, u32[]{:S(2)}, u32[]{:S(2)}) %collective-permute-start.3) | collective-permute-done | bytes 143392 | tf_op jit(solution)/shard_map/ppermute | solution.py:501
  24.3 1.5 %collective-permute-start.5 = (bf16[560,128]{1,0:T(8,128)(2,1)S(1)}, bf16[560,128]{1,0:T(8,128)(2,1)S(1)}, u32[]{:S(2)}, u32[]{:S(2)}) collective-permute-start(bf16[560,128]{1,0:T(8,128)(2,1)S(1)} %broadcast_select_fusion.2.after_ref), channel_id=1, source_target_pairs={{0,8},{4,12},{8,0},{12,4},{16,24},{20,28},{24,16},{28,20},{1,9},{5... | collective-permute-start | bytes 430088 | tf_op jit(solution)/shard_map/ppermute | solution.py:501
  25.8 0.0 copy-done.5
  25.8 1.1 %shard_map.159 = bf16[512,128]{1,0:T(8,128)(2,1)S(1)} custom-call(bf16[560,128]{1,0:T(8,128)(2,1)S(1)} %broadcast_select_fusion.2.after_ref, s32[128]{0:T(128)S(1)} %pad_add_fusion.scalars_ref, f32[2,16,11,8,128]{4,3,2,1,0:T(8,128)S(1)} %get-tuple-element.14.act, f32[2,16,11,8,128]{4,3,2,1,0:T(8,128)S(1)} %get-tuple-element.15.stem, ...), custom_call_target="tpu_custom_call" | custom-call | flops 2000000000 | bytes 4194304 | tf_op jit(solution)/shard_map/pallas_call | solution.py:590
  26.9 0.1 collective-permute-start.4
  27.0 1.3 %collective-permute-done.4 = bf16[512,128]{1,0:T(8,128)(2,1)S(1)} collective-permute-done((bf16[512,128]{1,0:T(8,128)(2,1)S(1)}, bf16[512,128]{1,0:T(8,128)(2,1)S(1)}, u32[]{:S(2)}, u32[]{:S(2)}) %collective-permute-start.4) | collective-permute-done | bytes 131104 | tf_op jit(solution)/shard_map/ppermute | solution.py:501
  28.4 0.6 %collective-permute-start.6 = (bf16[512,128]{1,0:T(8,128)(2,1)S(1)}, bf16[512,128]{1,0:T(8,128)(2,1)S(1)}, u32[]{:S(2)}, u32[]{:S(2)}) collective-permute-start(bf16[512,128]{1,0:T(8,128)(2,1)S(1)} %broadcast_select_fusion.5.after_too_ref), channel_id=1, source_target_pairs={{0,8},{4,12},{8,0},{12,4},{16,24},{20,28},{24,16},{28,20},{1,9},{5... | collective-permute-start | bytes 393224 | tf_op jit(solution)/shard_map/ppermute | solution.py:501
  29.0 1.8 %shard_map.160.after_too_ref.part_ref = bf16[8,9,16,128]{3,2,1,0:T(8,128)(2,1)S(1)} custom-call(bf16[560,128]{1,0:T(8,128)(2,1)S(1)} %broadcast_select_fusion.2.after_ref, bf16[512,128]{1,0:T(8,128)(2,1)S(1)} %broadcast_select_fusion.5.after_too_ref, f32[2,16,11,8,128]{4,3,2,1,0:T(8,128)S(1)} %get-tuple-element.14.act, ...), custom_call_target="tpu_custom_call" | custom-call | flops 2000000000 | bytes 4194304 | tf_op jit(solution)/shard_map/pallas_call | solution.py:602
  30.8 0.0 collective-permute-done.5
  30.8 1.6 %collective-permute-start.7 = (bf16[560,128]{1,0:T(8,128)(2,1)S(1)}, bf16[560,128]{1,0:T(8,128)(2,1)S(1)}, u32[]{:S(2)}, u32[]{:S(2)}) collective-permute-start(bf16[560,128]{1,0:T(8,128)(2,1)S(1)} %broadcast_select_fusion.1.after_ref), channel_id=1, source_target_pairs={{0,16},{4,20},{8,24},{12,28},{16,0},{20,4},{24,8},{28,12},{1,17},{... | collective-permute-start | bytes 430088 | tf_op jit(solution)/shard_map/ppermute | solution.py:501
  32.4 0.0 copy-start.4
  32.4 1.8 %shard_map.161.rest_ref = bf16[8,9,16,128]{3,2,1,0:T(8,128)(2,1)S(1)} custom-call(bf16[560,128]{1,0:T(8,128)(2,1)S(1)} %broadcast_select_fusion.1.after_ref, bf16[8,9,16,128]{3,2,1,0:T(8,128)(2,1)S(1)} %shard_map.160.after_too_ref.part_ref, f32[2,16,11,8,128]{4,3,2,1,0:T(8,128)S(1)} %get-tuple-element.14.act, ...), custom_call_target="tpu_custom_call" | custom-call | flops 2000000000 | bytes 4194304 | tf_op jit(solution)/shard_map/pallas_call | solution.py:602
  34.2 0.0 collective-permute-done.6
  34.3 1.3 %collective-permute-start.8 = (bf16[512,128]{1,0:T(8,128)(2,1)S(1)}, bf16[512,128]{1,0:T(8,128)(2,1)S(1)}, u32[]{:S(2)}, u32[]{:S(2)}) collective-permute-start(bf16[512,128]{1,0:T(8,128)(2,1)S(1)} %broadcast_select_fusion.4.after_ref), channel_id=1, source_target_pairs={{0,16},{4,20},{8,24},{12,28},{16,0},{20,4},{24,8},{28,12},{1,17},{... | collective-permute-start | bytes 393224 | tf_op jit(solution)/shard_map/ppermute | solution.py:501
  35.6 0.0 copy-done.4
  35.6 1.9 %shard_map.162 = bf16[4,8,8,256]{3,2,1,0:T(8,128)(2,1)} custom-call(s32[128]{0:T(128)S(1)} %pad_add_fusion.scalars_ref, bf16[8,9,16,128]{3,2,1,0:T(8,128)(2,1)S(1)} %shard_map.160.after_too_ref.part_ref, bf16[8,9,16,128]{3,2,1,0:T(8,128)(2,1)S(1)} %shard_map.161.rest_ref, bf16[3,3,3,128,256]{4,3,2,1,0:T(8,128)(2,1)S(1)} %copy-done.4, ...), custom_call_target="tpu_custom_call" | custom-call | flops 2000000000 | bytes 4194304 | tf_op jit(solution)/shard_map/pallas_call | solution.py:621
  37.5 0.0 collective-permute-done.7
  37.5 0.6 %slice.22 = bf16[32,48]{1,0:T(8,128)(2,1)} slice(bf16[560,128]{1,0:T(8,128)(2,1)S(1)} %broadcast_select_fusion), slice={[16:48], [0:48]} | slice | bytes 6144 | tf_op jit(solution)/shard_map/slice | solution.py:637
  38.1 0.7 %slice.23 = bf16[512,128]{1,0:T(8,128)(2,1)} slice(bf16[560,128]{1,0:T(8,128)(2,1)S(1)} %broadcast_select_fusion), slice={[48:560], [0:128]} | slice | bytes 262144 | tf_op jit(solution)/shard_map/slice | solution.py:638
  38.8 0.5 %collective-permute-done.8 = bf16[512,128]{1,0:T(8,128)(2,1)S(1)} collective-permute-done((bf16[512,128]{1,0:T(8,128)(2,1)S(1)}, bf16[512,128]{1,0:T(8,128)(2,1)S(1)}, u32[]{:S(2)}, u32[]{:S(2)}) %collective-permute-start.8) | collective-permute-done | bytes 131104 | tf_op jit(solution)/shard_map/ppermute | solution.py:501
  39.3 0.7 %broadcast_select_fusion.3 = bf16[512,128]{1,0:T(8,128)(2,1)} fusion(bf16[512,128]{1,0:T(8,128)(2,1)S(1)} %broadcast_select_fusion.4.after_ref, bf16[512,128]{1,0:T(8,128)(2,1)S(1)} %collective-permute-done.8, pred[128]{0:T(512)(128)(4,1)S(1)} %compare_bitcast_fusion), kind=kLoop, calls=%fused_computation.3 | loop fusion | flops 65536 | bytes 393344 | tf_op jit(solution)/shard_map/jit(_where)/select_n | solution.py:587
  (9 shorter events, 0.1 us)
Async XLA Ops:
  0.6 9.1 %copy-start = (bf16[1,2,16,16,128]{4,3,2,1,0:T(8,128)(2,1)S(1)}, bf16[1,2,16,16,128]{4,3,2,1,0:T(8,128)(2,1)}, u32[]{:S(2)}) copy-start(bf16[1,2,16,16,128]{4,3,2,1,0:T(8,128)(2,1)} %param.19) | copy-start | bytes 393220
  0.6 9.1 %copy-start.1 = (bf16[1,2,16,16,128]{4,3,2,1,0:T(8,128)(2,1)S(1)}, bf16[1,2,16,16,128]{4,3,2,1,0:T(8,128)(2,1)}, u32[]{:S(2)}) copy-start(bf16[1,2,16,16,128]{4,3,2,1,0:T(8,128)(2,1)} %param.20) | copy-start | bytes 393220
  0.7 9.1 %copy-start.2 = (bf16[3,3,3,3,128]{4,3,2,1,0:T(4,128)(2,1)S(1)}, bf16[3,3,3,3,128]{4,3,2,1,0:T(4,128)(2,1)}, u32[]{:S(2)}) copy-start(bf16[3,3,3,3,128]{4,3,2,1,0:T(4,128)(2,1)} %sw_ref.1) | copy-start | bytes 62212
  0.7 9.1 %copy-start.3 = (bf16[1,2,16,48]{3,2,1,0:T(8,128)(2,1)S(1)}, bf16[1,2,16,48]{3,2,1,0:T(8,128)(2,1)}, u32[]{:S(2)}) copy-start(bf16[1,2,16,48]{3,2,1,0:T(8,128)(2,1)} %param.18) | copy-start | bytes 9220
  0.7 19.0 %copy-start.6 = (f32[128]{0:T(128)S(1)}, f32[128]{0:T(128)}, u32[]{:S(2)}) copy-start(f32[128]{0:T(128)} %gain_ref.1) | copy-start | bytes 1540
  0.7 19.0 %copy-start.7 = (f32[128]{0:T(128)S(1)}, f32[128]{0:T(128)}, u32[]{:S(2)}) copy-start(f32[128]{0:T(128)} %bias_ref.1) | copy-start | bytes 1540
  2.5 17.2 %all-to-all-start = ((bf16[32,8,128]{2,1,0:T(8,128)(2,1)}), bf16[32,8,128]{2,1,0:T(8,128)(2,1)S(1)}, u32[]{:S(2)}, u32[]{:S(2)}) async-start(bf16[32,8,128]{2,1,0:T(8,128)(2,1)} %bitcast.31), calls=%async_computation | async-start | bytes 131072 | tf_op jit(solution)/shard_map/all_to_all | solution.py:548
  10.0 6.4 %collective-permute-start = (bf16[8,16,128]{2,1,0:T(8,128)(2,1)S(1)}, bf16[8,16,128]{2,1,0:T(8,128)(2,1)S(1)}, u32[]{:S(2)}, u32[]{:S(2)}) collective-permute-start(bf16[8,16,128]{2,1,0:T(8,128)(2,1)S(1)} %get-tuple-element.10), channel_id=1, source_target_pairs={{0,1},{1,2},{2,3},{3,0},{4,5},{5,6},{6,7},{7,4},{8,9},{9,10},{10,1... | collective-permute-start | bytes 98312 | tf_op jit(solution)/shard_map/ppermute | solution.py:506
  11.8 4.3 %collective-permute-start.1 = (bf16[4,16,128]{2,1,0:T(8,128)(2,1)S(1)}, bf16[4,16,128]{2,1,0:T(8,128)(2,1)S(1)}, u32[]{:S(2)}, u32[]{:S(2)}) collective-permute-start(bf16[4,16,128]{2,1,0:T(8,128)(2,1)S(1)} %get-tuple-element.11), channel_id=1, source_target_pairs={{0,3},{1,0},{2,1},{3,2},{4,7},{5,4},{6,5},{7,6},{8,11},{9,8},{10,9... | collective-permute-start | bytes 49160 | tf_op jit(solution)/shard_map/ppermute | solution.py:506
  13.8 5.8 %collective-permute-start.2 = (bf16[18,16,128]{2,1,0:T(8,128)(2,1)S(1)}, bf16[18,16,128]{2,1,0:T(8,128)(2,1)S(1)}, u32[]{:S(2)}, u32[]{:S(2)}) collective-permute-start(bf16[18,16,128]{2,1,0:T(8,128)(2,1)S(1)} %get-tuple-element.12), channel_id=1, source_target_pairs={{0,2},{1,3},{2,0},{3,1},{4,6},{5,7},{6,4},{7,5},{8,10},{9,11},{10,... | collective-permute-start | bytes 221192 | tf_op jit(solution)/shard_map/ppermute | solution.py:506
  19.7 6.2 %copy-start.5 = (bf16[3,3,3,128,128]{4,3,2,1,0:T(8,128)(2,1)S(1)}, bf16[3,3,3,128,128]{4,3,2,1,0:T(8,128)(2,1)}, u32[]{:S(2)}) copy-start(bf16[3,3,3,128,128]{4,3,2,1,0:T(8,128)(2,1)} %conv_ref.5) | copy-start | bytes 2654212
  22.8 1.4 %collective-permute-start.3 = (bf16[560,128]{1,0:T(8,128)(2,1)S(1)}, bf16[560,128]{1,0:T(8,128)(2,1)S(1)}, u32[]{:S(2)}, u32[]{:S(2)}) collective-permute-start(bf16[560,128]{1,0:T(8,128)(2,1)S(1)} %get-tuple-element.13), channel_id=1, source_target_pairs={{0,4},{4,0},{8,12},{12,8},{16,20},{20,16},{24,28},{28,24},{1,5},{5... | collective-permute-start | bytes 430088 | tf_op jit(solution)/shard_map/ppermute | solution.py:501
  24.3 6.5 %collective-permute-start.5 = (bf16[560,128]{1,0:T(8,128)(2,1)S(1)}, bf16[560,128]{1,0:T(8,128)(2,1)S(1)}, u32[]{:S(2)}, u32[]{:S(2)}) collective-permute-start(bf16[560,128]{1,0:T(8,128)(2,1)S(1)} %broadcast_select_fusion.2.after_ref), channel_id=1, source_target_pairs={{0,8},{4,12},{8,0},{12,4},{16,24},{20,28},{24,16},{28,20},{1,9},{5... | collective-permute-start | bytes 430088 | tf_op jit(solution)/shard_map/ppermute | solution.py:501
  26.9 1.4 %collective-permute-start.4 = (bf16[512,128]{1,0:T(8,128)(2,1)S(1)}, bf16[512,128]{1,0:T(8,128)(2,1)S(1)}, u32[]{:S(2)}, u32[]{:S(2)}) collective-permute-start(bf16[512,128]{1,0:T(8,128)(2,1)S(1)} %shard_map.159), channel_id=1, source_target_pairs={{0,4},{4,0},{8,12},{12,8},{16,20},{20,16},{24,28},{28,24},{1,5},{5... | collective-permute-start | bytes 393224 | tf_op jit(solution)/shard_map/ppermute | solution.py:501
  28.4 5.8 %collective-permute-start.6 = (bf16[512,128]{1,0:T(8,128)(2,1)S(1)}, bf16[512,128]{1,0:T(8,128)(2,1)S(1)}, u32[]{:S(2)}, u32[]{:S(2)}) collective-permute-start(bf16[512,128]{1,0:T(8,128)(2,1)S(1)} %broadcast_select_fusion.5.after_too_ref), channel_id=1, source_target_pairs={{0,8},{4,12},{8,0},{12,4},{16,24},{20,28},{24,16},{28,20},{1,9},{5... | collective-permute-start | bytes 393224 | tf_op jit(solution)/shard_map/ppermute | solution.py:501
  30.8 6.7 %collective-permute-start.7 = (bf16[560,128]{1,0:T(8,128)(2,1)S(1)}, bf16[560,128]{1,0:T(8,128)(2,1)S(1)}, u32[]{:S(2)}, u32[]{:S(2)}) collective-permute-start(bf16[560,128]{1,0:T(8,128)(2,1)S(1)} %broadcast_select_fusion.1.after_ref), channel_id=1, source_target_pairs={{0,16},{4,20},{8,24},{12,28},{16,0},{20,4},{24,8},{28,12},{1,17},{... | collective-permute-start | bytes 430088 | tf_op jit(solution)/shard_map/ppermute | solution.py:501
  32.4 3.2 %copy-start.4 = (bf16[3,3,3,128,256]{4,3,2,1,0:T(8,128)(2,1)S(1)}, bf16[3,3,3,128,256]{4,3,2,1,0:T(8,128)(2,1)}, u32[]{:S(2)}) copy-start(bf16[3,3,3,128,256]{4,3,2,1,0:T(8,128)(2,1)} %down_ref.1) | copy-start | bytes 5308420
  34.3 5.1 %collective-permute-start.8 = (bf16[512,128]{1,0:T(8,128)(2,1)S(1)}, bf16[512,128]{1,0:T(8,128)(2,1)S(1)}, u32[]{:S(2)}, u32[]{:S(2)}) collective-permute-start(bf16[512,128]{1,0:T(8,128)(2,1)S(1)} %broadcast_select_fusion.4.after_ref), channel_id=1, source_target_pairs={{0,16},{4,20},{8,24},{12,28},{16,0},{20,4},{24,8},{28,12},{1,17},{... | collective-permute-start | bytes 393224 | tf_op jit(solution)/shard_map/ppermute | solution.py:501

commit v5 on v4

--- a/solution.py
+++ b/solution.py
@@ -60,7 +60,7 @@
             out_ref[strip] = out.reshape(out_ref.shape[1:])
 
 
-def pack_kernel(pix_ref, sw_ref, act_ref, res_ref, down_ref, up_ref, mid_ref, sw, sems):
+def pack_kernel(pix_ref, sw_ref, act_ref, res_ref, down_ref, up_ref, mid_ref, weight_ref, sw, sems):
     copies = []
     for f in range(2):
         copies.append((act_ref.at[f, 14:16], down_ref.at[2 * f : 2 * f + 2]))
@@ -74,7 +74,7 @@
     pix = pix.astype(BF16).reshape(2, 16, 128)
     down_ref[6:8] = pix
     up_ref[2:4] = pix
-    mid_ref[0:2] = pix
+    mid_ref[...] = pix
     sw[...] = jnp.zeros(sw.shape, F32)
     for k in range(2):
         for e in range(3):
@@ -82,9 +82,7 @@
                 for b in range(3):
                     at = 27 * (k + e) + 9 * a + 3 * b
                     sw[at : at + 3, k * 128 : k * 128 + 128] = sw_ref[a, b, e].astype(F32)
-    for k in range(2):
-        half = sw[:, k * 128 : k * 128 + 128].astype(BF16)
-        mid_ref[2 + 8 * k : 10 + 8 * k] = half.reshape(8, 16, 128)
+    weight_ref[...] = sw[...].astype(BF16)
     for copy in copies:
         copy.wait()
 
@@ -102,7 +100,7 @@
     pc[j, :, 0:48] = pix_ref[...].reshape(32, 48).astype(F32)
     pc[lax.rem(j + strips - 1, strips)] = below_ref[6:8].reshape(32, 128).astype(F32)
     pc[lax.rem(j + 1, strips)] = above_ref[2:4].reshape(32, 128).astype(F32)
-    pc[lax.rem(j + 2, strips)] = mid_ref[0:2].reshape(32, 128).astype(F32)
+    pc[lax.rem(j + 2, strips)] = mid_ref[...].reshape(32, 128).astype(F32)
 
 
 def widen_cache(strips, j, cache, old_ref, below_ref, above_ref):
@@ -113,12 +111,6 @@
         cache[f, 32:288] = old_ref[f].reshape(256, 128).astype(F32)
         cache[f, 0:32] = below_ref[2 * f : 2 * f + 2].reshape(32, 128).astype(F32) * has_above
         cache[f, 288:304] = above_ref[f].astype(F32) * has_below
-
-
-def stem_weight_of(mid_ref):
-    return jnp.concatenate(
-        [mid_ref[2 + 8 * k : 10 + 8 * k].reshape(128, 128) for k in range(2)], axis=1
-    )
 
 
 def spread_matrix():
@@ -187,6 +179,7 @@
     below_ref,
     above_ref,
     mid_ref,
+    weight_ref,
     pay_ref,
     act,
     stem,
@@ -246,7 +239,7 @@
     own_even = jnp.where(low, first, pltpu.roll(second, 4, 1))
     own_odd = jnp.where(low, pltpu.roll(first, 4, 1), second)
     own = jnp.concatenate([own_even, own_odd], axis=0).reshape(176, 1024).astype(BF16)
-    weight = stem_weight_of(mid_ref)
+    weight = weight_ref[...]
     s1 = jnp.zeros((8, 256), F32)
     s2 = jnp.zeros((8, 256), F32)
     for chunk in range(8):
@@ -547,15 +540,16 @@
     lines = lines.reshape(strips * streams, half_per, 128)
     recv = lax.all_to_all(lines, ("strip", "stream"), 0, 0, tiled=True)
     recv = recv.reshape(strips, fill // 2, 128)
-    below, above, mid = pl.pallas_call(
+    below, above, mid, weight = pl.pallas_call(
         pack_kernel,
         out_shape=(
             jax.ShapeDtypeStruct((8, 16, 128), BF16),
             jax.ShapeDtypeStruct((4, 16, 128), BF16),
-            jax.ShapeDtypeStruct((18, 16, 128), BF16),
+            jax.ShapeDtypeStruct((2, 16, 128), BF16),
+            jax.ShapeDtypeStruct((128, 256), BF16),
         ),
         in_specs=[VM] * 2 + [ANY] * 2,
-        out_specs=(VM,) * 3,
+        out_specs=(VM,) * 4,
         scratch_shapes=[pltpu.VMEM((128, 256), F32), pltpu.SemaphoreType.DMA((6,))],
         compiler_params=pltpu.CompilerParams(vmem_limit_bytes=4 * mega),
     )(pix, stem_weight, acts, ress)
@@ -568,7 +562,7 @@
     first, act, stem = pl.pallas_call(
         functools.partial(stem_kernel, strips),
         out_shape=(jax.ShapeDtypeStruct((560, 128), BF16), window, window),
-        in_specs=[VM] * 9,
+        in_specs=[VM] * 10,
         out_specs=(VM,) * 3,
         scratch_shapes=[
             pltpu.VMEM((strips, 32, 128), F32),
@@ -578,7 +572,7 @@
         ],
         compiler_params=pltpu.CompilerParams(vmem_limit_bytes=24 * mega),
         cost_estimate=cost,
-    )(scalars, norm_gain, norm_bias, recv, pix, acts, below, above, mid)
+    )(scalars, norm_gain, norm_bias, recv, pix, acts, below, above, mid, weight)
     keeps = []
 
     def passed(value, bit):

time: 40.2 us -> 39.2 us (0.975)
  waiting for transfers between devices: 6.74 us -> 5.49 us
    ppermute x3, waiting for transfers between devices: 3.55 us -> 2.29 us  [shifted(): lax.ppermute(value, axis, [(i, (i + by) % size) for i in range(size)])]
  transfers between devices with their start and end apart: 10 -> 10, of which waited for: 5 -> 4; matrix products, arithmetic and copies ran while one was open for 4% -> 4% of each run, Pallas kernels for 17% -> 17%
where the time goes in v5:
time: 39.2 us; the launch traced here: 39 us
  starting transfers between devices  17.5 us (45%)
  Pallas kernels  11.7 us (30%)
  waiting for transfers between devices  5.49 us (14%)
  between operations  2.17 us (6%)
  local copies, waits for them, and re-layouts  1.3 us (3%)
  other arithmetic  0.88 us (2%)
    all_to_all x1, starting transfers between devices, body(): recv = lax.all_to_all(lines, ('strip', 'stream'), 0, 0, tiled=True)  7.3 us
    ppermute x6, starting transfers between devices, partner(): return lax.ppermute(value, axis, pairs)  5.43 us
    ppermute x3, starting transfers between devices, shifted(): lax.ppermute(value, axis, [(i, (i + by) % size) for i in range(size)])  4.75 us
    pallas_call x2, Pallas kernels, convolved(): pl.pallas_call(functools.partial(conv_kernel, strips, w0), out_shape=jax....  3.61 us
    ppermute x6, waiting for transfers between devices, partner(): return lax.ppermute(value, axis, pairs)  3.19 us
    pallas_call x1, Pallas kernels, body(): pl.pallas_call(functools.partial(stem_kernel, strips), out_shape=(jax.Sha...  3.13 us
    ppermute x3, waiting for transfers between devices, shifted(): lax.ppermute(value, axis, [(i, (i + by) % size) for i in range(size)])  2.29 us
    pallas_call x1, Pallas kernels, body(): pl.pallas_call(down_kernel, out_shape=jax.ShapeDtypeStruct((4, 8, 8, 256)...  1.93 us
  transfers between devices with their start and end apart: 10, of which 4 were waited for; matrix products, arithmetic and copies ran while one was open for 4% of the time, Pallas kernels for 17%

profile of v5, /device:TPU:0, one launch (start us, length us, event | category | flops | bytes accessed | tf_op | source)
XLA Modules:
  0.0 39.0 jit_solution(1549227982899952077)
XLA Ops:
  0.6 0.0 copy-start
  0.6 0.0 copy-start.1
  0.7 0.0 copy-start.2
  0.7 0.0 copy-start.3
  0.7 0.0 copy-start.6
  0.7 0.0 copy-start.7
  0.7 1.8 %shard_map.156 = bf16[4,8,8,128]{3,2,1,0:T(8,128)(2,1)} custom-call(bf16[48,128]{1,0:T(8,128)(2,1)} %bitcast.33, s32[1,128]{1,0:T(1,128)} %owner_ref.1, s32[1,128]{1,0:T(1,128)} %slot_ref.1), custom_call_target="tpu_custom_call" | custom-call | flops 2000000000 | bytes 4194304 | tf_op jit(solution)/shard_map/pallas_call | solution.py:529
  2.5 7.3 %all-to-all-start = ((bf16[32,8,128]{2,1,0:T(8,128)(2,1)}), bf16[32,8,128]{2,1,0:T(8,128)(2,1)S(1)}, u32[]{:S(2)}, u32[]{:S(2)}) async-start(bf16[32,8,128]{2,1,0:T(8,128)(2,1)} %bitcast.31), calls=%async_computation | async-start | bytes 131072 | tf_op jit(solution)/shard_map/all_to_all | solution.py:541
  9.8 0.0 copy-done
  9.8 0.0 copy-done.1
  9.8 0.0 copy-done.2
  9.8 0.0 copy-done.3
  9.8 0.1 shard_map.157
  10.0 1.8 %collective-permute-start = (bf16[8,16,128]{2,1,0:T(8,128)(2,1)S(1)}, bf16[8,16,128]{2,1,0:T(8,128)(2,1)S(1)}, u32[]{:S(2)}, u32[]{:S(2)}) collective-permute-start(bf16[8,16,128]{2,1,0:T(8,128)(2,1)S(1)} %get-tuple-element.11), channel_id=1, source_target_pairs={{0,1},{1,2},{2,3},{3,0},{4,5},{5,6},{6,7},{7,4},{8,9},{9,10},{10,1... | collective-permute-start | bytes 98312 | tf_op jit(solution)/shard_map/ppermute | solution.py:499
  11.8 2.1 %collective-permute-start.1 = (bf16[4,16,128]{2,1,0:T(8,128)(2,1)S(1)}, bf16[4,16,128]{2,1,0:T(8,128)(2,1)S(1)}, u32[]{:S(2)}, u32[]{:S(2)}) collective-permute-start(bf16[4,16,128]{2,1,0:T(8,128)(2,1)S(1)} %get-tuple-element.12), channel_id=1, source_target_pairs={{0,3},{1,0},{2,1},{3,2},{4,7},{5,4},{6,5},{7,6},{8,11},{9,8},{10,9... | collective-permute-start | bytes 49160 | tf_op jit(solution)/shard_map/ppermute | solution.py:499
  13.8 0.9 %collective-permute-start.2 = (bf16[2,16,128]{2,1,0:T(8,128)(2,1)S(1)}, bf16[2,16,128]{2,1,0:T(8,128)(2,1)S(1)}, u32[]{:S(2)}, u32[]{:S(2)}) collective-permute-start(bf16[2,16,128]{2,1,0:T(8,128)(2,1)S(1)} %get-tuple-element.13), channel_id=1, source_target_pairs={{0,2},{1,3},{2,0},{3,1},{4,6},{5,7},{6,4},{7,5},{8,10},{9,11},{10,... | collective-permute-start | bytes 24584 | tf_op jit(solution)/shard_map/ppermute | solution.py:499
  16.0 0.1 pad_add_fusion.scalars_ref
  16.1 2.3 %collective-permute-done.2.mid_ref = bf16[2,16,128]{2,1,0:T(8,128)(2,1)S(1)} collective-permute-done((bf16[2,16,128]{2,1,0:T(8,128)(2,1)S(1)}, bf16[2,16,128]{2,1,0:T(8,128)(2,1)S(1)}, u32[]{:S(2)}, u32[]{:S(2)}) %collective-permute-start.2) | collective-permute-done | bytes 8224 | tf_op jit(solution)/shard_map/ppermute | solution.py:499
  18.4 0.0 collective-permute-done.1.above_ref
  18.4 0.0 collective-permute-done.below_ref
  18.4 0.0 all-to-all-done
  18.4 0.0 copy-done.6
  18.4 0.0 copy-done.7
  18.4 0.0 copy-start.5
  18.4 3.1 %shard_map.158 = (bf16[560,128]{1,0:T(8,128)(2,1)S(1)}, f32[2,16,11,8,128]{4,3,2,1,0:T(8,128)S(1)}, f32[2,16,11,8,128]{4,3,2,1,0:T(8,128)S(1)}) custom-call(s32[128]{0:T(128)S(1)} %pad_add_fusion.scalars_ref, f32[128]{0:T(128)S(1)} %copy-done.6, f32[128]{0:T(128)S(1)} %copy-done.7, bf16[4,64,128]{2,1,0:T(8,128)(2,1)S(1)} %bitcast.26, ...), custom_call_target="tpu_custom_call" | custom-call | flops 2000000000 | bytes 4194304 | tf_op jit(solution)/shard_map/pallas_call | solution.py:562
  21.6 0.1 collective-permute-start.3
  21.7 1.3 %collective-permute-done.3 = bf16[560,128]{1,0:T(8,128)(2,1)S(1)} collective-permute-done((bf16[560,128]{1,0:T(8,128)(2,1)S(1)}, bf16[560,128]{1,0:T(8,128)(2,1)S(1)}, u32[]{:S(2)}, u32[]{:S(2)}) %collective-permute-start.3) | collective-permute-done | bytes 143392 | tf_op jit(solution)/shard_map/ppermute | solution.py:494
  23.0 1.8 %collective-permute-start.5 = (bf16[560,128]{1,0:T(8,128)(2,1)S(1)}, bf16[560,128]{1,0:T(8,128)(2,1)S(1)}, u32[]{:S(2)}, u32[]{:S(2)}) collective-permute-start(bf16[560,128]{1,0:T(8,128)(2,1)S(1)} %broadcast_select_fusion.2.after_ref), channel_id=1, source_target_pairs={{0,8},{4,12},{8,0},{12,4},{16,24},{20,28},{24,16},{28,20},{1,9},{5... | collective-permute-start | bytes 430088 | tf_op jit(solution)/shard_map/ppermute | solution.py:494
  24.9 0.0 copy-done.5
  24.9 1.1 %shard_map.159 = bf16[512,128]{1,0:T(8,128)(2,1)S(1)} custom-call(bf16[560,128]{1,0:T(8,128)(2,1)S(1)} %broadcast_select_fusion.2.after_ref, s32[128]{0:T(128)S(1)} %pad_add_fusion.scalars_ref, f32[2,16,11,8,128]{4,3,2,1,0:T(8,128)S(1)} %get-tuple-element.16.act, f32[2,16,11,8,128]{4,3,2,1,0:T(8,128)S(1)} %get-tuple-element.17.stem, ...), custom_call_target="tpu_custom_call" | custom-call | flops 2000000000 | bytes 4194304 | tf_op jit(solution)/shard_map/pallas_call | solution.py:584
  26.0 0.1 collective-permute-start.4
  26.1 1.3 %collective-permute-done.4 = bf16[512,128]{1,0:T(8,128)(2,1)S(1)} collective-permute-done((bf16[512,128]{1,0:T(8,128)(2,1)S(1)}, bf16[512,128]{1,0:T(8,128)(2,1)S(1)}, u32[]{:S(2)}, u32[]{:S(2)}) %collective-permute-start.4) | collective-permute-done | bytes 131104 | tf_op jit(solution)/shard_map/ppermute | solution.py:494
  27.4 0.3 collective-permute-start.6
  27.8 1.8 %shard_map.160.after_too_ref.part_ref = bf16[8,9,16,128]{3,2,1,0:T(8,128)(2,1)S(1)} custom-call(bf16[560,128]{1,0:T(8,128)(2,1)S(1)} %broadcast_select_fusion.2.after_ref, bf16[512,128]{1,0:T(8,128)(2,1)S(1)} %broadcast_select_fusion.5.after_too_ref, f32[2,16,11,8,128]{4,3,2,1,0:T(8,128)S(1)} %get-tuple-element.16.act, ...), custom_call_target="tpu_custom_call" | custom-call | flops 2000000000 | bytes 4194304 | tf_op jit(solution)/shard_map/pallas_call | solution.py:596
  29.6 0.0 collective-permute-done.5
  29.6 1.8 %collective-permute-start.7 = (bf16[560,128]{1,0:T(8,128)(2,1)S(1)}, bf16[560,128]{1,0:T(8,128)(2,1)S(1)}, u32[]{:S(2)}, u32[]{:S(2)}) collective-permute-start(bf16[560,128]{1,0:T(8,128)(2,1)S(1)} %broadcast_select_fusion.1.after_ref), channel_id=1, source_target_pairs={{0,16},{4,20},{8,24},{12,28},{16,0},{20,4},{24,8},{28,12},{1,17},{... | collective-permute-start | bytes 430088 | tf_op jit(solution)/shard_map/ppermute | solution.py:494
  31.4 0.0 copy-start.4
  31.5 1.8 %shard_map.161.rest_ref = bf16[8,9,16,128]{3,2,1,0:T(8,128)(2,1)S(1)} custom-call(bf16[560,128]{1,0:T(8,128)(2,1)S(1)} %broadcast_select_fusion.1.after_ref, bf16[8,9,16,128]{3,2,1,0:T(8,128)(2,1)S(1)} %shard_map.160.after_too_ref.part_ref, f32[2,16,11,8,128]{4,3,2,1,0:T(8,128)S(1)} %get-tuple-element.16.act, ...), custom_call_target="tpu_custom_call" | custom-call | flops 2000000000 | bytes 4194304 | tf_op jit(solution)/shard_map/pallas_call | solution.py:596
  33.3 0.0 collective-permute-done.6
  33.3 1.3 %collective-permute-start.8 = (bf16[512,128]{1,0:T(8,128)(2,1)S(1)}, bf16[512,128]{1,0:T(8,128)(2,1)S(1)}, u32[]{:S(2)}, u32[]{:S(2)}) collective-permute-start(bf16[512,128]{1,0:T(8,128)(2,1)S(1)} %broadcast_select_fusion.4.after_ref), channel_id=1, source_target_pairs={{0,16},{4,20},{8,24},{12,28},{16,0},{20,4},{24,8},{28,12},{1,17},{... | collective-permute-start | bytes 393224 | tf_op jit(solution)/shard_map/ppermute | solution.py:494
  34.6 0.0 copy-done.4
  34.6 1.9 %shard_map.162 = bf16[4,8,8,256]{3,2,1,0:T(8,128)(2,1)} custom-call(s32[128]{0:T(128)S(1)} %pad_add_fusion.scalars_ref, bf16[8,9,16,128]{3,2,1,0:T(8,128)(2,1)S(1)} %shard_map.160.after_too_ref.part_ref, bf16[8,9,16,128]{3,2,1,0:T(8,128)(2,1)S(1)} %shard_map.161.rest_ref, bf16[3,3,3,128,256]{4,3,2,1,0:T(8,128)(2,1)S(1)} %copy-done.4, ...), custom_call_target="tpu_custom_call" | custom-call | flops 2000000000 | bytes 4194304 | tf_op jit(solution)/shard_map/pallas_call | solution.py:615
  36.5 0.0 collective-permute-done.7
  36.6 0.6 %slice.22 = bf16[32,48]{1,0:T(8,128)(2,1)} slice(bf16[560,128]{1,0:T(8,128)(2,1)S(1)} %broadcast_select_fusion), slice={[16:48], [0:48]} | slice | bytes 6144 | tf_op jit(solution)/shard_map/slice | solution.py:631
  37.2 0.7 %slice.23 = bf16[512,128]{1,0:T(8,128)(2,1)} slice(bf16[560,128]{1,0:T(8,128)(2,1)S(1)} %broadcast_select_fusion), slice={[48:560], [0:128]} | slice | bytes 262144 | tf_op jit(solution)/shard_map/slice | solution.py:632
  37.8 0.5 %collective-permute-done.8 = bf16[512,128]{1,0:T(8,128)(2,1)S(1)} collective-permute-done((bf16[512,128]{1,0:T(8,128)(2,1)S(1)}, bf16[512,128]{1,0:T(8,128)(2,1)S(1)}, u32[]{:S(2)}, u32[]{:S(2)}) %collective-permute-start.8) | collective-permute-done | bytes 131104 | tf_op jit(solution)/shard_map/ppermute | solution.py:494
  38.4 0.7 %broadcast_select_fusion.3 = bf16[512,128]{1,0:T(8,128)(2,1)} fusion(bf16[512,128]{1,0:T(8,128)(2,1)S(1)} %broadcast_select_fusion.4.after_ref, bf16[512,128]{1,0:T(8,128)(2,1)S(1)} %collective-permute-done.8, pred[128]{0:T(512)(128)(4,1)S(1)} %compare_bitcast_fusion), kind=kLoop, calls=%fused_computation.3 | loop fusion | flops 65536 | bytes 393344 | tf_op jit(solution)/shard_map/jit(_where)/select_n | solution.py:581
  (9 shorter events, 0.1 us)
Async XLA Ops:
  0.6 9.1 %copy-start = (bf16[1,2,16,16,128]{4,3,2,1,0:T(8,128)(2,1)S(1)}, bf16[1,2,16,16,128]{4,3,2,1,0:T(8,128)(2,1)}, u32[]{:S(2)}) copy-start(bf16[1,2,16,16,128]{4,3,2,1,0:T(8,128)(2,1)} %param.19) | copy-start | bytes 393220
  0.6 9.1 %copy-start.1 = (bf16[1,2,16,16,128]{4,3,2,1,0:T(8,128)(2,1)S(1)}, bf16[1,2,16,16,128]{4,3,2,1,0:T(8,128)(2,1)}, u32[]{:S(2)}) copy-start(bf16[1,2,16,16,128]{4,3,2,1,0:T(8,128)(2,1)} %param.20) | copy-start | bytes 393220
  0.7 9.1 %copy-start.2 = (bf16[3,3,3,3,128]{4,3,2,1,0:T(4,128)(2,1)S(1)}, bf16[3,3,3,3,128]{4,3,2,1,0:T(4,128)(2,1)}, u32[]{:S(2)}) copy-start(bf16[3,3,3,3,128]{4,3,2,1,0:T(4,128)(2,1)} %sw_ref.1) | copy-start | bytes 62212
  0.7 9.1 %copy-start.3 = (bf16[1,2,16,48]{3,2,1,0:T(8,128)(2,1)S(1)}, bf16[1,2,16,48]{3,2,1,0:T(8,128)(2,1)}, u32[]{:S(2)}) copy-start(bf16[1,2,16,48]{3,2,1,0:T(8,128)(2,1)} %param.18) | copy-start | bytes 9220
  0.7 17.7 %copy-start.6 = (f32[128]{0:T(128)S(1)}, f32[128]{0:T(128)}, u32[]{:S(2)}) copy-start(f32[128]{0:T(128)} %gain_ref.1) | copy-start | bytes 1540
  0.7 17.7 %copy-start.7 = (f32[128]{0:T(128)S(1)}, f32[128]{0:T(128)}, u32[]{:S(2)}) copy-start(f32[128]{0:T(128)} %bias_ref.1) | copy-start | bytes 1540
  2.5 15.9 %all-to-all-start = ((bf16[32,8,128]{2,1,0:T(8,128)(2,1)}), bf16[32,8,128]{2,1,0:T(8,128)(2,1)S(1)}, u32[]{:S(2)}, u32[]{:S(2)}) async-start(bf16[32,8,128]{2,1,0:T(8,128)(2,1)} %bitcast.31), calls=%async_computation | async-start | bytes 131072 | tf_op jit(solution)/shard_map/all_to_all | solution.py:541
  10.0 8.4 %collective-permute-start = (bf16[8,16,128]{2,1,0:T(8,128)(2,1)S(1)}, bf16[8,16,128]{2,1,0:T(8,128)(2,1)S(1)}, u32[]{:S(2)}, u32[]{:S(2)}) collective-permute-start(bf16[8,16,128]{2,1,0:T(8,128)(2,1)S(1)} %get-tuple-element.11), channel_id=1, source_target_pairs={{0,1},{1,2},{2,3},{3,0},{4,5},{5,6},{6,7},{7,4},{8,9},{9,10},{10,1... | collective-permute-start | bytes 98312 | tf_op jit(solution)/shard_map/ppermute | solution.py:499
  11.8 6.6 %collective-permute-start.1 = (bf16[4,16,128]{2,1,0:T(8,128)(2,1)S(1)}, bf16[4,16,128]{2,1,0:T(8,128)(2,1)S(1)}, u32[]{:S(2)}, u32[]{:S(2)}) collective-permute-start(bf16[4,16,128]{2,1,0:T(8,128)(2,1)S(1)} %get-tuple-element.12), channel_id=1, source_target_pairs={{0,3},{1,0},{2,1},{3,2},{4,7},{5,4},{6,5},{7,6},{8,11},{9,8},{10,9... | collective-permute-start | bytes 49160 | tf_op jit(solution)/shard_map/ppermute | solution.py:499
  13.8 4.5 %collective-permute-start.2 = (bf16[2,16,128]{2,1,0:T(8,128)(2,1)S(1)}, bf16[2,16,128]{2,1,0:T(8,128)(2,1)S(1)}, u32[]{:S(2)}, u32[]{:S(2)}) collective-permute-start(bf16[2,16,128]{2,1,0:T(8,128)(2,1)S(1)} %get-tuple-element.13), channel_id=1, source_target_pairs={{0,2},{1,3},{2,0},{3,1},{4,6},{5,7},{6,4},{7,5},{8,10},{9,11},{10,... | collective-permute-start | bytes 24584 | tf_op jit(solution)/shard_map/ppermute | solution.py:499
  18.4 6.5 %copy-start.5 = (bf16[3,3,3,128,128]{4,3,2,1,0:T(8,128)(2,1)S(1)}, bf16[3,3,3,128,128]{4,3,2,1,0:T(8,128)(2,1)}, u32[]{:S(2)}) copy-start(bf16[3,3,3,128,128]{4,3,2,1,0:T(8,128)(2,1)} %conv_ref.5) | copy-start | bytes 2654212
  21.6 1.4 %collective-permute-start.3 = (bf16[560,128]{1,0:T(8,128)(2,1)S(1)}, bf16[560,128]{1,0:T(8,128)(2,1)S(1)}, u32[]{:S(2)}, u32[]{:S(2)}) collective-permute-start(bf16[560,128]{1,0:T(8,128)(2,1)S(1)} %get-tuple-element.15), channel_id=1, source_target_pairs={{0,4},{4,0},{8,12},{12,8},{16,20},{20,16},{24,28},{28,24},{1,5},{5... | collective-permute-start | bytes 430088 | tf_op jit(solution)/shard_map/ppermute | solution.py:494
  23.0 6.5 %collective-permute-start.5 = (bf16[560,128]{1,0:T(8,128)(2,1)S(1)}, bf16[560,128]{1,0:T(8,128)(2,1)S(1)}, u32[]{:S(2)}, u32[]{:S(2)}) collective-permute-start(bf16[560,128]{1,0:T(8,128)(2,1)S(1)} %broadcast_select_fusion.2.after_ref), channel_id=1, source_target_pairs={{0,8},{4,12},{8,0},{12,4},{16,24},{20,28},{24,16},{28,20},{1,9},{5... | collective-permute-start | bytes 430088 | tf_op jit(solution)/shard_map/ppermute | solution.py:494
  26.0 1.4 %collective-permute-start.4 = (bf16[512,128]{1,0:T(8,128)(2,1)S(1)}, bf16[512,128]{1,0:T(8,128)(2,1)S(1)}, u32[]{:S(2)}, u32[]{:S(2)}) collective-permute-start(bf16[512,128]{1,0:T(8,128)(2,1)S(1)} %shard_map.159), channel_id=1, source_target_pairs={{0,4},{4,0},{8,12},{12,8},{16,20},{20,16},{24,28},{28,24},{1,5},{5... | collective-permute-start | bytes 393224 | tf_op jit(solution)/shard_map/ppermute | solution.py:494
  27.4 5.8 %collective-permute-start.6 = (bf16[512,128]{1,0:T(8,128)(2,1)S(1)}, bf16[512,128]{1,0:T(8,128)(2,1)S(1)}, u32[]{:S(2)}, u32[]{:S(2)}) collective-permute-start(bf16[512,128]{1,0:T(8,128)(2,1)S(1)} %broadcast_select_fusion.5.after_too_ref), channel_id=1, source_target_pairs={{0,8},{4,12},{8,0},{12,4},{16,24},{20,28},{24,16},{28,20},{1,9},{5... | collective-permute-start | bytes 393224 | tf_op jit(solution)/shard_map/ppermute | solution.py:494
  29.6 6.9 %collective-permute-start.7 = (bf16[560,128]{1,0:T(8,128)(2,1)S(1)}, bf16[560,128]{1,0:T(8,128)(2,1)S(1)}, u32[]{:S(2)}, u32[]{:S(2)}) collective-permute-start(bf16[560,128]{1,0:T(8,128)(2,1)S(1)} %broadcast_select_fusion.1.after_ref), channel_id=1, source_target_pairs={{0,16},{4,20},{8,24},{12,28},{16,0},{20,4},{24,8},{28,12},{1,17},{... | collective-permute-start | bytes 430088 | tf_op jit(solution)/shard_map/ppermute | solution.py:494
  31.4 3.2 %copy-start.4 = (bf16[3,3,3,128,256]{4,3,2,1,0:T(8,128)(2,1)S(1)}, bf16[3,3,3,128,256]{4,3,2,1,0:T(8,128)(2,1)}, u32[]{:S(2)}) copy-start(bf16[3,3,3,128,256]{4,3,2,1,0:T(8,128)(2,1)} %down_ref.1) | copy-start | bytes 5308420
  33.3 5.1 %collective-permute-start.8 = (bf16[512,128]{1,0:T(8,128)(2,1)S(1)}, bf16[512,128]{1,0:T(8,128)(2,1)S(1)}, u32[]{:S(2)}, u32[]{:S(2)}) collective-permute-start(bf16[512,128]{1,0:T(8,128)(2,1)S(1)} %broadcast_select_fusion.4.after_ref), channel_id=1, source_target_pairs={{0,16},{4,20},{8,24},{12,28},{16,0},{20,4},{24,8},{28,12},{1,17},{... | collective-permute-start | bytes 393224 | tf_op jit(solution)/shard_map/ppermute | solution.py:494

commit v6 on v5

--- a/solution.py
+++ b/solution.py
@@ -139,6 +139,12 @@
     return scale, bias_ref[...].reshape(1, 128) - mean * scale
 
 
+def frame_row(rows, t):
+    t = jnp.maximum(t, 0)
+    mine = iota((8, 128), 0) == (t & 1) * 4 + (t >> 1)
+    return jnp.sum(jnp.where(mine, rows, 0.0), axis=0, keepdims=True)
+
+
 def silu(v):
     h = 0.5 * v
     return h + h * jnp.tanh(h)
@@ -181,7 +187,7 @@
     mid_ref,
     weight_ref,
     pay_ref,
-    act,
+    norm_ref,
     stem,
     pc,
     zs,
@@ -197,22 +203,29 @@
     sub = iota((128, 128), 0)
     crow, cframe = iota((128, 32), 1) % 16, iota((128, 32), 1) // 16
     csub = iota((128, 32), 0)
-    for s in range(strips):
-        pixels, slots = received(recv_ref[s])
+    arrived = [received(recv_ref[s]) for s in range(strips)]
+    old_hits = []
+    for a in range(3):
+        ct = cframe - a
+        cplace = jnp.where(ct >= 0, crow * 8 + (ct & 1) * 4 + (ct >> 1), -1)
+        old_hits.append(jnp.where(csub == cplace, 1.0, 0.0))
+    picks = []
+    for _, slots in arrived:
         frame, row = slots >> 4, slots & 15
-        source = jnp.concatenate([pixels, pc[s]], axis=0).astype(BF16)
         hits = []
         for a in range(3):
             t = frame + 2 - a
             place = jnp.where(t < FRAMES, row * 8 + (t & 1) * 4 + (t >> 1), -1)
             hit = jnp.where(sub.reshape(16, 8, 128) == place[None], 1.0, 0.0).reshape(128, 128)
-            ct = cframe - a
-            cplace = jnp.where(ct >= 0, crow * 8 + (ct & 1) * 4 + (ct >> 1), -1)
-            chit = jnp.where(csub == cplace, 1.0, 0.0)
-            hits.append(jnp.concatenate([hit, chit], axis=1).astype(BF16))
-        placed = dot(jnp.concatenate(hits, axis=0), source).reshape(3, 16, 8, 128)
+            hits.append(jnp.concatenate([hit, old_hits[a]], axis=1).astype(BF16))
+        picks.append(jnp.concatenate(hits, axis=0))
+    sources = [
+        jnp.concatenate([arrived[s][0], pc[s]], axis=0).astype(BF16) for s in range(strips)
+    ]
+    placed = [dot(picks[s], sources[s]).reshape(3, 16, 8, 128) for s in range(strips)]
+    for s in range(strips):
         for a in range(3):
-            zs[a, 4 + s * 16 : 4 + (s + 1) * 16] = placed[a]
+            zs[a, 4 + s * 16 : 4 + (s + 1) * 16] = placed[s][a]
     pixels, slots = received(recv_ref[j])
     goal = (slots >> 4) + 2 - valid
     place = jnp.where((goal >= 0) & (goal < 2), goal * 16 + (slots & 15), -1)
@@ -252,38 +265,23 @@
     s1 = s1[:, 0:128] + s1[:, 128:256]
     s2 = s2[:, 0:128] + s2[:, 128:256]
     scale, shift = norm_rows(strips, s1, s2, gain_ref, bias_ref)
-    low8 = iota((8, 128), 0) < 4
-    scales = (
-        jnp.where(low8, scale, pltpu.roll(scale, 4, 0)),
-        jnp.where(low8, pltpu.roll(scale, 4, 0), scale),
-    )
-    shifts = (
-        jnp.where(low8, shift, pltpu.roll(shift, 4, 0)),
-        jnp.where(low8, pltpu.roll(shift, 4, 0), shift),
-    )
-    half = iota((11, 8, 128), 1) // 4
-    line_of = j * 16 + iota((11, 8, 128), 0) - 2 + 8 * half
-    inside = jnp.where((line_of >= 0) & (line_of < rows_all), 1.0, 0.0)
-
-    def activate(w, carry):
-        for p in range(2):
-            act[p, w] = silu(stem[p, w] * scales[p] + shifts[p]) * inside
-        return carry
-
-    lax.fori_loop(0, 16, activate, 0, unroll=4)
-    act_rows = act.reshape(2 * 16 * 11 * 8, 128)
+    norm_ref[0] = scale
+    norm_ref[1] = shift
+    stem_rows = stem.reshape(2 * 16 * 11 * 8, 128)
     for i in range(2):
+        t = valid - 2 + i
+        scale_i, shift_i = frame_row(scale, t), frame_row(shift, t)
         for y in range(16):
-            block = act_rows[pl.ds(row_at(valid - 2 + i, y), 16, stride=88)]
+            block = stem_rows[pl.ds(row_at(t, y), 16, stride=88)]
+            block = silu(block * scale_i + shift_i)
             block = jnp.where(valid + i < 2, old_ref[1, y].astype(F32), block)
             to = 48 + i * 256 + y * 16
             pay_ref[to : to + 16] = block.astype(BF16)
 
 
 def last_kernel(
-    after_ref,
     scalars_ref,
-    act,
+    norm_ref,
     stem,
     old_ref,
     res_old_ref,
@@ -293,10 +291,11 @@
     pay_ref,
     lines,
 ):
-    del after_ref
     j = lax.axis_index("strip")
     valid = whole(scalars_ref, 0)
-    act_rows = act.reshape(2 * 16 * 11 * 8, 128)
+    scale, shift = norm_ref[0], norm_ref[1]
+    has_above = jnp.where(j > 0, 1.0, 0.0)
+    has_below = jnp.where(j < lax.axis_size("strip") - 1, 1.0, 0.0)
     stem_rows = stem.reshape(2 * 16 * 11 * 8, 128)
     column = iota((16, 128), 0)
 
@@ -310,15 +309,20 @@
 
         @pl.when(from_cache >= 2)
         def _(m=m, from_cache=from_cache):
+            t = from_cache - 2
+            scale_m, shift_m = frame_row(scale, t), frame_row(shift, t)
             for y in range(-1, 17):
-                block = act_rows[pl.ds(row_at(from_cache - 2, y), 16, stride=88)]
+                block = stem_rows[pl.ds(row_at(t, y), 16, stride=88)]
+                block = silu(block * scale_m + shift_m)
+                if y < 0:
+                    block = block * has_above
+                if y > 15:
+                    block = block * has_below
                 side_by_side(m, y, block)
 
         @pl.when(from_cache < 2)
         def _(m=m, from_cache=from_cache):
             f = jnp.clip(from_cache, 0, 1)
-            has_above = jnp.where(j > 0, 1.0, 0.0)
-            has_below = jnp.where(j < lax.axis_size("strip") - 1, 1.0, 0.0)
             side_by_side(m, -1, below_ref[2 * f + 1].astype(F32) * has_above)
             for y in range(16):
                 side_by_side(m, y, old_ref[f, y].astype(F32))
@@ -356,8 +360,12 @@
             block = block + out[i, y // 2, :, y % 2 * 128 : y % 2 * 128 + 128]
             if i == 0:
                 block = jnp.where(valid < 2, res_old_ref[1, y].astype(F32), block)
-            to = i * 256 + y * 16
-            pay_ref[to : to + 16] = block.astype(BF16)
+            pay_ref[i * 16 + y] = block
+
+
+def seal_kernel(after_ref, value_ref, out_ref):
+    del after_ref
+    out_ref[...] = value_ref[...].reshape(512, 128).astype(BF16)
 
 
 def conv_kernel(
@@ -365,7 +373,7 @@
     w0,
     after_ref,
     after_too_ref,
-    act,
+    norm_ref,
     stem,
     old_ref,
     below_ref,
@@ -378,6 +386,15 @@
     del after_ref, after_too_ref
     j = lax.axis_index("strip")
     widen_cache(strips, j, cache, old_ref, below_ref, above_ref)
+    low8 = iota((8, 128), 0) < 4
+    scales, shifts = [], []
+    for k, rows in enumerate((scales, shifts)):
+        v = norm_ref[k]
+        rows.append(jnp.where(low8, v, pltpu.roll(v, 4, 0)))
+        rows.append(jnp.where(low8, pltpu.roll(v, 4, 0), v))
+    half = iota((11, 8, 128), 1) // 4
+    line_of = j * 16 + iota((11, 8, 128), 0) - 2 + 8 * half
+    inside = jnp.where((line_of >= 0) & (line_of < strips * 16), 1.0, 0.0)
     at0 = iota((11, 8, 128), 1) == 0
     at4 = iota((11, 8, 128), 1) == 4
     edge = 0 if w0 == 0 else 9
@@ -386,20 +403,20 @@
 
     def arrange(w, carry):
         late = []
+        even, odd = [silu(stem[p, w] * scales[p] + shifts[p]) * inside for p in range(2)]
         for f in range(2):
             rows = [
                 jnp.broadcast_to(cache[f, pl.ds(y * 16 + w, 1)], (8, 128)) for y in range(19)
             ]
             upper, lower = jnp.stack(rows[0:11], axis=0), jnp.stack(rows[8:19], axis=0)
-            rolled = pltpu.roll(act[f, w], 1, 1)
+            rolled = pltpu.roll((even, odd)[f], 1, 1)
             late.append(jnp.where(at0, upper, jnp.where(at4, lower, rolled)))
-        even, odd = act[0, w], act[1, w]
         taps = ((late[0], late[1]), (late[1], even), (even, odd))
         for a in range(3):
             act3[w + shift, :, :, a * 128 : (a + 1) * 128] = jnp.concatenate(taps[a], axis=1).astype(BF16)
         return carry
 
-    lax.fori_loop(max(w0 - 1, 0), min(w0 + 9, 16), arrange, 0, unroll=3)
+    lax.fori_loop(max(w0 - 1, 0), min(w0 + 9, 16), arrange, 0, unroll=9)
     weights = pair_weight(conv_ref)
     outside = (j == 0) & (iota((9, 16, 128), 0) == 0) & (iota((9, 16, 128), 1) % 8 < 4)
     keep = jnp.where(outside, 0.0, 1.0)
@@ -487,6 +504,22 @@
                 for o in range(2):
                     block = lat[o, pl.ds(i * 8 + h * 4 + t, 8, stride=32)]
                     lat_ref[t, h * 4 + i, :, o * 128 : (o + 1) * 128] = block.astype(BF16)
+
+
+def finish_kernel(
+    bit, first_ref, first_in_ref, second_ref, second_in_ref, new_pix_ref, new_act_ref, new_res_ref
+):
+    target = first_ref[0:16].astype(jnp.int32)
+    mine = (target >> bit) & 1 == (lax.axis_index("stream") >> bit) & 1
+    mine = jnp.where(mine, 1.0, 0.0)[0:1] > 0.5
+
+    def chosen(own_ref, in_ref, start, stop):
+        own, other = own_ref[start:stop].astype(F32), in_ref[start:stop].astype(F32)
+        return jnp.where(mine, own, other).astype(BF16)
+
+    new_pix_ref[...] = chosen(first_ref, first_in_ref, 16, 48)[:, 0:48].reshape(2, 16, 48)
+    new_act_ref[...] = chosen(first_ref, first_in_ref, 48, 560).reshape(2, 16, 16, 128)
+    new_res_ref[...] = chosen(second_ref, second_in_ref, 0, 512).reshape(2, 16, 16, 128)
 
 
 def partner(value, axis, stride):
@@ -559,9 +592,13 @@
     scalars = jnp.concatenate([valid_frames, next_owner, jnp.zeros((126,), jnp.int32)])
     rows_all = strips * 16
     window = jax.ShapeDtypeStruct((2, 16, 11, 8, 128), F32)
-    first, act, stem = pl.pallas_call(
+    first, norm, stem = pl.pallas_call(
         functools.partial(stem_kernel, strips),
-        out_shape=(jax.ShapeDtypeStruct((560, 128), BF16), window, window),
+        out_shape=(
+            jax.ShapeDtypeStruct((560, 128), BF16),
+            jax.ShapeDtypeStruct((2, 8, 128), F32),
+            window,
+        ),
         in_specs=[VM] * 10,
         out_specs=(VM,) * 3,
         scratch_shapes=[
@@ -580,16 +617,23 @@
             keeps.append((value[0:1].astype(jnp.int32) >> bit) & 1 == (stream_pos >> bit) & 1)
         return jnp.where(keeps[bit], value, partner(value, "stream", 1 << bit))
 
-    first = passed(first, 0)
     second = pl.pallas_call(
         last_kernel,
-        out_shape=jax.ShapeDtypeStruct((512, 128), BF16),
-        in_specs=[ANY] + [VM] * 8,
+        out_shape=jax.ShapeDtypeStruct((32, 16, 128), F32),
+        in_specs=[VM] * 8,
         out_specs=VM,
         scratch_shapes=[pltpu.VMEM((4, 18, 16, 384), BF16)],
         compiler_params=pltpu.CompilerParams(vmem_limit_bytes=24 * mega),
         cost_estimate=cost,
-    )(first, scalars, act, stem, acts, ress, below, above, conv_weight)
+    )(scalars, norm, stem, acts, ress, below, above, conv_weight)
+    first = passed(first, 0)
+    second = pl.pallas_call(
+        seal_kernel,
+        out_shape=jax.ShapeDtypeStruct((512, 128), BF16),
+        in_specs=[ANY, VM],
+        out_specs=VM,
+        compiler_params=pltpu.CompilerParams(vmem_limit_bytes=8 * mega),
+    )(first, second)
     second = passed(second, 0)
 
     def convolved(w0, after, after_too):
@@ -604,7 +648,7 @@
             ],
             compiler_params=pltpu.CompilerParams(vmem_limit_bytes=24 * mega),
             cost_estimate=cost,
-        )(after, after_too, act, stem, acts, below, above, conv_weight)
+        )(after, after_too, norm, stem, acts, below, above, conv_weight)
 
     part = convolved(0, first, second)
     for bit in range(1, sections - 1):
@@ -625,12 +669,24 @@
         compiler_params=pltpu.CompilerParams(vmem_limit_bytes=24 * mega),
         cost_estimate=cost,
     )(scalars, part, rest, down_weight, ress, below, second)
-    if sections > 1:
-        first = passed(first, sections - 1)
-        second = passed(second, sections - 1)
-    new_pix = first[16:48, 0:48].reshape(1, 2, 16, 48)
-    new_act = first[48:].reshape(1, 2, 16, 16, 128)
-    return (latent[None], new_pix, new_act, second.reshape(1, 2, 16, 16, 128))
+    bit = sections - 1
+    new_pix, new_act, new_res = pl.pallas_call(
+        functools.partial(finish_kernel, bit),
+        out_shape=(
+            jax.ShapeDtypeStruct(pix.shape, BF16),
+            jax.ShapeDtypeStruct(acts.shape, BF16),
+            jax.ShapeDtypeStruct(ress.shape, BF16),
+        ),
+        in_specs=[VM] * 4,
+        out_specs=(VM,) * 3,
+        compiler_params=pltpu.CompilerParams(vmem_limit_bytes=8 * mega),
+    )(
+        first,
+        partner(first, "stream", 1 << bit),
+        second,
+        partner(second, "stream", 1 << bit),
+    )
+    return (latent[None], new_pix[None], new_act[None], new_res[None])
 
 
 def solution(mesh):

time: 39.2 us -> 38.7 us (0.987)
  waiting for transfers between devices: 5.49 us -> 6.92 us
  local copies, waits for them, and re-layouts: 1.3 us -> 0.04 us
  other arithmetic: 0.88 us -> 0.18 us
    ppermute x6, waiting for transfers between devices: 3.19 us -> 4.62 us  [partner(): return lax.ppermute(value, axis, pairs)]
    slice x2 -> x0, local copies, waits for them, and re-layouts: 1.26 us -> none  [the longest x1 0.66 us: body(): new_act = first[48:].reshape(1, 2, 16, 16, 128)]
    pallas_call x1 -> x3, Pallas kernels: 1.12 us -> 2.04 us  [the longest x1 1.27 us: body(): pl.pallas_call(last_kernel, out_shape=jax.ShapeDtypeStruct((32, 16, 128),...]
    select_n x6 -> x4, other arithmetic: 0.77 us -> 0.08 us  [passed(): return jnp.where(keeps[bit], value, partner(value, 'stream', 1 << bit))]
    pallas_call x1, Pallas kernels: 3.13 us -> 2.74 us  [body(): pl.pallas_call(functools.partial(stem_kernel, strips), out_shape=(jax.Sha...]
  transfers between devices with their start and end apart: 10 -> 10, of which waited for: 4 -> 5; matrix products, arithmetic and copies ran while one was open for 4% -> 0% of each run, Pallas kernels for 17% -> 17%
where the time goes in v6:
time: 38.7 us; the launch traced here: 38.5 us
  starting transfers between devices  17.3 us (45%)
  Pallas kernels  11.9 us (31%)
  waiting for transfers between devices  6.92 us (18%)
  between operations  2.16 us (6%)
    all_to_all x1, starting transfers between devices, body(): recv = lax.all_to_all(lines, ('strip', 'stream'), 0, 0, tiled=True)  7.3 us
    ppermute x6, starting transfers between devices, partner(): return lax.ppermute(value, axis, pairs)  5.26 us
    ppermute x3, starting transfers between devices, shifted(): lax.ppermute(value, axis, [(i, (i + by) % size) for i in range(size)])  4.75 us
    ppermute x6, waiting for transfers between devices, partner(): return lax.ppermute(value, axis, pairs)  4.62 us
    pallas_call x2, Pallas kernels, convolved(): pl.pallas_call(functools.partial(conv_kernel, strips, w0), out_shape=jax....  3.3 us
    pallas_call x1, Pallas kernels, body(): pl.pallas_call(functools.partial(stem_kernel, strips), out_shape=(jax.Sha...  2.74 us
    ppermute x3, waiting for transfers between devices, shifted(): lax.ppermute(value, axis, [(i, (i + by) % size) for i in range(size)])  2.29 us
    pallas_call x1, Pallas kernels, body(): pl.pallas_call(down_kernel, out_shape=jax.ShapeDtypeStruct((4, 8, 8, 256)...  1.9 us
  transfers between devices with their start and end apart: 10, of which 5 were waited for; matrix products, arithmetic and copies ran while one was open for 0% of the time, Pallas kernels for 17%

profile of v6, /device:TPU:0, one launch (start us, length us, event | category | flops | bytes accessed | tf_op | source)
XLA Modules:
  0.0 38.5 jit_solution(15200636238407757072)
XLA Ops:
  0.6 0.0 copy-start
  0.6 0.0 copy-start.1
  0.7 0.0 copy-start.2
  0.7 0.0 copy-start.3
  0.7 0.0 copy-start.6
  0.7 0.0 copy-start.7
  0.7 1.8 %shard_map.156 = bf16[4,8,8,128]{3,2,1,0:T(8,128)(2,1)} custom-call(bf16[48,128]{1,0:T(8,128)(2,1)} %bitcast.30, s32[1,128]{1,0:T(1,128)} %owner_ref.1, s32[1,128]{1,0:T(1,128)} %slot_ref.1), custom_call_target="tpu_custom_call" | custom-call | flops 2000000000 | bytes 4194304 | tf_op jit(solution)/shard_map/pallas_call | solution.py:562
  2.5 7.3 %all-to-all-start = ((bf16[32,8,128]{2,1,0:T(8,128)(2,1)}), bf16[32,8,128]{2,1,0:T(8,128)(2,1)S(1)}, u32[]{:S(2)}, u32[]{:S(2)}) async-start(bf16[32,8,128]{2,1,0:T(8,128)(2,1)} %bitcast.27), calls=%async_computation | async-start | bytes 131072 | tf_op jit(solution)/shard_map/all_to_all | solution.py:574
  9.8 0.0 copy-done
  9.8 0.0 copy-done.1
  9.8 0.0 copy-done.2
  9.8 0.0 copy-done.3
  9.8 0.1 shard_map.157
  10.0 1.8 %collective-permute-start = (bf16[8,16,128]{2,1,0:T(8,128)(2,1)S(1)}, bf16[8,16,128]{2,1,0:T(8,128)(2,1)S(1)}, u32[]{:S(2)}, u32[]{:S(2)}) collective-permute-start(bf16[8,16,128]{2,1,0:T(8,128)(2,1)S(1)} %get-tuple-element.14), channel_id=1, source_target_pairs={{0,1},{1,2},{2,3},{3,0},{4,5},{5,6},{6,7},{7,4},{8,9},{9,10},{10,1... | collective-permute-start | bytes 98312 | tf_op jit(solution)/shard_map/ppermute | solution.py:532
  11.8 2.1 %collective-permute-start.1 = (bf16[4,16,128]{2,1,0:T(8,128)(2,1)S(1)}, bf16[4,16,128]{2,1,0:T(8,128)(2,1)S(1)}, u32[]{:S(2)}, u32[]{:S(2)}) collective-permute-start(bf16[4,16,128]{2,1,0:T(8,128)(2,1)S(1)} %get-tuple-element.15), channel_id=1, source_target_pairs={{0,3},{1,0},{2,1},{3,2},{4,7},{5,4},{6,5},{7,6},{8,11},{9,8},{10,9... | collective-permute-start | bytes 49160 | tf_op jit(solution)/shard_map/ppermute | solution.py:532
  13.8 0.9 %collective-permute-start.2 = (bf16[2,16,128]{2,1,0:T(8,128)(2,1)S(1)}, bf16[2,16,128]{2,1,0:T(8,128)(2,1)S(1)}, u32[]{:S(2)}, u32[]{:S(2)}) collective-permute-start(bf16[2,16,128]{2,1,0:T(8,128)(2,1)S(1)} %get-tuple-element.16), channel_id=1, source_target_pairs={{0,2},{1,3},{2,0},{3,1},{4,6},{5,7},{6,4},{7,5},{8,10},{9,11},{10,... | collective-permute-start | bytes 24584 | tf_op jit(solution)/shard_map/ppermute | solution.py:532
  16.0 0.1 pad_add_fusion.scalars_ref
  16.1 2.3 %collective-permute-done.2.mid_ref = bf16[2,16,128]{2,1,0:T(8,128)(2,1)S(1)} collective-permute-done((bf16[2,16,128]{2,1,0:T(8,128)(2,1)S(1)}, bf16[2,16,128]{2,1,0:T(8,128)(2,1)S(1)}, u32[]{:S(2)}, u32[]{:S(2)}) %collective-permute-start.2) | collective-permute-done | bytes 8224 | tf_op jit(solution)/shard_map/ppermute | solution.py:532
  18.4 0.0 collective-permute-done.1.above_ref
  18.4 0.0 collective-permute-done.below_ref
  18.4 0.0 all-to-all-done
  18.4 0.0 copy-done.6
  18.4 0.0 copy-done.7
  18.4 0.0 copy-start.5
  18.4 2.7 %shard_map.158 = (bf16[560,128]{1,0:T(8,128)(2,1)S(1)}, f32[2,8,128]{2,1,0:T(8,128)S(1)}, f32[2,16,11,8,128]{4,3,2,1,0:T(8,128)S(1)}) custom-call(s32[128]{0:T(128)S(1)} %pad_add_fusion.scalars_ref, f32[128]{0:T(128)S(1)} %copy-done.6, f32[128]{0:T(128)S(1)} %copy-done.7, bf16[4,64,128]{2,1,0:T(8,128)(2,1)S(1)} %bitcast.24, bf16[2,16,48]{2,1,0:T(8,128)(2,1)S(1)} %bitcast.26, ...), custom_call_target="tpu_custom_call" | custom-call | flops 2000000000 | bytes 4194304 | tf_op jit(solution)/shard_map/pallas_call | solution.py:595
  21.2 0.1 collective-permute-start.3
  21.3 0.0 copy-done.5
  21.3 1.3 %shard_map.159.value_ref = f32[32,16,128]{2,1,0:T(8,128)S(1)} custom-call(s32[128]{0:T(128)S(1)} %pad_add_fusion.scalars_ref, f32[2,8,128]{2,1,0:T(8,128)S(1)} %get-tuple-element.19.norm_ref, f32[2,16,11,8,128]{4,3,2,1,0:T(8,128)S(1)} %get-tuple-element.20.stem, bf16[2,16,16,128]{3,2,1,0:T(8,128)(2,1)S(1)} %bitcast.18, ...), custom_call_target="tpu_custom_call" | custom-call | flops 2000000000 | bytes 4194304 | tf_op jit(solution)/shard_map/pallas_call | solution.py:620
  22.5 0.1 collective-permute-done.3
  22.6 1.8 %collective-permute-start.5 = (bf16[560,128]{1,0:T(8,128)(2,1)S(1)}, bf16[560,128]{1,0:T(8,128)(2,1)S(1)}, u32[]{:S(2)}, u32[]{:S(2)}) collective-permute-start(bf16[560,128]{1,0:T(8,128)(2,1)S(1)} %broadcast_select_fusion.1.after_ref), channel_id=1, source_target_pairs={{0,8},{4,12},{8,0},{12,4},{16,24},{20,28},{24,16},{28,20},{1,9},{5... | collective-permute-start | bytes 430088 | tf_op jit(solution)/shard_map/ppermute | solution.py:527
  24.5 0.1 collective-permute-start.4
  24.6 1.3 %collective-permute-done.4 = bf16[512,128]{1,0:T(8,128)(2,1)S(1)} collective-permute-done((bf16[512,128]{1,0:T(8,128)(2,1)S(1)}, bf16[512,128]{1,0:T(8,128)(2,1)S(1)}, u32[]{:S(2)}, u32[]{:S(2)}) %collective-permute-start.4) | collective-permute-done | bytes 131104 | tf_op jit(solution)/shard_map/ppermute | solution.py:527
  25.9 0.3 collective-permute-start.6
  26.2 1.6 %shard_map.161.after_too_ref.part_ref = bf16[8,9,16,128]{3,2,1,0:T(8,128)(2,1)S(1)} custom-call(bf16[560,128]{1,0:T(8,128)(2,1)S(1)} %broadcast_select_fusion.1.after_ref, bf16[512,128]{1,0:T(8,128)(2,1)S(1)} %broadcast_select_fusion.3.after_too_ref, f32[2,8,128]{2,1,0:T(8,128)S(1)} %get-tuple-element.19.norm_ref, ...), custom_call_target="tpu_custom_call" | custom-call | flops 2000000000 | bytes 4194304 | tf_op jit(solution)/shard_map/pallas_call | solution.py:640
  27.9 0.9 %collective-permute-done.5 = bf16[560,128]{1,0:T(8,128)(2,1)S(1)} collective-permute-done((bf16[560,128]{1,0:T(8,128)(2,1)S(1)}, bf16[560,128]{1,0:T(8,128)(2,1)S(1)}, u32[]{:S(2)}, u32[]{:S(2)}) %collective-permute-start.5) | collective-permute-done | bytes 143392 | tf_op jit(solution)/shard_map/ppermute | solution.py:527
  28.8 0.0 copy-start.4
  28.8 2.1 %collective-permute-start.7 = (bf16[560,128]{1,0:T(8,128)(2,1)S(1)}, bf16[560,128]{1,0:T(8,128)(2,1)S(1)}, u32[]{:S(2)}, u32[]{:S(2)}) collective-permute-start(bf16[560,128]{1,0:T(8,128)(2,1)S(1)} %broadcast_select_fusion.after_ref.first_ref), channel_id=1, source_target_pairs={{0,16},{4,20},{8,24},{12,28},{16,0},{20,4},{24,8},{28,12},{1,17},{... | collective-permute-start | bytes 430088 | tf_op jit(solution)/shard_map/ppermute | solution.py:527
  31.0 1.7 %shard_map.162.rest_ref = bf16[8,9,16,128]{3,2,1,0:T(8,128)(2,1)S(1)} custom-call(bf16[560,128]{1,0:T(8,128)(2,1)S(1)} %broadcast_select_fusion.after_ref.first_ref, bf16[8,9,16,128]{3,2,1,0:T(8,128)(2,1)S(1)} %shard_map.161.after_too_ref.part_ref, f32[2,8,128]{2,1,0:T(8,128)S(1)} %get-tuple-element.19.norm_ref, ...), custom_call_target="tpu_custom_call" | custom-call | flops 2000000000 | bytes 4194304 | tf_op jit(solution)/shard_map/pallas_call | solution.py:640
  32.7 0.0 collective-permute-done.6
  32.7 0.8 %collective-permute-start.8 = (bf16[512,128]{1,0:T(8,128)(2,1)S(1)}, bf16[512,128]{1,0:T(8,128)(2,1)S(1)}, u32[]{:S(2)}, u32[]{:S(2)}) collective-permute-start(bf16[512,128]{1,0:T(8,128)(2,1)S(1)} %broadcast_select_fusion.2.after_ref.second_ref), channel_id=1, source_target_pairs={{0,16},{4,20},{8,24},{12,28},{16,0},{20,4},{24,8},{28,12},{1,17},{... | collective-permute-start | bytes 393224 | tf_op jit(solution)/shard_map/ppermute | solution.py:527
  33.5 0.0 copy-done.4
  33.5 1.9 %shard_map.163 = bf16[4,8,8,256]{3,2,1,0:T(8,128)(2,1)} custom-call(s32[128]{0:T(128)S(1)} %pad_add_fusion.scalars_ref, bf16[8,9,16,128]{3,2,1,0:T(8,128)(2,1)S(1)} %shard_map.161.after_too_ref.part_ref, bf16[8,9,16,128]{3,2,1,0:T(8,128)(2,1)S(1)} %shard_map.162.rest_ref, bf16[3,3,3,128,256]{4,3,2,1,0:T(8,128)(2,1)S(1)} %copy-done.4, ...), custom_call_target="tpu_custom_call" | custom-call | flops 2000000000 | bytes 4194304 | tf_op jit(solution)/shard_map/pallas_call | solution.py:659
  35.4 0.0 collective-permute-done.7.first_in_ref
  35.4 2.4 %collective-permute-done.8.second_in_ref = bf16[512,128]{1,0:T(8,128)(2,1)S(1)} collective-permute-done((bf16[512,128]{1,0:T(8,128)(2,1)S(1)}, bf16[512,128]{1,0:T(8,128)(2,1)S(1)}, u32[]{:S(2)}, u32[]{:S(2)}) %collective-permute-start.8) | collective-permute-done | bytes 131104 | tf_op jit(solution)/shard_map/ppermute | solution.py:527
  37.7 0.8 %shard_map.164 = (bf16[2,16,48]{2,1,0:T(8,128)(2,1)}, bf16[2,16,16,128]{3,2,1,0:T(8,128)(2,1)}, bf16[2,16,16,128]{3,2,1,0:T(8,128)(2,1)}) custom-call(bf16[560,128]{1,0:T(8,128)(2,1)S(1)} %broadcast_select_fusion.after_ref.first_ref, bf16[560,128]{1,0:T(8,128)(2,1)S(1)} %collective-permute-done.7.first_in_ref, ...), custom_call_target="tpu_custom_call" | custom-call | tf_op jit(solution)/shard_map/pallas_call | solution.py:673
  (8 shorter events, 0.1 us)
Async XLA Ops:
  0.6 9.1 %copy-start = (bf16[1,2,16,16,128]{4,3,2,1,0:T(8,128)(2,1)S(1)}, bf16[1,2,16,16,128]{4,3,2,1,0:T(8,128)(2,1)}, u32[]{:S(2)}) copy-start(bf16[1,2,16,16,128]{4,3,2,1,0:T(8,128)(2,1)} %param.19) | copy-start | bytes 393220
  0.6 9.1 %copy-start.1 = (bf16[1,2,16,16,128]{4,3,2,1,0:T(8,128)(2,1)S(1)}, bf16[1,2,16,16,128]{4,3,2,1,0:T(8,128)(2,1)}, u32[]{:S(2)}) copy-start(bf16[1,2,16,16,128]{4,3,2,1,0:T(8,128)(2,1)} %param.20) | copy-start | bytes 393220
  0.7 9.1 %copy-start.2 = (bf16[3,3,3,3,128]{4,3,2,1,0:T(4,128)(2,1)S(1)}, bf16[3,3,3,3,128]{4,3,2,1,0:T(4,128)(2,1)}, u32[]{:S(2)}) copy-start(bf16[3,3,3,3,128]{4,3,2,1,0:T(4,128)(2,1)} %sw_ref.1) | copy-start | bytes 62212
  0.7 9.1 %copy-start.3 = (bf16[1,2,16,48]{3,2,1,0:T(8,128)(2,1)S(1)}, bf16[1,2,16,48]{3,2,1,0:T(8,128)(2,1)}, u32[]{:S(2)}) copy-start(bf16[1,2,16,48]{3,2,1,0:T(8,128)(2,1)} %param.18) | copy-start | bytes 9220
  0.7 17.7 %copy-start.6 = (f32[128]{0:T(128)S(1)}, f32[128]{0:T(128)}, u32[]{:S(2)}) copy-start(f32[128]{0:T(128)} %gain_ref.1) | copy-start | bytes 1540
  0.7 17.7 %copy-start.7 = (f32[128]{0:T(128)S(1)}, f32[128]{0:T(128)}, u32[]{:S(2)}) copy-start(f32[128]{0:T(128)} %bias_ref.1) | copy-start | bytes 1540
  2.5 15.9 %all-to-all-start = ((bf16[32,8,128]{2,1,0:T(8,128)(2,1)}), bf16[32,8,128]{2,1,0:T(8,128)(2,1)S(1)}, u32[]{:S(2)}, u32[]{:S(2)}) async-start(bf16[32,8,128]{2,1,0:T(8,128)(2,1)} %bitcast.27), calls=%async_computation | async-start | bytes 131072 | tf_op jit(solution)/shard_map/all_to_all | solution.py:574
  10.0 8.4 %collective-permute-start = (bf16[8,16,128]{2,1,0:T(8,128)(2,1)S(1)}, bf16[8,16,128]{2,1,0:T(8,128)(2,1)S(1)}, u32[]{:S(2)}, u32[]{:S(2)}) collective-permute-start(bf16[8,16,128]{2,1,0:T(8,128)(2,1)S(1)} %get-tuple-element.14), channel_id=1, source_target_pairs={{0,1},{1,2},{2,3},{3,0},{4,5},{5,6},{6,7},{7,4},{8,9},{9,10},{10,1... | collective-permute-start | bytes 98312 | tf_op jit(solution)/shard_map/ppermute | solution.py:532
  11.8 6.6 %collective-permute-start.1 = (bf16[4,16,128]{2,1,0:T(8,128)(2,1)S(1)}, bf16[4,16,128]{2,1,0:T(8,128)(2,1)S(1)}, u32[]{:S(2)}, u32[]{:S(2)}) collective-permute-start(bf16[4,16,128]{2,1,0:T(8,128)(2,1)S(1)} %get-tuple-element.15), channel_id=1, source_target_pairs={{0,3},{1,0},{2,1},{3,2},{4,7},{5,4},{6,5},{7,6},{8,11},{9,8},{10,9... | collective-permute-start | bytes 49160 | tf_op jit(solution)/shard_map/ppermute | solution.py:532
  13.8 4.5 %collective-permute-start.2 = (bf16[2,16,128]{2,1,0:T(8,128)(2,1)S(1)}, bf16[2,16,128]{2,1,0:T(8,128)(2,1)S(1)}, u32[]{:S(2)}, u32[]{:S(2)}) collective-permute-start(bf16[2,16,128]{2,1,0:T(8,128)(2,1)S(1)} %get-tuple-element.16), channel_id=1, source_target_pairs={{0,2},{1,3},{2,0},{3,1},{4,6},{5,7},{6,4},{7,5},{8,10},{9,11},{10,... | collective-permute-start | bytes 24584 | tf_op jit(solution)/shard_map/ppermute | solution.py:532
  18.4 2.8 %copy-start.5 = (bf16[3,3,3,128,128]{4,3,2,1,0:T(8,128)(2,1)S(1)}, bf16[3,3,3,128,128]{4,3,2,1,0:T(8,128)(2,1)}, u32[]{:S(2)}) copy-start(bf16[3,3,3,128,128]{4,3,2,1,0:T(8,128)(2,1)} %conv_ref.5) | copy-start | bytes 2654212
  21.2 1.4 %collective-permute-start.3 = (bf16[560,128]{1,0:T(8,128)(2,1)S(1)}, bf16[560,128]{1,0:T(8,128)(2,1)S(1)}, u32[]{:S(2)}, u32[]{:S(2)}) collective-permute-start(bf16[560,128]{1,0:T(8,128)(2,1)S(1)} %get-tuple-element.18), channel_id=1, source_target_pairs={{0,4},{4,0},{8,12},{12,8},{16,20},{20,16},{24,28},{28,24},{1,5},{5... | collective-permute-start | bytes 430088 | tf_op jit(solution)/shard_map/ppermute | solution.py:527
  22.6 6.2 %collective-permute-start.5 = (bf16[560,128]{1,0:T(8,128)(2,1)S(1)}, bf16[560,128]{1,0:T(8,128)(2,1)S(1)}, u32[]{:S(2)}, u32[]{:S(2)}) collective-permute-start(bf16[560,128]{1,0:T(8,128)(2,1)S(1)} %broadcast_select_fusion.1.after_ref), channel_id=1, source_target_pairs={{0,8},{4,12},{8,0},{12,4},{16,24},{20,28},{24,16},{28,20},{1,9},{5... | collective-permute-start | bytes 430088 | tf_op jit(solution)/shard_map/ppermute | solution.py:527
  24.5 1.4 %collective-permute-start.4 = (bf16[512,128]{1,0:T(8,128)(2,1)S(1)}, bf16[512,128]{1,0:T(8,128)(2,1)S(1)}, u32[]{:S(2)}, u32[]{:S(2)}) collective-permute-start(bf16[512,128]{1,0:T(8,128)(2,1)S(1)} %shard_map.160), channel_id=1, source_target_pairs={{0,4},{4,0},{8,12},{12,8},{16,20},{20,16},{24,28},{28,24},{1,5},{5... | collective-permute-start | bytes 393224 | tf_op jit(solution)/shard_map/ppermute | solution.py:527
  25.9 6.8 %collective-permute-start.6 = (bf16[512,128]{1,0:T(8,128)(2,1)S(1)}, bf16[512,128]{1,0:T(8,128)(2,1)S(1)}, u32[]{:S(2)}, u32[]{:S(2)}) collective-permute-start(bf16[512,128]{1,0:T(8,128)(2,1)S(1)} %broadcast_select_fusion.3.after_too_ref), channel_id=1, source_target_pairs={{0,8},{4,12},{8,0},{12,4},{16,24},{20,28},{24,16},{28,20},{1,9},{5... | collective-permute-start | bytes 393224 | tf_op jit(solution)/shard_map/ppermute | solution.py:527
  28.8 4.6 %copy-start.4 = (bf16[3,3,3,128,256]{4,3,2,1,0:T(8,128)(2,1)S(1)}, bf16[3,3,3,128,256]{4,3,2,1,0:T(8,128)(2,1)}, u32[]{:S(2)}) copy-start(bf16[3,3,3,128,256]{4,3,2,1,0:T(8,128)(2,1)} %down_ref.1) | copy-start | bytes 5308420
  28.8 6.5 %collective-permute-start.7 = (bf16[560,128]{1,0:T(8,128)(2,1)S(1)}, bf16[560,128]{1,0:T(8,128)(2,1)S(1)}, u32[]{:S(2)}, u32[]{:S(2)}) collective-permute-start(bf16[560,128]{1,0:T(8,128)(2,1)S(1)} %broadcast_select_fusion.after_ref.first_ref), channel_id=1, source_target_pairs={{0,16},{4,20},{8,24},{12,28},{16,0},{20,4},{24,8},{28,12},{1,17},{... | collective-permute-start | bytes 430088 | tf_op jit(solution)/shard_map/ppermute | solution.py:527
  32.7 5.0 %collective-permute-start.8 = (bf16[512,128]{1,0:T(8,128)(2,1)S(1)}, bf16[512,128]{1,0:T(8,128)(2,1)S(1)}, u32[]{:S(2)}, u32[]{:S(2)}) collective-permute-start(bf16[512,128]{1,0:T(8,128)(2,1)S(1)} %broadcast_select_fusion.2.after_ref.second_ref), channel_id=1, source_target_pairs={{0,16},{4,20},{8,24},{12,28},{16,0},{20,4},{24,8},{28,12},{1,17},{... | collective-permute-start | bytes 393224 | tf_op jit(solution)/shard_map/ppermute | solution.py:527

commit v7 on v6

--- a/solution.py
+++ b/solution.py
@@ -60,7 +60,7 @@
             out_ref[strip] = out.reshape(out_ref.shape[1:])
 
 
-def pack_kernel(pix_ref, sw_ref, act_ref, res_ref, down_ref, up_ref, mid_ref, weight_ref, sw, sems):
+def pack_kernel(pix_ref, sw_ref, act_ref, res_ref, down_ref, up_ref, near_ref, mid_ref, weight_ref, sw, sems):
     copies = []
     for f in range(2):
         copies.append((act_ref.at[f, 14:16], down_ref.at[2 * f : 2 * f + 2]))
@@ -72,7 +72,7 @@
     pix = pix_ref[...].reshape(32, 48).astype(F32)
     pix = jnp.concatenate([pix, jnp.zeros((32, 80), F32)], axis=1)
     pix = pix.astype(BF16).reshape(2, 16, 128)
-    down_ref[6:8] = pix
+    near_ref[...] = pix
     up_ref[2:4] = pix
     mid_ref[...] = pix
     sw[...] = jnp.zeros(sw.shape, F32)
@@ -98,7 +98,7 @@
 def gather_pixels(strips, j, pc, pix_ref, below_ref, above_ref, mid_ref):
     pc[j] = jnp.zeros((32, 128), F32)
     pc[j, :, 0:48] = pix_ref[...].reshape(32, 48).astype(F32)
-    pc[lax.rem(j + strips - 1, strips)] = below_ref[6:8].reshape(32, 128).astype(F32)
+    pc[lax.rem(j + strips - 1, strips)] = below_ref[...].reshape(32, 128).astype(F32)
     pc[lax.rem(j + 1, strips)] = above_ref[2:4].reshape(32, 128).astype(F32)
     pc[lax.rem(j + 2, strips)] = mid_ref[...].reshape(32, 128).astype(F32)
 
@@ -199,7 +199,7 @@
     rows_all = strips * 16
     gather_pixels(strips, j, pc, pix_ref, below_ref, above_ref, mid_ref)
     zs[:, 0:4] = jnp.zeros((3, 4, 8, 128), F32)
-    zs[:, 4 + rows_all :] = jnp.zeros((3, 4, 8, 128), F32)
+    zs[:, 4 + rows_all :] = jnp.zeros((3, 12, 8, 128), F32)
     sub = iota((128, 128), 0)
     crow, cframe = iota((128, 32), 1) % 16, iota((128, 32), 1) // 16
     csub = iota((128, 32), 0)
@@ -226,18 +226,18 @@
     for s in range(strips):
         for a in range(3):
             zs[a, 4 + s * 16 : 4 + (s + 1) * 16] = placed[s][a]
-    pixels, slots = received(recv_ref[j])
-    goal = (slots >> 4) + 2 - valid
-    place = jnp.where((goal >= 0) & (goal < 2), goal * 16 + (slots & 15), -1)
-    hit = jnp.where(iota((4, 8, 128), 0) * 8 + iota((4, 8, 128), 1) == place[None], 1.0, 0.0)
-    cgoal = iota((32, 32), 1) // 16 - valid
-    cplace = jnp.where((cgoal >= 0) & (cgoal < 2), cgoal * 16 + iota((32, 32), 1) % 16, -1)
-    chit = jnp.where(iota((32, 32), 0) == cplace, 1.0, 0.0)
-    source = jnp.concatenate([pixels, pc[j]], axis=0).astype(BF16)
-    fresh = dot(jnp.concatenate([hit.reshape(32, 128), chit], axis=1).astype(BF16), source)
     target = whole(scalars_ref, 1).astype(F32)
     pay_ref[0:16] = jnp.full((16, 128), target, F32).astype(BF16)
-    pay_ref[16:48] = fresh.astype(BF16)
+    last = valid - 1
+    line_rows = zs.reshape(3 * (rows_all + 16) * 8, 128)
+    lines = []
+    for a in range(3):
+        at = (a * (rows_all + 16) + 3 + j * 16) * 8 + (last & 1) * 4 + (last >> 1)
+        lines.append(line_rows[pl.ds(at, 24, stride=8)])
+    none = jnp.zeros((8, 128), F32)
+    left = jnp.where(iota((24, 128), 1) < 64, lines[0], pltpu.roll(lines[1], 64, 1))
+    pay_ref[16:48] = jnp.concatenate([left, none], axis=0).astype(BF16)
+    pay_ref[48:80] = jnp.concatenate([lines[2], none], axis=0).astype(BF16)
     high = rows_all + 4
     for b in range(3):
         for a in range(3):
@@ -268,15 +268,23 @@
     norm_ref[0] = scale
     norm_ref[1] = shift
     stem_rows = stem.reshape(2 * 16 * 11 * 8, 128)
-    for i in range(2):
-        t = valid - 2 + i
-        scale_i, shift_i = frame_row(scale, t), frame_row(shift, t)
-        for y in range(16):
-            block = stem_rows[pl.ds(row_at(t, y), 16, stride=88)]
-            block = silu(block * scale_i + shift_i)
-            block = jnp.where(valid + i < 2, old_ref[1, y].astype(F32), block)
-            to = 48 + i * 256 + y * 16
-            pay_ref[to : to + 16] = block.astype(BF16)
+    t = valid - 2
+    scale_t, shift_t = frame_row(scale, t), frame_row(shift, t)
+    for y in range(16):
+        block = silu(stem_rows[pl.ds(row_at(t, y), 16, stride=88)] * scale_t + shift_t)
+        block = jnp.where(valid < 2, old_ref[1, y].astype(F32), block)
+        pay_ref[80 + y * 16 : 96 + y * 16] = block.astype(BF16)
+    pieces = []
+    for row in (frame_row(scale, last), frame_row(shift, last)):
+        for _ in range(3):
+            piece = row.astype(BF16).astype(F32)
+            pieces.append(piece)
+            row = row - piece
+    row16 = iota((16, 128), 0)
+    norms = jnp.zeros((16, 128), F32)
+    for n, piece in enumerate(pieces):
+        norms = jnp.where(row16 == n, piece, norms)
+    pay_ref[336:352] = norms.astype(BF16)
 
 
 def last_kernel(
@@ -380,10 +388,12 @@
     above_ref,
     conv_ref,
     out_ref,
+    rows_ref,
     cache,
     act3,
 ):
-    del after_ref, after_too_ref
+    del after_too_ref
+    rows_ref[...] = after_ref[0:16] if w0 == 0 else jnp.zeros((16, 128), BF16)
     j = lax.axis_index("strip")
     widen_cache(strips, j, cache, old_ref, below_ref, above_ref)
     low8 = iota((8, 128), 0) < 4
@@ -485,7 +495,7 @@
             res3[at, :, :, 256:384] = even
             return carry
 
-        lax.fori_loop(0, 8, delay, 0, unroll=2)
+        lax.fori_loop(0, 8, delay, 0, unroll=8)
     total = jnp.zeros((256, 256), F32)
     for b in range(3):
         for e in range(3):
@@ -507,19 +517,49 @@
 
 
 def finish_kernel(
-    bit, first_ref, first_in_ref, second_ref, second_in_ref, new_pix_ref, new_act_ref, new_res_ref
+    bit,
+    after_ref,
+    first_ref,
+    first_in_ref,
+    weight_ref,
+    new_pix_ref,
+    new_act_ref,
+    rows,
+    patch,
+    frame,
 ):
+    del after_ref
     target = first_ref[0:16].astype(jnp.int32)
     mine = (target >> bit) & 1 == (lax.axis_index("stream") >> bit) & 1
     mine = jnp.where(mine, 1.0, 0.0)[0:1] > 0.5
 
-    def chosen(own_ref, in_ref, start, stop):
-        own, other = own_ref[start:stop].astype(F32), in_ref[start:stop].astype(F32)
-        return jnp.where(mine, own, other).astype(BF16)
-
-    new_pix_ref[...] = chosen(first_ref, first_in_ref, 16, 48)[:, 0:48].reshape(2, 16, 48)
-    new_act_ref[...] = chosen(first_ref, first_in_ref, 48, 560).reshape(2, 16, 16, 128)
-    new_res_ref[...] = chosen(second_ref, second_in_ref, 0, 512).reshape(2, 16, 16, 128)
+    def chosen(start, stop):
+        own, other = first_ref[start:stop].astype(F32), first_in_ref[start:stop].astype(F32)
+        return jnp.where(mine, own, other)
+
+    new_act_ref[0] = chosen(80, 336).astype(BF16).reshape(16, 16, 128)
+    left = chosen(16, 48)
+    rows[0] = left
+    rows[1] = pltpu.roll(left, 64, 1)
+    rows[2] = chosen(48, 80)
+    for i in range(2):
+        new_pix_ref[i] = rows[1 + i, 1:17, 0:48].astype(BF16)
+    norms = chosen(336, 352)
+    scale = norms[0:1] + norms[1:2] + norms[2:3]
+    shift = norms[3:4] + norms[4:5] + norms[5:6]
+    for b in range(3):
+        for a in range(3):
+            q = (b * 3 + a) * 48
+            patch[:, q : q + 48] = rows[a, b : b + 16, 0:48]
+    spread = dot(patch[...].astype(BF16), spread_matrix()).astype(BF16)
+    weight = weight_ref[...]
+    for chunk in range(8):
+        out = dot(spread[:, chunk * 128 : chunk * 128 + 128], weight).astype(BF16).astype(F32)
+        for n in range(2):
+            at = (2 * chunk + n) * 16
+            frame[at : at + 16] = silu(out[:, n * 128 : n * 128 + 128] * scale + shift)
+    for y in range(16):
+        new_act_ref[1, y] = frame[pl.ds(y, 16, stride=16)].astype(BF16)
 
 
 def partner(value, axis, stride):
@@ -573,20 +613,22 @@
     lines = lines.reshape(strips * streams, half_per, 128)
     recv = lax.all_to_all(lines, ("strip", "stream"), 0, 0, tiled=True)
     recv = recv.reshape(strips, fill // 2, 128)
-    below, above, mid, weight = pl.pallas_call(
+    below, above, near, mid, weight = pl.pallas_call(
         pack_kernel,
         out_shape=(
-            jax.ShapeDtypeStruct((8, 16, 128), BF16),
+            jax.ShapeDtypeStruct((6, 16, 128), BF16),
             jax.ShapeDtypeStruct((4, 16, 128), BF16),
+            jax.ShapeDtypeStruct((2, 16, 128), BF16),
             jax.ShapeDtypeStruct((2, 16, 128), BF16),
             jax.ShapeDtypeStruct((128, 256), BF16),
         ),
         in_specs=[VM] * 2 + [ANY] * 2,
-        out_specs=(VM,) * 4,
+        out_specs=(VM,) * 5,
         scratch_shapes=[pltpu.VMEM((128, 256), F32), pltpu.SemaphoreType.DMA((6,))],
         compiler_params=pltpu.CompilerParams(vmem_limit_bytes=4 * mega),
     )(pix, stem_weight, acts, ress)
     below = shifted(below, "strip", 1)
+    near = shifted(near, "strip", 1)
     above = shifted(above, "strip", -1)
     mid = shifted(mid, "strip", 2)
     scalars = jnp.concatenate([valid_frames, next_owner, jnp.zeros((126,), jnp.int32)])
@@ -595,7 +637,7 @@
     first, norm, stem = pl.pallas_call(
         functools.partial(stem_kernel, strips),
         out_shape=(
-            jax.ShapeDtypeStruct((560, 128), BF16),
+            jax.ShapeDtypeStruct((352, 128), BF16),
             jax.ShapeDtypeStruct((2, 8, 128), F32),
             window,
         ),
@@ -603,18 +645,21 @@
         out_specs=(VM,) * 3,
         scratch_shapes=[
             pltpu.VMEM((strips, 32, 128), F32),
-            pltpu.VMEM((3, rows_all + 8, 8, 128), F32),
+            pltpu.VMEM((3, rows_all + 16, 8, 128), F32),
             pltpu.VMEM((rows_all + 8, 8, 432), F32),
             pltpu.VMEM((rows_all + 4, 8, 1024), F32),
         ],
         compiler_params=pltpu.CompilerParams(vmem_limit_bytes=24 * mega),
         cost_estimate=cost,
-    )(scalars, norm_gain, norm_bias, recv, pix, acts, below, above, mid, weight)
+    )(scalars, norm_gain, norm_bias, recv, pix, acts, near, above, mid, weight)
     keeps = []
+
+    def kept(rows, bit):
+        return (rows[0:1].astype(jnp.int32) >> bit) & 1 == (stream_pos >> bit) & 1
 
     def passed(value, bit):
         if bit == len(keeps):
-            keeps.append((value[0:1].astype(jnp.int32) >> bit) & 1 == (stream_pos >> bit) & 1)
+            keeps.append(kept(value, bit))
         return jnp.where(keeps[bit], value, partner(value, "stream", 1 << bit))
 
     second = pl.pallas_call(
@@ -639,9 +684,12 @@
     def convolved(w0, after, after_too):
         return pl.pallas_call(
             functools.partial(conv_kernel, strips, w0),
-            out_shape=jax.ShapeDtypeStruct((8, 9, 16, 128), BF16),
-            in_specs=[ANY] * 2 + [VM] * 6,
-            out_specs=VM,
+            out_shape=(
+                jax.ShapeDtypeStruct((8, 9, 16, 128), BF16),
+                jax.ShapeDtypeStruct((16, 128), BF16),
+            ),
+            in_specs=[VM if w0 == 0 else ANY, ANY] + [VM] * 6,
+            out_specs=(VM,) * 2,
             scratch_shapes=[
                 pltpu.VMEM((2, 416, 128), F32),
                 pltpu.VMEM((10, 11, 16, 384), BF16),
@@ -650,10 +698,12 @@
             cost_estimate=cost,
         )(after, after_too, norm, stem, acts, below, above, conv_weight)
 
-    part = convolved(0, first, second)
+    part, rows = convolved(0, first, second)
     for bit in range(1, sections - 1):
+        if bit == 1:
+            keeps.append(kept(rows, bit))
         first = passed(first, bit)
-    rest = convolved(8, first, part)
+    rest, _ = convolved(8, first, part)
     for bit in range(1, sections - 1):
         second = passed(second, bit)
     latent = pl.pallas_call(
@@ -670,23 +720,26 @@
         cost_estimate=cost,
     )(scalars, part, rest, down_weight, ress, below, second)
     bit = sections - 1
-    new_pix, new_act, new_res = pl.pallas_call(
+    if bit == len(keeps):
+        keeps.append(kept(first, bit))
+    new_pix, new_act = pl.pallas_call(
         functools.partial(finish_kernel, bit),
         out_shape=(
             jax.ShapeDtypeStruct(pix.shape, BF16),
             jax.ShapeDtypeStruct(acts.shape, BF16),
-            jax.ShapeDtypeStruct(ress.shape, BF16),
         ),
-        in_specs=[VM] * 4,
-        out_specs=(VM,) * 3,
+        in_specs=[ANY] + [VM] * 3,
+        out_specs=(VM,) * 2,
+        scratch_shapes=[
+            pltpu.VMEM((3, 32, 128), F32),
+            pltpu.VMEM((16, 432), F32),
+            pltpu.VMEM((256, 128), F32),
+        ],
         compiler_params=pltpu.CompilerParams(vmem_limit_bytes=8 * mega),
-    )(
-        first,
-        partner(first, "stream", 1 << bit),
-        second,
-        partner(second, "stream", 1 << bit),
-    )
-    return (latent[None], new_pix[None], new_act[None], new_res[None])
+        cost_estimate=cost,
+    )(second, first, partner(first, "stream", 1 << bit), weight)
+    second = passed(second, bit)
+    return (latent[None], new_pix[None], new_act[None], second.reshape(1, 2, 16, 16, 128))
 
 
 def solution(mesh):

time: 38.7 us -> 37.7 us (0.974)
  waiting for transfers between devices: 6.92 us -> 3.43 us
  starting transfers between devices: 17.3 us -> 18.7 us
  other arithmetic: 0.18 us -> 0.85 us
  Pallas kernels: 11.9 us -> 12.4 us
    ppermute x6, waiting for transfers between devices: 4.62 us -> 2.7 us  [partner(): return lax.ppermute(value, axis, pairs)]
    ppermute x3 -> x4, waiting for transfers between devices: 2.29 us -> 0.73 us  [shifted(): lax.ppermute(value, axis, [(i, (i + by) % size) for i in range(size)])]
    ppermute x3 -> x4, starting transfers between devices: 4.75 us -> 6.26 us  [shifted(): lax.ppermute(value, axis, [(i, (i + by) % size) for i in range(size)])]
    select_n x4 -> x5, other arithmetic: 0.08 us -> 0.73 us  [passed(): return jnp.where(keeps[bit], value, partner(value, 'stream', 1 << bit))]
    pallas_call x1, Pallas kernels: 0.76 us -> 1.22 us  [body(): pl.pallas_call(functools.partial(finish_kernel, bit), out_shape=(jax.Shap...]
  transfers between devices with their start and end apart: 10 -> 11, of which waited for: 5 -> 5; matrix products, arithmetic and copies ran while one was open for 0% -> 0% of each run, Pallas kernels for 17% -> 28%
where the time goes in v7:
time: 37.7 us; the launch traced here: 37.6 us
  starting transfers between devices  18.7 us (50%)
  Pallas kernels  12.4 us (33%)
  waiting for transfers between devices  3.43 us (9%)
  between operations  2.14 us (6%)
  other arithmetic  0.85 us (2%)
    all_to_all x1, starting transfers between devices, body(): recv = lax.all_to_all(lines, ('strip', 'stream'), 0, 0, tiled=True)  7.3 us
    ppermute x4, starting transfers between devices, shifted(): lax.ppermute(value, axis, [(i, (i + by) % size) for i in range(size)])  6.26 us
    ppermute x6, starting transfers between devices, partner(): return lax.ppermute(value, axis, pairs)  5.17 us
    pallas_call x2, Pallas kernels, convolved(): pl.pallas_call(functools.partial(conv_kernel, strips, w0), out_shape=(jax...  3.67 us
    pallas_call x1, Pallas kernels, body(): pl.pallas_call(functools.partial(stem_kernel, strips), out_shape=(jax.Sha...  2.77 us
    ppermute x6, waiting for transfers between devices, partner(): return lax.ppermute(value, axis, pairs)  2.7 us
    pallas_call x1, Pallas kernels, body(): pl.pallas_call(functools.partial(sort_kernel, streams), out_shape=jax.Sha...  1.77 us
    pallas_call x1, Pallas kernels, body(): pl.pallas_call(down_kernel, out_shape=jax.ShapeDtypeStruct((4, 8, 8, 256)...  1.63 us
  transfers between devices with their start and end apart: 11, of which 5 were waited for; matrix products, arithmetic and copies ran while one was open for 0% of the time, Pallas kernels for 28%

profile of v7, /device:TPU:0, one launch (start us, length us, event | category | flops | bytes accessed | tf_op | source)
XLA Modules:
  0.0 37.6 jit_solution(524001292147784321)
XLA Ops:
  0.6 0.0 copy-start
  0.6 0.0 copy-start.1
  0.7 0.0 copy-start.2
  0.7 0.0 copy-start.3
  0.7 0.0 copy-start.6
  0.7 0.0 copy-start.7
  0.7 1.8 %shard_map.156 = bf16[4,8,8,128]{3,2,1,0:T(8,128)(2,1)} custom-call(bf16[48,128]{1,0:T(8,128)(2,1)} %bitcast.31, s32[1,128]{1,0:T(1,128)} %owner_ref.1, s32[1,128]{1,0:T(1,128)} %slot_ref.1), custom_call_target="tpu_custom_call" | custom-call | flops 2000000000 | bytes 4194304 | tf_op jit(solution)/shard_map/pallas_call | solution.py:602
  2.5 7.3 %all-to-all-start = ((bf16[32,8,128]{2,1,0:T(8,128)(2,1)}), bf16[32,8,128]{2,1,0:T(8,128)(2,1)S(1)}, u32[]{:S(2)}, u32[]{:S(2)}) async-start(bf16[32,8,128]{2,1,0:T(8,128)(2,1)} %bitcast.30), calls=%async_computation | async-start | bytes 131072 | tf_op jit(solution)/shard_map/all_to_all | solution.py:614
  9.8 0.0 copy-done
  9.8 0.0 copy-done.1
  9.8 0.0 copy-done.2
  9.8 0.0 copy-done.3
  9.8 0.1 shard_map.157
  10.0 1.8 %collective-permute-start = (bf16[2,16,128]{2,1,0:T(8,128)(2,1)S(1)}, bf16[2,16,128]{2,1,0:T(8,128)(2,1)S(1)}, u32[]{:S(2)}, u32[]{:S(2)}) collective-permute-start(bf16[2,16,128]{2,1,0:T(8,128)(2,1)S(1)} %get-tuple-element.17), channel_id=1, source_target_pairs={{0,1},{1,2},{2,3},{3,0},{4,5},{5,6},{6,7},{7,4},{8,9},{9,10},{10,1... | collective-permute-start | bytes 24584 | tf_op jit(solution)/shard_map/ppermute | solution.py:572
  11.8 2.4 %collective-permute-start.2 = (bf16[2,16,128]{2,1,0:T(8,128)(2,1)S(1)}, bf16[2,16,128]{2,1,0:T(8,128)(2,1)S(1)}, u32[]{:S(2)}, u32[]{:S(2)}) collective-permute-start(bf16[2,16,128]{2,1,0:T(8,128)(2,1)S(1)} %get-tuple-element.19), channel_id=1, source_target_pairs={{0,2},{1,3},{2,0},{3,1},{4,6},{5,7},{6,4},{7,5},{8,10},{9,11},{10,... | collective-permute-start | bytes 24584 | tf_op jit(solution)/shard_map/ppermute | solution.py:572
  14.2 1.4 %collective-permute-start.1 = (bf16[4,16,128]{2,1,0:T(8,128)(2,1)S(1)}, bf16[4,16,128]{2,1,0:T(8,128)(2,1)S(1)}, u32[]{:S(2)}, u32[]{:S(2)}) collective-permute-start(bf16[4,16,128]{2,1,0:T(8,128)(2,1)S(1)} %get-tuple-element.18), channel_id=1, source_target_pairs={{0,3},{1,0},{2,1},{3,2},{4,7},{5,4},{6,5},{7,6},{8,11},{9,8},{10,9... | collective-permute-start | bytes 49160 | tf_op jit(solution)/shard_map/ppermute | solution.py:572
  15.6 0.6 %collective-permute-start.4 = (bf16[6,16,128]{2,1,0:T(8,128)(2,1)S(1)}, bf16[6,16,128]{2,1,0:T(8,128)(2,1)S(1)}, u32[]{:S(2)}, u32[]{:S(2)}) collective-permute-start(bf16[6,16,128]{2,1,0:T(8,128)(2,1)S(1)} %get-tuple-element.24), channel_id=1, source_target_pairs={{0,1},{1,2},{2,3},{3,0},{4,5},{5,6},{6,7},{7,4},{8,9},{9,10},{10,1... | collective-permute-start | bytes 73736 | tf_op jit(solution)/shard_map/ppermute | solution.py:572
  17.5 0.1 pad_add_fusion.scalars_ref
  17.6 0.0 collective-permute-done.below_ref
  17.6 0.0 collective-permute-done.2.mid_ref
  17.6 0.3 collective-permute-done.1.above_ref
  17.9 0.0 all-to-all-done
  17.9 0.0 copy-done.6
  17.9 0.0 copy-done.7
  17.9 0.0 copy-start.5
  18.0 2.8 %shard_map.158 = (bf16[352,128]{1,0:T(8,128)(2,1)S(1)}, f32[2,8,128]{2,1,0:T(8,128)S(1)}, f32[2,16,11,8,128]{4,3,2,1,0:T(8,128)S(1)}) custom-call(s32[128]{0:T(128)S(1)} %pad_add_fusion.scalars_ref, f32[128]{0:T(128)S(1)} %copy-done.6, f32[128]{0:T(128)S(1)} %copy-done.7, bf16[4,64,128]{2,1,0:T(8,128)(2,1)S(1)} %bitcast.26, bf16[2,16,48]{2,1,0:T(8,128)(2,1)S(1)} %bitcast.28, ...), custom_call_target="tpu_custom_call" | custom-call | flops 2000000000 | bytes 4194304 | tf_op jit(solution)/shard_map/pallas_call | solution.py:637
  20.7 0.1 collective-permute-start.3
  20.8 0.4 %collective-permute-done.4.below_ref = bf16[6,16,128]{2,1,0:T(8,128)(2,1)S(1)} collective-permute-done((bf16[6,16,128]{2,1,0:T(8,128)(2,1)S(1)}, bf16[6,16,128]{2,1,0:T(8,128)(2,1)S(1)}, u32[]{:S(2)}, u32[]{:S(2)}) %collective-permute-start.4) | collective-permute-done | bytes 24608 | tf_op jit(solution)/shard_map/ppermute | solution.py:572
  21.2 0.0 copy-done.5
  21.2 1.2 %shard_map.159.value_ref = f32[32,16,128]{2,1,0:T(8,128)S(1)} custom-call(s32[128]{0:T(128)S(1)} %pad_add_fusion.scalars_ref, f32[2,8,128]{2,1,0:T(8,128)S(1)} %get-tuple-element.22.norm_ref, f32[2,16,11,8,128]{4,3,2,1,0:T(8,128)S(1)} %get-tuple-element.23.stem, bf16[2,16,16,128]{3,2,1,0:T(8,128)(2,1)S(1)} %bitcast.20, ...), custom_call_target="tpu_custom_call" | custom-call | flops 2000000000 | bytes 4194304 | tf_op jit(solution)/shard_map/pallas_call | solution.py:665
  22.4 0.0 collective-permute-done.3
  22.5 0.3 collective-permute-start.5
  22.7 1.4 %collective-permute-start.6 = (bf16[352,128]{1,0:T(8,128)(2,1)S(1)}, bf16[352,128]{1,0:T(8,128)(2,1)S(1)}, u32[]{:S(2)}, u32[]{:S(2)}) collective-permute-start(bf16[352,128]{1,0:T(8,128)(2,1)S(1)} %broadcast_select_fusion.4.after_ref), channel_id=1, source_target_pairs={{0,8},{4,12},{8,0},{12,4},{16,24},{20,28},{24,16},{28,20},{1,9},{5... | collective-permute-start | bytes 270344 | tf_op jit(solution)/shard_map/ppermute | solution.py:567
  24.1 0.0 collective-permute-done.5
  24.1 1.3 %collective-permute-start.7 = (bf16[512,128]{1,0:T(8,128)(2,1)S(1)}, bf16[512,128]{1,0:T(8,128)(2,1)S(1)}, u32[]{:S(2)}, u32[]{:S(2)}) collective-permute-start(bf16[512,128]{1,0:T(8,128)(2,1)S(1)} %broadcast_select_fusion.2.after_too_ref), channel_id=1, source_target_pairs={{0,8},{4,12},{8,0},{12,4},{16,24},{20,28},{24,16},{28,20},{1,9},{5... | collective-permute-start | bytes 393224 | tf_op jit(solution)/shard_map/ppermute | solution.py:567
  25.4 1.6 %shard_map.161 = (bf16[8,9,16,128]{3,2,1,0:T(8,128)(2,1)S(1)}, bf16[16,128]{1,0:T(8,128)(2,1)S(1)}) custom-call(bf16[352,128]{1,0:T(8,128)(2,1)S(1)} %broadcast_select_fusion.4.after_ref, bf16[512,128]{1,0:T(8,128)(2,1)S(1)} %broadcast_select_fusion.2.after_too_ref, f32[2,8,128]{2,1,0:T(8,128)S(1)} %get-tuple-element.22.norm_ref, ...), custom_call_target="tpu_custom_call" | custom-call | flops 2000000000 | bytes 4194304 | tf_op jit(solution)/shard_map/pallas_call | solution.py:685
  27.1 1.1 %collective-permute-done.6 = bf16[352,128]{1,0:T(8,128)(2,1)S(1)} collective-permute-done((bf16[352,128]{1,0:T(8,128)(2,1)S(1)}, bf16[352,128]{1,0:T(8,128)(2,1)S(1)}, u32[]{:S(2)}, u32[]{:S(2)}) %collective-permute-start.6) | collective-permute-done | bytes 90144 | tf_op jit(solution)/shard_map/ppermute | solution.py:567
  28.2 1.6 %collective-permute-start.8 = (bf16[352,128]{1,0:T(8,128)(2,1)S(1)}, bf16[352,128]{1,0:T(8,128)(2,1)S(1)}, u32[]{:S(2)}, u32[]{:S(2)}) collective-permute-start(bf16[352,128]{1,0:T(8,128)(2,1)S(1)} %broadcast_select_fusion.3.after_ref.first_ref), channel_id=1, source_target_pairs={{0,16},{4,20},{8,24},{12,28},{16,0},{20,4},{24,8},{28,12},{1,17},{... | collective-permute-start | bytes 270344 | tf_op jit(solution)/shard_map/ppermute | solution.py:567
  29.8 2.0 %shard_map.162 = (bf16[8,9,16,128]{3,2,1,0:T(8,128)(2,1)S(1)}, bf16[16,128]{1,0:T(8,128)(2,1)}) custom-call(bf16[352,128]{1,0:T(8,128)(2,1)S(1)} %broadcast_select_fusion.3.after_ref.first_ref, bf16[8,9,16,128]{3,2,1,0:T(8,128)(2,1)S(1)} %get-tuple-element.25.after_too_ref.part_ref, f32[2,8,128]{2,1,0:T(8,128)S(1)} %get-tuple-element.22.norm_ref, ...), custom_call_target="tpu_custom_call" | custom-call | flops 2000000000 | bytes 4194304 | tf_op jit(solution)/shard_map/pallas_call | solution.py:685
  31.8 0.0 collective-permute-done.7
  31.8 0.0 copy-start.4
  31.8 0.6 %collective-permute-start.9 = (bf16[512,128]{1,0:T(8,128)(2,1)S(1)}, bf16[512,128]{1,0:T(8,128)(2,1)S(1)}, u32[]{:S(2)}, u32[]{:S(2)}) collective-permute-start(bf16[512,128]{1,0:T(8,128)(2,1)S(1)} %broadcast_select_fusion.1.after_ref), channel_id=1, source_target_pairs={{0,16},{4,20},{8,24},{12,28},{16,0},{20,4},{24,8},{28,12},{1,17},{... | collective-permute-start | bytes 393224 | tf_op jit(solution)/shard_map/ppermute | solution.py:567
  32.4 0.4 collective-permute-done.8.first_in_ref
  32.8 1.2 %shard_map.164 = (bf16[2,16,48]{2,1,0:T(8,128)(2,1)}, bf16[2,16,16,128]{3,2,1,0:T(8,128)(2,1)}) custom-call(bf16[512,128]{1,0:T(8,128)(2,1)S(1)} %broadcast_select_fusion.1.after_ref, bf16[352,128]{1,0:T(8,128)(2,1)S(1)} %broadcast_select_fusion.3.after_ref.first_ref, bf16[352,128]{1,0:T(8,128)(2,1)S(1)} %collective-permute-done.8.first_in_ref, ...), custom_call_target="tpu_custom_call" | custom-call | flops 2000000000 | bytes 4194304 | tf_op jit(solution)/shard_map/pallas_call | solution.py:725
  34.0 0.0 copy-done.4
  34.0 1.6 %shard_map.163 = bf16[4,8,8,256]{3,2,1,0:T(8,128)(2,1)} custom-call(s32[128]{0:T(128)S(1)} %pad_add_fusion.scalars_ref, bf16[8,9,16,128]{3,2,1,0:T(8,128)(2,1)S(1)} %get-tuple-element.25.after_too_ref.part_ref, bf16[8,9,16,128]{3,2,1,0:T(8,128)(2,1)S(1)} %get-tuple-element.27.rest_ref, bf16[3,3,3,128,256]{4,3,2,1,0:T(8,128)(2,1)S(1)} %copy-done.4, ...), custom_call_target="tpu_custom_call" | custom-call | flops 2000000000 | bytes 4194304 | tf_op jit(solution)/shard_map/pallas_call | solution.py:709
  35.6 1.2 %collective-permute-done.9 = bf16[512,128]{1,0:T(8,128)(2,1)S(1)} collective-permute-done((bf16[512,128]{1,0:T(8,128)(2,1)S(1)}, bf16[512,128]{1,0:T(8,128)(2,1)S(1)}, u32[]{:S(2)}, u32[]{:S(2)}) %collective-permute-start.9) | collective-permute-done | bytes 131104 | tf_op jit(solution)/shard_map/ppermute | solution.py:567
  36.9 0.7 %broadcast_select_fusion = bf16[512,128]{1,0:T(8,128)(2,1)} fusion(bf16[512,128]{1,0:T(8,128)(2,1)S(1)} %broadcast_select_fusion.1.after_ref, bf16[512,128]{1,0:T(8,128)(2,1)S(1)} %collective-permute-done.9, pred[128]{0:T(512)(128)(4,1)S(1)} %compare_bitcast_fusion), kind=kLoop, calls=%fused_computation | loop fusion | flops 65536 | bytes 393344 | tf_op jit(solution)/shard_map/jit(_where)/select_n | solution.py:663
  (9 shorter events, 0.1 us)
Async XLA Ops:
  0.6 9.1 %copy-start = (bf16[1,2,16,16,128]{4,3,2,1,0:T(8,128)(2,1)S(1)}, bf16[1,2,16,16,128]{4,3,2,1,0:T(8,128)(2,1)}, u32[]{:S(2)}) copy-start(bf16[1,2,16,16,128]{4,3,2,1,0:T(8,128)(2,1)} %param.19) | copy-start | bytes 393220
  0.6 9.1 %copy-start.1 = (bf16[1,2,16,16,128]{4,3,2,1,0:T(8,128)(2,1)S(1)}, bf16[1,2,16,16,128]{4,3,2,1,0:T(8,128)(2,1)}, u32[]{:S(2)}) copy-start(bf16[1,2,16,16,128]{4,3,2,1,0:T(8,128)(2,1)} %param.20) | copy-start | bytes 393220
  0.7 9.1 %copy-start.2 = (bf16[3,3,3,3,128]{4,3,2,1,0:T(4,128)(2,1)S(1)}, bf16[3,3,3,3,128]{4,3,2,1,0:T(4,128)(2,1)}, u32[]{:S(2)}) copy-start(bf16[3,3,3,3,128]{4,3,2,1,0:T(4,128)(2,1)} %sw_ref.1) | copy-start | bytes 62212
  0.7 9.1 %copy-start.3 = (bf16[1,2,16,48]{3,2,1,0:T(8,128)(2,1)S(1)}, bf16[1,2,16,48]{3,2,1,0:T(8,128)(2,1)}, u32[]{:S(2)}) copy-start(bf16[1,2,16,48]{3,2,1,0:T(8,128)(2,1)} %param.18) | copy-start | bytes 9220
  0.7 17.3 %copy-start.6 = (f32[128]{0:T(128)S(1)}, f32[128]{0:T(128)}, u32[]{:S(2)}) copy-start(f32[128]{0:T(128)} %gain_ref.1) | copy-start | bytes 1540
  0.7 17.3 %copy-start.7 = (f32[128]{0:T(128)S(1)}, f32[128]{0:T(128)}, u32[]{:S(2)}) copy-start(f32[128]{0:T(128)} %bias_ref.1) | copy-start | bytes 1540
  2.5 15.5 %all-to-all-start = ((bf16[32,8,128]{2,1,0:T(8,128)(2,1)}), bf16[32,8,128]{2,1,0:T(8,128)(2,1)S(1)}, u32[]{:S(2)}, u32[]{:S(2)}) async-start(bf16[32,8,128]{2,1,0:T(8,128)(2,1)} %bitcast.30), calls=%async_computation | async-start | bytes 131072 | tf_op jit(solution)/shard_map/all_to_all | solution.py:614
  10.0 7.7 %collective-permute-start = (bf16[2,16,128]{2,1,0:T(8,128)(2,1)S(1)}, bf16[2,16,128]{2,1,0:T(8,128)(2,1)S(1)}, u32[]{:S(2)}, u32[]{:S(2)}) collective-permute-start(bf16[2,16,128]{2,1,0:T(8,128)(2,1)S(1)} %get-tuple-element.17), channel_id=1, source_target_pairs={{0,1},{1,2},{2,3},{3,0},{4,5},{5,6},{6,7},{7,4},{8,9},{9,10},{10,1... | collective-permute-start | bytes 24584 | tf_op jit(solution)/shard_map/ppermute | solution.py:572
  11.8 5.8 %collective-permute-start.2 = (bf16[2,16,128]{2,1,0:T(8,128)(2,1)S(1)}, bf16[2,16,128]{2,1,0:T(8,128)(2,1)S(1)}, u32[]{:S(2)}, u32[]{:S(2)}) collective-permute-start(bf16[2,16,128]{2,1,0:T(8,128)(2,1)S(1)} %get-tuple-element.19), channel_id=1, source_target_pairs={{0,2},{1,3},{2,0},{3,1},{4,6},{5,7},{6,4},{7,5},{8,10},{9,11},{10,... | collective-permute-start | bytes 24584 | tf_op jit(solution)/shard_map/ppermute | solution.py:572
  14.2 3.7 %collective-permute-start.1 = (bf16[4,16,128]{2,1,0:T(8,128)(2,1)S(1)}, bf16[4,16,128]{2,1,0:T(8,128)(2,1)S(1)}, u32[]{:S(2)}, u32[]{:S(2)}) collective-permute-start(bf16[4,16,128]{2,1,0:T(8,128)(2,1)S(1)} %get-tuple-element.18), channel_id=1, source_target_pairs={{0,3},{1,0},{2,1},{3,2},{4,7},{5,4},{6,5},{7,6},{8,11},{9,8},{10,9... | collective-permute-start | bytes 49160 | tf_op jit(solution)/shard_map/ppermute | solution.py:572
  15.6 5.6 %collective-permute-start.4 = (bf16[6,16,128]{2,1,0:T(8,128)(2,1)S(1)}, bf16[6,16,128]{2,1,0:T(8,128)(2,1)S(1)}, u32[]{:S(2)}, u32[]{:S(2)}) collective-permute-start(bf16[6,16,128]{2,1,0:T(8,128)(2,1)S(1)} %get-tuple-element.24), channel_id=1, source_target_pairs={{0,1},{1,2},{2,3},{3,0},{4,5},{5,6},{6,7},{7,4},{8,9},{9,10},{10,1... | collective-permute-start | bytes 73736 | tf_op jit(solution)/shard_map/ppermute | solution.py:572
  17.9 3.3 %copy-start.5 = (bf16[3,3,3,128,128]{4,3,2,1,0:T(8,128)(2,1)S(1)}, bf16[3,3,3,128,128]{4,3,2,1,0:T(8,128)(2,1)}, u32[]{:S(2)}) copy-start(bf16[3,3,3,128,128]{4,3,2,1,0:T(8,128)(2,1)} %conv_ref.5) | copy-start | bytes 2654212
  20.7 1.7 %collective-permute-start.3 = (bf16[352,128]{1,0:T(8,128)(2,1)S(1)}, bf16[352,128]{1,0:T(8,128)(2,1)S(1)}, u32[]{:S(2)}, u32[]{:S(2)}) collective-permute-start(bf16[352,128]{1,0:T(8,128)(2,1)S(1)} %get-tuple-element.21), channel_id=1, source_target_pairs={{0,4},{4,0},{8,12},{12,8},{16,20},{20,16},{24,28},{28,24},{1,5},{5... | collective-permute-start | bytes 270344 | tf_op jit(solution)/shard_map/ppermute | solution.py:567
  22.5 1.6 %collective-permute-start.5 = (bf16[512,128]{1,0:T(8,128)(2,1)S(1)}, bf16[512,128]{1,0:T(8,128)(2,1)S(1)}, u32[]{:S(2)}, u32[]{:S(2)}) collective-permute-start(bf16[512,128]{1,0:T(8,128)(2,1)S(1)} %shard_map.160), channel_id=1, source_target_pairs={{0,4},{4,0},{8,12},{12,8},{16,20},{20,16},{24,28},{28,24},{1,5},{5... | collective-permute-start | bytes 393224 | tf_op jit(solution)/shard_map/ppermute | solution.py:567
  22.7 5.4 %collective-permute-start.6 = (bf16[352,128]{1,0:T(8,128)(2,1)S(1)}, bf16[352,128]{1,0:T(8,128)(2,1)S(1)}, u32[]{:S(2)}, u32[]{:S(2)}) collective-permute-start(bf16[352,128]{1,0:T(8,128)(2,1)S(1)} %broadcast_select_fusion.4.after_ref), channel_id=1, source_target_pairs={{0,8},{4,12},{8,0},{12,4},{16,24},{20,28},{24,16},{28,20},{1,9},{5... | collective-permute-start | bytes 270344 | tf_op jit(solution)/shard_map/ppermute | solution.py:567
  24.1 7.7 %collective-permute-start.7 = (bf16[512,128]{1,0:T(8,128)(2,1)S(1)}, bf16[512,128]{1,0:T(8,128)(2,1)S(1)}, u32[]{:S(2)}, u32[]{:S(2)}) collective-permute-start(bf16[512,128]{1,0:T(8,128)(2,1)S(1)} %broadcast_select_fusion.2.after_too_ref), channel_id=1, source_target_pairs={{0,8},{4,12},{8,0},{12,4},{16,24},{20,28},{24,16},{28,20},{1,9},{5... | collective-permute-start | bytes 393224 | tf_op jit(solution)/shard_map/ppermute | solution.py:567
  28.2 4.6 %collective-permute-start.8 = (bf16[352,128]{1,0:T(8,128)(2,1)S(1)}, bf16[352,128]{1,0:T(8,128)(2,1)S(1)}, u32[]{:S(2)}, u32[]{:S(2)}) collective-permute-start(bf16[352,128]{1,0:T(8,128)(2,1)S(1)} %broadcast_select_fusion.3.after_ref.first_ref), channel_id=1, source_target_pairs={{0,16},{4,20},{8,24},{12,28},{16,0},{20,4},{24,8},{28,12},{1,17},{... | collective-permute-start | bytes 270344 | tf_op jit(solution)/shard_map/ppermute | solution.py:567
  31.8 2.2 %copy-start.4 = (bf16[3,3,3,128,256]{4,3,2,1,0:T(8,128)(2,1)S(1)}, bf16[3,3,3,128,256]{4,3,2,1,0:T(8,128)(2,1)}, u32[]{:S(2)}) copy-start(bf16[3,3,3,128,256]{4,3,2,1,0:T(8,128)(2,1)} %down_ref.1) | copy-start | bytes 5308420
  31.8 5.0 %collective-permute-start.9 = (bf16[512,128]{1,0:T(8,128)(2,1)S(1)}, bf16[512,128]{1,0:T(8,128)(2,1)S(1)}, u32[]{:S(2)}, u32[]{:S(2)}) collective-permute-start(bf16[512,128]{1,0:T(8,128)(2,1)S(1)} %broadcast_select_fusion.1.after_ref), channel_id=1, source_target_pairs={{0,16},{4,20},{8,24},{12,28},{16,0},{20,4},{24,8},{28,12},{1,17},{... | collective-permute-start | bytes 393224 | tf_op jit(solution)/shard_map/ppermute | solution.py:567

commit v8 on v7

--- a/solution.py
+++ b/solution.py
@@ -227,7 +227,6 @@
         for a in range(3):
             zs[a, 4 + s * 16 : 4 + (s + 1) * 16] = placed[s][a]
     target = whole(scalars_ref, 1).astype(F32)
-    pay_ref[0:16] = jnp.full((16, 128), target, F32).astype(BF16)
     last = valid - 1
     line_rows = zs.reshape(3 * (rows_all + 16) * 8, 128)
     lines = []
@@ -281,10 +280,10 @@
             pieces.append(piece)
             row = row - piece
     row16 = iota((16, 128), 0)
-    norms = jnp.zeros((16, 128), F32)
+    norms = jnp.where(row16 == 0, target, 0.0)
     for n, piece in enumerate(pieces):
-        norms = jnp.where(row16 == n, piece, norms)
-    pay_ref[336:352] = norms.astype(BF16)
+        norms = jnp.where(row16 == n + 1, piece, norms)
+    pay_ref[0:16] = norms.astype(BF16)
 
 
 def last_kernel(
@@ -529,7 +528,7 @@
     frame,
 ):
     del after_ref
-    target = first_ref[0:16].astype(jnp.int32)
+    target = first_ref[0:16].astype(F32).astype(jnp.int32)
     mine = (target >> bit) & 1 == (lax.axis_index("stream") >> bit) & 1
     mine = jnp.where(mine, 1.0, 0.0)[0:1] > 0.5
 
@@ -544,9 +543,9 @@
     rows[2] = chosen(48, 80)
     for i in range(2):
         new_pix_ref[i] = rows[1 + i, 1:17, 0:48].astype(BF16)
-    norms = chosen(336, 352)
-    scale = norms[0:1] + norms[1:2] + norms[2:3]
-    shift = norms[3:4] + norms[4:5] + norms[5:6]
+    norms = chosen(0, 16)
+    scale = norms[1:2] + norms[2:3] + norms[3:4]
+    shift = norms[4:5] + norms[5:6] + norms[6:7]
     for b in range(3):
         for a in range(3):
             q = (b * 3 + a) * 48
@@ -637,7 +636,7 @@
     first, norm, stem = pl.pallas_call(
         functools.partial(stem_kernel, strips),
         out_shape=(
-            jax.ShapeDtypeStruct((352, 128), BF16),
+            jax.ShapeDtypeStruct((336, 128), BF16),
             jax.ShapeDtypeStruct((2, 8, 128), F32),
             window,
         ),

time: 37.7 us -> 37.5 us (level)
  transfers between devices with their start and end apart: 11 -> 11, of which waited for: 5 -> 5; matrix products, arithmetic and copies ran while one was open for 0% -> 0% of each run, Pallas kernels for 28% -> 29%
where the time goes in v8:
time: 37.5 us; the launch traced here: 37.3 us
  starting transfers between devices  18.6 us (50%)
  Pallas kernels  12.5 us (33%)
  waiting for transfers between devices  3.12 us (8%)
  between operations  2.14 us (6%)
  other arithmetic  0.85 us (2%)
    all_to_all x1, starting transfers between devices, body(): recv = lax.all_to_all(lines, ('strip', 'stream'), 0, 0, tiled=True)  7.3 us
    ppermute x4, starting transfers between devices, shifted(): lax.ppermute(value, axis, [(i, (i + by) % size) for i in range(size)])  6.26 us
    ppermute x6, starting transfers between devices, partner(): return lax.ppermute(value, axis, pairs)  5.05 us
    pallas_call x2, Pallas kernels, convolved(): pl.pallas_call(functools.partial(conv_kernel, strips, w0), out_shape=(jax...  3.67 us
    pallas_call x1, Pallas kernels, body(): pl.pallas_call(functools.partial(stem_kernel, strips), out_shape=(jax.Sha...  2.77 us
    ppermute x6, waiting for transfers between devices, partner(): return lax.ppermute(value, axis, pairs)  2.39 us
    pallas_call x1, Pallas kernels, body(): pl.pallas_call(functools.partial(sort_kernel, streams), out_shape=jax.Sha...  1.77 us
    pallas_call x1, Pallas kernels, body(): pl.pallas_call(down_kernel, out_shape=jax.ShapeDtypeStruct((4, 8, 8, 256)...  1.64 us
  transfers between devices with their start and end apart: 11, of which 5 were waited for; matrix products, arithmetic and copies ran while one was open for 0% of the time, Pallas kernels for 29%

profile of v8, /device:TPU:0, one launch (start us, length us, event | category | flops | bytes accessed | tf_op | source)
XLA Modules:
  0.0 37.3 jit_solution(5615320206701971239)
XLA Ops:
  0.6 0.0 copy-start
  0.6 0.0 copy-start.1
  0.7 0.0 copy-start.2
  0.7 0.0 copy-start.3
  0.7 0.0 copy-start.6
  0.7 0.0 copy-start.7
  0.7 1.8 %shard_map.156 = bf16[4,8,8,128]{3,2,1,0:T(8,128)(2,1)} custom-call(bf16[48,128]{1,0:T(8,128)(2,1)} %bitcast.31, s32[1,128]{1,0:T(1,128)} %owner_ref.1, s32[1,128]{1,0:T(1,128)} %slot_ref.1), custom_call_target="tpu_custom_call" | custom-call | flops 2000000000 | bytes 4194304 | tf_op jit(solution)/shard_map/pallas_call | solution.py:601
  2.5 7.3 %all-to-all-start = ((bf16[32,8,128]{2,1,0:T(8,128)(2,1)}), bf16[32,8,128]{2,1,0:T(8,128)(2,1)S(1)}, u32[]{:S(2)}, u32[]{:S(2)}) async-start(bf16[32,8,128]{2,1,0:T(8,128)(2,1)} %bitcast.30), calls=%async_computation | async-start | bytes 131072 | tf_op jit(solution)/shard_map/all_to_all | solution.py:613
  9.8 0.0 copy-done
  9.8 0.0 copy-done.1
  9.8 0.0 copy-done.2
  9.8 0.0 copy-done.3
  9.8 0.1 shard_map.157
  10.0 1.8 %collective-permute-start = (bf16[2,16,128]{2,1,0:T(8,128)(2,1)S(1)}, bf16[2,16,128]{2,1,0:T(8,128)(2,1)S(1)}, u32[]{:S(2)}, u32[]{:S(2)}) collective-permute-start(bf16[2,16,128]{2,1,0:T(8,128)(2,1)S(1)} %get-tuple-element.17), channel_id=1, source_target_pairs={{0,1},{1,2},{2,3},{3,0},{4,5},{5,6},{6,7},{7,4},{8,9},{9,10},{10,1... | collective-permute-start | bytes 24584 | tf_op jit(solution)/shard_map/ppermute | solution.py:571
  11.8 2.4 %collective-permute-start.2 = (bf16[2,16,128]{2,1,0:T(8,128)(2,1)S(1)}, bf16[2,16,128]{2,1,0:T(8,128)(2,1)S(1)}, u32[]{:S(2)}, u32[]{:S(2)}) collective-permute-start(bf16[2,16,128]{2,1,0:T(8,128)(2,1)S(1)} %get-tuple-element.19), channel_id=1, source_target_pairs={{0,2},{1,3},{2,0},{3,1},{4,6},{5,7},{6,4},{7,5},{8,10},{9,11},{10,... | collective-permute-start | bytes 24584 | tf_op jit(solution)/shard_map/ppermute | solution.py:571
  14.2 1.4 %collective-permute-start.1 = (bf16[4,16,128]{2,1,0:T(8,128)(2,1)S(1)}, bf16[4,16,128]{2,1,0:T(8,128)(2,1)S(1)}, u32[]{:S(2)}, u32[]{:S(2)}) collective-permute-start(bf16[4,16,128]{2,1,0:T(8,128)(2,1)S(1)} %get-tuple-element.18), channel_id=1, source_target_pairs={{0,3},{1,0},{2,1},{3,2},{4,7},{5,4},{6,5},{7,6},{8,11},{9,8},{10,9... | collective-permute-start | bytes 49160 | tf_op jit(solution)/shard_map/ppermute | solution.py:571
  15.6 0.6 %collective-permute-start.4 = (bf16[6,16,128]{2,1,0:T(8,128)(2,1)S(1)}, bf16[6,16,128]{2,1,0:T(8,128)(2,1)S(1)}, u32[]{:S(2)}, u32[]{:S(2)}) collective-permute-start(bf16[6,16,128]{2,1,0:T(8,128)(2,1)S(1)} %get-tuple-element.24), channel_id=1, source_target_pairs={{0,1},{1,2},{2,3},{3,0},{4,5},{5,6},{6,7},{7,4},{8,9},{9,10},{10,1... | collective-permute-start | bytes 73736 | tf_op jit(solution)/shard_map/ppermute | solution.py:571
  17.5 0.1 pad_add_fusion.scalars_ref
  17.6 0.0 collective-permute-done.below_ref
  17.6 0.0 collective-permute-done.2.mid_ref
  17.6 0.3 collective-permute-done.1.above_ref
  17.9 0.0 all-to-all-done
  17.9 0.0 copy-done.6
  17.9 0.0 copy-done.7
  17.9 0.0 copy-start.5
  18.0 2.8 %shard_map.158 = (bf16[336,128]{1,0:T(8,128)(2,1)S(1)}, f32[2,8,128]{2,1,0:T(8,128)S(1)}, f32[2,16,11,8,128]{4,3,2,1,0:T(8,128)S(1)}) custom-call(s32[128]{0:T(128)S(1)} %pad_add_fusion.scalars_ref, f32[128]{0:T(128)S(1)} %copy-done.6, f32[128]{0:T(128)S(1)} %copy-done.7, bf16[4,64,128]{2,1,0:T(8,128)(2,1)S(1)} %bitcast.26, bf16[2,16,48]{2,1,0:T(8,128)(2,1)S(1)} %bitcast.28, ...), custom_call_target="tpu_custom_call" | custom-call | flops 2000000000 | bytes 4194304 | tf_op jit(solution)/shard_map/pallas_call | solution.py:636
  20.7 0.1 collective-permute-start.3
  20.8 0.4 %collective-permute-done.4.below_ref = bf16[6,16,128]{2,1,0:T(8,128)(2,1)S(1)} collective-permute-done((bf16[6,16,128]{2,1,0:T(8,128)(2,1)S(1)}, bf16[6,16,128]{2,1,0:T(8,128)(2,1)S(1)}, u32[]{:S(2)}, u32[]{:S(2)}) %collective-permute-start.4) | collective-permute-done | bytes 24608 | tf_op jit(solution)/shard_map/ppermute | solution.py:571
  21.2 0.0 copy-done.5
  21.2 1.3 %shard_map.159.value_ref = f32[32,16,128]{2,1,0:T(8,128)S(1)} custom-call(s32[128]{0:T(128)S(1)} %pad_add_fusion.scalars_ref, f32[2,8,128]{2,1,0:T(8,128)S(1)} %get-tuple-element.22.norm_ref, f32[2,16,11,8,128]{4,3,2,1,0:T(8,128)S(1)} %get-tuple-element.23.stem, bf16[2,16,16,128]{3,2,1,0:T(8,128)(2,1)S(1)} %bitcast.20, ...), custom_call_target="tpu_custom_call" | custom-call | flops 2000000000 | bytes 4194304 | tf_op jit(solution)/shard_map/pallas_call | solution.py:664
  22.5 0.0 collective-permute-done.3
  22.6 0.2 collective-permute-start.5
  22.7 1.5 %collective-permute-start.6 = (bf16[336,128]{1,0:T(8,128)(2,1)S(1)}, bf16[336,128]{1,0:T(8,128)(2,1)S(1)}, u32[]{:S(2)}, u32[]{:S(2)}) collective-permute-start(bf16[336,128]{1,0:T(8,128)(2,1)S(1)} %broadcast_select_fusion.4.after_ref), channel_id=1, source_target_pairs={{0,8},{4,12},{8,0},{12,4},{16,24},{20,28},{24,16},{28,20},{1,9},{5... | collective-permute-start | bytes 258056 | tf_op jit(solution)/shard_map/ppermute | solution.py:566
  24.2 0.0 collective-permute-done.5
  24.2 1.2 %collective-permute-start.7 = (bf16[512,128]{1,0:T(8,128)(2,1)S(1)}, bf16[512,128]{1,0:T(8,128)(2,1)S(1)}, u32[]{:S(2)}, u32[]{:S(2)}) collective-permute-start(bf16[512,128]{1,0:T(8,128)(2,1)S(1)} %broadcast_select_fusion.2.after_too_ref), channel_id=1, source_target_pairs={{0,8},{4,12},{8,0},{12,4},{16,24},{20,28},{24,16},{28,20},{1,9},{5... | collective-permute-start | bytes 393224 | tf_op jit(solution)/shard_map/ppermute | solution.py:566
  25.4 1.6 %shard_map.161 = (bf16[8,9,16,128]{3,2,1,0:T(8,128)(2,1)S(1)}, bf16[16,128]{1,0:T(8,128)(2,1)S(1)}) custom-call(bf16[336,128]{1,0:T(8,128)(2,1)S(1)} %broadcast_select_fusion.4.after_ref, bf16[512,128]{1,0:T(8,128)(2,1)S(1)} %broadcast_select_fusion.2.after_too_ref, f32[2,8,128]{2,1,0:T(8,128)S(1)} %get-tuple-element.22.norm_ref, ...), custom_call_target="tpu_custom_call" | custom-call | flops 2000000000 | bytes 4194304 | tf_op jit(solution)/shard_map/pallas_call | solution.py:684
  27.1 1.0 %collective-permute-done.6 = bf16[336,128]{1,0:T(8,128)(2,1)S(1)} collective-permute-done((bf16[336,128]{1,0:T(8,128)(2,1)S(1)}, bf16[336,128]{1,0:T(8,128)(2,1)S(1)}, u32[]{:S(2)}, u32[]{:S(2)}) %collective-permute-start.6) | collective-permute-done | bytes 86048 | tf_op jit(solution)/shard_map/ppermute | solution.py:566
  28.1 1.4 %collective-permute-start.8 = (bf16[336,128]{1,0:T(8,128)(2,1)S(1)}, bf16[336,128]{1,0:T(8,128)(2,1)S(1)}, u32[]{:S(2)}, u32[]{:S(2)}) collective-permute-start(bf16[336,128]{1,0:T(8,128)(2,1)S(1)} %broadcast_select_fusion.3.after_ref.first_ref), channel_id=1, source_target_pairs={{0,16},{4,20},{8,24},{12,28},{16,0},{20,4},{24,8},{28,12},{1,17},{... | collective-permute-start | bytes 258056 | tf_op jit(solution)/shard_map/ppermute | solution.py:566
  29.5 2.0 %shard_map.162 = (bf16[8,9,16,128]{3,2,1,0:T(8,128)(2,1)S(1)}, bf16[16,128]{1,0:T(8,128)(2,1)}) custom-call(bf16[336,128]{1,0:T(8,128)(2,1)S(1)} %broadcast_select_fusion.3.after_ref.first_ref, bf16[8,9,16,128]{3,2,1,0:T(8,128)(2,1)S(1)} %get-tuple-element.25.after_too_ref.part_ref, f32[2,8,128]{2,1,0:T(8,128)S(1)} %get-tuple-element.22.norm_ref, ...), custom_call_target="tpu_custom_call" | custom-call | flops 2000000000 | bytes 4194304 | tf_op jit(solution)/shard_map/pallas_call | solution.py:684
  31.5 0.0 collective-permute-done.7
  31.5 0.0 copy-start.4
  31.5 0.8 %collective-permute-start.9 = (bf16[512,128]{1,0:T(8,128)(2,1)S(1)}, bf16[512,128]{1,0:T(8,128)(2,1)S(1)}, u32[]{:S(2)}, u32[]{:S(2)}) collective-permute-start(bf16[512,128]{1,0:T(8,128)(2,1)S(1)} %broadcast_select_fusion.1.after_ref), channel_id=1, source_target_pairs={{0,16},{4,20},{8,24},{12,28},{16,0},{20,4},{24,8},{28,12},{1,17},{... | collective-permute-start | bytes 393224 | tf_op jit(solution)/shard_map/ppermute | solution.py:566
  32.3 0.3 collective-permute-done.8.first_in_ref
  32.6 1.2 %shard_map.164 = (bf16[2,16,48]{2,1,0:T(8,128)(2,1)}, bf16[2,16,16,128]{3,2,1,0:T(8,128)(2,1)}) custom-call(bf16[512,128]{1,0:T(8,128)(2,1)S(1)} %broadcast_select_fusion.1.after_ref, bf16[336,128]{1,0:T(8,128)(2,1)S(1)} %broadcast_select_fusion.3.after_ref.first_ref, bf16[336,128]{1,0:T(8,128)(2,1)S(1)} %collective-permute-done.8.first_in_ref, ...), custom_call_target="tpu_custom_call" | custom-call | flops 2000000000 | bytes 4194304 | tf_op jit(solution)/shard_map/pallas_call | solution.py:724
  33.9 0.0 copy-done.4
  33.9 1.6 %shard_map.163 = bf16[4,8,8,256]{3,2,1,0:T(8,128)(2,1)} custom-call(s32[128]{0:T(128)S(1)} %pad_add_fusion.scalars_ref, bf16[8,9,16,128]{3,2,1,0:T(8,128)(2,1)S(1)} %get-tuple-element.25.after_too_ref.part_ref, bf16[8,9,16,128]{3,2,1,0:T(8,128)(2,1)S(1)} %get-tuple-element.27.rest_ref, bf16[3,3,3,128,256]{4,3,2,1,0:T(8,128)(2,1)S(1)} %copy-done.4, ...), custom_call_target="tpu_custom_call" | custom-call | flops 2000000000 | bytes 4194304 | tf_op jit(solution)/shard_map/pallas_call | solution.py:708
  35.5 1.1 %collective-permute-done.9 = bf16[512,128]{1,0:T(8,128)(2,1)S(1)} collective-permute-done((bf16[512,128]{1,0:T(8,128)(2,1)S(1)}, bf16[512,128]{1,0:T(8,128)(2,1)S(1)}, u32[]{:S(2)}, u32[]{:S(2)}) %collective-permute-start.9) | collective-permute-done | bytes 131104 | tf_op jit(solution)/shard_map/ppermute | solution.py:566
  36.6 0.7 %broadcast_select_fusion = bf16[512,128]{1,0:T(8,128)(2,1)} fusion(bf16[512,128]{1,0:T(8,128)(2,1)S(1)} %broadcast_select_fusion.1.after_ref, bf16[512,128]{1,0:T(8,128)(2,1)S(1)} %collective-permute-done.9, pred[128]{0:T(512)(128)(4,1)S(1)} %compare_bitcast_fusion), kind=kLoop, calls=%fused_computation | loop fusion | flops 65536 | bytes 393344 | tf_op jit(solution)/shard_map/jit(_where)/select_n | solution.py:662
  (9 shorter events, 0.1 us)
Async XLA Ops:
  0.6 9.1 %copy-start = (bf16[1,2,16,16,128]{4,3,2,1,0:T(8,128)(2,1)S(1)}, bf16[1,2,16,16,128]{4,3,2,1,0:T(8,128)(2,1)}, u32[]{:S(2)}) copy-start(bf16[1,2,16,16,128]{4,3,2,1,0:T(8,128)(2,1)} %param.19) | copy-start | bytes 393220
  0.6 9.1 %copy-start.1 = (bf16[1,2,16,16,128]{4,3,2,1,0:T(8,128)(2,1)S(1)}, bf16[1,2,16,16,128]{4,3,2,1,0:T(8,128)(2,1)}, u32[]{:S(2)}) copy-start(bf16[1,2,16,16,128]{4,3,2,1,0:T(8,128)(2,1)} %param.20) | copy-start | bytes 393220
  0.7 9.1 %copy-start.2 = (bf16[3,3,3,3,128]{4,3,2,1,0:T(4,128)(2,1)S(1)}, bf16[3,3,3,3,128]{4,3,2,1,0:T(4,128)(2,1)}, u32[]{:S(2)}) copy-start(bf16[3,3,3,3,128]{4,3,2,1,0:T(4,128)(2,1)} %sw_ref.1) | copy-start | bytes 62212
  0.7 9.1 %copy-start.3 = (bf16[1,2,16,48]{3,2,1,0:T(8,128)(2,1)S(1)}, bf16[1,2,16,48]{3,2,1,0:T(8,128)(2,1)}, u32[]{:S(2)}) copy-start(bf16[1,2,16,48]{3,2,1,0:T(8,128)(2,1)} %param.18) | copy-start | bytes 9220
  0.7 17.3 %copy-start.6 = (f32[128]{0:T(128)S(1)}, f32[128]{0:T(128)}, u32[]{:S(2)}) copy-start(f32[128]{0:T(128)} %gain_ref.1) | copy-start | bytes 1540
  0.7 17.3 %copy-start.7 = (f32[128]{0:T(128)S(1)}, f32[128]{0:T(128)}, u32[]{:S(2)}) copy-start(f32[128]{0:T(128)} %bias_ref.1) | copy-start | bytes 1540
  2.5 15.5 %all-to-all-start = ((bf16[32,8,128]{2,1,0:T(8,128)(2,1)}), bf16[32,8,128]{2,1,0:T(8,128)(2,1)S(1)}, u32[]{:S(2)}, u32[]{:S(2)}) async-start(bf16[32,8,128]{2,1,0:T(8,128)(2,1)} %bitcast.30), calls=%async_computation | async-start | bytes 131072 | tf_op jit(solution)/shard_map/all_to_all | solution.py:613
  10.0 7.7 %collective-permute-start = (bf16[2,16,128]{2,1,0:T(8,128)(2,1)S(1)}, bf16[2,16,128]{2,1,0:T(8,128)(2,1)S(1)}, u32[]{:S(2)}, u32[]{:S(2)}) collective-permute-start(bf16[2,16,128]{2,1,0:T(8,128)(2,1)S(1)} %get-tuple-element.17), channel_id=1, source_target_pairs={{0,1},{1,2},{2,3},{3,0},{4,5},{5,6},{6,7},{7,4},{8,9},{9,10},{10,1... | collective-permute-start | bytes 24584 | tf_op jit(solution)/shard_map/ppermute | solution.py:571
  11.8 5.8 %collective-permute-start.2 = (bf16[2,16,128]{2,1,0:T(8,128)(2,1)S(1)}, bf16[2,16,128]{2,1,0:T(8,128)(2,1)S(1)}, u32[]{:S(2)}, u32[]{:S(2)}) collective-permute-start(bf16[2,16,128]{2,1,0:T(8,128)(2,1)S(1)} %get-tuple-element.19), channel_id=1, source_target_pairs={{0,2},{1,3},{2,0},{3,1},{4,6},{5,7},{6,4},{7,5},{8,10},{9,11},{10,... | collective-permute-start | bytes 24584 | tf_op jit(solution)/shard_map/ppermute | solution.py:571
  14.2 3.7 %collective-permute-start.1 = (bf16[4,16,128]{2,1,0:T(8,128)(2,1)S(1)}, bf16[4,16,128]{2,1,0:T(8,128)(2,1)S(1)}, u32[]{:S(2)}, u32[]{:S(2)}) collective-permute-start(bf16[4,16,128]{2,1,0:T(8,128)(2,1)S(1)} %get-tuple-element.18), channel_id=1, source_target_pairs={{0,3},{1,0},{2,1},{3,2},{4,7},{5,4},{6,5},{7,6},{8,11},{9,8},{10,9... | collective-permute-start | bytes 49160 | tf_op jit(solution)/shard_map/ppermute | solution.py:571
  15.6 5.6 %collective-permute-start.4 = (bf16[6,16,128]{2,1,0:T(8,128)(2,1)S(1)}, bf16[6,16,128]{2,1,0:T(8,128)(2,1)S(1)}, u32[]{:S(2)}, u32[]{:S(2)}) collective-permute-start(bf16[6,16,128]{2,1,0:T(8,128)(2,1)S(1)} %get-tuple-element.24), channel_id=1, source_target_pairs={{0,1},{1,2},{2,3},{3,0},{4,5},{5,6},{6,7},{7,4},{8,9},{9,10},{10,1... | collective-permute-start | bytes 73736 | tf_op jit(solution)/shard_map/ppermute | solution.py:571
  17.9 3.3 %copy-start.5 = (bf16[3,3,3,128,128]{4,3,2,1,0:T(8,128)(2,1)S(1)}, bf16[3,3,3,128,128]{4,3,2,1,0:T(8,128)(2,1)}, u32[]{:S(2)}) copy-start(bf16[3,3,3,128,128]{4,3,2,1,0:T(8,128)(2,1)} %conv_ref.5) | copy-start | bytes 2654212
  20.7 1.8 %collective-permute-start.3 = (bf16[336,128]{1,0:T(8,128)(2,1)S(1)}, bf16[336,128]{1,0:T(8,128)(2,1)S(1)}, u32[]{:S(2)}, u32[]{:S(2)}) collective-permute-start(bf16[336,128]{1,0:T(8,128)(2,1)S(1)} %get-tuple-element.21), channel_id=1, source_target_pairs={{0,4},{4,0},{8,12},{12,8},{16,20},{20,16},{24,28},{28,24},{1,5},{5... | collective-permute-start | bytes 258056 | tf_op jit(solution)/shard_map/ppermute | solution.py:566
  22.6 1.6 %collective-permute-start.5 = (bf16[512,128]{1,0:T(8,128)(2,1)S(1)}, bf16[512,128]{1,0:T(8,128)(2,1)S(1)}, u32[]{:S(2)}, u32[]{:S(2)}) collective-permute-start(bf16[512,128]{1,0:T(8,128)(2,1)S(1)} %shard_map.160), channel_id=1, source_target_pairs={{0,4},{4,0},{8,12},{12,8},{16,20},{20,16},{24,28},{28,24},{1,5},{5... | collective-permute-start | bytes 393224 | tf_op jit(solution)/shard_map/ppermute | solution.py:566
  22.7 5.3 %collective-permute-start.6 = (bf16[336,128]{1,0:T(8,128)(2,1)S(1)}, bf16[336,128]{1,0:T(8,128)(2,1)S(1)}, u32[]{:S(2)}, u32[]{:S(2)}) collective-permute-start(bf16[336,128]{1,0:T(8,128)(2,1)S(1)} %broadcast_select_fusion.4.after_ref), channel_id=1, source_target_pairs={{0,8},{4,12},{8,0},{12,4},{16,24},{20,28},{24,16},{28,20},{1,9},{5... | collective-permute-start | bytes 258056 | tf_op jit(solution)/shard_map/ppermute | solution.py:566
  24.2 7.3 %collective-permute-start.7 = (bf16[512,128]{1,0:T(8,128)(2,1)S(1)}, bf16[512,128]{1,0:T(8,128)(2,1)S(1)}, u32[]{:S(2)}, u32[]{:S(2)}) collective-permute-start(bf16[512,128]{1,0:T(8,128)(2,1)S(1)} %broadcast_select_fusion.2.after_too_ref), channel_id=1, source_target_pairs={{0,8},{4,12},{8,0},{12,4},{16,24},{20,28},{24,16},{28,20},{1,9},{5... | collective-permute-start | bytes 393224 | tf_op jit(solution)/shard_map/ppermute | solution.py:566
  28.1 4.6 %collective-permute-start.8 = (bf16[336,128]{1,0:T(8,128)(2,1)S(1)}, bf16[336,128]{1,0:T(8,128)(2,1)S(1)}, u32[]{:S(2)}, u32[]{:S(2)}) collective-permute-start(bf16[336,128]{1,0:T(8,128)(2,1)S(1)} %broadcast_select_fusion.3.after_ref.first_ref), channel_id=1, source_target_pairs={{0,16},{4,20},{8,24},{12,28},{16,0},{20,4},{24,8},{28,12},{1,17},{... | collective-permute-start | bytes 258056 | tf_op jit(solution)/shard_map/ppermute | solution.py:566
  31.5 2.3 %copy-start.4 = (bf16[3,3,3,128,256]{4,3,2,1,0:T(8,128)(2,1)S(1)}, bf16[3,3,3,128,256]{4,3,2,1,0:T(8,128)(2,1)}, u32[]{:S(2)}) copy-start(bf16[3,3,3,128,256]{4,3,2,1,0:T(8,128)(2,1)} %down_ref.1) | copy-start | bytes 5308420
  31.5 5.0 %collective-permute-start.9 = (bf16[512,128]{1,0:T(8,128)(2,1)S(1)}, bf16[512,128]{1,0:T(8,128)(2,1)S(1)}, u32[]{:S(2)}, u32[]{:S(2)}) collective-permute-start(bf16[512,128]{1,0:T(8,128)(2,1)S(1)} %broadcast_select_fusion.1.after_ref), channel_id=1, source_target_pairs={{0,16},{4,20},{8,24},{12,28},{16,0},{20,4},{24,8},{28,12},{1,17},{... | collective-permute-start | bytes 393224 | tf_op jit(solution)/shard_map/ppermute | solution.py:566

commit v9 on v8

--- a/solution.py
+++ b/solution.py
@@ -233,10 +233,8 @@
     for a in range(3):
         at = (a * (rows_all + 16) + 3 + j * 16) * 8 + (last & 1) * 4 + (last >> 1)
         lines.append(line_rows[pl.ds(at, 24, stride=8)])
-    none = jnp.zeros((8, 128), F32)
     left = jnp.where(iota((24, 128), 1) < 64, lines[0], pltpu.roll(lines[1], 64, 1))
-    pay_ref[16:48] = jnp.concatenate([left, none], axis=0).astype(BF16)
-    pay_ref[48:80] = jnp.concatenate([lines[2], none], axis=0).astype(BF16)
+    pay_ref[16:64] = jnp.concatenate([left, lines[2]], axis=0).astype(BF16)
     high = rows_all + 4
     for b in range(3):
         for a in range(3):
@@ -272,7 +270,7 @@
     for y in range(16):
         block = silu(stem_rows[pl.ds(row_at(t, y), 16, stride=88)] * scale_t + shift_t)
         block = jnp.where(valid < 2, old_ref[1, y].astype(F32), block)
-        pay_ref[80 + y * 16 : 96 + y * 16] = block.astype(BF16)
+        pay_ref[64 + y * 16 : 80 + y * 16] = block.astype(BF16)
     pieces = []
     for row in (frame_row(scale, last), frame_row(shift, last)):
         for _ in range(3):
@@ -536,11 +534,12 @@
         own, other = first_ref[start:stop].astype(F32), first_in_ref[start:stop].astype(F32)
         return jnp.where(mine, own, other)
 
-    new_act_ref[0] = chosen(80, 336).astype(BF16).reshape(16, 16, 128)
-    left = chosen(16, 48)
+    new_act_ref[0] = chosen(64, 320).astype(BF16).reshape(16, 16, 128)
+    lines = chosen(16, 64)
+    left = lines[0:24]
     rows[0] = left
     rows[1] = pltpu.roll(left, 64, 1)
-    rows[2] = chosen(48, 80)
+    rows[2] = lines[24:48]
     for i in range(2):
         new_pix_ref[i] = rows[1 + i, 1:17, 0:48].astype(BF16)
     norms = chosen(0, 16)
@@ -636,7 +635,7 @@
     first, norm, stem = pl.pallas_call(
         functools.partial(stem_kernel, strips),
         out_shape=(
-            jax.ShapeDtypeStruct((336, 128), BF16),
+            jax.ShapeDtypeStruct((320, 128), BF16),
             jax.ShapeDtypeStruct((2, 8, 128), F32),
             window,
         ),
@@ -730,7 +729,7 @@
         in_specs=[ANY] + [VM] * 3,
         out_specs=(VM,) * 2,
         scratch_shapes=[
-            pltpu.VMEM((3, 32, 128), F32),
+            pltpu.VMEM((3, 24, 128), F32),
             pltpu.VMEM((16, 432), F32),
             pltpu.VMEM((256, 128), F32),
         ],

time: 37.5 us -> 37.4 us (level)
  no operation moved by 1% of the time
where the time goes in v9:
time: 37.4 us; the launch traced here: 37.2 us
  starting transfers between devices  18.7 us (50%)
  Pallas kernels  12.5 us (33%)
  waiting for transfers between devices  2.93 us (8%)
  between operations  2.15 us (6%)
  other arithmetic  0.84 us (2%)
    all_to_all x1, starting transfers between devices, body(): recv = lax.all_to_all(lines, ('strip', 'stream'), 0, 0, tiled=True)  7.3 us
    ppermute x4, starting transfers between devices, shifted(): lax.ppermute(value, axis, [(i, (i + by) % size) for i in range(size)])  6.26 us
    ppermute x6, starting transfers between devices, partner(): return lax.ppermute(value, axis, pairs)  5.17 us
    pallas_call x2, Pallas kernels, convolved(): pl.pallas_call(functools.partial(conv_kernel, strips, w0), out_shape=(jax...  3.67 us
    pallas_call x1, Pallas kernels, body(): pl.pallas_call(functools.partial(stem_kernel, strips), out_shape=(jax.Sha...  2.77 us
    ppermute x6, waiting for transfers between devices, partner(): return lax.ppermute(value, axis, pairs)  2.2 us
    pallas_call x1, Pallas kernels, body(): pl.pallas_call(functools.partial(sort_kernel, streams), out_shape=jax.Sha...  1.77 us
    pallas_call x1, Pallas kernels, body(): pl.pallas_call(down_kernel, out_shape=jax.ShapeDtypeStruct((4, 8, 8, 256)...  1.63 us
  transfers between devices with their start and end apart: 11, of which 5 were waited for; matrix products, arithmetic and copies ran while one was open for 0% of the time, Pallas kernels for 29%

profile of v9, /device:TPU:0, one launch (start us, length us, event | category | flops | bytes accessed | tf_op | source)
XLA Modules:
  0.0 37.2 jit_solution(17374195032140181390)
XLA Ops:
  0.6 0.0 copy-start
  0.6 0.0 copy-start.1
  0.7 0.0 copy-start.2
  0.7 0.0 copy-start.3
  0.7 0.0 copy-start.6
  0.7 0.0 copy-start.7
  0.7 1.8 %shard_map.156 = bf16[4,8,8,128]{3,2,1,0:T(8,128)(2,1)} custom-call(bf16[48,128]{1,0:T(8,128)(2,1)} %bitcast.31, s32[1,128]{1,0:T(1,128)} %owner_ref.1, s32[1,128]{1,0:T(1,128)} %slot_ref.1), custom_call_target="tpu_custom_call" | custom-call | flops 2000000000 | bytes 4194304 | tf_op jit(solution)/shard_map/pallas_call | solution.py:600
  2.5 7.3 %all-to-all-start = ((bf16[32,8,128]{2,1,0:T(8,128)(2,1)}), bf16[32,8,128]{2,1,0:T(8,128)(2,1)S(1)}, u32[]{:S(2)}, u32[]{:S(2)}) async-start(bf16[32,8,128]{2,1,0:T(8,128)(2,1)} %bitcast.30), calls=%async_computation | async-start | bytes 131072 | tf_op jit(solution)/shard_map/all_to_all | solution.py:612
  9.8 0.0 copy-done
  9.8 0.0 copy-done.1
  9.8 0.0 copy-done.2
  9.8 0.0 copy-done.3
  9.8 0.1 shard_map.157
  10.0 1.8 %collective-permute-start = (bf16[2,16,128]{2,1,0:T(8,128)(2,1)S(1)}, bf16[2,16,128]{2,1,0:T(8,128)(2,1)S(1)}, u32[]{:S(2)}, u32[]{:S(2)}) collective-permute-start(bf16[2,16,128]{2,1,0:T(8,128)(2,1)S(1)} %get-tuple-element.17), channel_id=1, source_target_pairs={{0,1},{1,2},{2,3},{3,0},{4,5},{5,6},{6,7},{7,4},{8,9},{9,10},{10,1... | collective-permute-start | bytes 24584 | tf_op jit(solution)/shard_map/ppermute | solution.py:570
  11.8 2.4 %collective-permute-start.2 = (bf16[2,16,128]{2,1,0:T(8,128)(2,1)S(1)}, bf16[2,16,128]{2,1,0:T(8,128)(2,1)S(1)}, u32[]{:S(2)}, u32[]{:S(2)}) collective-permute-start(bf16[2,16,128]{2,1,0:T(8,128)(2,1)S(1)} %get-tuple-element.19), channel_id=1, source_target_pairs={{0,2},{1,3},{2,0},{3,1},{4,6},{5,7},{6,4},{7,5},{8,10},{9,11},{10,... | collective-permute-start | bytes 24584 | tf_op jit(solution)/shard_map/ppermute | solution.py:570
  14.2 1.4 %collective-permute-start.1 = (bf16[4,16,128]{2,1,0:T(8,128)(2,1)S(1)}, bf16[4,16,128]{2,1,0:T(8,128)(2,1)S(1)}, u32[]{:S(2)}, u32[]{:S(2)}) collective-permute-start(bf16[4,16,128]{2,1,0:T(8,128)(2,1)S(1)} %get-tuple-element.18), channel_id=1, source_target_pairs={{0,3},{1,0},{2,1},{3,2},{4,7},{5,4},{6,5},{7,6},{8,11},{9,8},{10,9... | collective-permute-start | bytes 49160 | tf_op jit(solution)/shard_map/ppermute | solution.py:570
  15.6 0.6 %collective-permute-start.4 = (bf16[6,16,128]{2,1,0:T(8,128)(2,1)S(1)}, bf16[6,16,128]{2,1,0:T(8,128)(2,1)S(1)}, u32[]{:S(2)}, u32[]{:S(2)}) collective-permute-start(bf16[6,16,128]{2,1,0:T(8,128)(2,1)S(1)} %get-tuple-element.24), channel_id=1, source_target_pairs={{0,1},{1,2},{2,3},{3,0},{4,5},{5,6},{6,7},{7,4},{8,9},{9,10},{10,1... | collective-permute-start | bytes 73736 | tf_op jit(solution)/shard_map/ppermute | solution.py:570
  17.5 0.1 pad_add_fusion.scalars_ref
  17.6 0.0 collective-permute-done.below_ref
  17.6 0.0 collective-permute-done.2.mid_ref
  17.6 0.3 collective-permute-done.1.above_ref
  17.9 0.0 all-to-all-done
  17.9 0.0 copy-done.6
  17.9 0.0 copy-done.7
  17.9 0.0 copy-start.5
  18.0 2.8 %shard_map.158 = (bf16[320,128]{1,0:T(8,128)(2,1)S(1)}, f32[2,8,128]{2,1,0:T(8,128)S(1)}, f32[2,16,11,8,128]{4,3,2,1,0:T(8,128)S(1)}) custom-call(s32[128]{0:T(128)S(1)} %pad_add_fusion.scalars_ref, f32[128]{0:T(128)S(1)} %copy-done.6, f32[128]{0:T(128)S(1)} %copy-done.7, bf16[4,64,128]{2,1,0:T(8,128)(2,1)S(1)} %bitcast.26, bf16[2,16,48]{2,1,0:T(8,128)(2,1)S(1)} %bitcast.28, ...), custom_call_target="tpu_custom_call" | custom-call | flops 2000000000 | bytes 4194304 | tf_op jit(solution)/shard_map/pallas_call | solution.py:635
  20.7 0.1 collective-permute-start.3
  20.8 0.4 %collective-permute-done.4.below_ref = bf16[6,16,128]{2,1,0:T(8,128)(2,1)S(1)} collective-permute-done((bf16[6,16,128]{2,1,0:T(8,128)(2,1)S(1)}, bf16[6,16,128]{2,1,0:T(8,128)(2,1)S(1)}, u32[]{:S(2)}, u32[]{:S(2)}) %collective-permute-start.4) | collective-permute-done | bytes 24608 | tf_op jit(solution)/shard_map/ppermute | solution.py:570
  21.2 0.0 copy-done.5
  21.2 1.3 %shard_map.159.value_ref = f32[32,16,128]{2,1,0:T(8,128)S(1)} custom-call(s32[128]{0:T(128)S(1)} %pad_add_fusion.scalars_ref, f32[2,8,128]{2,1,0:T(8,128)S(1)} %get-tuple-element.22.norm_ref, f32[2,16,11,8,128]{4,3,2,1,0:T(8,128)S(1)} %get-tuple-element.23.stem, bf16[2,16,16,128]{3,2,1,0:T(8,128)(2,1)S(1)} %bitcast.20, ...), custom_call_target="tpu_custom_call" | custom-call | flops 2000000000 | bytes 4194304 | tf_op jit(solution)/shard_map/pallas_call | solution.py:663
  22.5 0.0 collective-permute-done.3
  22.6 0.2 collective-permute-start.5
  22.7 1.5 %collective-permute-start.6 = (bf16[320,128]{1,0:T(8,128)(2,1)S(1)}, bf16[320,128]{1,0:T(8,128)(2,1)S(1)}, u32[]{:S(2)}, u32[]{:S(2)}) collective-permute-start(bf16[320,128]{1,0:T(8,128)(2,1)S(1)} %broadcast_select_fusion.4.after_ref), channel_id=1, source_target_pairs={{0,8},{4,12},{8,0},{12,4},{16,24},{20,28},{24,16},{28,20},{1,9},{5... | collective-permute-start | bytes 245768 | tf_op jit(solution)/shard_map/ppermute | solution.py:565
  24.2 0.0 collective-permute-done.5
  24.2 1.3 %collective-permute-start.7 = (bf16[512,128]{1,0:T(8,128)(2,1)S(1)}, bf16[512,128]{1,0:T(8,128)(2,1)S(1)}, u32[]{:S(2)}, u32[]{:S(2)}) collective-permute-start(bf16[512,128]{1,0:T(8,128)(2,1)S(1)} %broadcast_select_fusion.2.after_too_ref), channel_id=1, source_target_pairs={{0,8},{4,12},{8,0},{12,4},{16,24},{20,28},{24,16},{28,20},{1,9},{5... | collective-permute-start | bytes 393224 | tf_op jit(solution)/shard_map/ppermute | solution.py:565
  25.5 1.6 %shard_map.161 = (bf16[8,9,16,128]{3,2,1,0:T(8,128)(2,1)S(1)}, bf16[16,128]{1,0:T(8,128)(2,1)S(1)}) custom-call(bf16[320,128]{1,0:T(8,128)(2,1)S(1)} %broadcast_select_fusion.4.after_ref, bf16[512,128]{1,0:T(8,128)(2,1)S(1)} %broadcast_select_fusion.2.after_too_ref, f32[2,8,128]{2,1,0:T(8,128)S(1)} %get-tuple-element.22.norm_ref, ...), custom_call_target="tpu_custom_call" | custom-call | flops 2000000000 | bytes 4194304 | tf_op jit(solution)/shard_map/pallas_call | solution.py:683
  27.2 0.8 %collective-permute-done.6 = bf16[320,128]{1,0:T(8,128)(2,1)S(1)} collective-permute-done((bf16[320,128]{1,0:T(8,128)(2,1)S(1)}, bf16[320,128]{1,0:T(8,128)(2,1)S(1)}, u32[]{:S(2)}, u32[]{:S(2)}) %collective-permute-start.6) | collective-permute-done | bytes 81952 | tf_op jit(solution)/shard_map/ppermute | solution.py:565
  28.0 1.4 %collective-permute-start.8 = (bf16[320,128]{1,0:T(8,128)(2,1)S(1)}, bf16[320,128]{1,0:T(8,128)(2,1)S(1)}, u32[]{:S(2)}, u32[]{:S(2)}) collective-permute-start(bf16[320,128]{1,0:T(8,128)(2,1)S(1)} %broadcast_select_fusion.3.after_ref.first_ref), channel_id=1, source_target_pairs={{0,16},{4,20},{8,24},{12,28},{16,0},{20,4},{24,8},{28,12},{1,17},{... | collective-permute-start | bytes 245768 | tf_op jit(solution)/shard_map/ppermute | solution.py:565
  29.4 2.0 %shard_map.162 = (bf16[8,9,16,128]{3,2,1,0:T(8,128)(2,1)S(1)}, bf16[16,128]{1,0:T(8,128)(2,1)}) custom-call(bf16[320,128]{1,0:T(8,128)(2,1)S(1)} %broadcast_select_fusion.3.after_ref.first_ref, bf16[8,9,16,128]{3,2,1,0:T(8,128)(2,1)S(1)} %get-tuple-element.25.after_too_ref.part_ref, f32[2,8,128]{2,1,0:T(8,128)S(1)} %get-tuple-element.22.norm_ref, ...), custom_call_target="tpu_custom_call" | custom-call | flops 2000000000 | bytes 4194304 | tf_op jit(solution)/shard_map/pallas_call | solution.py:683
  31.4 0.0 collective-permute-done.7
  31.4 0.0 copy-start.4
  31.5 0.8 %collective-permute-start.9 = (bf16[512,128]{1,0:T(8,128)(2,1)S(1)}, bf16[512,128]{1,0:T(8,128)(2,1)S(1)}, u32[]{:S(2)}, u32[]{:S(2)}) collective-permute-start(bf16[512,128]{1,0:T(8,128)(2,1)S(1)} %broadcast_select_fusion.1.after_ref), channel_id=1, source_target_pairs={{0,16},{4,20},{8,24},{12,28},{16,0},{20,4},{24,8},{28,12},{1,17},{... | collective-permute-start | bytes 393224 | tf_op jit(solution)/shard_map/ppermute | solution.py:565
  32.3 0.3 collective-permute-done.8.first_in_ref
  32.5 1.2 %shard_map.164 = (bf16[2,16,48]{2,1,0:T(8,128)(2,1)}, bf16[2,16,16,128]{3,2,1,0:T(8,128)(2,1)}) custom-call(bf16[512,128]{1,0:T(8,128)(2,1)S(1)} %broadcast_select_fusion.1.after_ref, bf16[320,128]{1,0:T(8,128)(2,1)S(1)} %broadcast_select_fusion.3.after_ref.first_ref, bf16[320,128]{1,0:T(8,128)(2,1)S(1)} %collective-permute-done.8.first_in_ref, ...), custom_call_target="tpu_custom_call" | custom-call | flops 2000000000 | bytes 4194304 | tf_op jit(solution)/shard_map/pallas_call | solution.py:723
  33.8 0.0 copy-done.4
  33.8 1.6 %shard_map.163 = bf16[4,8,8,256]{3,2,1,0:T(8,128)(2,1)} custom-call(s32[128]{0:T(128)S(1)} %pad_add_fusion.scalars_ref, bf16[8,9,16,128]{3,2,1,0:T(8,128)(2,1)S(1)} %get-tuple-element.25.after_too_ref.part_ref, bf16[8,9,16,128]{3,2,1,0:T(8,128)(2,1)S(1)} %get-tuple-element.27.rest_ref, bf16[3,3,3,128,256]{4,3,2,1,0:T(8,128)(2,1)S(1)} %copy-done.4, ...), custom_call_target="tpu_custom_call" | custom-call | flops 2000000000 | bytes 4194304 | tf_op jit(solution)/shard_map/pallas_call | solution.py:707
  35.4 1.1 %collective-permute-done.9 = bf16[512,128]{1,0:T(8,128)(2,1)S(1)} collective-permute-done((bf16[512,128]{1,0:T(8,128)(2,1)S(1)}, bf16[512,128]{1,0:T(8,128)(2,1)S(1)}, u32[]{:S(2)}, u32[]{:S(2)}) %collective-permute-start.9) | collective-permute-done | bytes 131104 | tf_op jit(solution)/shard_map/ppermute | solution.py:565
  36.5 0.7 %broadcast_select_fusion = bf16[512,128]{1,0:T(8,128)(2,1)} fusion(bf16[512,128]{1,0:T(8,128)(2,1)S(1)} %broadcast_select_fusion.1.after_ref, bf16[512,128]{1,0:T(8,128)(2,1)S(1)} %collective-permute-done.9, pred[128]{0:T(512)(128)(4,1)S(1)} %compare_bitcast_fusion), kind=kLoop, calls=%fused_computation | loop fusion | flops 65536 | bytes 393344 | tf_op jit(solution)/shard_map/jit(_where)/select_n | solution.py:661
  (9 shorter events, 0.1 us)
Async XLA Ops:
  0.6 9.1 %copy-start = (bf16[1,2,16,16,128]{4,3,2,1,0:T(8,128)(2,1)S(1)}, bf16[1,2,16,16,128]{4,3,2,1,0:T(8,128)(2,1)}, u32[]{:S(2)}) copy-start(bf16[1,2,16,16,128]{4,3,2,1,0:T(8,128)(2,1)} %param.19) | copy-start | bytes 393220
  0.6 9.1 %copy-start.1 = (bf16[1,2,16,16,128]{4,3,2,1,0:T(8,128)(2,1)S(1)}, bf16[1,2,16,16,128]{4,3,2,1,0:T(8,128)(2,1)}, u32[]{:S(2)}) copy-start(bf16[1,2,16,16,128]{4,3,2,1,0:T(8,128)(2,1)} %param.20) | copy-start | bytes 393220
  0.7 9.1 %copy-start.2 = (bf16[3,3,3,3,128]{4,3,2,1,0:T(4,128)(2,1)S(1)}, bf16[3,3,3,3,128]{4,3,2,1,0:T(4,128)(2,1)}, u32[]{:S(2)}) copy-start(bf16[3,3,3,3,128]{4,3,2,1,0:T(4,128)(2,1)} %sw_ref.1) | copy-start | bytes 62212
  0.7 9.1 %copy-start.3 = (bf16[1,2,16,48]{3,2,1,0:T(8,128)(2,1)S(1)}, bf16[1,2,16,48]{3,2,1,0:T(8,128)(2,1)}, u32[]{:S(2)}) copy-start(bf16[1,2,16,48]{3,2,1,0:T(8,128)(2,1)} %param.18) | copy-start | bytes 9220
  0.7 17.3 %copy-start.6 = (f32[128]{0:T(128)S(1)}, f32[128]{0:T(128)}, u32[]{:S(2)}) copy-start(f32[128]{0:T(128)} %gain_ref.1) | copy-start | bytes 1540
  0.7 17.3 %copy-start.7 = (f32[128]{0:T(128)S(1)}, f32[128]{0:T(128)}, u32[]{:S(2)}) copy-start(f32[128]{0:T(128)} %bias_ref.1) | copy-start | bytes 1540
  2.5 15.5 %all-to-all-start = ((bf16[32,8,128]{2,1,0:T(8,128)(2,1)}), bf16[32,8,128]{2,1,0:T(8,128)(2,1)S(1)}, u32[]{:S(2)}, u32[]{:S(2)}) async-start(bf16[32,8,128]{2,1,0:T(8,128)(2,1)} %bitcast.30), calls=%async_computation | async-start | bytes 131072 | tf_op jit(solution)/shard_map/all_to_all | solution.py:612
  10.0 7.7 %collective-permute-start = (bf16[2,16,128]{2,1,0:T(8,128)(2,1)S(1)}, bf16[2,16,128]{2,1,0:T(8,128)(2,1)S(1)}, u32[]{:S(2)}, u32[]{:S(2)}) collective-permute-start(bf16[2,16,128]{2,1,0:T(8,128)(2,1)S(1)} %get-tuple-element.17), channel_id=1, source_target_pairs={{0,1},{1,2},{2,3},{3,0},{4,5},{5,6},{6,7},{7,4},{8,9},{9,10},{10,1... | collective-permute-start | bytes 24584 | tf_op jit(solution)/shard_map/ppermute | solution.py:570
  11.8 5.8 %collective-permute-start.2 = (bf16[2,16,128]{2,1,0:T(8,128)(2,1)S(1)}, bf16[2,16,128]{2,1,0:T(8,128)(2,1)S(1)}, u32[]{:S(2)}, u32[]{:S(2)}) collective-permute-start(bf16[2,16,128]{2,1,0:T(8,128)(2,1)S(1)} %get-tuple-element.19), channel_id=1, source_target_pairs={{0,2},{1,3},{2,0},{3,1},{4,6},{5,7},{6,4},{7,5},{8,10},{9,11},{10,... | collective-permute-start | bytes 24584 | tf_op jit(solution)/shard_map/ppermute | solution.py:570
  14.2 3.7 %collective-permute-start.1 = (bf16[4,16,128]{2,1,0:T(8,128)(2,1)S(1)}, bf16[4,16,128]{2,1,0:T(8,128)(2,1)S(1)}, u32[]{:S(2)}, u32[]{:S(2)}) collective-permute-start(bf16[4,16,128]{2,1,0:T(8,128)(2,1)S(1)} %get-tuple-element.18), channel_id=1, source_target_pairs={{0,3},{1,0},{2,1},{3,2},{4,7},{5,4},{6,5},{7,6},{8,11},{9,8},{10,9... | collective-permute-start | bytes 49160 | tf_op jit(solution)/shard_map/ppermute | solution.py:570
  15.6 5.6 %collective-permute-start.4 = (bf16[6,16,128]{2,1,0:T(8,128)(2,1)S(1)}, bf16[6,16,128]{2,1,0:T(8,128)(2,1)S(1)}, u32[]{:S(2)}, u32[]{:S(2)}) collective-permute-start(bf16[6,16,128]{2,1,0:T(8,128)(2,1)S(1)} %get-tuple-element.24), channel_id=1, source_target_pairs={{0,1},{1,2},{2,3},{3,0},{4,5},{5,6},{6,7},{7,4},{8,9},{9,10},{10,1... | collective-permute-start | bytes 73736 | tf_op jit(solution)/shard_map/ppermute | solution.py:570
  17.9 3.3 %copy-start.5 = (bf16[3,3,3,128,128]{4,3,2,1,0:T(8,128)(2,1)S(1)}, bf16[3,3,3,128,128]{4,3,2,1,0:T(8,128)(2,1)}, u32[]{:S(2)}) copy-start(bf16[3,3,3,128,128]{4,3,2,1,0:T(8,128)(2,1)} %conv_ref.5) | copy-start | bytes 2654212
  20.7 1.8 %collective-permute-start.3 = (bf16[320,128]{1,0:T(8,128)(2,1)S(1)}, bf16[320,128]{1,0:T(8,128)(2,1)S(1)}, u32[]{:S(2)}, u32[]{:S(2)}) collective-permute-start(bf16[320,128]{1,0:T(8,128)(2,1)S(1)} %get-tuple-element.21), channel_id=1, source_target_pairs={{0,4},{4,0},{8,12},{12,8},{16,20},{20,16},{24,28},{28,24},{1,5},{5... | collective-permute-start | bytes 245768 | tf_op jit(solution)/shard_map/ppermute | solution.py:565
  22.6 1.6 %collective-permute-start.5 = (bf16[512,128]{1,0:T(8,128)(2,1)S(1)}, bf16[512,128]{1,0:T(8,128)(2,1)S(1)}, u32[]{:S(2)}, u32[]{:S(2)}) collective-permute-start(bf16[512,128]{1,0:T(8,128)(2,1)S(1)} %shard_map.160), channel_id=1, source_target_pairs={{0,4},{4,0},{8,12},{12,8},{16,20},{20,16},{24,28},{28,24},{1,5},{5... | collective-permute-start | bytes 393224 | tf_op jit(solution)/shard_map/ppermute | solution.py:565
  22.7 5.3 %collective-permute-start.6 = (bf16[320,128]{1,0:T(8,128)(2,1)S(1)}, bf16[320,128]{1,0:T(8,128)(2,1)S(1)}, u32[]{:S(2)}, u32[]{:S(2)}) collective-permute-start(bf16[320,128]{1,0:T(8,128)(2,1)S(1)} %broadcast_select_fusion.4.after_ref), channel_id=1, source_target_pairs={{0,8},{4,12},{8,0},{12,4},{16,24},{20,28},{24,16},{28,20},{1,9},{5... | collective-permute-start | bytes 245768 | tf_op jit(solution)/shard_map/ppermute | solution.py:565
  24.2 7.2 %collective-permute-start.7 = (bf16[512,128]{1,0:T(8,128)(2,1)S(1)}, bf16[512,128]{1,0:T(8,128)(2,1)S(1)}, u32[]{:S(2)}, u32[]{:S(2)}) collective-permute-start(bf16[512,128]{1,0:T(8,128)(2,1)S(1)} %broadcast_select_fusion.2.after_too_ref), channel_id=1, source_target_pairs={{0,8},{4,12},{8,0},{12,4},{16,24},{20,28},{24,16},{28,20},{1,9},{5... | collective-permute-start | bytes 393224 | tf_op jit(solution)/shard_map/ppermute | solution.py:565
  28.0 4.5 %collective-permute-start.8 = (bf16[320,128]{1,0:T(8,128)(2,1)S(1)}, bf16[320,128]{1,0:T(8,128)(2,1)S(1)}, u32[]{:S(2)}, u32[]{:S(2)}) collective-permute-start(bf16[320,128]{1,0:T(8,128)(2,1)S(1)} %broadcast_select_fusion.3.after_ref.first_ref), channel_id=1, source_target_pairs={{0,16},{4,20},{8,24},{12,28},{16,0},{20,4},{24,8},{28,12},{1,17},{... | collective-permute-start | bytes 245768 | tf_op jit(solution)/shard_map/ppermute | solution.py:565
  31.4 2.3 %copy-start.4 = (bf16[3,3,3,128,256]{4,3,2,1,0:T(8,128)(2,1)S(1)}, bf16[3,3,3,128,256]{4,3,2,1,0:T(8,128)(2,1)}, u32[]{:S(2)}) copy-start(bf16[3,3,3,128,256]{4,3,2,1,0:T(8,128)(2,1)} %down_ref.1) | copy-start | bytes 5308420
  31.5 5.0 %collective-permute-start.9 = (bf16[512,128]{1,0:T(8,128)(2,1)S(1)}, bf16[512,128]{1,0:T(8,128)(2,1)S(1)}, u32[]{:S(2)}, u32[]{:S(2)}) collective-permute-start(bf16[512,128]{1,0:T(8,128)(2,1)S(1)} %broadcast_select_fusion.1.after_ref), channel_id=1, source_target_pairs={{0,16},{4,20},{8,24},{12,28},{16,0},{20,4},{24,8},{28,12},{1,17},{... | collective-permute-start | bytes 393224 | tf_op jit(solution)/shard_map/ppermute | solution.py:565
